TPU v7x, 32 devices: a whole 2x2x4 slice. The times are simulated.
32 devices in a mesh: clip: 8 (over y, x, core), seq: 4 (over z).
Axes of the slice: x: 2, y: 2, z: 4, core: 2. Of those that a mesh axis runs over, the one named last changes fastest.
Arguments:
- frames: bfloat16 [8, 4, 16, 16, 320], P('clip', 'seq'), may hold values from -6 to 6
- cotangent: bfloat16 [8, 4, 16, 16, 320], P('clip', 'seq'), may hold values from -6 to 6
- w_space: bfloat16 [320, 9, 320], P('seq'), may hold values from -0.109375 to 0.109375
- w_time: bfloat16 [3, 320, 320], replicated, may hold values from -0.1875 to 0.1875
Outputs:
- frames_grad: bfloat16 [8, 4, 16, 16, 320], P('clip', 'seq')
- space_grad: float32 [320, 9, 320], P('seq')
- time_grad: float32 [3, 320, 320], replicated
All inputs are finite; a program needn't handle non-finite values.
Results may differ from a plain program's by a relative error of at most 0.0085.
Values may be sent and summed in bfloat16 or wider, within the bound.
No kernel may reach another device: no remote copies, remote signals or barrier semaphores. Data moves between devices by JAX's collectives and lax.ppermute only.
A program may use at most 64 MiB of HBM per device.

v0:
```python
import math

import jax
import jax.numpy as jnp
from jax import lax
from jax.sharding import PartitionSpec as P


def padded_2(cells, sides, width):
    for axis, dim in sides:
        count = lax.axis_size(axis)
        ends = count - 1
        head = lax.slice_in_dim(cells, 0, width, axis=dim)
        tail = lax.slice_in_dim(cells, cells.shape[dim] - width, cells.shape[dim], axis=dim)
        cells = jnp.concatenate(
            [
                lax.ppermute(tail, axis, [(i, (i + 1) % count) for i in range(ends)]),
                cells,
                lax.ppermute(head, axis, [((i + 1) % count, i) for i in range(ends)]),
            ],
            axis=dim,
        )
    return cells


def temporal_grads(acts, g_pad, w_time):
    count = acts.shape[0]
    chans = acts.shape[-1]
    flat_acts = acts.reshape(-1, chans)
    act_grad = jnp.zeros(flat_acts.shape, jnp.float32)
    time_terms = []
    for k in range(3):
        shifted = g_pad[2 - k : 2 - k + count].reshape(-1, chans)
        act_grad = act_grad + lax.dot_general(
            shifted, w_time[k], (((1,), (1,)), ((), ())), preferred_element_type=jnp.float32
        )
        time_terms.append(
            lax.dot_general(
                flat_acts, shifted, (((0,), (0,)), ((), ())), preferred_element_type=jnp.float32
            )
        )
    return (act_grad.astype(jnp.bfloat16).reshape(acts.shape), jnp.stack(time_terms, axis=0))


def per_device(frames, cotangent, w_space, w_time):
    weights = lax.all_gather(w_space, "seq", axis=0, tiled=True)
    clip_x = frames[0]
    clip_g = cotangent[0]
    count, height, width, chans = clip_x.shape
    factor = 1.0 / math.sqrt(lax.axis_size("clip") * count * lax.axis_size("seq") * height * width)
    padded = jnp.pad(clip_x, ((0, 0), (1, 1), (1, 1), (0, 0)))
    pieces = [
        padded[:, i : i + height, j : j + width, :].reshape(-1, chans)
        for i in range(3)
        for j in range(3)
    ]
    pre_act = jnp.zeros((count * height * width, chans), jnp.float32)
    for tap in range(9):
        pre_act = pre_act + jnp.dot(
            pieces[tap], weights[:, tap, :], preferred_element_type=jnp.float32
        )
    acts = jax.nn.silu(pre_act).astype(jnp.bfloat16).reshape(1, count, height, width, chans)
    g_rims = padded_2(cotangent, (("seq", 1),), 1)
    g_pad = g_rims[0].reshape(count + 2, height * width, chans)
    act_grad, time_terms = temporal_grads(
        acts[0].reshape(count, height * width, chans), g_pad, w_time
    )
    sigma = jax.nn.sigmoid(pre_act)
    pre_grad = (
        act_grad.reshape(-1, chans).astype(jnp.float32) * sigma * (1.0 + pre_act * (1.0 - sigma))
    ).astype(jnp.bfloat16)
    terms = []
    for tap in range(9):
        part = pieces[tap]
        terms.append(
            lax.dot_general(
                part, pre_grad, (((0,), (0,)), ((), ())), preferred_element_type=jnp.float32
            )
        )
    space_share = lax.psum_scatter(
        jnp.stack(terms, axis=1) * factor, "seq", scatter_dimension=0, tiled=True
    )
    space_grad = lax.psum(space_share, "clip")
    time_grad = lax.psum(time_terms * factor, ("clip", "seq"))
    grad_pad = jnp.pad(
        pre_grad.reshape(count, height, width, chans), ((0, 0), (1, 1), (1, 1), (0, 0))
    )
    input_grad = clip_g.reshape(-1, chans).astype(jnp.float32)
    for i in range(3):
        for j in range(3):
            piece = grad_pad[:, 2 - i : 2 - i + height, 2 - j : 2 - j + width, :].reshape(-1, chans)
            input_grad = input_grad + lax.dot_general(
                piece,
                weights[:, 3 * i + j, :],
                (((1,), (1,)), ((), ())),
                preferred_element_type=jnp.float32,
            )
    frames_grad = input_grad.astype(jnp.bfloat16).reshape(1, count, height, width, chans)
    return (frames_grad, space_grad, time_grad)


def solution(mesh):
    in_specs = (
        P("clip", "seq", None, None, None),
        P("clip", "seq", None, None, None),
        P("seq", None, None),
        P(),
    )
    out_specs = (P("clip", "seq", None, None, None), P("seq", None, None), P())
    return jax.shard_map(
        per_device, mesh=mesh, in_specs=in_specs, out_specs=out_specs, check_vma=False
    )
```

profile of v0, /device:TPU:0, one launch (start us, length us, event | category | flops | bytes accessed | tf_op | source)
XLA Modules:
  0.0 361.0 jit_solution(12757745852941347413)
XLA Ops:
  7.2 0.7 all-gather.2.cloned.1.call-update
  7.9 4.9 %collective-permute-start.1 = (bf16[1,1,16,16,320]{4,3,2,1,0:T(8,128)(2,1)}, bf16[1,1,16,16,320]{4,3,2,1,0:T(8,128)(2,1)S(1)}, u32[]{:S(2)}, u32[]{:S(2)}) collective-permute-start(bf16[1,1,16,16,320]{4,3,2,1,0:T(8,128)(2,1)} %param.5), channel_id=1, source_target_pairs={{0,1},{1,2},{2,3},{4,5},{5,6},{6,7},{8,9},{9,10},{10,11},{12,13},{... | collective-permute-start | bytes 491528 | tf_op jit(solution)/shard_map/ppermute | solution.py:17
  12.9 1.3 collective-permute-start
  14.2 2.0 fusion.19
  16.2 3.4 pad_slice_fusion.8
  19.7 2.0 fusion.17
  21.7 38.6 %all-gather.2.cloned.1.call-done = bf16[320,9,320]{2,0,1:T(8,128)(2,1)} async-done(((bf16[80,9,320]{2,0,1:T(8,128)(2,1)}), bf16[320,9,320]{2,0,1:T(8,128)(2,1)}) %all-gather.2.cloned.1.call-update) | async-done | bytes 1843216 | tf_op jit(solution)/shard_map/all_gather | solution.py:46
  60.3 1.4 fusion.25
  61.7 1.3 convolution_add_fusion.15
  63.0 1.3 convolution_add_fusion.14
  64.4 0.3 convolution_add_fusion.13
  64.7 0.3 convolution_add_fusion.12
  65.1 0.3 convolution_add_fusion.11
  65.4 0.3 convolution_add_fusion.10
  65.7 0.3 convolution_add_fusion.9
  66.0 0.3 convolution_add_fusion.8
  66.3 1.5 fusion.16
  67.8 0.3 fusion.8
  68.1 0.3 fusion.7
  68.4 0.3 fusion.6
  68.8 0.3 fusion.5
  69.0 0.3 fusion.4
  69.3 0.3 fusion.3
  69.6 0.3 fusion.2
  69.9 0.3 fusion.1
  70.2 0.3 fusion
  70.5 2.4 broadcast_multiply_fusion
  73.0 0.8 copy-done.6
  73.8 0.8 copy.10
  74.8 0.3 convolution_bitcast_fusion
  75.1 0.3 convolution_bitcast_fusion.1
  75.4 1.2 convolution_bitcast_fusion.2
  76.6 1.3 maximum_multiply_fusion
  77.8 0.9 pad_slice_fusion
  78.8 1.2 convolution_add_fusion.7
  80.0 1.2 convolution_add_fusion.6
  81.3 0.3 convolution_add_fusion.5
  81.5 0.3 convolution_add_fusion.4
  81.8 0.3 fusion.26
  82.4 0.3 convolution_add_fusion.3
  82.6 69.8 %reduce-scatter.2.cloned.1.call-done = f32[80,9,320]{2,0,1:T(8,128)} async-done(((f32[320,9,320]{2,0,1:T(8,128)}), f32[80,9,320]{2,0,1:T(8,128)}) %reduce-scatter.2.cloned.1.call-update) | async-done | bytes 921616 | tf_op jit(solution)/shard_map/reduce_scatter | solution.py:80
  152.5 0.3 convolution_add_fusion.2
  152.7 0.3 fusion.15
  153.0 0.8 copy.12
  153.8 136.9 %all-reduce.7.cloned.1.call-done = f32[3,320,320]{2,1,0:T(8,128)} async-done(((f32[3,320,320]{2,1,0:T(8,128)}), f32[3,320,320]{2,1,0:T(8,128)}) %all-reduce.7.cloned.1.call-update) | async-done | bytes 1228816 | tf_op jit(solution)/shard_map/psum | solution.py:84
  290.8 60.3 %all-reduce.5.cloned.1.call-done = f32[80,9,320]{2,0,1:T(8,128)} async-done(((f32[80,9,320]{2,0,1:T(8,128)}), f32[80,9,320]{2,0,1:T(8,128)}) %all-reduce.5.cloned.1.call-update) | async-done | bytes 921616 | tf_op jit(solution)/shard_map/psum | solution.py:83
  351.1 2.3 copy.25
  353.4 1.1 copy.26
  (40 shorter events, 0.7 us)
Async XLA Ops:
  7.2 53.1 %all-gather.2.cloned.1.call-start = ((), (), s32[]{:S(2)}) async-start(), calls=%async_computation.1 | async-start | bytes 2764800 | tf_op jit(solution)/shard_map/all_gather | solution.py:46
  7.9 144.5 %reduce-scatter.2.cloned.1.call-start = ((), (), s32[]{:S(2)}) async-start(), calls=%async_computation.2 | async-start | bytes 5529600 | tf_op jit(solution)/shard_map/reduce_scatter | solution.py:80
  7.9 11.7 %collective-permute-start.1 = (bf16[1,1,16,16,320]{4,3,2,1,0:T(8,128)(2,1)}, bf16[1,1,16,16,320]{4,3,2,1,0:T(8,128)(2,1)S(1)}, u32[]{:S(2)}, u32[]{:S(2)}) collective-permute-start(bf16[1,1,16,16,320]{4,3,2,1,0:T(8,128)(2,1)} %param.5), channel_id=1, source_target_pairs={{0,1},{1,2},{2,3},{4,5},{5,6},{6,7},{8,9},{9,10},{10,11},{12,13},{... | collective-permute-start | bytes 491528 | tf_op jit(solution)/shard_map/ppermute | solution.py:17
  12.9 53.4 %collective-permute-start = (bf16[1,1,16,16,320]{4,3,2,1,0:T(8,128)(2,1)}, bf16[1,1,16,16,320]{4,3,2,1,0:T(8,128)(2,1)}, u32[]{:S(2)}, u32[]{:S(2)}) collective-permute-start(bf16[1,1,16,16,320]{4,3,2,1,0:T(8,128)(2,1)} %param.5), channel_id=1, source_target_pairs={{1,0},{2,1},{3,2},{5,4},{6,5},{7,6},{9,8},{10,9},{11,10},{13,12},{... | collective-permute-start | bytes 491528 | tf_op jit(solution)/shard_map/ppermute | solution.py:19
  19.7 2.0 copy-start.13
  21.7 43.0 %copy-start.1 = (bf16[1,1,16,16,320]{4,3,2,1,0:T(8,128)(2,1)S(1)}, bf16[1,1,16,16,320]{4,3,2,1,0:T(8,128)(2,1)}, u32[]{:S(2)}) copy-start(bf16[1,1,16,16,320]{4,3,2,1,0:T(8,128)(2,1)} %param.4) | copy-start | bytes 491524
  60.3 4.1 %copy-start = (bf16[320,9,320]{2,0,1:T(8,128)(2,1)S(1)}, bf16[320,9,320]{2,0,1:T(8,128)(2,1)}, u32[]{:S(2)}) copy-start(bf16[320,9,320]{2,0,1:T(8,128)(2,1)} %all-gather.2.cloned.1.call-done) | copy-start | bytes 5529604
  60.3 4.1 %copy-start.2 = (bf16[1,16,16,320]{3,2,1,0:T(8,128)(2,1)S(1)}, bf16[1,16,16,320]{3,2,1,0:T(8,128)(2,1)}, u32[]{:S(2)}) copy-start(bf16[1,16,16,320]{3,2,1,0:T(8,128)(2,1)} %get-tuple-element.17) | copy-start | bytes 491524
  65.0 1.3 copy-start.11
  65.0 1.3 copy-start.12
  66.0 2.2 copy-start.4
  66.3 2.5 copy-start.9
  66.3 2.2 copy-start.3
  72.9 0.9 copy-start.6
  72.9 1.9 copy-start.10
  72.9 1.9 copy-start.14
  72.9 217.8 %all-reduce.7.cloned.1.call-start = ((), (), s32[]{:S(2)}) async-start(), calls=%async_computation.4 | async-start | bytes 2949120 | tf_op jit(solution)/shard_map/psum | solution.py:84
  78.7 2.8 copy-start.8
  78.8 272.3 %all-reduce.5.cloned.1.call-start = ((), (), s32[]{:S(2)}) async-start(), calls=%async_computation.3 | async-start | bytes 2211840 | tf_op jit(solution)/shard_map/psum | solution.py:83
  81.2 1.1 copy-start.7
  290.8 62.6 %copy-start.5 = (f32[3,320,320]{2,1,0:T(8,128)S(1)}, f32[3,320,320]{2,1,0:T(8,128)}, u32[]{:S(2)}) copy-start(f32[3,320,320]{2,1,0:T(8,128)} %all-reduce.7.cloned.1.call-done) | copy-start | bytes 3686404
Sparse Core Ops, SparseCore 0:
  9.6 50.6 all-gather.1
  73.1 79.3 reduce-scatter.1
  159.2 131.4 all-reduce.6
  294.2 56.8 all-reduce.4
where the time goes:
time: 361 us
  waiting for transfers between devices  306 us (85%)
  matrix products  20 us (6%)
  between operations  14.2 us (4%)
  local copies, waits for them, and re-layouts  10.5 us (3%)
  starting transfers between devices  6.39 us (2%)
  other arithmetic  3.67 us (1%)
    psum x1, waiting for transfers between devices, per_device(): time_grad = lax.psum(time_terms * factor, ('clip', 'seq'))  137 us
    reduce_scatter x1, waiting for transfers between devices, per_device(): lax.psum_scatter(jnp.stack(terms, axis=1) * factor, 'seq', scatter_dimens...  69.8 us
    psum x1, waiting for transfers between devices, per_device(): space_grad = lax.psum(space_share, 'clip')  60.3 us
    all_gather x1, waiting for transfers between devices, per_device(): weights = lax.all_gather(w_space, 'seq', axis=0, tiled=True)  38.6 us
  transfers between devices with their start and end apart: 6, of which 4 were waited for; matrix products, arithmetic and copies ran while one was open for 6% of the time, Pallas kernels for 0%

commit v1 on v0

--- a/solution.py
+++ b/solution.py
@@ -1,8 +1,11 @@
+import functools
 import math
 
 import jax
 import jax.numpy as jnp
 from jax import lax
+from jax.experimental import pallas as pl
+from jax.experimental.pallas import tpu as pltpu
 from jax.sharding import PartitionSpec as P
 
 
@@ -42,7 +45,7 @@
     return (act_grad.astype(jnp.bfloat16).reshape(acts.shape), jnp.stack(time_terms, axis=0))
 
 
-def per_device(frames, cotangent, w_space, w_time):
+def per_device_general(frames, cotangent, w_space, w_time):
     weights = lax.all_gather(w_space, "seq", axis=0, tiled=True)
     clip_x = frames[0]
     clip_g = cotangent[0]
@@ -99,6 +102,353 @@
     return (frames_grad, space_grad, time_grad)
 
 
+BF16 = jnp.bfloat16
+F32 = jnp.float32
+LANES = 128
+VMEM = pl.BlockSpec(memory_space=pltpu.VMEM)
+NN = (((1,), (0,)), ((), ()))
+NT = (((1,), (1,)), ((), ()))
+TN = (((0,), (0,)), ((), ()))
+
+
+def round_up(value, unit):
+    return -(-value // unit) * unit
+
+
+def mm(lhs, rhs, dims):
+    return lax.dot_general(lhs, rhs, dims, preferred_element_type=F32)
+
+
+def call(kernel, outs, *args, scratch=()):
+    return pl.pallas_call(
+        kernel,
+        out_shape=tuple(jax.ShapeDtypeStruct(shape, dtype) for shape, dtype in outs),
+        in_specs=[VMEM] * len(args),
+        out_specs=(VMEM,) * len(outs),
+        scratch_shapes=list(scratch),
+        compiler_params=pltpu.CompilerParams(vmem_limit_bytes=48 * 1024 * 1024),
+    )(*args)
+
+
+class Plan:
+    def __init__(self, clips, seqs, height, width, chans):
+        self.clips, self.seqs = clips, seqs
+        self.height, self.width, self.chans = height, width, chans
+        self.group = clips // 2
+        self.slab = chans // max(self.group, 1)
+        self.rows = chans // seqs
+        self.pixels = height * width
+        self.cols = 9 * self.slab
+        self.half = round_up(round_up(self.cols, 2 * LANES) // 2, LANES)
+        self.tcols = round_up(3 * self.slab, LANES)
+        self.thalf = chans // 2
+        self.factor = 1.0 / math.sqrt(clips * seqs * self.pixels)
+
+    def fits(self):
+        return (
+            self.group == 4
+            and self.slab * self.group == self.chans
+            and self.rows * self.seqs == self.chans
+            and self.slab % 16 == 0
+            and self.rows % 16 == 0
+            and self.thalf % 16 == 0
+            and self.pixels % LANES == 0
+            and self.seqs >= 2
+        )
+
+    def place(self):
+        clip = lax.axis_index("clip")
+        return clip % self.group, clip // self.group, lax.axis_index("seq")
+
+
+def prepare(plan, f_ref, g_ref, w_ref, fg_ref, gt_ref, wp_ref):
+    low, _, _ = plan.place()
+    chans, slab = plan.chans, plan.slab
+    grad = g_ref[...].T
+    gt_ref[...] = grad
+    fg_ref[chans:, :] = grad
+    fg_ref[:chans, :] = f_ref[...].T
+    for index in range(plan.group):
+
+        @pl.when(low == index)
+        def _():
+            wp_ref[...] = jnp.concatenate(
+                [w_ref[tap][:, slab * index : slab * (index + 1)] for tap in range(9)], axis=1
+            )
+
+
+def shifts(plan, lanes):
+    lane = lax.broadcasted_iota(jnp.int32, (1, lanes), 1) % plan.pixels
+    row, col = lane // plan.width, lane % plan.width
+    found = []
+    for i in range(3):
+        for j in range(3):
+            inside = (
+                (row + (i - 1) >= 0)
+                & (row + (i - 1) < plan.height)
+                & (col + (j - 1) >= 0)
+                & (col + (j - 1) < plan.width)
+            )
+            found.append(((i - 1) * plan.width + (j - 1), inside))
+    return found
+
+
+def rolled(value, distance):
+    lanes = value.shape[1]
+    return value if distance == 0 else pltpu.roll(value, (-distance) % lanes, 1)
+
+
+def group_frames(plan, own_ref, pair_ref, core_ref, part):
+    chans = plan.chans
+    first = slice(part * chans, (part + 1) * chans)
+    second = slice((2 + part) * chans, (3 + part) * chans)
+    return [own_ref[first, :], core_ref[first, :], pair_ref[first, :], core_ref[second, :]]
+
+
+def forward(plan, *refs):
+    w_refs = refs[: plan.seqs]
+    own_ref, pair_ref, core_ref = refs[plan.seqs : plan.seqs + 3]
+    w_all, f_all, a_ref, d_ref = refs[plan.seqs + 3 : plan.seqs + 7]
+    taps = refs[plan.seqs + 7]
+    _, _, z = plan.place()
+    rows, slab = plan.rows, plan.slab
+    for k, w_ref in enumerate(w_refs):
+        owner = (z - k + plan.seqs) % plan.seqs
+        w_all[pl.ds(pl.multiple_of(owner * rows, 16), rows), :] = w_ref[...]
+    for d, frame in enumerate(group_frames(plan, own_ref, pair_ref, core_ref, 0)):
+        f_all[:, d * plan.pixels : (d + 1) * plan.pixels] = frame
+    taps[...] = mm(w_all[...], f_all[...], TN)
+    total = None
+    for tap, (distance, inside) in enumerate(shifts(plan, f_all.shape[1])):
+        term = rolled(taps[tap * slab : (tap + 1) * slab, :], distance)
+        term = jnp.where(inside, term, 0.0)
+        total = term if total is None else total + term
+    sigma = 1.0 / (1.0 + jnp.exp(-total))
+    a_ref[...] = (total * sigma).astype(BF16)
+    d_ref[...] = sigma * (1.0 + total * (1.0 - sigma))
+
+
+def cotangents(plan, fg_refs, halo_refs):
+    before = group_frames(plan, *halo_refs, 0)
+    after = group_frames(plan, *halo_refs, 1)
+    here = group_frames(plan, *fg_refs, 1)
+    return [after, here, before]
+
+
+def temporal(plan, a_ref, *refs):
+    fg_refs, halo_refs = refs[:3], refs[3:6]
+    send_ref, keep_ref, total = refs[6:]
+    _, high, _ = plan.place()
+    pixels = plan.pixels
+    acts = a_ref[...]
+    parts = []
+    for grads in cotangents(plan, fg_refs, halo_refs):
+        term = None
+        for d, grad in enumerate(grads):
+            here = mm(grad, acts[:, d * pixels : (d + 1) * pixels], NT)
+            term = here if term is None else term + here
+        parts.append(term)
+    pad = plan.tcols - 3 * plan.slab
+    if pad:
+        parts.append(jnp.zeros((plan.chans, pad), F32))
+    total[...] = jnp.concatenate(parts, axis=1)
+    size = plan.thalf
+    keep_ref[...] = total[pl.ds(pl.multiple_of(high * size, 16), size), :]
+    send_ref[...] = total[pl.ds(pl.multiple_of((1 - high) * size, 16), size), :].astype(BF16)
+
+
+def spatial(plan, *refs):
+    w_all, f_all, d_ref, wt_ref = refs[:4]
+    fg_refs, halo_refs = refs[4:7], refs[7:10]
+    s_send, s_keep, f_send, f_keep, expanded, total = refs[10:]
+    low, high, _ = plan.place()
+    pixels, slab, chans = plan.pixels, plan.slab, plan.chans
+    parts = [None] * plan.group
+    for k, grads in enumerate(cotangents(plan, fg_refs, halo_refs)):
+        weight = wt_ref[k, pl.ds(pl.multiple_of(low * slab, 16), slab), :]
+        for d, grad in enumerate(grads):
+            here = mm(weight, grad, NN)
+            parts[d] = here if parts[d] is None else parts[d] + here
+    act_grad = jnp.concatenate(parts, axis=1).astype(BF16).astype(F32)
+    pre_grad = (act_grad * d_ref[...]).astype(BF16).astype(F32)
+    for tap, (distance, _) in enumerate(shifts(plan, pre_grad.shape[1])):
+        inside = shifts(plan, pre_grad.shape[1])[8 - tap][1]
+        term = jnp.where(inside, rolled(pre_grad, -distance), 0.0)
+        expanded[tap * slab : (tap + 1) * slab, :] = term.astype(BF16)
+    total[:, : plan.cols] = mm(f_all[...], expanded[...], NT)
+    if plan.cols < total.shape[1]:
+        total[:, plan.cols :] = jnp.zeros((chans, total.shape[1] - plan.cols), F32)
+    size = plan.half
+    s_keep[...] = total[:, pl.ds(pl.multiple_of(high * size, LANES), size)]
+    s_send[...] = total[:, pl.ds(pl.multiple_of((1 - high) * size, LANES), size)].astype(BF16)
+    grads = mm(w_all[...], expanded[...], NN)
+    for d in range(2):
+        f_keep[d * chans : (d + 1) * chans, :] = grads[:, d * pixels : (d + 1) * pixels]
+        there = grads[:, (2 + d) * pixels : (3 + d) * pixels]
+        f_send[d * chans : (d + 1) * chans, :] = there.astype(BF16)
+
+
+def frame_half(plan, keep_ref, got_ref, send_ref, own_ref):
+    chans = plan.chans
+    own_ref[...] = keep_ref[:chans, :] + got_ref[:chans, :].astype(F32)
+    send_ref[...] = (keep_ref[chans:, :] + got_ref[chans:, :].astype(F32)).astype(BF16)
+
+
+def frame_end(plan, own_ref, got_ref, g_ref, out_ref):
+    total = own_ref[...] + got_ref[...].astype(F32)
+    out_ref[...] = (g_ref[...].astype(F32) + total.T).astype(BF16)
+
+
+def space_rows(plan, keep_ref, got_ref, *refs):
+    own_ref, send_refs, total = refs[0], refs[1:-1], refs[-1]
+    _, _, z = plan.place()
+    total[...] = keep_ref[...] + got_ref[...].astype(F32)
+    rows = plan.rows
+    own_ref[...] = total[pl.ds(pl.multiple_of(z * rows, 16), rows), :]
+    for k, ref in enumerate(send_refs, 1):
+        other = (z + k) % plan.seqs
+        ref[...] = total[pl.ds(pl.multiple_of(other * rows, 16), rows), :].astype(BF16)
+
+
+def space_end(plan, *refs):
+    pieces, out_ref, held = refs[:-2], refs[-2], refs[-1]
+    low, high, _ = plan.place()
+    group, slab = plan.group, plan.slab
+    for m, piece in enumerate(pieces):
+        other = high if m < group else 1 - high
+        lane = pl.multiple_of(other * plan.half, LANES)
+        held[low ^ (m % group), :, pl.ds(lane, plan.half)] = piece[...].astype(F32) * plan.factor
+    for tap in range(9):
+        out_ref[tap] = jnp.concatenate(
+            [held[index, :, tap * slab : (tap + 1) * slab] for index in range(group)], axis=1
+        )
+
+
+def time_end(plan, *refs):
+    pieces, out_ref, held = refs[:-2], refs[-2], refs[-1]
+    low, high, _ = plan.place()
+    group, slab, size = plan.group, plan.slab, plan.thalf
+    for d in range(group):
+        held[pl.ds(pl.multiple_of(high * size, 16), size), :] = pieces[d][...].astype(F32)
+        held[pl.ds(pl.multiple_of((1 - high) * size, 16), size), :] = pieces[d + group][...].astype(F32)
+        turned = held[...].T * plan.factor
+        for k in range(3):
+            here = pl.ds(pl.multiple_of((low ^ d) * slab, 16), slab)
+            out_ref[k, here, :] = turned[k * slab : (k + 1) * slab, :]
+
+
+def per_device(plan, frames, cotangent, w_space, w_time):
+    pixels, chans, group, seqs = plan.pixels, plan.chans, plan.group, plan.seqs
+    slab, rows, cols = plan.slab, plan.rows, plan.cols
+    part = lambda fn: functools.partial(fn, plan)
+
+    def swap(value, distance):
+        return lax.ppermute(value, "clip", [(i, i ^ distance) for i in range(plan.clips)])
+
+    def turn(value, k):
+        return lax.ppermute(value, "seq", [(i, (i + k) % seqs) for i in range(seqs)])
+
+    clip_f, clip_g = frames.reshape(pixels, chans), cotangent.reshape(pixels, chans)
+    own, grad, piece = call(
+        part(prepare),
+        [((2 * chans, pixels), BF16), ((chans, pixels), BF16), ((rows, cols), BF16)],
+        clip_f,
+        clip_g,
+        jnp.transpose(w_space, (1, 0, 2)),
+    )
+    before = lax.ppermute(grad, "seq", [(i, i + 1) for i in range(seqs - 1)])
+    after = lax.ppermute(grad, "seq", [(i + 1, i) for i in range(seqs - 1)])
+    pieces = [piece] + [turn(piece, k) for k in range(1, seqs)]
+
+    def gathered(block):
+        pair = swap(block, 2)
+        return block, pair, swap(jnp.concatenate([block, pair], axis=0), 1)
+
+    fg = gathered(own)
+    halo = gathered(jnp.concatenate([before, after], axis=0))
+    lanes = group * pixels
+    w_all, f_all, acts, slope = call(
+        part(forward),
+        [((chans, cols), BF16), ((chans, lanes), BF16), ((slab, lanes), BF16), ((slab, lanes), F32)],
+        *pieces,
+        *fg,
+        scratch=[pltpu.VMEM((cols, lanes), F32)],
+    )
+    t_send, t_keep = call(
+        part(temporal),
+        [((plan.thalf, plan.tcols), BF16), ((plan.thalf, plan.tcols), F32)],
+        acts,
+        *fg,
+        *halo,
+        scratch=[pltpu.VMEM((chans, plan.tcols), F32)],
+    )
+    t_got = swap(t_send, group)
+    s_send, s_keep, f_send, f_keep = call(
+        part(spatial),
+        [
+            ((chans, plan.half), BF16),
+            ((chans, plan.half), F32),
+            ((2 * chans, pixels), BF16),
+            ((2 * chans, pixels), F32),
+        ],
+        w_all,
+        f_all,
+        slope,
+        w_time,
+        *fg,
+        *halo,
+        scratch=[pltpu.VMEM((cols, lanes), BF16), pltpu.VMEM((chans, 2 * plan.half), F32)],
+    )
+    s_got = swap(s_send, group)
+    f_got = swap(f_send, 2)
+
+    t_part = (t_keep + t_got.astype(F32)).astype(BF16)
+    t_sum = t_keep + t_got.astype(F32)
+    for k in range(1, seqs):
+        t_sum = t_sum + turn(t_part, k).astype(F32)
+    t_sum = t_sum.astype(BF16)
+
+    s_own, *s_parts = call(
+        part(space_rows),
+        [((rows, plan.half), F32)] + [((rows, plan.half), BF16)] * (seqs - 1),
+        s_keep,
+        s_got,
+        scratch=[pltpu.VMEM((chans, plan.half), F32)],
+    )
+    s_sum = s_own
+    for k in range(1, seqs):
+        s_sum = s_sum + turn(s_parts[k - 1], k).astype(F32)
+    s_sum = s_sum.astype(BF16)
+
+    f_half, f_own = call(
+        part(frame_half), [((chans, pixels), BF16), ((chans, pixels), F32)], f_keep, f_got
+    )
+    f_other = swap(f_half, 1)
+    (f_out,) = call(part(frame_end), [((pixels, chans), BF16)], f_own, f_other, clip_g)
+
+    def everywhere(value):
+        held = {0: value}
+        for distance in (2, group, group + 2):
+            held[distance] = swap(value, distance)
+        for distance in (0, 2, group, group + 2):
+            held[distance + 1] = swap(held[distance], 1)
+        return [held[distance] for distance in range(2 * group)]
+
+    (t_out,) = call(
+        part(time_end),
+        [((3, chans, chans), F32)],
+        *everywhere(t_sum),
+        scratch=[pltpu.VMEM((chans, plan.tcols), F32)],
+    )
+    (s_out,) = call(
+        part(space_end),
+        [((9, rows, chans), F32)],
+        *everywhere(s_sum),
+        scratch=[pltpu.VMEM((group, rows, 2 * plan.half), F32)],
+    )
+    return f_out.reshape(frames.shape), jnp.transpose(s_out, (1, 0, 2)), t_out
+
+
 def solution(mesh):
     in_specs = (
         P("clip", "seq", None, None, None),
@@ -107,6 +457,12 @@
         P(),
     )
     out_specs = (P("clip", "seq", None, None, None), P("seq", None, None), P())
-    return jax.shard_map(
-        per_device, mesh=mesh, in_specs=in_specs, out_specs=out_specs, check_vma=False
-    )
+
+    def body(frames, cotangent, w_space, w_time):
+        one, count, height, width, chans = frames.shape
+        plan = Plan(mesh.shape["clip"], mesh.shape["seq"], height, width, chans)
+        if one == 1 and count == 1 and plan.fits():
+            return per_device(plan, frames, cotangent, w_space, w_time)
+        return per_device_general(frames, cotangent, w_space, w_time)
+
+    return jax.shard_map(body, mesh=mesh, in_specs=in_specs, out_specs=out_specs, check_vma=False)

time: 361 us -> 85 us (0.24)
  waiting for transfers between devices: 306 us -> 36.4 us
  starting transfers between devices: 6.39 us -> 34.7 us
  matrix products: 20 us -> 0 us
  between operations: 14.2 us -> 0.83 us
  Pallas kernels: 0 us -> 9.61 us
  local copies, waits for them, and re-layouts: 10.5 us -> 2.93 us
    psum x2 -> x0, waiting for transfers between devices: 197 us -> none  [the longest x1 137 us: per_device(): time_grad = lax.psum(time_terms * factor, ('clip', 'seq'))]
    reduce_scatter x1 -> x0, waiting for transfers between devices: 69.8 us -> none  [per_device(): lax.psum_scatter(jnp.stack(terms, axis=1) * factor, 'seq', scatter_dimens...]
    all_gather x1 -> x0, waiting for transfers between devices: 38.6 us -> none  [per_device(): weights = lax.all_gather(w_space, 'seq', axis=0, tiled=True)]
    ppermute x2 -> x33, waiting for transfers between devices: 0.01 us -> 36.4 us  [the longest x22 18.4 us: swap(): lax.ppermute(value, 'clip', [(i, i ^ distance) for i in range(plan.clips)])]
    ppermute x2 -> x33, starting transfers between devices: 6.23 us -> 34.7 us  [the longest x22 15.7 us: swap(): lax.ppermute(value, 'clip', [(i, i ^ distance) for i in range(plan.clips)])]
    dot_general x33 -> x0, matrix products: 20 us -> none  [the longest x9 5.82 us: per_device(): jnp.dot(pieces[tap], weights[:, tap, :], preferred_element_type=jnp.float32)]
    pallas_call x0 -> x9, Pallas kernels: none -> 9.61 us  [call(): pl.pallas_call(kernel, out_shape=tuple((jax.ShapeDtypeStruct(shape, dtype...]
    slice x2 -> x0, local copies, waits for them, and re-layouts: 4.35 us -> none  [the longest x1 3.43 us: per_device(): padded[:, i:i + height, j:j + width, :].reshape(-1, chans)]
  transfers between devices with their start and end apart: 6 -> 33, of which waited for: 4 -> 15; matrix products, arithmetic and copies ran while one was open for 6% -> 0% of each run, Pallas kernels for 0% -> 9%
where the time goes in v1:
time: 85 us; the launch traced here: 84.6 us
  waiting for transfers between devices  36.4 us (43%)
  starting transfers between devices  34.7 us (41%)
  Pallas kernels  9.61 us (11%)
  local copies, waits for them, and re-layouts  2.93 us (3%)
    ppermute x22, waiting for transfers between devices, swap(): lax.ppermute(value, 'clip', [(i, i ^ distance) for i in range(plan.clips)])  18.4 us
    ppermute x22, starting transfers between devices, swap(): lax.ppermute(value, 'clip', [(i, i ^ distance) for i in range(plan.clips)])  15.7 us
    ppermute x9, waiting for transfers between devices, turn(): lax.ppermute(value, 'seq', [(i, (i + k) % seqs) for i in range(seqs)])  13.3 us
    ppermute x9, starting transfers between devices, turn(): lax.ppermute(value, 'seq', [(i, (i + k) % seqs) for i in range(seqs)])  12.8 us
    pallas_call x9, Pallas kernels, call(): pl.pallas_call(kernel, out_shape=tuple((jax.ShapeDtypeStruct(shape, dtype...  9.61 us
    ppermute x1, starting transfers between devices, per_device(): before = lax.ppermute(grad, 'seq', [(i, i + 1) for i in range(seqs - 1)])  4.94 us
    ppermute x1, waiting for transfers between devices, per_device(): after = lax.ppermute(grad, 'seq', [(i + 1, i) for i in range(seqs - 1)])  4.11 us
    unnamed x9, local copies, waits for them, and re-layouts  2.91 us
  transfers between devices with their start and end apart: 33, of which 15 were waited for; matrix products, arithmetic and copies ran while one was open for 0% of the time, Pallas kernels for 9%

profile of v1, /device:TPU:0, one launch (start us, length us, event | category | flops | bytes accessed | tf_op | source)
XLA Modules:
  0.0 84.6 jit_solution(10149475290201023860)
XLA Ops:
  0.6 0.9 %copy-done = bf16[1,1,16,16,320]{4,3,2,1,0:T(8,128)(2,1)S(1)} copy-done((bf16[1,1,16,16,320]{4,3,2,1,0:T(8,128)(2,1)S(1)}, bf16[1,1,16,16,320]{4,3,2,1,0:T(8,128)(2,1)}, u32[]{:S(2)}) %copy-start) | copy-done | bytes 163864
  1.6 1.0 %copy-done.2 = bf16[80,9,320]{2,0,1:T(8,128)(2,1)S(1)} copy-done((bf16[80,9,320]{2,0,1:T(8,128)(2,1)S(1)}, bf16[80,9,320]{2,0,1:T(8,128)(2,1)}, u32[]{:S(2)}) %copy-start.2) | copy-done | bytes 460824
  2.6 0.9 %copy-done.3 = bf16[1,1,16,16,320]{4,3,2,1,0:T(8,128)(2,1)S(1)} copy-done((bf16[1,1,16,16,320]{4,3,2,1,0:T(8,128)(2,1)S(1)}, bf16[1,1,16,16,320]{4,3,2,1,0:T(8,128)(2,1)}, u32[]{:S(2)}) %copy-start.3) | copy-done | bytes 163864
  3.5 0.3 shard_map.67
  3.8 4.9 %collective-permute-start.5 = (bf16[320,256]{1,0:T(8,128)(2,1)S(1)}, bf16[320,256]{1,0:T(8,128)(2,1)S(1)}, u32[]{:S(2)}, u32[]{:S(2)}) collective-permute-start(bf16[320,256]{1,0:T(8,128)(2,1)S(1)} %get-tuple-element.27), channel_id=1, source_target_pairs={{0,1},{1,2},{2,3},{4,5},{5,6},{6,7},{8,9},{9,10},{10,11},{12,13},{... | collective-permute-start | bytes 491528 | tf_op jit(solution)/shard_map/ppermute | solution.py:359
  8.8 1.3 %collective-permute-start.6 = (bf16[320,256]{1,0:T(8,128)(2,1)S(1)}, bf16[320,256]{1,0:T(8,128)(2,1)S(1)}, u32[]{:S(2)}, u32[]{:S(2)}) collective-permute-start(bf16[320,256]{1,0:T(8,128)(2,1)S(1)} %get-tuple-element.27), channel_id=1, source_target_pairs={{1,0},{2,1},{3,2},{5,4},{6,5},{7,6},{9,8},{10,9},{11,10},{13,12},{... | collective-permute-start | bytes 491528 | tf_op jit(solution)/shard_map/ppermute | solution.py:360
  10.1 1.5 %collective-permute-start.3 = (bf16[640,256]{1,0:T(8,128)(2,1)S(1)}, bf16[640,256]{1,0:T(8,128)(2,1)S(1)}, u32[]{:S(2)}, u32[]{:S(2)}) collective-permute-start(bf16[640,256]{1,0:T(8,128)(2,1)S(1)} %get-tuple-element.23.refs_4_.refs_0_), channel_id=1, source_target_pairs={{0,8},{4,12},{8,0},{12,4},{16,24},{20,28},{24,16},{28,20},{1,9},{5... | collective-permute-start | bytes 983048 | tf_op jit(solution)/shard_map/ppermute | solution.py:346
  11.6 0.6 collective-permute-done.5
  12.3 4.1 %collective-permute-done.6 = bf16[320,256]{1,0:T(8,128)(2,1)S(1)} collective-permute-done((bf16[320,256]{1,0:T(8,128)(2,1)S(1)}, bf16[320,256]{1,0:T(8,128)(2,1)S(1)}, u32[]{:S(2)}, u32[]{:S(2)}) %collective-permute-start.6) | collective-permute-done | bytes 163872 | tf_op jit(solution)/shard_map/ppermute | solution.py:360
  16.4 1.5 %collective-permute-start.7 = (bf16[640,256]{1,0:T(8,128)(2,1)S(1)}, bf16[640,256]{1,0:T(8,128)(2,1)S(1)}, u32[]{:S(2)}, u32[]{:S(2)}) collective-permute-start(bf16[640,256]{1,0:T(8,128)(2,1)S(1)} %constant_dynamic-update-slice_fusion.refs_7_.refs_3_), channel_id=1, source_target_pairs={{0,8},{4,12},{8,0},{12,4},{16,24},{20,28},{24,16},{28,20},{1,9},{5... | collective-permute-start | bytes 983048 | tf_op jit(solution)/shard_map/ppermute | solution.py:346
  17.9 2.8 %collective-permute-done.3.refs_5_.refs_1_ = bf16[640,256]{1,0:T(8,128)(2,1)S(1)} collective-permute-done((bf16[640,256]{1,0:T(8,128)(2,1)S(1)}, bf16[640,256]{1,0:T(8,128)(2,1)S(1)}, u32[]{:S(2)}, u32[]{:S(2)}) %collective-permute-start.3) | collective-permute-done | bytes 327712 | tf_op jit(solution)/shard_map/ppermute | solution.py:346
  20.9 5.5 %collective-permute-done.7.refs_8_.refs_4_ = bf16[640,256]{1,0:T(8,128)(2,1)S(1)} collective-permute-done((bf16[640,256]{1,0:T(8,128)(2,1)S(1)}, bf16[640,256]{1,0:T(8,128)(2,1)S(1)}, u32[]{:S(2)}, u32[]{:S(2)}) %collective-permute-start.7) | collective-permute-done | bytes 327712 | tf_op jit(solution)/shard_map/ppermute | solution.py:346
  26.5 4.4 %collective-permute-start.2 = (bf16[80,720]{1,0:T(8,128)(2,1)S(1)}, bf16[80,720]{1,0:T(8,128)(2,1)S(1)}, u32[]{:S(2)}, u32[]{:S(2)}) collective-permute-start(bf16[80,720]{1,0:T(8,128)(2,1)S(1)} %get-tuple-element.22.refs_0_), channel_id=1, source_target_pairs={{0,3},{1,0},{2,1},{3,2},{4,7},{5,4},{6,5},{7,6},{8,11},{9,8},{10,9... | collective-permute-start | bytes 345608 | tf_op jit(solution)/shard_map/ppermute | solution.py:349
  30.9 1.0 %collective-permute-start = (bf16[80,720]{1,0:T(8,128)(2,1)S(1)}, bf16[80,720]{1,0:T(8,128)(2,1)S(1)}, u32[]{:S(2)}, u32[]{:S(2)}) collective-permute-start(bf16[80,720]{1,0:T(8,128)(2,1)S(1)} %get-tuple-element.22.refs_0_), channel_id=1, source_target_pairs={{0,1},{1,2},{2,3},{3,0},{4,5},{5,6},{6,7},{7,4},{8,9},{9,10},{10,1... | collective-permute-start | bytes 345608 | tf_op jit(solution)/shard_map/ppermute | solution.py:349
  31.9 2.7 %collective-permute-done.2.refs_3_ = bf16[80,720]{1,0:T(8,128)(2,1)S(1)} collective-permute-done((bf16[80,720]{1,0:T(8,128)(2,1)S(1)}, bf16[80,720]{1,0:T(8,128)(2,1)S(1)}, u32[]{:S(2)}, u32[]{:S(2)}) %collective-permute-start.2) | collective-permute-done | bytes 115232 | tf_op jit(solution)/shard_map/ppermute | solution.py:349
  34.7 7.8 %collective-permute-done.1.refs_2_ = bf16[80,720]{1,0:T(8,128)(2,1)S(1)} collective-permute-done((bf16[80,720]{1,0:T(8,128)(2,1)S(1)}, bf16[80,720]{1,0:T(8,128)(2,1)S(1)}, u32[]{:S(2)}, u32[]{:S(2)}) %collective-permute-start.1) | collective-permute-done | bytes 115232 | tf_op jit(solution)/shard_map/ppermute | solution.py:349
  42.5 1.4 %shard_map.68 = (bf16[320,720]{1,0:T(8,128)(2,1)S(1)}, bf16[320,1024]{1,0:T(8,128)(2,1)S(1)}, bf16[80,1024]{1,0:T(8,128)(2,1)S(1)}, f32[80,1024]{1,0:T(8,128)S(1)}) custom-call(bf16[80,720]{1,0:T(8,128)(2,1)S(1)} %get-tuple-element.22.refs_0_, bf16[80,720]{1,0:T(8,128)(2,1)S(1)} %collective-permute-done.refs_1_, ...), custom_call_target="tpu_custom_call" | custom-call | tf_op jit(solution)/shard_map/pallas_call | solution.py:123
  43.9 0.7 shard_map.74
  44.6 1.6 %collective-permute-start.22 = (bf16[160,256]{1,0:T(8,128)(2,1)S(1)}, bf16[160,256]{1,0:T(8,128)(2,1)S(1)}, u32[]{:S(2)}, u32[]{:S(2)}) collective-permute-start(bf16[160,256]{1,0:T(8,128)(2,1)S(1)} %get-tuple-element.40), channel_id=1, source_target_pairs={{0,16},{4,20},{8,24},{12,28},{16,0},{20,4},{24,8},{28,12},{1,17},{... | collective-permute-start | bytes 245768 | tf_op jit(solution)/shard_map/ppermute | solution.py:346
  46.2 2.9 %collective-permute-done.22 = bf16[160,256]{1,0:T(8,128)(2,1)S(1)} collective-permute-done((bf16[160,256]{1,0:T(8,128)(2,1)S(1)}, bf16[160,256]{1,0:T(8,128)(2,1)S(1)}, u32[]{:S(2)}, u32[]{:S(2)}) %collective-permute-start.22) | collective-permute-done | bytes 81952 | tf_op jit(solution)/shard_map/ppermute | solution.py:346
  49.1 1.3 %collective-permute-start.25 = (bf16[160,256]{1,0:T(8,128)(2,1)S(1)}, bf16[160,256]{1,0:T(8,128)(2,1)S(1)}, u32[]{:S(2)}, u32[]{:S(2)}) collective-permute-start(bf16[160,256]{1,0:T(8,128)(2,1)S(1)} %fusion), channel_id=1, source_target_pairs={{0,3},{1,0},{2,1},{3,2},{4,7},{5,4},{6,5},{7,6},{8,11},{9,8},{10,9... | collective-permute-start | bytes 245768 | tf_op jit(solution)/shard_map/ppermute | solution.py:349
  50.5 1.1 %collective-permute-start.24 = (bf16[160,256]{1,0:T(8,128)(2,1)S(1)}, bf16[160,256]{1,0:T(8,128)(2,1)S(1)}, u32[]{:S(2)}, u32[]{:S(2)}) collective-permute-start(bf16[160,256]{1,0:T(8,128)(2,1)S(1)} %fusion), channel_id=1, source_target_pairs={{0,2},{1,3},{2,0},{3,1},{4,6},{5,7},{6,4},{7,5},{8,10},{9,11},{10,... | collective-permute-start | bytes 245768 | tf_op jit(solution)/shard_map/ppermute | solution.py:349
  51.5 1.9 %collective-permute-start.23 = (bf16[160,256]{1,0:T(8,128)(2,1)S(1)}, bf16[160,256]{1,0:T(8,128)(2,1)S(1)}, u32[]{:S(2)}, u32[]{:S(2)}) collective-permute-start(bf16[160,256]{1,0:T(8,128)(2,1)S(1)} %fusion), channel_id=1, source_target_pairs={{0,1},{1,2},{2,3},{3,0},{4,5},{5,6},{6,7},{7,4},{8,9},{9,10},{10,1... | collective-permute-start | bytes 245768 | tf_op jit(solution)/shard_map/ppermute | solution.py:349
  53.5 3.0 %shard_map.69 = (bf16[320,384]{1,0:T(8,128)(2,1)S(1)}, f32[320,384]{1,0:T(8,128)S(1)}, bf16[640,256]{1,0:T(8,128)(2,1)S(1)}, f32[640,256]{1,0:T(8,128)S(1)}) custom-call(bf16[320,720]{1,0:T(8,128)(2,1)S(1)} %get-tuple-element.24.refs_0_, bf16[320,1024]{1,0:T(8,128)(2,1)S(1)} %get-tuple-element.25.refs_1_, f32[80,1024]{1,0:T(8,128)S(1)} %get-tuple-element.26.refs_2_, ...), custom_call_target="tpu_custom_call" | custom-call | tf_op jit(solution)/shard_map/pallas_call | solution.py:123
  56.5 1.5 %collective-permute-start.9 = (bf16[640,256]{1,0:T(8,128)(2,1)S(1)}, bf16[640,256]{1,0:T(8,128)(2,1)S(1)}, u32[]{:S(2)}, u32[]{:S(2)}) collective-permute-start(bf16[640,256]{1,0:T(8,128)(2,1)S(1)} %get-tuple-element.29), channel_id=1, source_target_pairs={{0,8},{4,12},{8,0},{12,4},{16,24},{20,28},{24,16},{28,20},{1,9},{5... | collective-permute-start | bytes 983048 | tf_op jit(solution)/shard_map/ppermute | solution.py:346
  58.0 1.5 %collective-permute-start.11 = (bf16[320,384]{1,0:T(8,128)(2,1)S(1)}, bf16[320,384]{1,0:T(8,128)(2,1)S(1)}, u32[]{:S(2)}, u32[]{:S(2)}) collective-permute-start(bf16[320,384]{1,0:T(8,128)(2,1)S(1)} %get-tuple-element.33), channel_id=1, source_target_pairs={{0,16},{4,20},{8,24},{12,28},{16,0},{20,4},{24,8},{28,12},{1,17},{... | collective-permute-start | bytes 737288 | tf_op jit(solution)/shard_map/ppermute | solution.py:346
  59.6 0.7 collective-permute-start.31
  60.4 1.3 %collective-permute-start.29 = (bf16[160,256]{1,0:T(8,128)(2,1)S(1)}, bf16[160,256]{1,0:T(8,128)(2,1)S(1)}, u32[]{:S(2)}, u32[]{:S(2)}) collective-permute-start(bf16[160,256]{1,0:T(8,128)(2,1)S(1)} %add_convert_fusion.refs_0_), channel_id=1, source_target_pairs={{0,16},{4,20},{8,24},{12,28},{16,0},{20,4},{24,8},{28,12},{1,17},{... | collective-permute-start | bytes 245768 | tf_op jit(solution)/shard_map/ppermute | solution.py:346
  61.7 1.5 %collective-permute-start.27 = (bf16[160,256]{1,0:T(8,128)(2,1)S(1)}, bf16[160,256]{1,0:T(8,128)(2,1)S(1)}, u32[]{:S(2)}, u32[]{:S(2)}) collective-permute-start(bf16[160,256]{1,0:T(8,128)(2,1)S(1)} %add_convert_fusion.refs_0_), channel_id=1, source_target_pairs={{0,8},{4,12},{8,0},{12,4},{16,24},{20,28},{24,16},{28,20},{1,9},{5... | collective-permute-start | bytes 245768 | tf_op jit(solution)/shard_map/ppermute | solution.py:346
  63.2 1.5 %collective-permute-done.11.got_ref = bf16[320,384]{1,0:T(8,128)(2,1)S(1)} collective-permute-done((bf16[320,384]{1,0:T(8,128)(2,1)S(1)}, bf16[320,384]{1,0:T(8,128)(2,1)S(1)}, u32[]{:S(2)}, u32[]{:S(2)}) %collective-permute-start.11) | collective-permute-done | bytes 245792 | tf_op jit(solution)/shard_map/ppermute | solution.py:346
  64.7 0.1 shard_map.72
  64.8 0.4 collective-permute-start.12
  65.2 1.9 %collective-permute-done.31.refs_6_ = bf16[160,256]{1,0:T(8,128)(2,1)S(1)} collective-permute-done((bf16[160,256]{1,0:T(8,128)(2,1)S(1)}, bf16[160,256]{1,0:T(8,128)(2,1)S(1)}, u32[]{:S(2)}, u32[]{:S(2)}) %collective-permute-start.31) | collective-permute-done | bytes 81952 | tf_op jit(solution)/shard_map/ppermute | solution.py:346
  67.1 1.2 %collective-permute-start.13 = (bf16[80,384]{1,0:T(8,128)(2,1)S(1)}, bf16[80,384]{1,0:T(8,128)(2,1)S(1)}, u32[]{:S(2)}, u32[]{:S(2)}) collective-permute-start(bf16[80,384]{1,0:T(8,128)(2,1)S(1)} %get-tuple-element.36), channel_id=1, source_target_pairs={{0,2},{1,3},{2,0},{3,1},{4,6},{5,7},{6,4},{7,5},{8,10},{9,11},{10,... | collective-permute-start | bytes 184328 | tf_op jit(solution)/shard_map/ppermute | solution.py:349
  68.3 1.4 %collective-permute-start.14 = (bf16[80,384]{1,0:T(8,128)(2,1)S(1)}, bf16[80,384]{1,0:T(8,128)(2,1)S(1)}, u32[]{:S(2)}, u32[]{:S(2)}) collective-permute-start(bf16[80,384]{1,0:T(8,128)(2,1)S(1)} %get-tuple-element.37), channel_id=1, source_target_pairs={{0,3},{1,0},{2,1},{3,2},{4,7},{5,4},{6,5},{7,6},{8,11},{9,8},{10,9... | collective-permute-start | bytes 184328 | tf_op jit(solution)/shard_map/ppermute | solution.py:349
  69.9 0.5 collective-permute-start.32
  70.4 0.5 collective-permute-done.12
  70.9 1.8 %collective-permute-done.13 = bf16[80,384]{1,0:T(8,128)(2,1)S(1)} collective-permute-done((bf16[80,384]{1,0:T(8,128)(2,1)S(1)}, bf16[80,384]{1,0:T(8,128)(2,1)S(1)}, u32[]{:S(2)}, u32[]{:S(2)}) %collective-permute-start.13) | collective-permute-done | bytes 61472 | tf_op jit(solution)/shard_map/ppermute | solution.py:349
  72.7 0.5 collective-permute-done.14
  73.3 1.5 %collective-permute-start.20 = (bf16[80,384]{1,0:T(8,128)(2,1)S(1)}, bf16[80,384]{1,0:T(8,128)(2,1)S(1)}, u32[]{:S(2)}, u32[]{:S(2)}) collective-permute-start(bf16[80,384]{1,0:T(8,128)(2,1)S(1)} %add_convert_fusion.1.refs_0_), channel_id=1, source_target_pairs={{0,24},{4,28},{8,16},{12,20},{16,8},{20,12},{24,0},{28,4},{1,25},{... | collective-permute-start | bytes 184328 | tf_op jit(solution)/shard_map/ppermute | solution.py:346
  74.8 1.5 %collective-permute-start.18 = (bf16[80,384]{1,0:T(8,128)(2,1)S(1)}, bf16[80,384]{1,0:T(8,128)(2,1)S(1)}, u32[]{:S(2)}, u32[]{:S(2)}) collective-permute-start(bf16[80,384]{1,0:T(8,128)(2,1)S(1)} %add_convert_fusion.1.refs_0_), channel_id=1, source_target_pairs={{0,16},{4,20},{8,24},{12,28},{16,0},{20,4},{24,8},{28,12},{1,17},{... | collective-permute-start | bytes 184328 | tf_op jit(solution)/shard_map/ppermute | solution.py:346
  76.3 0.5 collective-permute-start.16
  76.8 1.9 %collective-permute-done.20.refs_6_ = bf16[80,384]{1,0:T(8,128)(2,1)S(1)} collective-permute-done((bf16[80,384]{1,0:T(8,128)(2,1)S(1)}, bf16[80,384]{1,0:T(8,128)(2,1)S(1)}, u32[]{:S(2)}, u32[]{:S(2)}) %collective-permute-start.20) | collective-permute-done | bytes 61472 | tf_op jit(solution)/shard_map/ppermute | solution.py:346
  78.7 1.2 %collective-permute-done.18.refs_4_ = bf16[80,384]{1,0:T(8,128)(2,1)S(1)} collective-permute-done((bf16[80,384]{1,0:T(8,128)(2,1)S(1)}, bf16[80,384]{1,0:T(8,128)(2,1)S(1)}, u32[]{:S(2)}, u32[]{:S(2)}) %collective-permute-start.18) | collective-permute-done | bytes 61472 | tf_op jit(solution)/shard_map/ppermute | solution.py:346
  79.9 0.6 collective-permute-done.16.refs_2_
  80.5 1.6 %shard_map.75 = f32[3,320,320]{2,1,0:T(8,128)} custom-call(bf16[160,256]{1,0:T(8,128)(2,1)S(1)} %add_convert_fusion.refs_0_, bf16[160,256]{1,0:T(8,128)(2,1)S(1)} %collective-permute-done.26.refs_1_, bf16[160,256]{1,0:T(8,128)(2,1)S(1)} %collective-permute-done.27.refs_2_, bf16[160,256]{1,0:T(8,128)(2,1)S(1)} %collective-permute-done.28.refs_3_, ...), custom_call_target="tpu_custom_call" | custom-call | tf_op jit(solution)/shard_map/pallas_call | solution.py:123
  82.2 1.6 %shard_map.73 = f32[9,80,320]{2,1,0:T(8,128)} custom-call(bf16[80,384]{1,0:T(8,128)(2,1)S(1)} %add_convert_fusion.1.refs_0_, bf16[80,384]{1,0:T(8,128)(2,1)S(1)} %collective-permute-done.15.refs_1_, bf16[80,384]{1,0:T(8,128)(2,1)S(1)} %collective-permute-done.16.refs_2_, bf16[80,384]{1,0:T(8,128)(2,1)S(1)} %collective-permute-done.17.refs_3_, ...), custom_call_target="tpu_custom_call" | custom-call | tf_op jit(solution)/shard_map/pallas_call | solution.py:123
  83.8 0.9 %shard_map.71 = bf16[256,320]{1,0:T(8,128)(2,1)} custom-call(f32[320,256]{1,0:T(8,128)S(1)} %get-tuple-element.30.own_ref, bf16[320,256]{1,0:T(8,128)(2,1)S(1)} %collective-permute-done.10.got_ref, bf16[256,320]{1,0:T(8,128)(2,1)S(1)} %bitcast.6), custom_call_target="tpu_custom_call" | custom-call | tf_op jit(solution)/shard_map/pallas_call | solution.py:123
  (42 shorter events, 0.6 us)
Async XLA Ops:
  0.6 0.9 %copy-start = (bf16[1,1,16,16,320]{4,3,2,1,0:T(8,128)(2,1)S(1)}, bf16[1,1,16,16,320]{4,3,2,1,0:T(8,128)(2,1)}, u32[]{:S(2)}) copy-start(bf16[1,1,16,16,320]{4,3,2,1,0:T(8,128)(2,1)} %param.5) | copy-start | bytes 491524
  1.6 1.1 %copy-start.2 = (bf16[80,9,320]{2,0,1:T(8,128)(2,1)S(1)}, bf16[80,9,320]{2,0,1:T(8,128)(2,1)}, u32[]{:S(2)}) copy-start(bf16[80,9,320]{2,0,1:T(8,128)(2,1)} %param.6) | copy-start | bytes 1382404
  2.6 0.9 %copy-start.3 = (bf16[1,1,16,16,320]{4,3,2,1,0:T(8,128)(2,1)S(1)}, bf16[1,1,16,16,320]{4,3,2,1,0:T(8,128)(2,1)}, u32[]{:S(2)}) copy-start(bf16[1,1,16,16,320]{4,3,2,1,0:T(8,128)(2,1)} %param.4) | copy-start | bytes 491524
  3.8 8.4 %collective-permute-start.5 = (bf16[320,256]{1,0:T(8,128)(2,1)S(1)}, bf16[320,256]{1,0:T(8,128)(2,1)S(1)}, u32[]{:S(2)}, u32[]{:S(2)}) collective-permute-start(bf16[320,256]{1,0:T(8,128)(2,1)S(1)} %get-tuple-element.27), channel_id=1, source_target_pairs={{0,1},{1,2},{2,3},{4,5},{5,6},{6,7},{8,9},{9,10},{10,11},{12,13},{... | collective-permute-start | bytes 491528 | tf_op jit(solution)/shard_map/ppermute | solution.py:359
  8.8 7.6 %collective-permute-start.6 = (bf16[320,256]{1,0:T(8,128)(2,1)S(1)}, bf16[320,256]{1,0:T(8,128)(2,1)S(1)}, u32[]{:S(2)}, u32[]{:S(2)}) collective-permute-start(bf16[320,256]{1,0:T(8,128)(2,1)S(1)} %get-tuple-element.27), channel_id=1, source_target_pairs={{1,0},{2,1},{3,2},{5,4},{6,5},{7,6},{9,8},{10,9},{11,10},{13,12},{... | collective-permute-start | bytes 491528 | tf_op jit(solution)/shard_map/ppermute | solution.py:360
  10.1 10.7 %collective-permute-start.3 = (bf16[640,256]{1,0:T(8,128)(2,1)S(1)}, bf16[640,256]{1,0:T(8,128)(2,1)S(1)}, u32[]{:S(2)}, u32[]{:S(2)}) collective-permute-start(bf16[640,256]{1,0:T(8,128)(2,1)S(1)} %get-tuple-element.23.refs_4_.refs_0_), channel_id=1, source_target_pairs={{0,8},{4,12},{8,0},{12,4},{16,24},{20,28},{24,16},{28,20},{1,9},{5... | collective-permute-start | bytes 983048 | tf_op jit(solution)/shard_map/ppermute | solution.py:346
  16.4 10.0 %collective-permute-start.7 = (bf16[640,256]{1,0:T(8,128)(2,1)S(1)}, bf16[640,256]{1,0:T(8,128)(2,1)S(1)}, u32[]{:S(2)}, u32[]{:S(2)}) collective-permute-start(bf16[640,256]{1,0:T(8,128)(2,1)S(1)} %constant_dynamic-update-slice_fusion.refs_7_.refs_3_), channel_id=1, source_target_pairs={{0,8},{4,12},{8,0},{12,4},{16,24},{20,28},{24,16},{28,20},{1,9},{5... | collective-permute-start | bytes 983048 | tf_op jit(solution)/shard_map/ppermute | solution.py:346
  20.8 21.7 %collective-permute-start.4 = (bf16[1280,256]{1,0:T(8,128)(2,1)S(1)}, bf16[1280,256]{1,0:T(8,128)(2,1)S(1)}, u32[]{:S(2)}, u32[]{:S(2)}) collective-permute-start(bf16[1280,256]{1,0:T(8,128)(2,1)S(1)} %pad_maximum_fusion), channel_id=1, source_target_pairs={{0,4},{4,0},{8,12},{12,8},{16,20},{20,16},{24,28},{28,24},{1,5},{5... | collective-permute-start | bytes 1966088 | tf_op jit(solution)/shard_map/ppermute | solution.py:346
  26.4 17.4 %collective-permute-start.8 = (bf16[1280,256]{1,0:T(8,128)(2,1)S(1)}, bf16[1280,256]{1,0:T(8,128)(2,1)S(1)}, u32[]{:S(2)}, u32[]{:S(2)}) collective-permute-start(bf16[1280,256]{1,0:T(8,128)(2,1)S(1)} %pad_maximum_fusion.1), channel_id=1, source_target_pairs={{0,4},{4,0},{8,12},{12,8},{16,20},{20,16},{24,28},{28,24},{1,5},{5... | collective-permute-start | bytes 1966088 | tf_op jit(solution)/shard_map/ppermute | solution.py:346
  26.5 8.2 %collective-permute-start.2 = (bf16[80,720]{1,0:T(8,128)(2,1)S(1)}, bf16[80,720]{1,0:T(8,128)(2,1)S(1)}, u32[]{:S(2)}, u32[]{:S(2)}) collective-permute-start(bf16[80,720]{1,0:T(8,128)(2,1)S(1)} %get-tuple-element.22.refs_0_), channel_id=1, source_target_pairs={{0,3},{1,0},{2,1},{3,2},{4,7},{5,4},{6,5},{7,6},{8,11},{9,8},{10,9... | collective-permute-start | bytes 345608 | tf_op jit(solution)/shard_map/ppermute | solution.py:349
  30.9 11.5 %collective-permute-start.1 = (bf16[80,720]{1,0:T(8,128)(2,1)S(1)}, bf16[80,720]{1,0:T(8,128)(2,1)S(1)}, u32[]{:S(2)}, u32[]{:S(2)}) collective-permute-start(bf16[80,720]{1,0:T(8,128)(2,1)S(1)} %get-tuple-element.22.refs_0_), channel_id=1, source_target_pairs={{0,2},{1,3},{2,0},{3,1},{4,6},{5,7},{6,4},{7,5},{8,10},{9,11},{10,... | collective-permute-start | bytes 345608 | tf_op jit(solution)/shard_map/ppermute | solution.py:349
  30.9 11.5 %collective-permute-start = (bf16[80,720]{1,0:T(8,128)(2,1)S(1)}, bf16[80,720]{1,0:T(8,128)(2,1)S(1)}, u32[]{:S(2)}, u32[]{:S(2)}) collective-permute-start(bf16[80,720]{1,0:T(8,128)(2,1)S(1)} %get-tuple-element.22.refs_0_), channel_id=1, source_target_pairs={{0,1},{1,2},{2,3},{3,0},{4,5},{5,6},{6,7},{7,4},{8,9},{9,10},{10,1... | collective-permute-start | bytes 345608 | tf_op jit(solution)/shard_map/ppermute | solution.py:349
  44.6 4.5 %collective-permute-start.22 = (bf16[160,256]{1,0:T(8,128)(2,1)S(1)}, bf16[160,256]{1,0:T(8,128)(2,1)S(1)}, u32[]{:S(2)}, u32[]{:S(2)}) collective-permute-start(bf16[160,256]{1,0:T(8,128)(2,1)S(1)} %get-tuple-element.40), channel_id=1, source_target_pairs={{0,16},{4,20},{8,24},{12,28},{16,0},{20,4},{24,8},{28,12},{1,17},{... | collective-permute-start | bytes 245768 | tf_op jit(solution)/shard_map/ppermute | solution.py:346
  49.1 10.4 %collective-permute-start.25 = (bf16[160,256]{1,0:T(8,128)(2,1)S(1)}, bf16[160,256]{1,0:T(8,128)(2,1)S(1)}, u32[]{:S(2)}, u32[]{:S(2)}) collective-permute-start(bf16[160,256]{1,0:T(8,128)(2,1)S(1)} %fusion), channel_id=1, source_target_pairs={{0,3},{1,0},{2,1},{3,2},{4,7},{5,4},{6,5},{7,6},{8,11},{9,8},{10,9... | collective-permute-start | bytes 245768 | tf_op jit(solution)/shard_map/ppermute | solution.py:349
  50.5 9.1 %collective-permute-start.24 = (bf16[160,256]{1,0:T(8,128)(2,1)S(1)}, bf16[160,256]{1,0:T(8,128)(2,1)S(1)}, u32[]{:S(2)}, u32[]{:S(2)}) collective-permute-start(bf16[160,256]{1,0:T(8,128)(2,1)S(1)} %fusion), channel_id=1, source_target_pairs={{0,2},{1,3},{2,0},{3,1},{4,6},{5,7},{6,4},{7,5},{8,10},{9,11},{10,... | collective-permute-start | bytes 245768 | tf_op jit(solution)/shard_map/ppermute | solution.py:349
  51.5 8.1 %collective-permute-start.23 = (bf16[160,256]{1,0:T(8,128)(2,1)S(1)}, bf16[160,256]{1,0:T(8,128)(2,1)S(1)}, u32[]{:S(2)}, u32[]{:S(2)}) collective-permute-start(bf16[160,256]{1,0:T(8,128)(2,1)S(1)} %fusion), channel_id=1, source_target_pairs={{0,1},{1,2},{2,3},{3,0},{4,5},{5,6},{6,7},{7,4},{8,9},{9,10},{10,1... | collective-permute-start | bytes 245768 | tf_op jit(solution)/shard_map/ppermute | solution.py:349
  56.5 11.8 %collective-permute-start.9 = (bf16[640,256]{1,0:T(8,128)(2,1)S(1)}, bf16[640,256]{1,0:T(8,128)(2,1)S(1)}, u32[]{:S(2)}, u32[]{:S(2)}) collective-permute-start(bf16[640,256]{1,0:T(8,128)(2,1)S(1)} %get-tuple-element.29), channel_id=1, source_target_pairs={{0,8},{4,12},{8,0},{12,4},{16,24},{20,28},{24,16},{28,20},{1,9},{5... | collective-permute-start | bytes 983048 | tf_op jit(solution)/shard_map/ppermute | solution.py:346
  58.0 6.7 %collective-permute-start.11 = (bf16[320,384]{1,0:T(8,128)(2,1)S(1)}, bf16[320,384]{1,0:T(8,128)(2,1)S(1)}, u32[]{:S(2)}, u32[]{:S(2)}) collective-permute-start(bf16[320,384]{1,0:T(8,128)(2,1)S(1)} %get-tuple-element.33), channel_id=1, source_target_pairs={{0,16},{4,20},{8,24},{12,28},{16,0},{20,4},{24,8},{28,12},{1,17},{... | collective-permute-start | bytes 737288 | tf_op jit(solution)/shard_map/ppermute | solution.py:346
  59.6 7.5 %collective-permute-start.31 = (bf16[160,256]{1,0:T(8,128)(2,1)S(1)}, bf16[160,256]{1,0:T(8,128)(2,1)S(1)}, u32[]{:S(2)}, u32[]{:S(2)}) collective-permute-start(bf16[160,256]{1,0:T(8,128)(2,1)S(1)} %add_convert_fusion.refs_0_), channel_id=1, source_target_pairs={{0,24},{4,28},{8,16},{12,20},{16,8},{20,12},{24,0},{28,4},{1,25},{... | collective-permute-start | bytes 245768 | tf_op jit(solution)/shard_map/ppermute | solution.py:346
  60.4 9.5 %collective-permute-start.29 = (bf16[160,256]{1,0:T(8,128)(2,1)S(1)}, bf16[160,256]{1,0:T(8,128)(2,1)S(1)}, u32[]{:S(2)}, u32[]{:S(2)}) collective-permute-start(bf16[160,256]{1,0:T(8,128)(2,1)S(1)} %add_convert_fusion.refs_0_), channel_id=1, source_target_pairs={{0,16},{4,20},{8,24},{12,28},{16,0},{20,4},{24,8},{28,12},{1,17},{... | collective-permute-start | bytes 245768 | tf_op jit(solution)/shard_map/ppermute | solution.py:346
  61.7 8.2 %collective-permute-start.27 = (bf16[160,256]{1,0:T(8,128)(2,1)S(1)}, bf16[160,256]{1,0:T(8,128)(2,1)S(1)}, u32[]{:S(2)}, u32[]{:S(2)}) collective-permute-start(bf16[160,256]{1,0:T(8,128)(2,1)S(1)} %add_convert_fusion.refs_0_), channel_id=1, source_target_pairs={{0,8},{4,12},{8,0},{12,4},{16,24},{20,28},{24,16},{28,20},{1,9},{5... | collective-permute-start | bytes 245768 | tf_op jit(solution)/shard_map/ppermute | solution.py:346
  64.8 6.1 %collective-permute-start.12 = (bf16[80,384]{1,0:T(8,128)(2,1)S(1)}, bf16[80,384]{1,0:T(8,128)(2,1)S(1)}, u32[]{:S(2)}, u32[]{:S(2)}) collective-permute-start(bf16[80,384]{1,0:T(8,128)(2,1)S(1)} %get-tuple-element.35), channel_id=1, source_target_pairs={{0,1},{1,2},{2,3},{3,0},{4,5},{5,6},{6,7},{7,4},{8,9},{9,10},{10,1... | collective-permute-start | bytes 184328 | tf_op jit(solution)/shard_map/ppermute | solution.py:349
  67.1 5.6 %collective-permute-start.13 = (bf16[80,384]{1,0:T(8,128)(2,1)S(1)}, bf16[80,384]{1,0:T(8,128)(2,1)S(1)}, u32[]{:S(2)}, u32[]{:S(2)}) collective-permute-start(bf16[80,384]{1,0:T(8,128)(2,1)S(1)} %get-tuple-element.36), channel_id=1, source_target_pairs={{0,2},{1,3},{2,0},{3,1},{4,6},{5,7},{6,4},{7,5},{8,10},{9,11},{10,... | collective-permute-start | bytes 184328 | tf_op jit(solution)/shard_map/ppermute | solution.py:349
  68.3 4.9 %collective-permute-start.14 = (bf16[80,384]{1,0:T(8,128)(2,1)S(1)}, bf16[80,384]{1,0:T(8,128)(2,1)S(1)}, u32[]{:S(2)}, u32[]{:S(2)}) collective-permute-start(bf16[80,384]{1,0:T(8,128)(2,1)S(1)} %get-tuple-element.37), channel_id=1, source_target_pairs={{0,3},{1,0},{2,1},{3,2},{4,7},{5,4},{6,5},{7,6},{8,11},{9,8},{10,9... | collective-permute-start | bytes 184328 | tf_op jit(solution)/shard_map/ppermute | solution.py:349
  69.8 3.4 %collective-permute-start.26 = (bf16[160,256]{1,0:T(8,128)(2,1)S(1)}, bf16[160,256]{1,0:T(8,128)(2,1)S(1)}, u32[]{:S(2)}, u32[]{:S(2)}) collective-permute-start(bf16[160,256]{1,0:T(8,128)(2,1)S(1)} %add_convert_fusion.refs_0_), channel_id=1, source_target_pairs={{0,4},{4,0},{8,12},{12,8},{16,20},{20,16},{24,28},{28,24},{1,5},{5... | collective-permute-start | bytes 245768 | tf_op jit(solution)/shard_map/ppermute | solution.py:346
  69.9 4.9 %collective-permute-start.32 = (bf16[160,256]{1,0:T(8,128)(2,1)S(1)}, bf16[160,256]{1,0:T(8,128)(2,1)S(1)}, u32[]{:S(2)}, u32[]{:S(2)}) collective-permute-start(bf16[160,256]{1,0:T(8,128)(2,1)S(1)} %collective-permute-done.31.refs_6_), channel_id=1, source_target_pairs={{0,4},{4,0},{8,12},{12,8},{16,20},{20,16},{24,28},{28,24},{1,5},{5... | collective-permute-start | bytes 245768 | tf_op jit(solution)/shard_map/ppermute | solution.py:346
  70.9 5.4 %collective-permute-start.30 = (bf16[160,256]{1,0:T(8,128)(2,1)S(1)}, bf16[160,256]{1,0:T(8,128)(2,1)S(1)}, u32[]{:S(2)}, u32[]{:S(2)}) collective-permute-start(bf16[160,256]{1,0:T(8,128)(2,1)S(1)} %collective-permute-done.29.refs_4_), channel_id=1, source_target_pairs={{0,4},{4,0},{8,12},{12,8},{16,20},{20,16},{24,28},{28,24},{1,5},{5... | collective-permute-start | bytes 245768 | tf_op jit(solution)/shard_map/ppermute | solution.py:346
  72.7 4.1 %collective-permute-start.28 = (bf16[160,256]{1,0:T(8,128)(2,1)S(1)}, bf16[160,256]{1,0:T(8,128)(2,1)S(1)}, u32[]{:S(2)}, u32[]{:S(2)}) collective-permute-start(bf16[160,256]{1,0:T(8,128)(2,1)S(1)} %collective-permute-done.27.refs_2_), channel_id=1, source_target_pairs={{0,4},{4,0},{8,12},{12,8},{16,20},{20,16},{24,28},{28,24},{1,5},{5... | collective-permute-start | bytes 245768 | tf_op jit(solution)/shard_map/ppermute | solution.py:346
  73.2 10.6 %collective-permute-start.10 = (bf16[320,256]{1,0:T(8,128)(2,1)S(1)}, bf16[320,256]{1,0:T(8,128)(2,1)S(1)}, u32[]{:S(2)}, u32[]{:S(2)}) collective-permute-start(bf16[320,256]{1,0:T(8,128)(2,1)S(1)} %get-tuple-element.31), channel_id=1, source_target_pairs={{0,4},{4,0},{8,12},{12,8},{16,20},{20,16},{24,28},{28,24},{1,5},{5... | collective-permute-start | bytes 491528 | tf_op jit(solution)/shard_map/ppermute | solution.py:346
  73.3 5.4 %collective-permute-start.20 = (bf16[80,384]{1,0:T(8,128)(2,1)S(1)}, bf16[80,384]{1,0:T(8,128)(2,1)S(1)}, u32[]{:S(2)}, u32[]{:S(2)}) collective-permute-start(bf16[80,384]{1,0:T(8,128)(2,1)S(1)} %add_convert_fusion.1.refs_0_), channel_id=1, source_target_pairs={{0,24},{4,28},{8,16},{12,20},{16,8},{20,12},{24,0},{28,4},{1,25},{... | collective-permute-start | bytes 184328 | tf_op jit(solution)/shard_map/ppermute | solution.py:346
  74.8 5.1 %collective-permute-start.18 = (bf16[80,384]{1,0:T(8,128)(2,1)S(1)}, bf16[80,384]{1,0:T(8,128)(2,1)S(1)}, u32[]{:S(2)}, u32[]{:S(2)}) collective-permute-start(bf16[80,384]{1,0:T(8,128)(2,1)S(1)} %add_convert_fusion.1.refs_0_), channel_id=1, source_target_pairs={{0,16},{4,20},{8,24},{12,28},{16,0},{20,4},{24,8},{28,12},{1,17},{... | collective-permute-start | bytes 184328 | tf_op jit(solution)/shard_map/ppermute | solution.py:346
  76.3 4.2 %collective-permute-start.16 = (bf16[80,384]{1,0:T(8,128)(2,1)S(1)}, bf16[80,384]{1,0:T(8,128)(2,1)S(1)}, u32[]{:S(2)}, u32[]{:S(2)}) collective-permute-start(bf16[80,384]{1,0:T(8,128)(2,1)S(1)} %add_convert_fusion.1.refs_0_), channel_id=1, source_target_pairs={{0,8},{4,12},{8,0},{12,4},{16,24},{20,28},{24,16},{28,20},{1,9},{5... | collective-permute-start | bytes 184328 | tf_op jit(solution)/shard_map/ppermute | solution.py:346
  76.8 5.3 %collective-permute-start.15 = (bf16[80,384]{1,0:T(8,128)(2,1)S(1)}, bf16[80,384]{1,0:T(8,128)(2,1)S(1)}, u32[]{:S(2)}, u32[]{:S(2)}) collective-permute-start(bf16[80,384]{1,0:T(8,128)(2,1)S(1)} %add_convert_fusion.1.refs_0_), channel_id=1, source_target_pairs={{0,4},{4,0},{8,12},{12,8},{16,20},{20,16},{24,28},{28,24},{1,5},{5... | collective-permute-start | bytes 184328 | tf_op jit(solution)/shard_map/ppermute | solution.py:346
  78.7 3.4 %collective-permute-start.21 = (bf16[80,384]{1,0:T(8,128)(2,1)S(1)}, bf16[80,384]{1,0:T(8,128)(2,1)S(1)}, u32[]{:S(2)}, u32[]{:S(2)}) collective-permute-start(bf16[80,384]{1,0:T(8,128)(2,1)S(1)} %collective-permute-done.20.refs_6_), channel_id=1, source_target_pairs={{0,4},{4,0},{8,12},{12,8},{16,20},{20,16},{24,28},{28,24},{1,5},{5... | collective-permute-start | bytes 184328 | tf_op jit(solution)/shard_map/ppermute | solution.py:346
  79.9 2.2 %collective-permute-start.19 = (bf16[80,384]{1,0:T(8,128)(2,1)S(1)}, bf16[80,384]{1,0:T(8,128)(2,1)S(1)}, u32[]{:S(2)}, u32[]{:S(2)}) collective-permute-start(bf16[80,384]{1,0:T(8,128)(2,1)S(1)} %collective-permute-done.18.refs_4_), channel_id=1, source_target_pairs={{0,4},{4,0},{8,12},{12,8},{16,20},{20,16},{24,28},{28,24},{1,5},{5... | collective-permute-start | bytes 184328 | tf_op jit(solution)/shard_map/ppermute | solution.py:346
  80.5 1.6 %collective-permute-start.17 = (bf16[80,384]{1,0:T(8,128)(2,1)S(1)}, bf16[80,384]{1,0:T(8,128)(2,1)S(1)}, u32[]{:S(2)}, u32[]{:S(2)}) collective-permute-start(bf16[80,384]{1,0:T(8,128)(2,1)S(1)} %collective-permute-done.16.refs_2_), channel_id=1, source_target_pairs={{0,4},{4,0},{8,12},{12,8},{16,20},{20,16},{24,28},{28,24},{1,5},{5... | collective-permute-start | bytes 184328 | tf_op jit(solution)/shard_map/ppermute | solution.py:346
  82.1 1.7 %copy-start.1 = (bf16[1,1,16,16,320]{4,3,2,1,0:T(8,128)(2,1)S(1)}, bf16[1,1,16,16,320]{4,3,2,1,0:T(8,128)(2,1)}, u32[]{:S(2)}) copy-start(bf16[1,1,16,16,320]{4,3,2,1,0:T(8,128)(2,1)} %param.5) | copy-start | bytes 491524

commit v2 on v1

--- a/solution.py
+++ b/solution.py
@@ -161,20 +161,32 @@
         return clip % self.group, clip // self.group, lax.axis_index("seq")
 
 
-def prepare(plan, f_ref, g_ref, w_ref, fg_ref, gt_ref, wp_ref):
-    low, _, _ = plan.place()
-    chans, slab = plan.chans, plan.slab
+def prepare(plan, f_hbm, g_hbm, w_hbm, fg_ref, gt_ref, wp_ref, wh_ref, f_ref, g_ref, w_ref, sems):
+    low, high, _ = plan.place()
+    chans, slab, half = plan.chans, plan.slab, plan.half
+    copies = [
+        pltpu.make_async_copy(src, dst, sems.at[index])
+        for index, (src, dst) in enumerate(((g_hbm, g_ref), (w_hbm, w_ref), (f_hbm, f_ref)))
+    ]
+    for copy in copies:
+        copy.start()
+    copies[0].wait()
     grad = g_ref[...].T
     gt_ref[...] = grad
     fg_ref[chans:, :] = grad
-    fg_ref[:chans, :] = f_ref[...].T
+    copies[1].wait()
     for index in range(plan.group):
 
         @pl.when(low == index)
         def _():
-            wp_ref[...] = jnp.concatenate(
-                [w_ref[tap][:, slab * index : slab * (index + 1)] for tap in range(9)], axis=1
-            )
+            taps = [w_ref[tap][:, slab * index : slab * (index + 1)] for tap in range(9)]
+            if plan.cols < 2 * half:
+                taps.append(jnp.zeros((plan.rows, 2 * half - plan.cols), BF16))
+            wp_ref[...] = jnp.concatenate(taps, axis=1)
+
+    wh_ref[...] = wp_ref[:, pl.ds(pl.multiple_of(high * half, LANES), half)]
+    copies[2].wait()
+    fg_ref[:chans, :] = f_ref[...].T
 
 
 def shifts(plan, lanes):
@@ -205,19 +217,28 @@
     return [own_ref[first, :], core_ref[first, :], pair_ref[first, :], core_ref[second, :]]
 
 
-def forward(plan, *refs):
-    w_refs = refs[: plan.seqs]
-    own_ref, pair_ref, core_ref = refs[plan.seqs : plan.seqs + 3]
-    w_all, f_all, a_ref, d_ref = refs[plan.seqs + 3 : plan.seqs + 7]
-    taps = refs[plan.seqs + 7]
-    _, _, z = plan.place()
-    rows, slab = plan.rows, plan.slab
-    for k, w_ref in enumerate(w_refs):
-        owner = (z - k + plan.seqs) % plan.seqs
-        w_all[pl.ds(pl.multiple_of(owner * rows, 16), rows), :] = w_ref[...]
+def weights(plan, *refs):
+    own_ref, got_refs, other_ref = refs[0], refs[1 : plan.seqs], refs[plan.seqs]
+    mine_ref, pair_ref, w_all, w_turned, both_ref = refs[plan.seqs + 1 :]
+    _, high, z = plan.place()
+    rows, half = plan.rows, plan.half
+    here = pl.ds(pl.multiple_of(high * half, LANES), half)
+    there = pl.ds(pl.multiple_of((1 - high) * half, LANES), half)
+    w_all[pl.ds(pl.multiple_of(z * rows, 16), rows), :] = own_ref[...]
+    for k, got_ref in enumerate(got_refs, 1):
+        place = pl.ds(pl.multiple_of((z - k + plan.seqs) % plan.seqs * rows, 16), rows)
+        w_all[place, here] = got_ref[...]
+        w_all[place, there] = other_ref[(k - 1) * rows : k * rows, :]
+    w_turned[...] = w_all[...].T
+    both_ref[: 2 * plan.chans, :] = mine_ref[...]
+    both_ref[2 * plan.chans :, :] = pair_ref[...]
+
+
+def forward(plan, w_turned, own_ref, pair_ref, core_ref, f_all, a_ref, d_ref, taps):
+    slab = plan.slab
     for d, frame in enumerate(group_frames(plan, own_ref, pair_ref, core_ref, 0)):
         f_all[:, d * plan.pixels : (d + 1) * plan.pixels] = frame
-    taps[...] = mm(w_all[...], f_all[...], TN)
+    taps[...] = mm(w_turned[: plan.cols, :], f_all[...], NN)
     total = None
     for tap, (distance, inside) in enumerate(shifts(plan, f_all.shape[1])):
         term = rolled(taps[tap * slab : (tap + 1) * slab, :], distance)
@@ -281,11 +302,17 @@
     size = plan.half
     s_keep[...] = total[:, pl.ds(pl.multiple_of(high * size, LANES), size)]
     s_send[...] = total[:, pl.ds(pl.multiple_of((1 - high) * size, LANES), size)].astype(BF16)
-    grads = mm(w_all[...], expanded[...], NN)
+    grads = mm(w_all[:, : plan.cols], expanded[...], NN)
     for d in range(2):
         f_keep[d * chans : (d + 1) * chans, :] = grads[:, d * pixels : (d + 1) * pixels]
         there = grads[:, (2 + d) * pixels : (3 + d) * pixels]
         f_send[d * chans : (d + 1) * chans, :] = there.astype(BF16)
+
+
+def time_rows(plan, keep_ref, got_ref, after_ref, own_ref, send_ref):
+    total = keep_ref[...] + got_ref[...].astype(F32)
+    own_ref[...] = total
+    send_ref[...] = total.astype(BF16)
 
 
 def frame_half(plan, keep_ref, got_ref, send_ref, own_ref):
@@ -345,32 +372,63 @@
     def swap(value, distance):
         return lax.ppermute(value, "clip", [(i, i ^ distance) for i in range(plan.clips)])
 
+    def neighbours(value):
+        z = lax.axis_index("seq")
+        found = []
+        for first in range(2):
+            other = {i: i for i in range(seqs)}
+            for i in range(first, seqs - 1, 2):
+                other[i], other[i + 1] = i + 1, i
+            found.append(lax.ppermute(value, "seq", list(other.items())))
+        low, high = jnp.where(z % 2 == 1, *found), jnp.where(z % 2 == 1, *found[::-1])
+        zero = jnp.zeros_like(value)
+        return jnp.where(z == 0, zero, low), jnp.where(z == seqs - 1, zero, high)
+
     def turn(value, k):
         return lax.ppermute(value, "seq", [(i, (i + k) % seqs) for i in range(seqs)])
 
     clip_f, clip_g = frames.reshape(pixels, chans), cotangent.reshape(pixels, chans)
-    own, grad, piece = call(
+    taps = jnp.transpose(w_space, (1, 0, 2))
+    outs = [
+        ((2 * chans, pixels), BF16),
+        ((chans, pixels), BF16),
+        ((rows, 2 * plan.half), BF16),
+        ((rows, plan.half), BF16),
+    ]
+    own, grad, piece, part_piece = pl.pallas_call(
         part(prepare),
-        [((2 * chans, pixels), BF16), ((chans, pixels), BF16), ((rows, cols), BF16)],
-        clip_f,
-        clip_g,
-        jnp.transpose(w_space, (1, 0, 2)),
-    )
-    before = lax.ppermute(grad, "seq", [(i, i + 1) for i in range(seqs - 1)])
-    after = lax.ppermute(grad, "seq", [(i + 1, i) for i in range(seqs - 1)])
-    pieces = [piece] + [turn(piece, k) for k in range(1, seqs)]
-
-    def gathered(block):
-        pair = swap(block, 2)
-        return block, pair, swap(jnp.concatenate([block, pair], axis=0), 1)
-
-    fg = gathered(own)
-    halo = gathered(jnp.concatenate([before, after], axis=0))
+        out_shape=tuple(jax.ShapeDtypeStruct(shape, dtype) for shape, dtype in outs),
+        in_specs=[pl.BlockSpec(memory_space=pl.ANY)] * 3,
+        out_specs=(VMEM,) * len(outs),
+        scratch_shapes=[
+            pltpu.VMEM(clip_f.shape, BF16),
+            pltpu.VMEM(clip_g.shape, BF16),
+            pltpu.VMEM(taps.shape, BF16),
+            pltpu.SemaphoreType.DMA((3,)),
+        ],
+    )(clip_f, clip_g, taps)
+    before, after = neighbours(grad)
+    got = [turn(part_piece, k) for k in range(1, seqs)]
+    other = swap(jnp.concatenate(got, axis=0), group)
+    pair = swap(own, 2)
+    w_all, w_turned, both = call(
+        part(weights),
+        [((chans, 2 * plan.half), BF16), ((2 * plan.half, chans), BF16), ((4 * chans, pixels), BF16)],
+        piece,
+        *got,
+        other,
+        own,
+        pair,
+    )
+    fg = (own, pair, swap(both, 1))
+    halo_own = jnp.concatenate([before, after], axis=0)
+    halo_pair = swap(halo_own, 2)
+    halo = (halo_own, halo_pair, swap(jnp.concatenate([halo_own, halo_pair], axis=0), 1))
     lanes = group * pixels
-    w_all, f_all, acts, slope = call(
+    f_all, acts, slope = call(
         part(forward),
-        [((chans, cols), BF16), ((chans, lanes), BF16), ((slab, lanes), BF16), ((slab, lanes), F32)],
-        *pieces,
+        [((chans, lanes), BF16), ((slab, lanes), BF16), ((slab, lanes), F32)],
+        w_turned,
         *fg,
         scratch=[pltpu.VMEM((cols, lanes), F32)],
     )
@@ -402,8 +460,9 @@
     s_got = swap(s_send, group)
     f_got = swap(f_send, 2)
 
-    t_part = (t_keep + t_got.astype(F32)).astype(BF16)
-    t_sum = t_keep + t_got.astype(F32)
+    t_sum, t_part = call(
+        part(time_rows), [(t_keep.shape, F32), (t_keep.shape, BF16)], t_keep, t_got, s_send
+    )
     for k in range(1, seqs):
         t_sum = t_sum + turn(t_part, k).astype(F32)
     t_sum = t_sum.astype(BF16)

time: 85 us -> 70.7 us (0.83)
  waiting for transfers between devices: 36.4 us -> 23.1 us
  local copies, waits for them, and re-layouts: 2.93 us -> 0.02 us
  Pallas kernels: 9.61 us -> 11.7 us
    ppermute x9, waiting for transfers between devices: 13.3 us -> 8.35 us  [turn(): lax.ppermute(value, 'seq', [(i, (i + k) % seqs) for i in range(seqs)])]
    ppermute x22 -> x23, waiting for transfers between devices: 18.4 us -> 13.5 us  [swap(): lax.ppermute(value, 'clip', [(i, i ^ distance) for i in range(plan.clips)])]
    ppermute x2, waiting for transfers between devices: 4.73 us -> 1.24 us  [neighbours(): found.append(lax.ppermute(value, 'seq', list(other.items())))]
    unnamed x9 -> x6, local copies, waits for them, and re-layouts: 2.91 us -> 0.02 us
    pallas_call x0 -> x1, Pallas kernels: none -> 2.16 us  [per_device(): pl.pallas_call(part(prepare), out_shape=tuple((jax.ShapeDtypeStruct(shape...]
    ppermute x9, starting transfers between devices: 12.8 us -> 10.9 us  [turn(): lax.ppermute(value, 'seq', [(i, (i + k) % seqs) for i in range(seqs)])]
    ppermute x22 -> x23, starting transfers between devices: 15.7 us -> 17 us  [swap(): lax.ppermute(value, 'clip', [(i, i ^ distance) for i in range(plan.clips)])]
    pallas_call x9 -> x10, Pallas kernels: 9.61 us -> 9.54 us  [call(): pl.pallas_call(kernel, out_shape=tuple((jax.ShapeDtypeStruct(shape, dtype...]
  transfers between devices with their start and end apart: 33 -> 34, of which waited for: 15 -> 14; matrix products, arithmetic and copies ran while one was open for 0% -> 0% of each run, Pallas kernels for 9% -> 11%
where the time goes in v2:
time: 70.7 us; the launch traced here: 70.4 us
  starting transfers between devices  34.6 us (49%)
  waiting for transfers between devices  23.1 us (33%)
  Pallas kernels  11.7 us (17%)
  between operations  0.85 us (1%)
    ppermute x23, starting transfers between devices, swap(): lax.ppermute(value, 'clip', [(i, i ^ distance) for i in range(plan.clips)])  17 us
    ppermute x23, waiting for transfers between devices, swap(): lax.ppermute(value, 'clip', [(i, i ^ distance) for i in range(plan.clips)])  13.5 us
    ppermute x9, starting transfers between devices, turn(): lax.ppermute(value, 'seq', [(i, (i + k) % seqs) for i in range(seqs)])  10.9 us
    pallas_call x10, Pallas kernels, call(): pl.pallas_call(kernel, out_shape=tuple((jax.ShapeDtypeStruct(shape, dtype...  9.54 us
    ppermute x9, waiting for transfers between devices, turn(): lax.ppermute(value, 'seq', [(i, (i + k) % seqs) for i in range(seqs)])  8.35 us
    ppermute x2, starting transfers between devices, neighbours(): found.append(lax.ppermute(value, 'seq', list(other.items())))  6.71 us
    pallas_call x1, Pallas kernels, per_device(): pl.pallas_call(part(prepare), out_shape=tuple((jax.ShapeDtypeStruct(shape...  2.16 us
  transfers between devices with their start and end apart: 34, of which 14 were waited for; matrix products, arithmetic and copies ran while one was open for 0% of the time, Pallas kernels for 11%

profile of v2, /device:TPU:0, one launch (start us, length us, event | category | flops | bytes accessed | tf_op | source)
XLA Modules:
  0.0 70.4 jit_solution(9608616880715666350)
XLA Ops:
  0.6 2.2 %shard_map.67 = (bf16[640,256]{1,0:T(8,128)(2,1)}, bf16[320,256]{1,0:T(8,128)(2,1)}, bf16[80,768]{1,0:T(8,128)(2,1)}, bf16[80,384]{1,0:T(8,128)(2,1)}) custom-call(bf16[256,320]{1,0:T(8,128)(2,1)} %bitcast.10, bf16[256,320]{1,0:T(8,128)(2,1)} %bitcast.5, bf16[9,80,320]{2,1,0:T(8,128)(2,1)} %bitcast.8), custom_call_target="tpu_custom_call" | custom-call | tf_op jit(solution)/shard_map/pallas_call | solution.py:398
  2.8 1.7 %collective-permute-start.7 = (bf16[320,256]{1,0:T(8,128)(2,1)}, bf16[320,256]{1,0:T(8,128)(2,1)S(1)}, u32[]{:S(2)}, u32[]{:S(2)}) collective-permute-start(bf16[320,256]{1,0:T(8,128)(2,1)} %get-tuple-element.35), channel_id=1, source_target_pairs={{0,0},{1,2},{2,1},{3,3},{4,4},{5,6},{6,5},{7,7},{8,8},{9,10},{10,9... | collective-permute-start | bytes 491528 | tf_op jit(solution)/shard_map/ppermute | solution.py:382
  4.5 5.0 %collective-permute-start.6 = (bf16[320,256]{1,0:T(8,128)(2,1)}, bf16[320,256]{1,0:T(8,128)(2,1)S(1)}, u32[]{:S(2)}, u32[]{:S(2)}) collective-permute-start(bf16[320,256]{1,0:T(8,128)(2,1)} %get-tuple-element.35), channel_id=1, source_target_pairs={{0,1},{1,0},{2,3},{3,2},{4,5},{5,4},{6,7},{7,6},{8,9},{9,8},{10,11... | collective-permute-start | bytes 491528 | tf_op jit(solution)/shard_map/ppermute | solution.py:382
  9.5 1.3 %collective-permute-start.2 = (bf16[80,384]{1,0:T(8,128)(2,1)}, bf16[80,384]{1,0:T(8,128)(2,1)S(1)}, u32[]{:S(2)}, u32[]{:S(2)}) collective-permute-start(bf16[80,384]{1,0:T(8,128)(2,1)} %get-tuple-element.28), channel_id=1, source_target_pairs={{0,3},{1,0},{2,1},{3,2},{4,7},{5,4},{6,5},{7,6},{8,11},{9,8},{10,9... | collective-permute-start | bytes 184328 | tf_op jit(solution)/shard_map/ppermute | solution.py:388
  10.9 0.2 collective-permute-start.1
  11.1 1.1 %collective-permute-start = (bf16[80,384]{1,0:T(8,128)(2,1)}, bf16[80,384]{1,0:T(8,128)(2,1)S(1)}, u32[]{:S(2)}, u32[]{:S(2)}) collective-permute-start(bf16[80,384]{1,0:T(8,128)(2,1)} %get-tuple-element.28), channel_id=1, source_target_pairs={{0,1},{1,2},{2,3},{3,0},{4,5},{5,6},{6,7},{7,4},{8,9},{9,10},{10,1... | collective-permute-start | bytes 184328 | tf_op jit(solution)/shard_map/ppermute | solution.py:388
  12.2 1.5 %collective-permute-start.4 = (bf16[640,256]{1,0:T(8,128)(2,1)}, bf16[640,256]{1,0:T(8,128)(2,1)S(1)}, u32[]{:S(2)}, u32[]{:S(2)}) collective-permute-start(bf16[640,256]{1,0:T(8,128)(2,1)} %get-tuple-element.29.refs_5_.own_ref.refs_4_.refs_0_), channel_id=1, source_target_pairs={{0,8},{4,12},{8,0},{12,4},{16,24},{20,28},{24,16},{28,20},{1,9},{5... | collective-permute-start | bytes 983048 | tf_op jit(solution)/shard_map/ppermute | solution.py:373
  13.7 1.2 %collective-permute-done.6 = bf16[320,256]{1,0:T(8,128)(2,1)S(1)} collective-permute-done((bf16[320,256]{1,0:T(8,128)(2,1)}, bf16[320,256]{1,0:T(8,128)(2,1)S(1)}, u32[]{:S(2)}, u32[]{:S(2)}) %collective-permute-start.6) | collective-permute-done | bytes 163872 | tf_op jit(solution)/shard_map/ppermute | solution.py:382
  15.0 1.5 %collective-permute-start.8 = (bf16[640,256]{1,0:T(8,128)(2,1)S(1)}, bf16[640,256]{1,0:T(8,128)(2,1)S(1)}, u32[]{:S(2)}, u32[]{:S(2)}) collective-permute-start(bf16[640,256]{1,0:T(8,128)(2,1)S(1)} %pad_maximum_fusion.1.refs_7_.refs_3_), channel_id=1, source_target_pairs={{0,8},{4,12},{8,0},{12,4},{16,24},{20,28},{24,16},{28,20},{1,9},{5... | collective-permute-start | bytes 983048 | tf_op jit(solution)/shard_map/ppermute | solution.py:373
  16.5 0.9 %collective-permute-done.1.refs_2_ = bf16[80,384]{1,0:T(8,128)(2,1)S(1)} collective-permute-done((bf16[80,384]{1,0:T(8,128)(2,1)}, bf16[80,384]{1,0:T(8,128)(2,1)S(1)}, u32[]{:S(2)}, u32[]{:S(2)}) %collective-permute-start.1) | collective-permute-done | bytes 61472 | tf_op jit(solution)/shard_map/ppermute | solution.py:388
  17.5 1.3 %collective-permute-done.refs_1_ = bf16[80,384]{1,0:T(8,128)(2,1)S(1)} collective-permute-done((bf16[80,384]{1,0:T(8,128)(2,1)}, bf16[80,384]{1,0:T(8,128)(2,1)S(1)}, u32[]{:S(2)}, u32[]{:S(2)}) %collective-permute-start) | collective-permute-done | bytes 61472 | tf_op jit(solution)/shard_map/ppermute | solution.py:388
  18.8 1.6 %collective-permute-start.3 = (bf16[240,384]{1,0:T(8,128)(2,1)S(1)}, bf16[240,384]{1,0:T(8,128)(2,1)S(1)}, u32[]{:S(2)}, u32[]{:S(2)}) collective-permute-start(bf16[240,384]{1,0:T(8,128)(2,1)S(1)} %pad_maximum_fusion.2), channel_id=1, source_target_pairs={{0,16},{4,20},{8,24},{12,28},{16,0},{20,4},{24,8},{28,12},{1,17},{... | collective-permute-start | bytes 552968 | tf_op jit(solution)/shard_map/ppermute | solution.py:373
  20.4 4.0 %collective-permute-done.3.refs_4_ = bf16[240,384]{1,0:T(8,128)(2,1)S(1)} collective-permute-done((bf16[240,384]{1,0:T(8,128)(2,1)S(1)}, bf16[240,384]{1,0:T(8,128)(2,1)S(1)}, u32[]{:S(2)}, u32[]{:S(2)}) %collective-permute-start.3) | collective-permute-done | bytes 184352 | tf_op jit(solution)/shard_map/ppermute | solution.py:373
  24.4 0.3 shard_map.68
  24.7 0.1 collective-permute-start.5
  24.8 3.0 %collective-permute-done.8.refs_8_.refs_4_ = bf16[640,256]{1,0:T(8,128)(2,1)S(1)} collective-permute-done((bf16[640,256]{1,0:T(8,128)(2,1)S(1)}, bf16[640,256]{1,0:T(8,128)(2,1)S(1)}, u32[]{:S(2)}, u32[]{:S(2)}) %collective-permute-start.8) | collective-permute-done | bytes 327712 | tf_op jit(solution)/shard_map/ppermute | solution.py:373
  27.8 0.1 collective-permute-start.9
  27.9 1.3 %shard_map.69 = (bf16[320,1024]{1,0:T(8,128)(2,1)S(1)}, bf16[80,1024]{1,0:T(8,128)(2,1)S(1)}, f32[80,1024]{1,0:T(8,128)S(1)}) custom-call(bf16[768,320]{1,0:T(8,128)(2,1)S(1)} %get-tuple-element.31.w_turned, bf16[640,256]{1,0:T(8,128)(2,1)S(1)} %copy-done, bf16[640,256]{1,0:T(8,128)(2,1)S(1)} %collective-permute-done.4.refs_6_.pair_ref.refs_5_.refs_1_, ...), custom_call_target="tpu_custom_call" | custom-call | tf_op jit(solution)/shard_map/pallas_call | solution.py:123
  29.2 0.8 %collective-permute-done.9.refs_9_.refs_5_ = bf16[1280,256]{1,0:T(8,128)(2,1)S(1)} collective-permute-done((bf16[1280,256]{1,0:T(8,128)(2,1)S(1)}, bf16[1280,256]{1,0:T(8,128)(2,1)S(1)}, u32[]{:S(2)}, u32[]{:S(2)}) %collective-permute-start.9) | collective-permute-done | bytes 655392 | tf_op jit(solution)/shard_map/ppermute | solution.py:373
  30.0 0.8 %shard_map.75 = (bf16[160,256]{1,0:T(8,128)(2,1)S(1)}, f32[160,256]{1,0:T(8,128)S(1)}) custom-call(bf16[80,1024]{1,0:T(8,128)(2,1)S(1)} %get-tuple-element.46.a_ref, bf16[640,256]{1,0:T(8,128)(2,1)S(1)} %copy-done, bf16[640,256]{1,0:T(8,128)(2,1)S(1)} %collective-permute-done.4.refs_6_.pair_ref.refs_5_.refs_1_, ...), custom_call_target="tpu_custom_call" | custom-call | tf_op jit(solution)/shard_map/pallas_call | solution.py:123
  30.7 1.6 %collective-permute-start.23 = (bf16[160,256]{1,0:T(8,128)(2,1)S(1)}, bf16[160,256]{1,0:T(8,128)(2,1)S(1)}, u32[]{:S(2)}, u32[]{:S(2)}) collective-permute-start(bf16[160,256]{1,0:T(8,128)(2,1)S(1)} %get-tuple-element.48), channel_id=1, source_target_pairs={{0,16},{4,20},{8,24},{12,28},{16,0},{20,4},{24,8},{28,12},{1,17},{... | collective-permute-start | bytes 245768 | tf_op jit(solution)/shard_map/ppermute | solution.py:373
  32.3 3.0 %shard_map.70 = (bf16[320,384]{1,0:T(8,128)(2,1)S(1)}, f32[320,384]{1,0:T(8,128)S(1)}, bf16[640,256]{1,0:T(8,128)(2,1)S(1)}, f32[640,256]{1,0:T(8,128)S(1)}) custom-call(bf16[320,768]{1,0:T(8,128)(2,1)S(1)} %get-tuple-element.30.refs_0_, bf16[320,1024]{1,0:T(8,128)(2,1)S(1)} %get-tuple-element.33.refs_1_, f32[80,1024]{1,0:T(8,128)S(1)} %get-tuple-element.34.refs_2_, ...), custom_call_target="tpu_custom_call" | custom-call | tf_op jit(solution)/shard_map/pallas_call | solution.py:123
  35.4 2.8 %collective-permute-start.26 = (bf16[160,256]{1,0:T(8,128)(2,1)S(1)}, bf16[160,256]{1,0:T(8,128)(2,1)S(1)}, u32[]{:S(2)}, u32[]{:S(2)}) collective-permute-start(bf16[160,256]{1,0:T(8,128)(2,1)S(1)} %get-tuple-element.50), channel_id=1, source_target_pairs={{0,3},{1,0},{2,1},{3,2},{4,7},{5,4},{6,5},{7,6},{8,11},{9,8},{10,9... | collective-permute-start | bytes 245768 | tf_op jit(solution)/shard_map/ppermute | solution.py:388
  38.2 0.9 %collective-permute-start.25 = (bf16[160,256]{1,0:T(8,128)(2,1)S(1)}, bf16[160,256]{1,0:T(8,128)(2,1)S(1)}, u32[]{:S(2)}, u32[]{:S(2)}) collective-permute-start(bf16[160,256]{1,0:T(8,128)(2,1)S(1)} %get-tuple-element.50), channel_id=1, source_target_pairs={{0,2},{1,3},{2,0},{3,1},{4,6},{5,7},{6,4},{7,5},{8,10},{9,11},{10,... | collective-permute-start | bytes 245768 | tf_op jit(solution)/shard_map/ppermute | solution.py:388
  39.0 1.6 %collective-permute-start.24 = (bf16[160,256]{1,0:T(8,128)(2,1)S(1)}, bf16[160,256]{1,0:T(8,128)(2,1)S(1)}, u32[]{:S(2)}, u32[]{:S(2)}) collective-permute-start(bf16[160,256]{1,0:T(8,128)(2,1)S(1)} %get-tuple-element.50), channel_id=1, source_target_pairs={{0,1},{1,2},{2,3},{3,0},{4,5},{5,6},{6,7},{7,4},{8,9},{9,10},{10,1... | collective-permute-start | bytes 245768 | tf_op jit(solution)/shard_map/ppermute | solution.py:388
  40.6 1.5 %collective-permute-start.10 = (bf16[640,256]{1,0:T(8,128)(2,1)S(1)}, bf16[640,256]{1,0:T(8,128)(2,1)S(1)}, u32[]{:S(2)}, u32[]{:S(2)}) collective-permute-start(bf16[640,256]{1,0:T(8,128)(2,1)S(1)} %get-tuple-element.37), channel_id=1, source_target_pairs={{0,8},{4,12},{8,0},{12,4},{16,24},{20,28},{24,16},{28,20},{1,9},{5... | collective-permute-start | bytes 983048 | tf_op jit(solution)/shard_map/ppermute | solution.py:373
  42.1 1.4 %collective-permute-start.12 = (bf16[320,384]{1,0:T(8,128)(2,1)S(1)}, bf16[320,384]{1,0:T(8,128)(2,1)S(1)}, u32[]{:S(2)}, u32[]{:S(2)}) collective-permute-start(bf16[320,384]{1,0:T(8,128)(2,1)S(1)} %get-tuple-element.41.after_ref), channel_id=1, source_target_pairs={{0,16},{4,20},{8,24},{12,28},{16,0},{20,4},{24,8},{28,12},{1,17},{... | collective-permute-start | bytes 737288 | tf_op jit(solution)/shard_map/ppermute | solution.py:373
  43.6 3.2 %collective-permute-done.25 = bf16[160,256]{1,0:T(8,128)(2,1)S(1)} collective-permute-done((bf16[160,256]{1,0:T(8,128)(2,1)S(1)}, bf16[160,256]{1,0:T(8,128)(2,1)S(1)}, u32[]{:S(2)}, u32[]{:S(2)}) %collective-permute-start.25) | collective-permute-done | bytes 81952 | tf_op jit(solution)/shard_map/ppermute | solution.py:388
  46.8 2.4 %collective-permute-start.32 = (bf16[160,256]{1,0:T(8,128)(2,1)S(1)}, bf16[160,256]{1,0:T(8,128)(2,1)S(1)}, u32[]{:S(2)}, u32[]{:S(2)}) collective-permute-start(bf16[160,256]{1,0:T(8,128)(2,1)S(1)} %add_convert_fusion.refs_0_), channel_id=1, source_target_pairs={{0,24},{4,28},{8,16},{12,20},{16,8},{20,12},{24,0},{28,4},{1,25},{... | collective-permute-start | bytes 245768 | tf_op jit(solution)/shard_map/ppermute | solution.py:373
  49.2 0.6 collective-permute-start.30
  49.8 0.5 collective-permute-start.28
  50.3 0.1 shard_map.73
  50.5 1.9 %collective-permute-done.32.refs_6_ = bf16[160,256]{1,0:T(8,128)(2,1)S(1)} collective-permute-done((bf16[160,256]{1,0:T(8,128)(2,1)S(1)}, bf16[160,256]{1,0:T(8,128)(2,1)S(1)}, u32[]{:S(2)}, u32[]{:S(2)}) %collective-permute-start.32) | collective-permute-done | bytes 81952 | tf_op jit(solution)/shard_map/ppermute | solution.py:373
  52.3 2.1 %collective-permute-start.14 = (bf16[80,384]{1,0:T(8,128)(2,1)S(1)}, bf16[80,384]{1,0:T(8,128)(2,1)S(1)}, u32[]{:S(2)}, u32[]{:S(2)}) collective-permute-start(bf16[80,384]{1,0:T(8,128)(2,1)S(1)} %get-tuple-element.44), channel_id=1, source_target_pairs={{0,2},{1,3},{2,0},{3,1},{4,6},{5,7},{6,4},{7,5},{8,10},{9,11},{10,... | collective-permute-start | bytes 184328 | tf_op jit(solution)/shard_map/ppermute | solution.py:388
  54.5 0.8 %collective-permute-start.15 = (bf16[80,384]{1,0:T(8,128)(2,1)S(1)}, bf16[80,384]{1,0:T(8,128)(2,1)S(1)}, u32[]{:S(2)}, u32[]{:S(2)}) collective-permute-start(bf16[80,384]{1,0:T(8,128)(2,1)S(1)} %get-tuple-element.45), channel_id=1, source_target_pairs={{0,3},{1,0},{2,1},{3,2},{4,7},{5,4},{6,5},{7,6},{8,11},{9,8},{10,9... | collective-permute-start | bytes 184328 | tf_op jit(solution)/shard_map/ppermute | solution.py:388
  55.5 0.5 collective-permute-start.33
  56.0 0.9 %collective-permute-done.13 = bf16[80,384]{1,0:T(8,128)(2,1)S(1)} collective-permute-done((bf16[80,384]{1,0:T(8,128)(2,1)S(1)}, bf16[80,384]{1,0:T(8,128)(2,1)S(1)}, u32[]{:S(2)}, u32[]{:S(2)}) %collective-permute-start.13) | collective-permute-done | bytes 61472 | tf_op jit(solution)/shard_map/ppermute | solution.py:388
  56.9 1.4 %collective-permute-done.14 = bf16[80,384]{1,0:T(8,128)(2,1)S(1)} collective-permute-done((bf16[80,384]{1,0:T(8,128)(2,1)S(1)}, bf16[80,384]{1,0:T(8,128)(2,1)S(1)}, u32[]{:S(2)}, u32[]{:S(2)}) %collective-permute-start.14) | collective-permute-done | bytes 61472 | tf_op jit(solution)/shard_map/ppermute | solution.py:388
  58.3 0.6 collective-permute-done.15
  58.9 2.4 %collective-permute-start.21 = (bf16[80,384]{1,0:T(8,128)(2,1)S(1)}, bf16[80,384]{1,0:T(8,128)(2,1)S(1)}, u32[]{:S(2)}, u32[]{:S(2)}) collective-permute-start(bf16[80,384]{1,0:T(8,128)(2,1)S(1)} %add_convert_fusion.1.refs_0_), channel_id=1, source_target_pairs={{0,24},{4,28},{8,16},{12,20},{16,8},{20,12},{24,0},{28,4},{1,25},{... | collective-permute-start | bytes 184328 | tf_op jit(solution)/shard_map/ppermute | solution.py:373
  61.3 0.8 %collective-permute-start.19 = (bf16[80,384]{1,0:T(8,128)(2,1)S(1)}, bf16[80,384]{1,0:T(8,128)(2,1)S(1)}, u32[]{:S(2)}, u32[]{:S(2)}) collective-permute-start(bf16[80,384]{1,0:T(8,128)(2,1)S(1)} %add_convert_fusion.1.refs_0_), channel_id=1, source_target_pairs={{0,16},{4,20},{8,24},{12,28},{16,0},{20,4},{24,8},{28,12},{1,17},{... | collective-permute-start | bytes 184328 | tf_op jit(solution)/shard_map/ppermute | solution.py:373
  62.1 0.4 collective-permute-start.17
  62.5 1.8 %collective-permute-done.21.refs_6_ = bf16[80,384]{1,0:T(8,128)(2,1)S(1)} collective-permute-done((bf16[80,384]{1,0:T(8,128)(2,1)S(1)}, bf16[80,384]{1,0:T(8,128)(2,1)S(1)}, u32[]{:S(2)}, u32[]{:S(2)}) %collective-permute-start.21) | collective-permute-done | bytes 61472 | tf_op jit(solution)/shard_map/ppermute | solution.py:373
  64.3 1.3 %collective-permute-done.19.refs_4_ = bf16[80,384]{1,0:T(8,128)(2,1)S(1)} collective-permute-done((bf16[80,384]{1,0:T(8,128)(2,1)S(1)}, bf16[80,384]{1,0:T(8,128)(2,1)S(1)}, u32[]{:S(2)}, u32[]{:S(2)}) %collective-permute-start.19) | collective-permute-done | bytes 61472 | tf_op jit(solution)/shard_map/ppermute | solution.py:373
  65.6 0.7 collective-permute-done.17.refs_2_
  66.3 1.6 %shard_map.77 = f32[3,320,320]{2,1,0:T(8,128)} custom-call(bf16[160,256]{1,0:T(8,128)(2,1)S(1)} %add_convert_fusion.refs_0_, bf16[160,256]{1,0:T(8,128)(2,1)S(1)} %collective-permute-done.27.refs_1_, bf16[160,256]{1,0:T(8,128)(2,1)S(1)} %collective-permute-done.28.refs_2_, bf16[160,256]{1,0:T(8,128)(2,1)S(1)} %collective-permute-done.29.refs_3_, ...), custom_call_target="tpu_custom_call" | custom-call | tf_op jit(solution)/shard_map/pallas_call | solution.py:123
  67.9 1.6 %shard_map.74 = f32[9,80,320]{2,1,0:T(8,128)} custom-call(bf16[80,384]{1,0:T(8,128)(2,1)S(1)} %add_convert_fusion.1.refs_0_, bf16[80,384]{1,0:T(8,128)(2,1)S(1)} %collective-permute-done.16.refs_1_, bf16[80,384]{1,0:T(8,128)(2,1)S(1)} %collective-permute-done.17.refs_2_, bf16[80,384]{1,0:T(8,128)(2,1)S(1)} %collective-permute-done.18.refs_3_, ...), custom_call_target="tpu_custom_call" | custom-call | tf_op jit(solution)/shard_map/pallas_call | solution.py:123
  69.6 0.9 %shard_map.72 = bf16[256,320]{1,0:T(8,128)(2,1)} custom-call(f32[320,256]{1,0:T(8,128)S(1)} %get-tuple-element.38.own_ref, bf16[320,256]{1,0:T(8,128)(2,1)S(1)} %collective-permute-done.11.got_ref, bf16[256,320]{1,0:T(8,128)(2,1)S(1)} %bitcast.6), custom_call_target="tpu_custom_call" | custom-call | tf_op jit(solution)/shard_map/pallas_call | solution.py:123
  (43 shorter events, 0.5 us)
Async XLA Ops:
  2.8 21.6 %copy-start = (bf16[640,256]{1,0:T(8,128)(2,1)S(1)}, bf16[640,256]{1,0:T(8,128)(2,1)}, u32[]{:S(2)}) copy-start(bf16[640,256]{1,0:T(8,128)(2,1)} %get-tuple-element.29.refs_5_.own_ref.refs_4_.refs_0_) | copy-start | bytes 983044
  2.8 21.6 %copy-start.2 = (bf16[80,768]{1,0:T(8,128)(2,1)S(1)}, bf16[80,768]{1,0:T(8,128)(2,1)}, u32[]{:S(2)}) copy-start(bf16[80,768]{1,0:T(8,128)(2,1)} %get-tuple-element.27.refs_0_) | copy-start | bytes 368644
  2.8 9.4 %collective-permute-start.7 = (bf16[320,256]{1,0:T(8,128)(2,1)}, bf16[320,256]{1,0:T(8,128)(2,1)S(1)}, u32[]{:S(2)}, u32[]{:S(2)}) collective-permute-start(bf16[320,256]{1,0:T(8,128)(2,1)} %get-tuple-element.35), channel_id=1, source_target_pairs={{0,0},{1,2},{2,1},{3,3},{4,4},{5,6},{6,5},{7,7},{8,8},{9,10},{10,9... | collective-permute-start | bytes 491528 | tf_op jit(solution)/shard_map/ppermute | solution.py:382
  4.5 10.4 %collective-permute-start.6 = (bf16[320,256]{1,0:T(8,128)(2,1)}, bf16[320,256]{1,0:T(8,128)(2,1)S(1)}, u32[]{:S(2)}, u32[]{:S(2)}) collective-permute-start(bf16[320,256]{1,0:T(8,128)(2,1)} %get-tuple-element.35), channel_id=1, source_target_pairs={{0,1},{1,0},{2,3},{3,2},{4,5},{5,4},{6,7},{7,6},{8,9},{9,8},{10,11... | collective-permute-start | bytes 491528 | tf_op jit(solution)/shard_map/ppermute | solution.py:382
  9.5 7.0 %collective-permute-start.2 = (bf16[80,384]{1,0:T(8,128)(2,1)}, bf16[80,384]{1,0:T(8,128)(2,1)S(1)}, u32[]{:S(2)}, u32[]{:S(2)}) collective-permute-start(bf16[80,384]{1,0:T(8,128)(2,1)} %get-tuple-element.28), channel_id=1, source_target_pairs={{0,3},{1,0},{2,1},{3,2},{4,7},{5,4},{6,5},{7,6},{8,11},{9,8},{10,9... | collective-permute-start | bytes 184328 | tf_op jit(solution)/shard_map/ppermute | solution.py:388
  10.9 6.6 %collective-permute-start.1 = (bf16[80,384]{1,0:T(8,128)(2,1)}, bf16[80,384]{1,0:T(8,128)(2,1)S(1)}, u32[]{:S(2)}, u32[]{:S(2)}) collective-permute-start(bf16[80,384]{1,0:T(8,128)(2,1)} %get-tuple-element.28), channel_id=1, source_target_pairs={{0,2},{1,3},{2,0},{3,1},{4,6},{5,7},{6,4},{7,5},{8,10},{9,11},{10,... | collective-permute-start | bytes 184328 | tf_op jit(solution)/shard_map/ppermute | solution.py:388
  11.1 7.7 %collective-permute-start = (bf16[80,384]{1,0:T(8,128)(2,1)}, bf16[80,384]{1,0:T(8,128)(2,1)S(1)}, u32[]{:S(2)}, u32[]{:S(2)}) collective-permute-start(bf16[80,384]{1,0:T(8,128)(2,1)} %get-tuple-element.28), channel_id=1, source_target_pairs={{0,1},{1,2},{2,3},{3,0},{4,5},{5,6},{6,7},{7,4},{8,9},{9,10},{10,1... | collective-permute-start | bytes 184328 | tf_op jit(solution)/shard_map/ppermute | solution.py:388
  12.2 12.2 %collective-permute-start.4 = (bf16[640,256]{1,0:T(8,128)(2,1)}, bf16[640,256]{1,0:T(8,128)(2,1)S(1)}, u32[]{:S(2)}, u32[]{:S(2)}) collective-permute-start(bf16[640,256]{1,0:T(8,128)(2,1)} %get-tuple-element.29.refs_5_.own_ref.refs_4_.refs_0_), channel_id=1, source_target_pairs={{0,8},{4,12},{8,0},{12,4},{16,24},{20,28},{24,16},{28,20},{1,9},{5... | collective-permute-start | bytes 983048 | tf_op jit(solution)/shard_map/ppermute | solution.py:373
  15.0 12.8 %collective-permute-start.8 = (bf16[640,256]{1,0:T(8,128)(2,1)S(1)}, bf16[640,256]{1,0:T(8,128)(2,1)S(1)}, u32[]{:S(2)}, u32[]{:S(2)}) collective-permute-start(bf16[640,256]{1,0:T(8,128)(2,1)S(1)} %pad_maximum_fusion.1.refs_7_.refs_3_), channel_id=1, source_target_pairs={{0,8},{4,12},{8,0},{12,4},{16,24},{20,28},{24,16},{28,20},{1,9},{5... | collective-permute-start | bytes 983048 | tf_op jit(solution)/shard_map/ppermute | solution.py:373
  18.8 5.6 %collective-permute-start.3 = (bf16[240,384]{1,0:T(8,128)(2,1)S(1)}, bf16[240,384]{1,0:T(8,128)(2,1)S(1)}, u32[]{:S(2)}, u32[]{:S(2)}) collective-permute-start(bf16[240,384]{1,0:T(8,128)(2,1)S(1)} %pad_maximum_fusion.2), channel_id=1, source_target_pairs={{0,16},{4,20},{8,24},{12,28},{16,0},{20,4},{24,8},{28,12},{1,17},{... | collective-permute-start | bytes 552968 | tf_op jit(solution)/shard_map/ppermute | solution.py:373
  24.7 3.2 %collective-permute-start.5 = (bf16[1280,256]{1,0:T(8,128)(2,1)S(1)}, bf16[1280,256]{1,0:T(8,128)(2,1)S(1)}, u32[]{:S(2)}, u32[]{:S(2)}) collective-permute-start(bf16[1280,256]{1,0:T(8,128)(2,1)S(1)} %get-tuple-element.32), channel_id=1, source_target_pairs={{0,4},{4,0},{8,12},{12,8},{16,20},{20,16},{24,28},{28,24},{1,5},{5... | collective-permute-start | bytes 1966088 | tf_op jit(solution)/shard_map/ppermute | solution.py:373
  27.8 2.2 %collective-permute-start.9 = (bf16[1280,256]{1,0:T(8,128)(2,1)S(1)}, bf16[1280,256]{1,0:T(8,128)(2,1)S(1)}, u32[]{:S(2)}, u32[]{:S(2)}) collective-permute-start(bf16[1280,256]{1,0:T(8,128)(2,1)S(1)} %pad_maximum_fusion), channel_id=1, source_target_pairs={{0,4},{4,0},{8,12},{12,8},{16,20},{20,16},{24,28},{28,24},{1,5},{5... | collective-permute-start | bytes 1966088 | tf_op jit(solution)/shard_map/ppermute | solution.py:373
  30.7 4.6 %collective-permute-start.23 = (bf16[160,256]{1,0:T(8,128)(2,1)S(1)}, bf16[160,256]{1,0:T(8,128)(2,1)S(1)}, u32[]{:S(2)}, u32[]{:S(2)}) collective-permute-start(bf16[160,256]{1,0:T(8,128)(2,1)S(1)} %get-tuple-element.48), channel_id=1, source_target_pairs={{0,16},{4,20},{8,24},{12,28},{16,0},{20,4},{24,8},{28,12},{1,17},{... | collective-permute-start | bytes 245768 | tf_op jit(solution)/shard_map/ppermute | solution.py:373
  35.4 8.2 %collective-permute-start.26 = (bf16[160,256]{1,0:T(8,128)(2,1)S(1)}, bf16[160,256]{1,0:T(8,128)(2,1)S(1)}, u32[]{:S(2)}, u32[]{:S(2)}) collective-permute-start(bf16[160,256]{1,0:T(8,128)(2,1)S(1)} %get-tuple-element.50), channel_id=1, source_target_pairs={{0,3},{1,0},{2,1},{3,2},{4,7},{5,4},{6,5},{7,6},{8,11},{9,8},{10,9... | collective-permute-start | bytes 245768 | tf_op jit(solution)/shard_map/ppermute | solution.py:388
  38.2 8.6 %collective-permute-start.25 = (bf16[160,256]{1,0:T(8,128)(2,1)S(1)}, bf16[160,256]{1,0:T(8,128)(2,1)S(1)}, u32[]{:S(2)}, u32[]{:S(2)}) collective-permute-start(bf16[160,256]{1,0:T(8,128)(2,1)S(1)} %get-tuple-element.50), channel_id=1, source_target_pairs={{0,2},{1,3},{2,0},{3,1},{4,6},{5,7},{6,4},{7,5},{8,10},{9,11},{10,... | collective-permute-start | bytes 245768 | tf_op jit(solution)/shard_map/ppermute | solution.py:388
  39.0 7.7 %collective-permute-start.24 = (bf16[160,256]{1,0:T(8,128)(2,1)S(1)}, bf16[160,256]{1,0:T(8,128)(2,1)S(1)}, u32[]{:S(2)}, u32[]{:S(2)}) collective-permute-start(bf16[160,256]{1,0:T(8,128)(2,1)S(1)} %get-tuple-element.50), channel_id=1, source_target_pairs={{0,1},{1,2},{2,3},{3,0},{4,5},{5,6},{6,7},{7,4},{8,9},{9,10},{10,1... | collective-permute-start | bytes 245768 | tf_op jit(solution)/shard_map/ppermute | solution.py:388
  40.6 13.8 %collective-permute-start.10 = (bf16[640,256]{1,0:T(8,128)(2,1)S(1)}, bf16[640,256]{1,0:T(8,128)(2,1)S(1)}, u32[]{:S(2)}, u32[]{:S(2)}) collective-permute-start(bf16[640,256]{1,0:T(8,128)(2,1)S(1)} %get-tuple-element.37), channel_id=1, source_target_pairs={{0,8},{4,12},{8,0},{12,4},{16,24},{20,28},{24,16},{28,20},{1,9},{5... | collective-permute-start | bytes 983048 | tf_op jit(solution)/shard_map/ppermute | solution.py:373
  42.1 8.2 %collective-permute-start.12 = (bf16[320,384]{1,0:T(8,128)(2,1)S(1)}, bf16[320,384]{1,0:T(8,128)(2,1)S(1)}, u32[]{:S(2)}, u32[]{:S(2)}) collective-permute-start(bf16[320,384]{1,0:T(8,128)(2,1)S(1)} %get-tuple-element.41.after_ref), channel_id=1, source_target_pairs={{0,16},{4,20},{8,24},{12,28},{16,0},{20,4},{24,8},{28,12},{1,17},{... | collective-permute-start | bytes 737288 | tf_op jit(solution)/shard_map/ppermute | solution.py:373
  46.8 5.6 %collective-permute-start.32 = (bf16[160,256]{1,0:T(8,128)(2,1)S(1)}, bf16[160,256]{1,0:T(8,128)(2,1)S(1)}, u32[]{:S(2)}, u32[]{:S(2)}) collective-permute-start(bf16[160,256]{1,0:T(8,128)(2,1)S(1)} %add_convert_fusion.refs_0_), channel_id=1, source_target_pairs={{0,24},{4,28},{8,16},{12,20},{16,8},{20,12},{24,0},{28,4},{1,25},{... | collective-permute-start | bytes 245768 | tf_op jit(solution)/shard_map/ppermute | solution.py:373
  49.2 6.2 %collective-permute-start.30 = (bf16[160,256]{1,0:T(8,128)(2,1)S(1)}, bf16[160,256]{1,0:T(8,128)(2,1)S(1)}, u32[]{:S(2)}, u32[]{:S(2)}) collective-permute-start(bf16[160,256]{1,0:T(8,128)(2,1)S(1)} %add_convert_fusion.refs_0_), channel_id=1, source_target_pairs={{0,16},{4,20},{8,24},{12,28},{16,0},{20,4},{24,8},{28,12},{1,17},{... | collective-permute-start | bytes 245768 | tf_op jit(solution)/shard_map/ppermute | solution.py:373
  49.8 5.7 %collective-permute-start.28 = (bf16[160,256]{1,0:T(8,128)(2,1)S(1)}, bf16[160,256]{1,0:T(8,128)(2,1)S(1)}, u32[]{:S(2)}, u32[]{:S(2)}) collective-permute-start(bf16[160,256]{1,0:T(8,128)(2,1)S(1)} %add_convert_fusion.refs_0_), channel_id=1, source_target_pairs={{0,8},{4,12},{8,0},{12,4},{16,24},{20,28},{24,16},{28,20},{1,9},{5... | collective-permute-start | bytes 245768 | tf_op jit(solution)/shard_map/ppermute | solution.py:373
  50.4 6.5 %collective-permute-start.13 = (bf16[80,384]{1,0:T(8,128)(2,1)S(1)}, bf16[80,384]{1,0:T(8,128)(2,1)S(1)}, u32[]{:S(2)}, u32[]{:S(2)}) collective-permute-start(bf16[80,384]{1,0:T(8,128)(2,1)S(1)} %get-tuple-element.43), channel_id=1, source_target_pairs={{0,1},{1,2},{2,3},{3,0},{4,5},{5,6},{6,7},{7,4},{8,9},{9,10},{10,1... | collective-permute-start | bytes 184328 | tf_op jit(solution)/shard_map/ppermute | solution.py:388
  52.3 5.9 %collective-permute-start.14 = (bf16[80,384]{1,0:T(8,128)(2,1)S(1)}, bf16[80,384]{1,0:T(8,128)(2,1)S(1)}, u32[]{:S(2)}, u32[]{:S(2)}) collective-permute-start(bf16[80,384]{1,0:T(8,128)(2,1)S(1)} %get-tuple-element.44), channel_id=1, source_target_pairs={{0,2},{1,3},{2,0},{3,1},{4,6},{5,7},{6,4},{7,5},{8,10},{9,11},{10,... | collective-permute-start | bytes 184328 | tf_op jit(solution)/shard_map/ppermute | solution.py:388
  54.5 4.4 %collective-permute-start.15 = (bf16[80,384]{1,0:T(8,128)(2,1)S(1)}, bf16[80,384]{1,0:T(8,128)(2,1)S(1)}, u32[]{:S(2)}, u32[]{:S(2)}) collective-permute-start(bf16[80,384]{1,0:T(8,128)(2,1)S(1)} %get-tuple-element.45), channel_id=1, source_target_pairs={{0,3},{1,0},{2,1},{3,2},{4,7},{5,4},{6,5},{7,6},{8,11},{9,8},{10,9... | collective-permute-start | bytes 184328 | tf_op jit(solution)/shard_map/ppermute | solution.py:388
  55.4 3.6 %collective-permute-start.27 = (bf16[160,256]{1,0:T(8,128)(2,1)S(1)}, bf16[160,256]{1,0:T(8,128)(2,1)S(1)}, u32[]{:S(2)}, u32[]{:S(2)}) collective-permute-start(bf16[160,256]{1,0:T(8,128)(2,1)S(1)} %add_convert_fusion.refs_0_), channel_id=1, source_target_pairs={{0,4},{4,0},{8,12},{12,8},{16,20},{20,16},{24,28},{28,24},{1,5},{5... | collective-permute-start | bytes 245768 | tf_op jit(solution)/shard_map/ppermute | solution.py:373
  55.5 5.8 %collective-permute-start.33 = (bf16[160,256]{1,0:T(8,128)(2,1)S(1)}, bf16[160,256]{1,0:T(8,128)(2,1)S(1)}, u32[]{:S(2)}, u32[]{:S(2)}) collective-permute-start(bf16[160,256]{1,0:T(8,128)(2,1)S(1)} %collective-permute-done.32.refs_6_), channel_id=1, source_target_pairs={{0,4},{4,0},{8,12},{12,8},{16,20},{20,16},{24,28},{28,24},{1,5},{5... | collective-permute-start | bytes 245768 | tf_op jit(solution)/shard_map/ppermute | solution.py:373
  56.9 5.2 %collective-permute-start.31 = (bf16[160,256]{1,0:T(8,128)(2,1)S(1)}, bf16[160,256]{1,0:T(8,128)(2,1)S(1)}, u32[]{:S(2)}, u32[]{:S(2)}) collective-permute-start(bf16[160,256]{1,0:T(8,128)(2,1)S(1)} %collective-permute-done.30.refs_4_), channel_id=1, source_target_pairs={{0,4},{4,0},{8,12},{12,8},{16,20},{20,16},{24,28},{28,24},{1,5},{5... | collective-permute-start | bytes 245768 | tf_op jit(solution)/shard_map/ppermute | solution.py:373
  58.3 4.2 %collective-permute-start.29 = (bf16[160,256]{1,0:T(8,128)(2,1)S(1)}, bf16[160,256]{1,0:T(8,128)(2,1)S(1)}, u32[]{:S(2)}, u32[]{:S(2)}) collective-permute-start(bf16[160,256]{1,0:T(8,128)(2,1)S(1)} %collective-permute-done.28.refs_2_), channel_id=1, source_target_pairs={{0,4},{4,0},{8,12},{12,8},{16,20},{20,16},{24,28},{28,24},{1,5},{5... | collective-permute-start | bytes 245768 | tf_op jit(solution)/shard_map/ppermute | solution.py:373
  58.9 10.7 %collective-permute-start.11 = (bf16[320,256]{1,0:T(8,128)(2,1)S(1)}, bf16[320,256]{1,0:T(8,128)(2,1)S(1)}, u32[]{:S(2)}, u32[]{:S(2)}) collective-permute-start(bf16[320,256]{1,0:T(8,128)(2,1)S(1)} %get-tuple-element.39), channel_id=1, source_target_pairs={{0,4},{4,0},{8,12},{12,8},{16,20},{20,16},{24,28},{28,24},{1,5},{5... | collective-permute-start | bytes 491528 | tf_op jit(solution)/shard_map/ppermute | solution.py:373
  58.9 5.4 %collective-permute-start.21 = (bf16[80,384]{1,0:T(8,128)(2,1)S(1)}, bf16[80,384]{1,0:T(8,128)(2,1)S(1)}, u32[]{:S(2)}, u32[]{:S(2)}) collective-permute-start(bf16[80,384]{1,0:T(8,128)(2,1)S(1)} %add_convert_fusion.1.refs_0_), channel_id=1, source_target_pairs={{0,24},{4,28},{8,16},{12,20},{16,8},{20,12},{24,0},{28,4},{1,25},{... | collective-permute-start | bytes 184328 | tf_op jit(solution)/shard_map/ppermute | solution.py:373
  61.3 4.3 %collective-permute-start.19 = (bf16[80,384]{1,0:T(8,128)(2,1)S(1)}, bf16[80,384]{1,0:T(8,128)(2,1)S(1)}, u32[]{:S(2)}, u32[]{:S(2)}) collective-permute-start(bf16[80,384]{1,0:T(8,128)(2,1)S(1)} %add_convert_fusion.1.refs_0_), channel_id=1, source_target_pairs={{0,16},{4,20},{8,24},{12,28},{16,0},{20,4},{24,8},{28,12},{1,17},{... | collective-permute-start | bytes 184328 | tf_op jit(solution)/shard_map/ppermute | solution.py:373
  62.1 4.2 %collective-permute-start.17 = (bf16[80,384]{1,0:T(8,128)(2,1)S(1)}, bf16[80,384]{1,0:T(8,128)(2,1)S(1)}, u32[]{:S(2)}, u32[]{:S(2)}) collective-permute-start(bf16[80,384]{1,0:T(8,128)(2,1)S(1)} %add_convert_fusion.1.refs_0_), channel_id=1, source_target_pairs={{0,8},{4,12},{8,0},{12,4},{16,24},{20,28},{24,16},{28,20},{1,9},{5... | collective-permute-start | bytes 184328 | tf_op jit(solution)/shard_map/ppermute | solution.py:373
  62.5 5.4 %collective-permute-start.16 = (bf16[80,384]{1,0:T(8,128)(2,1)S(1)}, bf16[80,384]{1,0:T(8,128)(2,1)S(1)}, u32[]{:S(2)}, u32[]{:S(2)}) collective-permute-start(bf16[80,384]{1,0:T(8,128)(2,1)S(1)} %add_convert_fusion.1.refs_0_), channel_id=1, source_target_pairs={{0,4},{4,0},{8,12},{12,8},{16,20},{20,16},{24,28},{28,24},{1,5},{5... | collective-permute-start | bytes 184328 | tf_op jit(solution)/shard_map/ppermute | solution.py:373
  64.3 3.6 %collective-permute-start.22 = (bf16[80,384]{1,0:T(8,128)(2,1)S(1)}, bf16[80,384]{1,0:T(8,128)(2,1)S(1)}, u32[]{:S(2)}, u32[]{:S(2)}) collective-permute-start(bf16[80,384]{1,0:T(8,128)(2,1)S(1)} %collective-permute-done.21.refs_6_), channel_id=1, source_target_pairs={{0,4},{4,0},{8,12},{12,8},{16,20},{20,16},{24,28},{28,24},{1,5},{5... | collective-permute-start | bytes 184328 | tf_op jit(solution)/shard_map/ppermute | solution.py:373
  65.6 2.3 %collective-permute-start.20 = (bf16[80,384]{1,0:T(8,128)(2,1)S(1)}, bf16[80,384]{1,0:T(8,128)(2,1)S(1)}, u32[]{:S(2)}, u32[]{:S(2)}) collective-permute-start(bf16[80,384]{1,0:T(8,128)(2,1)S(1)} %collective-permute-done.19.refs_4_), channel_id=1, source_target_pairs={{0,4},{4,0},{8,12},{12,8},{16,20},{20,16},{24,28},{28,24},{1,5},{5... | collective-permute-start | bytes 184328 | tf_op jit(solution)/shard_map/ppermute | solution.py:373
  66.3 1.6 %collective-permute-start.18 = (bf16[80,384]{1,0:T(8,128)(2,1)S(1)}, bf16[80,384]{1,0:T(8,128)(2,1)S(1)}, u32[]{:S(2)}, u32[]{:S(2)}) collective-permute-start(bf16[80,384]{1,0:T(8,128)(2,1)S(1)} %collective-permute-done.17.refs_2_), channel_id=1, source_target_pairs={{0,4},{4,0},{8,12},{12,8},{16,20},{20,16},{24,28},{28,24},{1,5},{5... | collective-permute-start | bytes 184328 | tf_op jit(solution)/shard_map/ppermute | solution.py:373
  67.9 1.7 %copy-start.1 = (bf16[1,1,16,16,320]{4,3,2,1,0:T(8,128)(2,1)S(1)}, bf16[1,1,16,16,320]{4,3,2,1,0:T(8,128)(2,1)}, u32[]{:S(2)}) copy-start(bf16[1,1,16,16,320]{4,3,2,1,0:T(8,128)(2,1)} %param.5) | copy-start | bytes 491524

commit v3 on v2

v3 whole, which is shorter than its diff:
```python
import functools
import math

import jax
import jax.numpy as jnp
from jax import lax
from jax.experimental import pallas as pl
from jax.experimental.pallas import tpu as pltpu
from jax.sharding import PartitionSpec as P


def padded_2(cells, sides, width):
    for axis, dim in sides:
        count = lax.axis_size(axis)
        ends = count - 1
        head = lax.slice_in_dim(cells, 0, width, axis=dim)
        tail = lax.slice_in_dim(cells, cells.shape[dim] - width, cells.shape[dim], axis=dim)
        cells = jnp.concatenate(
            [
                lax.ppermute(tail, axis, [(i, (i + 1) % count) for i in range(ends)]),
                cells,
                lax.ppermute(head, axis, [((i + 1) % count, i) for i in range(ends)]),
            ],
            axis=dim,
        )
    return cells


def temporal_grads(acts, g_pad, w_time):
    count = acts.shape[0]
    chans = acts.shape[-1]
    flat_acts = acts.reshape(-1, chans)
    act_grad = jnp.zeros(flat_acts.shape, jnp.float32)
    time_terms = []
    for k in range(3):
        shifted = g_pad[2 - k : 2 - k + count].reshape(-1, chans)
        act_grad = act_grad + lax.dot_general(
            shifted, w_time[k], (((1,), (1,)), ((), ())), preferred_element_type=jnp.float32
        )
        time_terms.append(
            lax.dot_general(
                flat_acts, shifted, (((0,), (0,)), ((), ())), preferred_element_type=jnp.float32
            )
        )
    return (act_grad.astype(jnp.bfloat16).reshape(acts.shape), jnp.stack(time_terms, axis=0))


def per_device_general(frames, cotangent, w_space, w_time):
    weights = lax.all_gather(w_space, "seq", axis=0, tiled=True)
    clip_x = frames[0]
    clip_g = cotangent[0]
    count, height, width, chans = clip_x.shape
    factor = 1.0 / math.sqrt(lax.axis_size("clip") * count * lax.axis_size("seq") * height * width)
    padded = jnp.pad(clip_x, ((0, 0), (1, 1), (1, 1), (0, 0)))
    pieces = [
        padded[:, i : i + height, j : j + width, :].reshape(-1, chans)
        for i in range(3)
        for j in range(3)
    ]
    pre_act = jnp.zeros((count * height * width, chans), jnp.float32)
    for tap in range(9):
        pre_act = pre_act + jnp.dot(
            pieces[tap], weights[:, tap, :], preferred_element_type=jnp.float32
        )
    acts = jax.nn.silu(pre_act).astype(jnp.bfloat16).reshape(1, count, height, width, chans)
    g_rims = padded_2(cotangent, (("seq", 1),), 1)
    g_pad = g_rims[0].reshape(count + 2, height * width, chans)
    act_grad, time_terms = temporal_grads(
        acts[0].reshape(count, height * width, chans), g_pad, w_time
    )
    sigma = jax.nn.sigmoid(pre_act)
    pre_grad = (
        act_grad.reshape(-1, chans).astype(jnp.float32) * sigma * (1.0 + pre_act * (1.0 - sigma))
    ).astype(jnp.bfloat16)
    terms = []
    for tap in range(9):
        part = pieces[tap]
        terms.append(
            lax.dot_general(
                part, pre_grad, (((0,), (0,)), ((), ())), preferred_element_type=jnp.float32
            )
        )
    space_share = lax.psum_scatter(
        jnp.stack(terms, axis=1) * factor, "seq", scatter_dimension=0, tiled=True
    )
    space_grad = lax.psum(space_share, "clip")
    time_grad = lax.psum(time_terms * factor, ("clip", "seq"))
    grad_pad = jnp.pad(
        pre_grad.reshape(count, height, width, chans), ((0, 0), (1, 1), (1, 1), (0, 0))
    )
    input_grad = clip_g.reshape(-1, chans).astype(jnp.float32)
    for i in range(3):
        for j in range(3):
            piece = grad_pad[:, 2 - i : 2 - i + height, 2 - j : 2 - j + width, :].reshape(-1, chans)
            input_grad = input_grad + lax.dot_general(
                piece,
                weights[:, 3 * i + j, :],
                (((1,), (1,)), ((), ())),
                preferred_element_type=jnp.float32,
            )
    frames_grad = input_grad.astype(jnp.bfloat16).reshape(1, count, height, width, chans)
    return (frames_grad, space_grad, time_grad)


BF16 = jnp.bfloat16
F32 = jnp.float32
LANES = 128
VMEM = pl.BlockSpec(memory_space=pltpu.VMEM)
NN = (((1,), (0,)), ((), ()))
NT = (((1,), (1,)), ((), ()))
TN = (((0,), (0,)), ((), ()))


def round_up(value, unit):
    return -(-value // unit) * unit


def mm(lhs, rhs, dims):
    return lax.dot_general(lhs, rhs, dims, preferred_element_type=F32)


def call(kernel, outs, *args, after=(), scratch=()):
    def body(*refs):
        kernel(*refs[: len(args)], *refs[len(args) + len(after) :])

    return pl.pallas_call(
        body,
        out_shape=tuple(jax.ShapeDtypeStruct(shape, dtype) for shape, dtype in outs),
        in_specs=[VMEM] * len(args) + [pl.BlockSpec(memory_space=pl.ANY)] * len(after),
        out_specs=(VMEM,) * len(outs),
        scratch_shapes=list(scratch),
        compiler_params=pltpu.CompilerParams(vmem_limit_bytes=48 * 1024 * 1024),
    )(*args, *after)


class Plan:
    def __init__(self, clips, seqs, height, width, chans):
        self.clips, self.seqs = clips, seqs
        self.height, self.width, self.chans = height, width, chans
        self.group = clips // 2
        self.slab = chans // max(self.group, 1)
        self.rows = chans // seqs
        self.pixels = height * width
        self.cols = 9 * self.slab
        self.half = round_up(round_up(self.cols, 2 * LANES) // 2, LANES)
        self.tcols = round_up(3 * self.slab, LANES)
        self.thalf = chans // 2
        self.factor = 1.0 / math.sqrt(clips * seqs * self.pixels)

    def fits(self):
        return (
            self.group == 4
            and self.slab * self.group == self.chans
            and self.rows * self.seqs == self.chans
            and self.slab % 16 == 0
            and self.rows % 16 == 0
            and self.thalf % 16 == 0
            and self.pixels % LANES == 0
            and self.seqs == 4
        )

    def place(self):
        clip = lax.axis_index("clip")
        return clip % self.group, clip // self.group, lax.axis_index("seq")


def prepare(plan, f_hbm, g_hbm, w_hbm, ft_ref, gt_ref, wp_ref, wh_ref, f_ref, g_ref, w_ref, sems):
    low, high, _ = plan.place()
    slab, half = plan.slab, plan.half
    copies = [
        pltpu.make_async_copy(src, dst, sems.at[index])
        for index, (src, dst) in enumerate(((g_hbm, g_ref), (w_hbm, w_ref), (f_hbm, f_ref)))
    ]
    for copy in copies:
        copy.start()
    copies[0].wait()
    gt_ref[...] = g_ref[...].T
    copies[1].wait()
    for index in range(plan.group):

        @pl.when(low == index)
        def _():
            taps = [w_ref[tap][:, slab * index : slab * (index + 1)] for tap in range(9)]
            if plan.cols < 2 * half:
                taps.append(jnp.zeros((plan.rows, 2 * half - plan.cols), BF16))
            wp_ref[...] = jnp.concatenate(taps, axis=1)

    wh_ref[...] = wp_ref[:, pl.ds(pl.multiple_of(high * half, LANES), half)]
    copies[2].wait()
    ft_ref[...] = f_ref[...].T


def shifts(plan, lanes):
    lane = lax.broadcasted_iota(jnp.int32, (1, lanes), 1) % plan.pixels
    row, col = lane // plan.width, lane % plan.width
    found = []
    for i in range(3):
        for j in range(3):
            inside = (
                (row + (i - 1) >= 0)
                & (row + (i - 1) < plan.height)
                & (col + (j - 1) >= 0)
                & (col + (j - 1) < plan.width)
            )
            found.append(((i - 1) * plan.width + (j - 1), inside))
    return found


def rolled(value, distance):
    lanes = value.shape[1]
    return value if distance == 0 else pltpu.roll(value, (-distance) % lanes, 1)


def weights(plan, *refs):
    own_ref, got_refs, other_ref = refs[0], refs[1 : plan.seqs], refs[plan.seqs]
    w_all, w_turned = refs[plan.seqs + 1 :]
    _, high, z = plan.place()
    rows, half = plan.rows, plan.half
    here = pl.ds(pl.multiple_of(high * half, LANES), half)
    there = pl.ds(pl.multiple_of((1 - high) * half, LANES), half)
    w_all[pl.ds(pl.multiple_of(z * rows, 16), rows), :] = own_ref[...]
    for k, got_ref in enumerate(got_refs, 1):
        place = pl.ds(pl.multiple_of((z - k + plan.seqs) % plan.seqs * rows, 16), rows)
        w_all[place, here] = got_ref[...]
        w_all[place, there] = other_ref[(k - 1) * rows : k * rows, :]
    w_turned[...] = w_all[...].T


def forward(plan, w_turned, *refs):
    slab = plan.slab
    frames, (f_all, a_ref, d_ref, taps) = refs[: plan.group], refs[plan.group :]
    for d, frame in enumerate(frames):
        f_all[:, d * plan.pixels : (d + 1) * plan.pixels] = frame[...]
    taps[...] = mm(w_turned[: plan.cols, :], f_all[...], NN)
    total = None
    for tap, (distance, inside) in enumerate(shifts(plan, f_all.shape[1])):
        term = rolled(taps[tap * slab : (tap + 1) * slab, :], distance)
        term = jnp.where(inside, term, 0.0)
        total = term if total is None else total + term
    sigma = 1.0 / (1.0 + jnp.exp(-total))
    a_ref[...] = (total * sigma).astype(BF16)
    d_ref[...] = sigma * (1.0 + total * (1.0 - sigma))


def act_grads(plan, before_ref, own_ref, after_ref, wt_ref, send_ref, mine_ref, core_ref, total):
    low, _, _ = plan.place()
    slab = plan.slab
    here = mm(wt_ref[0], after_ref[...], NN)
    here = here + mm(wt_ref[1], own_ref[...], NN)
    here = here + mm(wt_ref[2], before_ref[...], NN)
    total[...] = here.astype(BF16)
    for d, ref in enumerate((mine_ref, core_ref)):
        place = slice(d * slab, (d + 1) * slab)
        ref[...] = total[pl.ds(pl.multiple_of((low ^ d) * slab, 16), slab), :]
        send_ref[place, :] = total[pl.ds(pl.multiple_of((low ^ (d + 2)) * slab, 16), slab), :]


def temporal(plan, a_ref, *refs):
    group, pixels, chans = plan.group, plan.pixels, plan.chans
    here_refs, halo_refs = refs[:group], refs[group : 2 * group]
    send_ref, keep_ref, total = refs[2 * group :]
    _, high, _ = plan.place()
    acts = a_ref[...]
    after = [ref[chans:, :] for ref in halo_refs]
    before = [ref[:chans, :] for ref in halo_refs]
    parts = []
    for grads in (after, [ref[...] for ref in here_refs], before):
        term = None
        for d in range(group):
            here = mm(grads[d], acts[:, d * pixels : (d + 1) * pixels], NT)
            term = here if term is None else term + here
        parts.append(term)
    if plan.tcols > 3 * plan.slab:
        parts.append(jnp.zeros((chans, plan.tcols - 3 * plan.slab), F32))
    total[...] = jnp.concatenate(parts, axis=1)
    size = plan.thalf
    keep_ref[...] = total[pl.ds(pl.multiple_of(high * size, 16), size), :]
    send_ref[...] = total[pl.ds(pl.multiple_of((1 - high) * size, 16), size), :].astype(BF16)


def spatial(plan, w_all, f_all, d_ref, mine_ref, core_ref, pair_ref, last_ref, *refs):
    s_send, s_keep, f_send, f_keep, expanded, total = refs
    _, high, _ = plan.place()
    pixels, slab, chans = plan.pixels, plan.slab, plan.chans
    parts = [mine_ref[...], core_ref[...], pair_ref[:slab, :], last_ref[...]]
    parts = [part.astype(F32) for part in parts]
    act_grad = jnp.concatenate(parts, axis=1)
    pre_grad = (act_grad * d_ref[...]).astype(BF16).astype(F32)
    moves = shifts(plan, pre_grad.shape[1])
    for tap, (distance, _) in enumerate(moves):
        inside = moves[8 - tap][1]
        term = jnp.where(inside, rolled(pre_grad, -distance), 0.0)
        expanded[tap * slab : (tap + 1) * slab, :] = term.astype(BF16)
    total[:, : plan.cols] = mm(f_all[...], expanded[...], NT)
    if plan.cols < total.shape[1]:
        total[:, plan.cols :] = jnp.zeros((chans, total.shape[1] - plan.cols), F32)
    size = plan.half
    s_keep[...] = total[:, pl.ds(pl.multiple_of(high * size, LANES), size)]
    s_send[...] = total[:, pl.ds(pl.multiple_of((1 - high) * size, LANES), size)].astype(BF16)
    grads = mm(w_all[:, : plan.cols], expanded[...], NN)
    for index in range(2):
        d = 2 * index
        here = slice(index * chans, (index + 1) * chans)
        f_keep[here, :] = grads[:, d * pixels : (d + 1) * pixels]
        f_send[here, :] = grads[:, (d + 1) * pixels : (d + 2) * pixels].astype(BF16)


def added(keep_ref, got_ref, own_ref, send_ref):
    total = keep_ref[...] + got_ref[...].astype(F32)
    own_ref[...] = total
    send_ref[...] = total.astype(BF16)


def space_halves(plan, keep_ref, got_ref, own_ref, send_ref, total):
    _, _, z = plan.place()
    rows = plan.rows
    total[...] = keep_ref[...] + got_ref[...].astype(F32)
    for n in range(2):
        place = slice(n * rows, (n + 1) * rows)
        own_ref[place, :] = total[pl.ds(pl.multiple_of((z ^ (2 * n)) * rows, 16), rows), :]
        send_ref[place, :] = total[pl.ds(pl.multiple_of((z ^ (2 * n + 1)) * rows, 16), rows), :].astype(BF16)


def space_quarter(plan, keep_ref, got_ref, own_ref, send_ref):
    rows = plan.rows
    own_ref[...] = keep_ref[:rows, :] + got_ref[:rows, :].astype(F32)
    send_ref[...] = (keep_ref[rows:, :] + got_ref[rows:, :].astype(F32)).astype(BF16)


def summed(own_ref, *refs):
    total = own_ref[...]
    for ref in refs[:-1]:
        total = total + ref[...].astype(F32)
    refs[-1][...] = total.astype(BF16)


def stacked(*refs):
    out_ref, first = refs[-1], 0
    for ref in refs[:-1]:
        out_ref[first : first + ref.shape[0], :] = ref[...]
        first += ref.shape[0]


def frame_half(plan, keep_ref, got_ref, send_ref, own_ref):
    chans = plan.chans
    own_ref[...] = keep_ref[:chans, :] + got_ref[:chans, :].astype(F32)
    send_ref[...] = (keep_ref[chans:, :] + got_ref[chans:, :].astype(F32)).astype(BF16)


def ends(plan, t_own, t_got, *refs):
    chips, (f_own, f_got, g_ref, t_sum, s_all, f_out) = refs[:4], refs[4:]
    summed(t_own, t_got, t_sum)
    stacked(*chips, s_all)
    total = f_own[...] + f_got[...].astype(F32)
    f_out[...] = (g_ref[...].astype(F32) + total.T).astype(BF16)


def space_end(plan, here_ref, core_ref, out_ref, token_ref, held):
    low, high, _ = plan.place()
    group, slab, rows = plan.group, plan.slab, plan.rows
    for core, ref in enumerate((here_ref, core_ref)):
        for chip in range(4):
            other = high if chip < 2 else 1 - high
            lane = pl.multiple_of(other * plan.half, LANES)
            piece = ref[chip * rows : (chip + 1) * rows, :].astype(F32) * plan.factor
            held[low ^ (2 * (chip % 2) + core), :, pl.ds(lane, plan.half)] = piece
    for tap in range(9):
        out_ref[tap] = jnp.concatenate(
            [held[index, :, tap * slab : (tap + 1) * slab] for index in range(group)], axis=1
        )
    token_ref[...] = jnp.zeros_like(token_ref)


def time_end(plan, here_ref, core_ref, out_ref, held):
    low, high, _ = plan.place()
    slab, size = plan.slab, plan.thalf
    near = pl.ds(pl.multiple_of(high * size, 16), size)
    far = pl.ds(pl.multiple_of((1 - high) * size, 16), size)
    for core, ref in enumerate((here_ref, core_ref)):
        for pair in range(2):
            held[near, :] = ref[pair * size : (pair + 1) * size, :].astype(F32)
            held[far, :] = ref[(2 + pair) * size : (3 + pair) * size, :].astype(F32)
            turned = held[...].T * plan.factor
            for k in range(3):
                here = pl.ds(pl.multiple_of((low ^ (2 * pair + core)) * slab, 16), slab)
                out_ref[k, here, :] = turned[k * slab : (k + 1) * slab, :]


def per_device(plan, frames, cotangent, w_space, w_time):
    pixels, chans, group, seqs = plan.pixels, plan.chans, plan.group, plan.seqs
    slab, rows, half = plan.slab, plan.rows, plan.half
    lanes = group * pixels
    part = lambda fn: functools.partial(fn, plan)

    def swap(value, distance):
        return lax.ppermute(value, "clip", [(i, i ^ distance) for i in range(plan.clips)])

    def trade(value, distance):
        return lax.ppermute(value, "seq", [(i, i ^ distance) for i in range(seqs)])

    def turn(value, k):
        return lax.ppermute(value, "seq", [(i, (i + k) % seqs) for i in range(seqs)])

    def neighbours(value):
        z = lax.axis_index("seq")
        found = []
        for first in range(2):
            other = {i: i for i in range(seqs)}
            for i in range(first, seqs - 1, 2):
                other[i], other[i + 1] = i + 1, i
            found.append(lax.ppermute(value, "seq", list(other.items())))
        low, high = jnp.where(z % 2 == 1, *found), jnp.where(z % 2 == 1, *found[::-1])
        zero = jnp.zeros_like(value)
        return jnp.where(z == 0, zero, low), jnp.where(z == seqs - 1, zero, high)

    def gathered(own, pair):
        return own, swap(own, 1), pair, swap(pair, 1)

    def chips(value):
        return value, swap(value, 2), swap(value, group), swap(value, group + 2)

    clip_f, clip_g = frames.reshape(pixels, chans), cotangent.reshape(pixels, chans)
    taps = jnp.transpose(w_space, (1, 0, 2))
    frame = (chans, pixels)
    outs = [(frame, BF16), (frame, BF16), ((rows, 2 * half), BF16), ((rows, half), BF16)]
    frame_f, frame_g, piece, half_piece = pl.pallas_call(
        part(prepare),
        out_shape=tuple(jax.ShapeDtypeStruct(shape, dtype) for shape, dtype in outs),
        in_specs=[pl.BlockSpec(memory_space=pl.ANY)] * 3,
        out_specs=(VMEM,) * len(outs),
        scratch_shapes=[
            pltpu.VMEM(clip_f.shape, BF16),
            pltpu.VMEM(clip_g.shape, BF16),
            pltpu.VMEM(taps.shape, BF16),
            pltpu.SemaphoreType.DMA((3,)),
        ],
        compiler_params=pltpu.CompilerParams(vmem_limit_bytes=55_900_000),
    )(clip_f, clip_g, taps)

    w_got = [turn(half_piece, k) for k in range(1, seqs)]
    w_other = swap(jnp.concatenate(w_got, axis=0), group)
    pair_f, pair_g = swap(frame_f, 2), swap(frame_g, 2)
    before, after = neighbours(frame_g)
    d_send, d_mine, d_core = call(
        part(act_grads),
        [((2 * slab, pixels), BF16), ((slab, pixels), BF16), ((slab, pixels), BF16)],
        before,
        frame_g,
        after,
        w_time,
        scratch=[pltpu.VMEM(frame, BF16)],
    )
    d_pair = swap(d_send, 2)
    w_all, w_turned = call(
        part(weights),
        [((chans, 2 * half), BF16), ((2 * half, chans), BF16)],
        piece,
        *w_got,
        w_other,
        after=[pair_g],
    )
    (halo,) = call(
        stacked, [((2 * chans, pixels), BF16)], before, after, after=[w_all, d_pair]
    )
    f_all, acts, slope = call(
        part(forward),
        [((chans, lanes), BF16), ((slab, lanes), BF16), ((slab, lanes), F32)],
        w_turned,
        *gathered(frame_f, pair_f),
        after=[d_pair],
        scratch=[pltpu.VMEM((plan.cols, lanes), F32)],
    )
    s_send, s_keep, f_send, f_keep = call(
        part(spatial),
        [
            ((chans, half), BF16),
            ((chans, half), F32),
            ((2 * chans, pixels), BF16),
            ((2 * chans, pixels), F32),
        ],
        w_all,
        f_all,
        slope,
        d_mine,
        swap(d_core, 1),
        d_pair,
        swap(d_pair[slab:], 1),
        scratch=[pltpu.VMEM((plan.cols, lanes), BF16), pltpu.VMEM((chans, 2 * half), F32)],
    )
    time = (plan.thalf, plan.tcols)
    t_send, t_keep = call(
        part(temporal),
        [(time, BF16), (time, F32)],
        acts,
        *gathered(frame_g, pair_g),
        *gathered(halo, swap(halo, 2)),
        scratch=[pltpu.VMEM((chans, plan.tcols), F32)],
    )

    f_half, f_own = call(
        part(frame_half), [(frame, BF16), (frame, F32)], f_keep, swap(f_send, 1)
    )
    f_other = swap(f_half, 2)
    t_own, t_part = call(added, [(time, F32), (time, BF16)], t_keep, swap(t_send, group))
    t_own, t_part2 = call(added, [(time, F32), (time, BF16)], t_own, trade(t_part, 1))
    t_got = trade(t_part2, 2)
    s_own, s_part = call(
        part(space_halves),
        [((2 * rows, half), F32), ((2 * rows, half), BF16)],
        s_keep,
        swap(s_send, group),
        scratch=[pltpu.VMEM((chans, half), F32)],
    )
    s_own, s_part = call(
        part(space_quarter),
        [((rows, half), F32), ((rows, half), BF16)],
        s_own,
        trade(s_part, 1),
        after=[t_part],
    )
    (s_sum,) = call(
        summed, [((rows, half), BF16)], s_own, trade(s_part, 2), after=[f_other]
    )
    t_sum, s_all, f_out = call(
        part(ends),
        [(time, BF16), ((4 * rows, half), BF16), ((pixels, chans), BF16)],
        t_own,
        t_got,
        *chips(s_sum),
        f_own,
        f_other,
        clip_g,
    )
    s_out, token = call(
        part(space_end),
        [((9, rows, chans), F32), ((8, LANES), F32)],
        s_all,
        swap(s_all, 1),
        scratch=[pltpu.VMEM((group, rows, 2 * half), F32)],
    )
    (t_all,) = call(
        stacked, [((4 * plan.thalf, plan.tcols), BF16)], *chips(t_sum), after=[token]
    )
    (t_out,) = call(
        part(time_end),
        [((3, chans, chans), F32)],
        t_all,
        swap(t_all, 1),
        scratch=[pltpu.VMEM((chans, plan.tcols), F32)],
    )
    return f_out.reshape(frames.shape), jnp.transpose(s_out, (1, 0, 2)), t_out


def solution(mesh):
    in_specs = (
        P("clip", "seq", None, None, None),
        P("clip", "seq", None, None, None),
        P("seq", None, None),
        P(),
    )
    out_specs = (P("clip", "seq", None, None, None), P("seq", None, None), P())

    def body(frames, cotangent, w_space, w_time):
        one, count, height, width, chans = frames.shape
        plan = Plan(mesh.shape["clip"], mesh.shape["seq"], height, width, chans)
        if one == 1 and count == 1 and plan.fits():
            return per_device(plan, frames, cotangent, w_space, w_time)
        return per_device_general(frames, cotangent, w_space, w_time)

    return jax.shard_map(body, mesh=mesh, in_specs=in_specs, out_specs=out_specs, check_vma=False)
```

time: 70.7 us -> 68.9 us (0.975)
  Pallas kernels: 11.7 us -> 9.96 us
    ppermute x9 -> x3, waiting for transfers between devices: 8.35 us -> 0.01 us  [turn(): lax.ppermute(value, 'seq', [(i, (i + k) % seqs) for i in range(seqs)])]
    ppermute x23 -> x25, waiting for transfers between devices: 13.5 us -> 21.4 us  [swap(): lax.ppermute(value, 'clip', [(i, i ^ distance) for i in range(plan.clips)])]
    ppermute x0 -> x4, starting transfers between devices: none -> 5.12 us  [trade(): return lax.ppermute(value, 'seq', [(i, i ^ distance) for i in range(seqs)])]
    ppermute x2, starting transfers between devices: 6.71 us -> 2.72 us  [neighbours(): found.append(lax.ppermute(value, 'seq', list(other.items())))]
    ppermute x9 -> x3, starting transfers between devices: 10.9 us -> 7.01 us  [turn(): lax.ppermute(value, 'seq', [(i, (i + k) % seqs) for i in range(seqs)])]
    ppermute x23 -> x25, starting transfers between devices: 17 us -> 19.5 us  [swap(): lax.ppermute(value, 'clip', [(i, i ^ distance) for i in range(plan.clips)])]
    ppermute x0 -> x4, waiting for transfers between devices: none -> 1.86 us  [trade(): return lax.ppermute(value, 'seq', [(i, i ^ distance) for i in range(seqs)])]
    pallas_call x10 -> x16, Pallas kernels: 9.54 us -> 8.49 us  [call(): pl.pallas_call(body, out_shape=tuple((jax.ShapeDtypeStruct(shape, dtype)...]
  transfers between devices with their start and end apart: 34 -> 34, of which waited for: 14 -> 16; matrix products, arithmetic and copies ran while one was open for 0% -> 0% of each run, Pallas kernels for 11% -> 9%
where the time goes in v3:
time: 68.9 us; the launch traced here: 68.7 us
  starting transfers between devices  34.4 us (50%)
  waiting for transfers between devices  23.5 us (34%)
  Pallas kernels  9.96 us (14%)
  between operations  0.81 us (1%)
    ppermute x25, waiting for transfers between devices, swap(): lax.ppermute(value, 'clip', [(i, i ^ distance) for i in range(plan.clips)])  21.4 us
    ppermute x25, starting transfers between devices, swap(): lax.ppermute(value, 'clip', [(i, i ^ distance) for i in range(plan.clips)])  19.5 us
    pallas_call x16, Pallas kernels, call(): pl.pallas_call(body, out_shape=tuple((jax.ShapeDtypeStruct(shape, dtype)...  8.49 us
    ppermute x3, starting transfers between devices, turn(): lax.ppermute(value, 'seq', [(i, (i + k) % seqs) for i in range(seqs)])  7.01 us
    ppermute x4, starting transfers between devices, trade(): return lax.ppermute(value, 'seq', [(i, i ^ distance) for i in range(seqs)])  5.12 us
    ppermute x2, starting transfers between devices, neighbours(): found.append(lax.ppermute(value, 'seq', list(other.items())))  2.72 us
    ppermute x4, waiting for transfers between devices, trade(): return lax.ppermute(value, 'seq', [(i, i ^ distance) for i in range(seqs)])  1.86 us
    pallas_call x1, Pallas kernels, per_device(): pl.pallas_call(part(prepare), out_shape=tuple((jax.ShapeDtypeStruct(shape...  1.47 us
  transfers between devices with their start and end apart: 34, of which 16 were waited for; matrix products, arithmetic and copies ran while one was open for 0% of the time, Pallas kernels for 9%

profile of v3, /device:TPU:0, one launch (start us, length us, event | category | flops | bytes accessed | tf_op | source)
XLA Modules:
  0.0 68.7 jit_solution(8894377241324660480)
XLA Ops:
  0.6 1.5 %shard_map.67 = (bf16[320,256]{1,0:T(8,128)(2,1)S(1)}, bf16[320,256]{1,0:T(8,128)(2,1)S(1)}, bf16[80,768]{1,0:T(8,128)(2,1)S(1)}, bf16[80,384]{1,0:T(8,128)(2,1)S(1)}) custom-call(bf16[256,320]{1,0:T(8,128)(2,1)} %bitcast.8, bf16[256,320]{1,0:T(8,128)(2,1)} %bitcast.5, bf16[9,80,320]{2,1,0:T(8,128)(2,1)} %bitcast.7), custom_call_target="tpu_custom_call" | custom-call | tf_op jit(solution)/shard_map/pallas_call | solution.py:426
  2.1 3.1 %collective-permute-start = (bf16[80,384]{1,0:T(8,128)(2,1)S(1)}, bf16[80,384]{1,0:T(8,128)(2,1)S(1)}, u32[]{:S(2)}, u32[]{:S(2)}) collective-permute-start(bf16[80,384]{1,0:T(8,128)(2,1)S(1)} %get-tuple-element.37), channel_id=1, source_target_pairs={{0,1},{1,2},{2,3},{3,0},{4,5},{5,6},{6,7},{7,4},{8,9},{9,10},{10,1... | collective-permute-start | bytes 184328 | tf_op jit(solution)/shard_map/ppermute | solution.py:402
  5.2 2.6 %collective-permute-start.1 = (bf16[80,384]{1,0:T(8,128)(2,1)S(1)}, bf16[80,384]{1,0:T(8,128)(2,1)S(1)}, u32[]{:S(2)}, u32[]{:S(2)}) collective-permute-start(bf16[80,384]{1,0:T(8,128)(2,1)S(1)} %get-tuple-element.37), channel_id=1, source_target_pairs={{0,2},{1,3},{2,0},{3,1},{4,6},{5,7},{6,4},{7,5},{8,10},{9,11},{10,... | collective-permute-start | bytes 184328 | tf_op jit(solution)/shard_map/ppermute | solution.py:402
  7.8 1.3 %collective-permute-start.2 = (bf16[80,384]{1,0:T(8,128)(2,1)S(1)}, bf16[80,384]{1,0:T(8,128)(2,1)S(1)}, u32[]{:S(2)}, u32[]{:S(2)}) collective-permute-start(bf16[80,384]{1,0:T(8,128)(2,1)S(1)} %get-tuple-element.37), channel_id=1, source_target_pairs={{0,3},{1,0},{2,1},{3,2},{4,7},{5,4},{6,5},{7,6},{8,11},{9,8},{10,9... | collective-permute-start | bytes 184328 | tf_op jit(solution)/shard_map/ppermute | solution.py:402
  9.1 0.7 collective-permute-start.9
  9.8 2.1 %collective-permute-start.8 = (bf16[320,256]{1,0:T(8,128)(2,1)S(1)}, bf16[320,256]{1,0:T(8,128)(2,1)S(1)}, u32[]{:S(2)}, u32[]{:S(2)}) collective-permute-start(bf16[320,256]{1,0:T(8,128)(2,1)S(1)} %get-tuple-element.38.refs_1_), channel_id=1, source_target_pairs={{0,1},{1,0},{2,3},{3,2},{4,5},{5,4},{6,7},{7,6},{8,9},{9,8},{10,11... | collective-permute-start | bytes 491528 | tf_op jit(solution)/shard_map/ppermute | solution.py:411
  11.9 1.6 %collective-permute-start.4 = (bf16[320,256]{1,0:T(8,128)(2,1)S(1)}, bf16[320,256]{1,0:T(8,128)(2,1)S(1)}, u32[]{:S(2)}, u32[]{:S(2)}) collective-permute-start(bf16[320,256]{1,0:T(8,128)(2,1)S(1)} %get-tuple-element.38.refs_1_), channel_id=1, source_target_pairs={{0,8},{4,12},{8,0},{12,4},{16,24},{20,28},{24,16},{28,20},{1,9},{5... | collective-permute-start | bytes 491528 | tf_op jit(solution)/shard_map/ppermute | solution.py:396
  13.5 0.4 collective-permute-start.6
  13.9 1.7 %collective-permute-start.3 = (bf16[240,384]{1,0:T(8,128)(2,1)S(1)}, bf16[240,384]{1,0:T(8,128)(2,1)S(1)}, u32[]{:S(2)}, u32[]{:S(2)}) collective-permute-start(bf16[240,384]{1,0:T(8,128)(2,1)S(1)} %pad_maximum_fusion), channel_id=1, source_target_pairs={{0,16},{4,20},{8,24},{12,28},{16,0},{20,4},{24,8},{28,12},{1,17},{... | collective-permute-start | bytes 552968 | tf_op jit(solution)/shard_map/ppermute | solution.py:396
  16.0 0.4 shard_map.69
  16.4 1.5 %collective-permute-start.10 = (bf16[160,256]{1,0:T(8,128)(2,1)S(1)}, bf16[160,256]{1,0:T(8,128)(2,1)S(1)}, u32[]{:S(2)}, u32[]{:S(2)}) collective-permute-start(bf16[160,256]{1,0:T(8,128)(2,1)S(1)} %get-tuple-element.41), channel_id=1, source_target_pairs={{0,8},{4,12},{8,0},{12,4},{16,24},{20,28},{24,16},{28,20},{1,9},{5... | collective-permute-start | bytes 245768 | tf_op jit(solution)/shard_map/ppermute | solution.py:396
  17.9 0.9 %collective-permute-done.4.refs_5_.refs_3_ = bf16[320,256]{1,0:T(8,128)(2,1)S(1)} collective-permute-done((bf16[320,256]{1,0:T(8,128)(2,1)S(1)}, bf16[320,256]{1,0:T(8,128)(2,1)S(1)}, u32[]{:S(2)}, u32[]{:S(2)}) %collective-permute-start.4) | collective-permute-done | bytes 163872 | tf_op jit(solution)/shard_map/ppermute | solution.py:396
  18.8 0.7 %collective-permute-done.3.refs_4_ = bf16[240,384]{1,0:T(8,128)(2,1)S(1)} collective-permute-done((bf16[240,384]{1,0:T(8,128)(2,1)S(1)}, bf16[240,384]{1,0:T(8,128)(2,1)S(1)}, u32[]{:S(2)}, u32[]{:S(2)}) %collective-permute-start.3) | collective-permute-done | bytes 184352 | tf_op jit(solution)/shard_map/ppermute | solution.py:396
  19.8 2.2 %collective-permute-done.10.refs_5_.refs_3_ = bf16[160,256]{1,0:T(8,128)(2,1)S(1)} collective-permute-done((bf16[160,256]{1,0:T(8,128)(2,1)S(1)}, bf16[160,256]{1,0:T(8,128)(2,1)S(1)}, u32[]{:S(2)}, u32[]{:S(2)}) %collective-permute-start.10) | collective-permute-done | bytes 81952 | tf_op jit(solution)/shard_map/ppermute | solution.py:396
  22.0 1.5 %collective-permute-start.14 = (bf16[640,256]{1,0:T(8,128)(2,1)S(1)}, bf16[640,256]{1,0:T(8,128)(2,1)S(1)}, u32[]{:S(2)}, u32[]{:S(2)}) collective-permute-start(bf16[640,256]{1,0:T(8,128)(2,1)S(1)} %shard_map.71.refs_5_), channel_id=1, source_target_pairs={{0,8},{4,12},{8,0},{12,4},{16,24},{20,28},{24,16},{28,20},{1,9},{5... | collective-permute-start | bytes 983048 | tf_op jit(solution)/shard_map/ppermute | solution.py:396
  23.6 0.5 collective-permute-start.7
  24.1 0.5 collective-permute-start.20
  24.6 0.4 collective-permute-done.5.refs_2_
  25.2 1.3 %shard_map.70 = (bf16[320,1024]{1,0:T(8,128)(2,1)S(1)}, bf16[80,1024]{1,0:T(8,128)(2,1)S(1)}, f32[80,1024]{1,0:T(8,128)S(1)}) custom-call(bf16[768,320]{1,0:T(8,128)(2,1)S(1)} %get-tuple-element.39.refs_0_, bf16[320,256]{1,0:T(8,128)(2,1)S(1)} %get-tuple-element.40.refs_1_, bf16[320,256]{1,0:T(8,128)(2,1)S(1)} %collective-permute-done.5.refs_2_, ...), custom_call_target="tpu_custom_call" | custom-call | tf_op jit(solution)/shard_map/pallas_call | solution.py:126
  26.5 1.4 %shard_map.75 = (bf16[320,384]{1,0:T(8,128)(2,1)S(1)}, f32[320,384]{1,0:T(8,128)S(1)}, bf16[640,256]{1,0:T(8,128)(2,1)S(1)}, f32[640,256]{1,0:T(8,128)S(1)}) custom-call(bf16[320,768]{1,0:T(8,128)(2,1)S(1)} %get-tuple-element.43.refs_2_.refs_0_, bf16[320,1024]{1,0:T(8,128)(2,1)S(1)} %get-tuple-element.50.refs_1_, f32[80,1024]{1,0:T(8,128)S(1)} %get-tuple-element.51.refs_2_, ...), custom_call_target="tpu_custom_call" | custom-call | tf_op jit(solution)/shard_map/pallas_call | solution.py:126
  27.9 1.6 %collective-permute-start.21 = (bf16[320,384]{1,0:T(8,128)(2,1)S(1)}, bf16[320,384]{1,0:T(8,128)(2,1)S(1)}, u32[]{:S(2)}, u32[]{:S(2)}) collective-permute-start(bf16[320,384]{1,0:T(8,128)(2,1)S(1)} %get-tuple-element.55), channel_id=1, source_target_pairs={{0,16},{4,20},{8,24},{12,28},{16,0},{20,4},{24,8},{28,12},{1,17},{... | collective-permute-start | bytes 737288 | tf_op jit(solution)/shard_map/ppermute | solution.py:396
  29.7 0.3 collective-permute-start.15
  30.2 0.3 collective-permute-start.11
  30.5 5.6 %collective-permute-done.21.refs_1_ = bf16[320,384]{1,0:T(8,128)(2,1)S(1)} collective-permute-done((bf16[320,384]{1,0:T(8,128)(2,1)S(1)}, bf16[320,384]{1,0:T(8,128)(2,1)S(1)}, u32[]{:S(2)}, u32[]{:S(2)}) %collective-permute-start.21) | collective-permute-done | bytes 245792 | tf_op jit(solution)/shard_map/ppermute | solution.py:396
  36.2 0.4 collective-permute-start.22
  36.7 0.8 %collective-permute-done.12.refs_4_ = bf16[320,256]{1,0:T(8,128)(2,1)S(1)} collective-permute-done((bf16[320,256]{1,0:T(8,128)(2,1)S(1)}, bf16[320,256]{1,0:T(8,128)(2,1)S(1)}, u32[]{:S(2)}, u32[]{:S(2)}) %collective-permute-start.12) | collective-permute-done | bytes 163872 | tf_op jit(solution)/shard_map/ppermute | solution.py:396
  37.5 0.8 %shard_map.72 = (bf16[160,256]{1,0:T(8,128)(2,1)S(1)}, f32[160,256]{1,0:T(8,128)S(1)}) custom-call(bf16[80,1024]{1,0:T(8,128)(2,1)S(1)} %get-tuple-element.42.refs_0_, bf16[320,256]{1,0:T(8,128)(2,1)S(1)} %get-tuple-element.38.refs_1_, bf16[320,256]{1,0:T(8,128)(2,1)S(1)} %collective-permute-done.11.refs_2_, ...), custom_call_target="tpu_custom_call" | custom-call | tf_op jit(solution)/shard_map/pallas_call | solution.py:126
  38.3 1.6 %collective-permute-start.16 = (bf16[160,256]{1,0:T(8,128)(2,1)S(1)}, bf16[160,256]{1,0:T(8,128)(2,1)S(1)}, u32[]{:S(2)}, u32[]{:S(2)}) collective-permute-start(bf16[160,256]{1,0:T(8,128)(2,1)S(1)} %get-tuple-element.45), channel_id=1, source_target_pairs={{0,16},{4,20},{8,24},{12,28},{16,0},{20,4},{24,8},{28,12},{1,17},{... | collective-permute-start | bytes 245768 | tf_op jit(solution)/shard_map/ppermute | solution.py:396
  40.0 0.6 collective-permute-start.25
  40.6 2.3 %collective-permute-done.16.refs_1_ = bf16[160,256]{1,0:T(8,128)(2,1)S(1)} collective-permute-done((bf16[160,256]{1,0:T(8,128)(2,1)S(1)}, bf16[160,256]{1,0:T(8,128)(2,1)S(1)}, u32[]{:S(2)}, u32[]{:S(2)}) %collective-permute-start.16) | collective-permute-done | bytes 81952 | tf_op jit(solution)/shard_map/ppermute | solution.py:396
  42.9 1.0 %collective-permute-start.17 = (bf16[160,256]{1,0:T(8,128)(2,1)S(1)}, bf16[160,256]{1,0:T(8,128)(2,1)S(1)}, u32[]{:S(2)}, u32[]{:S(2)}) collective-permute-start(bf16[160,256]{1,0:T(8,128)(2,1)S(1)} %get-tuple-element.47.refs_2_), channel_id=1, source_target_pairs={{0,1},{1,0},{2,3},{3,2},{4,5},{5,4},{6,7},{7,6},{8,9},{9,8},{10,11... | collective-permute-start | bytes 245768 | tf_op jit(solution)/shard_map/ppermute | solution.py:399
  43.9 2.3 %collective-permute-start.23 = (bf16[80,384]{1,0:T(8,128)(2,1)S(1)}, bf16[80,384]{1,0:T(8,128)(2,1)S(1)}, u32[]{:S(2)}, u32[]{:S(2)}) collective-permute-start(bf16[80,384]{1,0:T(8,128)(2,1)S(1)} %get-tuple-element.59), channel_id=1, source_target_pairs={{0,2},{1,3},{2,0},{3,1},{4,6},{5,7},{6,4},{7,5},{8,10},{9,11},{10,... | collective-permute-start | bytes 184328 | tf_op jit(solution)/shard_map/ppermute | solution.py:399
  46.2 1.9 %collective-permute-done.17.refs_1_ = bf16[160,256]{1,0:T(8,128)(2,1)S(1)} collective-permute-done((bf16[160,256]{1,0:T(8,128)(2,1)S(1)}, bf16[160,256]{1,0:T(8,128)(2,1)S(1)}, u32[]{:S(2)}, u32[]{:S(2)}) %collective-permute-start.17) | collective-permute-done | bytes 81952 | tf_op jit(solution)/shard_map/ppermute | solution.py:399
  48.0 1.4 %collective-permute-start.18 = (bf16[160,256]{1,0:T(8,128)(2,1)S(1)}, bf16[160,256]{1,0:T(8,128)(2,1)S(1)}, u32[]{:S(2)}, u32[]{:S(2)}) collective-permute-start(bf16[160,256]{1,0:T(8,128)(2,1)S(1)} %get-tuple-element.49), channel_id=1, source_target_pairs={{0,2},{1,3},{2,0},{3,1},{4,6},{5,7},{6,4},{7,5},{8,10},{9,11},{10,... | collective-permute-start | bytes 245768 | tf_op jit(solution)/shard_map/ppermute | solution.py:399
  49.5 0.6 collective-permute-start.26
  50.1 1.5 %collective-permute-start.27 = (bf16[80,384]{1,0:T(8,128)(2,1)S(1)}, bf16[80,384]{1,0:T(8,128)(2,1)S(1)}, u32[]{:S(2)}, u32[]{:S(2)}) collective-permute-start(bf16[80,384]{1,0:T(8,128)(2,1)S(1)} %shard_map.79.refs_2_), channel_id=1, source_target_pairs={{0,16},{4,20},{8,24},{12,28},{16,0},{20,4},{24,8},{28,12},{1,17},{... | collective-permute-start | bytes 184328 | tf_op jit(solution)/shard_map/ppermute | solution.py:396
  51.6 1.4 %collective-permute-start.28 = (bf16[80,384]{1,0:T(8,128)(2,1)S(1)}, bf16[80,384]{1,0:T(8,128)(2,1)S(1)}, u32[]{:S(2)}, u32[]{:S(2)}) collective-permute-start(bf16[80,384]{1,0:T(8,128)(2,1)S(1)} %shard_map.79.refs_2_), channel_id=1, source_target_pairs={{0,24},{4,28},{8,16},{12,20},{16,8},{20,12},{24,0},{28,4},{1,25},{... | collective-permute-start | bytes 184328 | tf_op jit(solution)/shard_map/ppermute | solution.py:396
  53.0 0.7 %collective-permute-done.26.refs_3_ = bf16[80,384]{1,0:T(8,128)(2,1)S(1)} collective-permute-done((bf16[80,384]{1,0:T(8,128)(2,1)S(1)}, bf16[80,384]{1,0:T(8,128)(2,1)S(1)}, u32[]{:S(2)}, u32[]{:S(2)}) %collective-permute-start.26) | collective-permute-done | bytes 61472 | tf_op jit(solution)/shard_map/ppermute | solution.py:396
  53.8 0.5 collective-permute-done.27.refs_4_
  54.3 2.4 %collective-permute-done.28.refs_5_ = bf16[80,384]{1,0:T(8,128)(2,1)S(1)} collective-permute-done((bf16[80,384]{1,0:T(8,128)(2,1)S(1)}, bf16[80,384]{1,0:T(8,128)(2,1)S(1)}, u32[]{:S(2)}, u32[]{:S(2)}) %collective-permute-start.28) | collective-permute-done | bytes 61472 | tf_op jit(solution)/shard_map/ppermute | solution.py:396
  56.7 0.9 %shard_map.80 = (bf16[160,256]{1,0:T(8,128)(2,1)S(1)}, bf16[320,384]{1,0:T(8,128)(2,1)S(1)}, bf16[256,320]{1,0:T(8,128)(2,1)}) custom-call(f32[160,256]{1,0:T(8,128)S(1)} %get-tuple-element.48.refs_0_, bf16[160,256]{1,0:T(8,128)(2,1)S(1)} %collective-permute-done.18.refs_1_, bf16[80,384]{1,0:T(8,128)(2,1)S(1)} %shard_map.79.refs_2_, ...), custom_call_target="tpu_custom_call" | custom-call | tf_op jit(solution)/shard_map/pallas_call | solution.py:126
  57.6 1.5 %collective-permute-start.30 = (bf16[160,256]{1,0:T(8,128)(2,1)S(1)}, bf16[160,256]{1,0:T(8,128)(2,1)S(1)}, u32[]{:S(2)}, u32[]{:S(2)}) collective-permute-start(bf16[160,256]{1,0:T(8,128)(2,1)S(1)} %get-tuple-element.67.refs_0_), channel_id=1, source_target_pairs={{0,8},{4,12},{8,0},{12,4},{16,24},{20,28},{24,16},{28,20},{1,9},{5... | collective-permute-start | bytes 245768 | tf_op jit(solution)/shard_map/ppermute | solution.py:396
  59.1 0.5 collective-permute-start.31
  59.6 1.5 %collective-permute-start.32 = (bf16[160,256]{1,0:T(8,128)(2,1)S(1)}, bf16[160,256]{1,0:T(8,128)(2,1)S(1)}, u32[]{:S(2)}, u32[]{:S(2)}) collective-permute-start(bf16[160,256]{1,0:T(8,128)(2,1)S(1)} %get-tuple-element.67.refs_0_), channel_id=1, source_target_pairs={{0,24},{4,28},{8,16},{12,20},{16,8},{20,12},{24,0},{28,4},{1,25},{... | collective-permute-start | bytes 245768 | tf_op jit(solution)/shard_map/ppermute | solution.py:396
  61.1 1.6 %shard_map.81 = (f32[9,80,320]{2,1,0:T(8,128)}, f32[8,128]{1,0:T(8,128)S(1)}) custom-call(bf16[320,384]{1,0:T(8,128)(2,1)S(1)} %get-tuple-element.65.refs_0_, bf16[320,384]{1,0:T(8,128)(2,1)S(1)} %collective-permute-done.29.refs_1_), custom_call_target="tpu_custom_call" | custom-call | tf_op jit(solution)/shard_map/pallas_call | solution.py:126
  62.7 2.7 %collective-permute-done.31.refs_2_ = bf16[160,256]{1,0:T(8,128)(2,1)S(1)} collective-permute-done((bf16[160,256]{1,0:T(8,128)(2,1)S(1)}, bf16[160,256]{1,0:T(8,128)(2,1)S(1)}, u32[]{:S(2)}, u32[]{:S(2)}) %collective-permute-start.31) | collective-permute-done | bytes 81952 | tf_op jit(solution)/shard_map/ppermute | solution.py:396
  65.5 1.6 %collective-permute-done.33.refs_1_ = bf16[640,256]{1,0:T(8,128)(2,1)S(1)} collective-permute-done((bf16[640,256]{1,0:T(8,128)(2,1)S(1)}, bf16[640,256]{1,0:T(8,128)(2,1)S(1)}, u32[]{:S(2)}, u32[]{:S(2)}) %collective-permute-start.33) | collective-permute-done | bytes 327712 | tf_op jit(solution)/shard_map/ppermute | solution.py:396
  67.1 1.6 %shard_map.83 = f32[3,320,320]{2,1,0:T(8,128)} custom-call(bf16[640,256]{1,0:T(8,128)(2,1)S(1)} %shard_map.82.refs_0_, bf16[640,256]{1,0:T(8,128)(2,1)S(1)} %collective-permute-done.33.refs_1_), custom_call_target="tpu_custom_call" | custom-call | tf_op jit(solution)/shard_map/pallas_call | solution.py:126
  (44 shorter events, 1.7 us)
Async XLA Ops:
  0.6 15.3 %copy-start.1 = (bf16[3,320,320]{2,1,0:T(8,128)(2,1)S(1)}, bf16[3,320,320]{2,1,0:T(8,128)(2,1)}, u32[]{:S(2)}) copy-start(bf16[3,320,320]{2,1,0:T(8,128)(2,1)} %refs_3_.1) | copy-start | bytes 1843204
  2.1 9.7 %collective-permute-start = (bf16[80,384]{1,0:T(8,128)(2,1)S(1)}, bf16[80,384]{1,0:T(8,128)(2,1)S(1)}, u32[]{:S(2)}, u32[]{:S(2)}) collective-permute-start(bf16[80,384]{1,0:T(8,128)(2,1)S(1)} %get-tuple-element.37), channel_id=1, source_target_pairs={{0,1},{1,2},{2,3},{3,0},{4,5},{5,6},{6,7},{7,4},{8,9},{9,10},{10,1... | collective-permute-start | bytes 184328 | tf_op jit(solution)/shard_map/ppermute | solution.py:402
  5.2 8.3 %collective-permute-start.1 = (bf16[80,384]{1,0:T(8,128)(2,1)S(1)}, bf16[80,384]{1,0:T(8,128)(2,1)S(1)}, u32[]{:S(2)}, u32[]{:S(2)}) collective-permute-start(bf16[80,384]{1,0:T(8,128)(2,1)S(1)} %get-tuple-element.37), channel_id=1, source_target_pairs={{0,2},{1,3},{2,0},{3,1},{4,6},{5,7},{6,4},{7,5},{8,10},{9,11},{10,... | collective-permute-start | bytes 184328 | tf_op jit(solution)/shard_map/ppermute | solution.py:402
  7.8 6.1 %collective-permute-start.2 = (bf16[80,384]{1,0:T(8,128)(2,1)S(1)}, bf16[80,384]{1,0:T(8,128)(2,1)S(1)}, u32[]{:S(2)}, u32[]{:S(2)}) collective-permute-start(bf16[80,384]{1,0:T(8,128)(2,1)S(1)} %get-tuple-element.37), channel_id=1, source_target_pairs={{0,3},{1,0},{2,1},{3,2},{4,7},{5,4},{6,5},{7,6},{8,11},{9,8},{10,9... | collective-permute-start | bytes 184328 | tf_op jit(solution)/shard_map/ppermute | solution.py:402
  9.1 6.5 %collective-permute-start.9 = (bf16[320,256]{1,0:T(8,128)(2,1)S(1)}, bf16[320,256]{1,0:T(8,128)(2,1)S(1)}, u32[]{:S(2)}, u32[]{:S(2)}) collective-permute-start(bf16[320,256]{1,0:T(8,128)(2,1)S(1)} %get-tuple-element.38.refs_1_), channel_id=1, source_target_pairs={{0,0},{1,2},{2,1},{3,3},{4,4},{5,6},{6,5},{7,7},{8,8},{9,10},{10,9... | collective-permute-start | bytes 491528 | tf_op jit(solution)/shard_map/ppermute | solution.py:411
  9.8 6.1 %collective-permute-start.8 = (bf16[320,256]{1,0:T(8,128)(2,1)S(1)}, bf16[320,256]{1,0:T(8,128)(2,1)S(1)}, u32[]{:S(2)}, u32[]{:S(2)}) collective-permute-start(bf16[320,256]{1,0:T(8,128)(2,1)S(1)} %get-tuple-element.38.refs_1_), channel_id=1, source_target_pairs={{0,1},{1,0},{2,3},{3,2},{4,5},{5,4},{6,7},{7,6},{8,9},{9,8},{10,11... | collective-permute-start | bytes 491528 | tf_op jit(solution)/shard_map/ppermute | solution.py:411
  11.9 7.0 %collective-permute-start.4 = (bf16[320,256]{1,0:T(8,128)(2,1)S(1)}, bf16[320,256]{1,0:T(8,128)(2,1)S(1)}, u32[]{:S(2)}, u32[]{:S(2)}) collective-permute-start(bf16[320,256]{1,0:T(8,128)(2,1)S(1)} %get-tuple-element.38.refs_1_), channel_id=1, source_target_pairs={{0,8},{4,12},{8,0},{12,4},{16,24},{20,28},{24,16},{28,20},{1,9},{5... | collective-permute-start | bytes 491528 | tf_op jit(solution)/shard_map/ppermute | solution.py:396
  13.5 10.1 %collective-permute-start.6 = (bf16[320,256]{1,0:T(8,128)(2,1)S(1)}, bf16[320,256]{1,0:T(8,128)(2,1)S(1)}, u32[]{:S(2)}, u32[]{:S(2)}) collective-permute-start(bf16[320,256]{1,0:T(8,128)(2,1)S(1)} %get-tuple-element.40.refs_1_), channel_id=1, source_target_pairs={{0,8},{4,12},{8,0},{12,4},{16,24},{20,28},{24,16},{28,20},{1,9},{5... | collective-permute-start | bytes 491528 | tf_op jit(solution)/shard_map/ppermute | solution.py:396
  13.9 5.6 %collective-permute-start.3 = (bf16[240,384]{1,0:T(8,128)(2,1)S(1)}, bf16[240,384]{1,0:T(8,128)(2,1)S(1)}, u32[]{:S(2)}, u32[]{:S(2)}) collective-permute-start(bf16[240,384]{1,0:T(8,128)(2,1)S(1)} %pad_maximum_fusion), channel_id=1, source_target_pairs={{0,16},{4,20},{8,24},{12,28},{16,0},{20,4},{24,8},{28,12},{1,17},{... | collective-permute-start | bytes 552968 | tf_op jit(solution)/shard_map/ppermute | solution.py:396
  16.4 5.6 %collective-permute-start.10 = (bf16[160,256]{1,0:T(8,128)(2,1)S(1)}, bf16[160,256]{1,0:T(8,128)(2,1)S(1)}, u32[]{:S(2)}, u32[]{:S(2)}) collective-permute-start(bf16[160,256]{1,0:T(8,128)(2,1)S(1)} %get-tuple-element.41), channel_id=1, source_target_pairs={{0,8},{4,12},{8,0},{12,4},{16,24},{20,28},{24,16},{28,20},{1,9},{5... | collective-permute-start | bytes 245768 | tf_op jit(solution)/shard_map/ppermute | solution.py:396
  22.0 7.7 %collective-permute-start.14 = (bf16[640,256]{1,0:T(8,128)(2,1)S(1)}, bf16[640,256]{1,0:T(8,128)(2,1)S(1)}, u32[]{:S(2)}, u32[]{:S(2)}) collective-permute-start(bf16[640,256]{1,0:T(8,128)(2,1)S(1)} %shard_map.71.refs_5_), channel_id=1, source_target_pairs={{0,8},{4,12},{8,0},{12,4},{16,24},{20,28},{24,16},{28,20},{1,9},{5... | collective-permute-start | bytes 983048 | tf_op jit(solution)/shard_map/ppermute | solution.py:396
  23.6 1.4 %collective-permute-start.5 = (bf16[320,256]{1,0:T(8,128)(2,1)S(1)}, bf16[320,256]{1,0:T(8,128)(2,1)S(1)}, u32[]{:S(2)}, u32[]{:S(2)}) collective-permute-start(bf16[320,256]{1,0:T(8,128)(2,1)S(1)} %get-tuple-element.40.refs_1_), channel_id=1, source_target_pairs={{0,4},{4,0},{8,12},{12,8},{16,20},{20,16},{24,28},{28,24},{1,5},{5... | collective-permute-start | bytes 491528 | tf_op jit(solution)/shard_map/ppermute | solution.py:396
  23.6 1.6 %collective-permute-start.7 = (bf16[320,256]{1,0:T(8,128)(2,1)S(1)}, bf16[320,256]{1,0:T(8,128)(2,1)S(1)}, u32[]{:S(2)}, u32[]{:S(2)}) collective-permute-start(bf16[320,256]{1,0:T(8,128)(2,1)S(1)} %collective-permute-done.6.refs_3_), channel_id=1, source_target_pairs={{0,4},{4,0},{8,12},{12,8},{16,20},{20,16},{24,28},{28,24},{1,5},{5... | collective-permute-start | bytes 491528 | tf_op jit(solution)/shard_map/ppermute | solution.py:396
  24.1 2.4 %collective-permute-start.19 = (bf16[80,256]{1,0:T(8,128)(2,1)S(1)}, bf16[80,256]{1,0:T(8,128)(2,1)S(1)}, u32[]{:S(2)}, u32[]{:S(2)}) collective-permute-start(bf16[80,256]{1,0:T(8,128)(2,1)S(1)} %get-tuple-element.53), channel_id=1, source_target_pairs={{0,4},{4,0},{8,12},{12,8},{16,20},{20,16},{24,28},{28,24},{1,5},{5... | collective-permute-start | bytes 122888 | tf_op jit(solution)/shard_map/ppermute | solution.py:396
  24.1 2.4 %collective-permute-start.20 = (bf16[80,256]{1,0:T(8,128)(2,1)S(1)}, bf16[80,256]{1,0:T(8,128)(2,1)S(1)}, u32[]{:S(2)}, u32[]{:S(2)}) collective-permute-start(bf16[80,256]{1,0:T(8,128)(2,1)S(1)} %slice.4), channel_id=1, source_target_pairs={{0,4},{4,0},{8,12},{12,8},{16,20},{20,16},{24,28},{28,24},{1,5},{5... | collective-permute-start | bytes 122888 | tf_op jit(solution)/shard_map/ppermute | solution.py:396
  27.9 8.2 %collective-permute-start.21 = (bf16[320,384]{1,0:T(8,128)(2,1)S(1)}, bf16[320,384]{1,0:T(8,128)(2,1)S(1)}, u32[]{:S(2)}, u32[]{:S(2)}) collective-permute-start(bf16[320,384]{1,0:T(8,128)(2,1)S(1)} %get-tuple-element.55), channel_id=1, source_target_pairs={{0,16},{4,20},{8,24},{12,28},{16,0},{20,4},{24,8},{28,12},{1,17},{... | collective-permute-start | bytes 737288 | tf_op jit(solution)/shard_map/ppermute | solution.py:396
  29.5 8.0 %collective-permute-start.13 = (bf16[640,256]{1,0:T(8,128)(2,1)S(1)}, bf16[640,256]{1,0:T(8,128)(2,1)S(1)}, u32[]{:S(2)}, u32[]{:S(2)}) collective-permute-start(bf16[640,256]{1,0:T(8,128)(2,1)S(1)} %shard_map.71.refs_5_), channel_id=1, source_target_pairs={{0,4},{4,0},{8,12},{12,8},{16,20},{20,16},{24,28},{28,24},{1,5},{5... | collective-permute-start | bytes 983048 | tf_op jit(solution)/shard_map/ppermute | solution.py:396
  29.7 7.8 %collective-permute-start.15 = (bf16[640,256]{1,0:T(8,128)(2,1)S(1)}, bf16[640,256]{1,0:T(8,128)(2,1)S(1)}, u32[]{:S(2)}, u32[]{:S(2)}) collective-permute-start(bf16[640,256]{1,0:T(8,128)(2,1)S(1)} %collective-permute-done.14.refs_7_), channel_id=1, source_target_pairs={{0,4},{4,0},{8,12},{12,8},{16,20},{20,16},{24,28},{28,24},{1,5},{5... | collective-permute-start | bytes 983048 | tf_op jit(solution)/shard_map/ppermute | solution.py:396
  30.0 9.9 %collective-permute-start.24 = (bf16[640,256]{1,0:T(8,128)(2,1)S(1)}, bf16[640,256]{1,0:T(8,128)(2,1)S(1)}, u32[]{:S(2)}, u32[]{:S(2)}) collective-permute-start(bf16[640,256]{1,0:T(8,128)(2,1)S(1)} %get-tuple-element.61), channel_id=1, source_target_pairs={{0,4},{4,0},{8,12},{12,8},{16,20},{20,16},{24,28},{28,24},{1,5},{5... | collective-permute-start | bytes 983048 | tf_op jit(solution)/shard_map/ppermute | solution.py:396
  30.2 6.0 %collective-permute-start.11 = (bf16[320,256]{1,0:T(8,128)(2,1)S(1)}, bf16[320,256]{1,0:T(8,128)(2,1)S(1)}, u32[]{:S(2)}, u32[]{:S(2)}) collective-permute-start(bf16[320,256]{1,0:T(8,128)(2,1)S(1)} %get-tuple-element.38.refs_1_), channel_id=1, source_target_pairs={{0,4},{4,0},{8,12},{12,8},{16,20},{20,16},{24,28},{28,24},{1,5},{5... | collective-permute-start | bytes 491528 | tf_op jit(solution)/shard_map/ppermute | solution.py:396
  36.1 1.4 %collective-permute-start.12 = (bf16[320,256]{1,0:T(8,128)(2,1)S(1)}, bf16[320,256]{1,0:T(8,128)(2,1)S(1)}, u32[]{:S(2)}, u32[]{:S(2)}) collective-permute-start(bf16[320,256]{1,0:T(8,128)(2,1)S(1)} %collective-permute-done.4.refs_5_.refs_3_), channel_id=1, source_target_pairs={{0,4},{4,0},{8,12},{12,8},{16,20},{20,16},{24,28},{28,24},{1,5},{5... | collective-permute-start | bytes 491528 | tf_op jit(solution)/shard_map/ppermute | solution.py:396
  36.2 7.6 %collective-permute-start.22 = (bf16[160,384]{1,0:T(8,128)(2,1)S(1)}, bf16[160,384]{1,0:T(8,128)(2,1)S(1)}, u32[]{:S(2)}, u32[]{:S(2)}) collective-permute-start(bf16[160,384]{1,0:T(8,128)(2,1)S(1)} %get-tuple-element.57), channel_id=1, source_target_pairs={{0,1},{1,0},{2,3},{3,2},{4,5},{5,4},{6,7},{7,6},{8,9},{9,8},{10,11... | collective-permute-start | bytes 368648 | tf_op jit(solution)/shard_map/ppermute | solution.py:399
  38.3 18.5 %copy-start = (bf16[1,1,16,16,320]{4,3,2,1,0:T(8,128)(2,1)S(1)}, bf16[1,1,16,16,320]{4,3,2,1,0:T(8,128)(2,1)}, u32[]{:S(2)}) copy-start(bf16[1,1,16,16,320]{4,3,2,1,0:T(8,128)(2,1)} %param.5) | copy-start | bytes 491524
  38.3 4.6 %collective-permute-start.16 = (bf16[160,256]{1,0:T(8,128)(2,1)S(1)}, bf16[160,256]{1,0:T(8,128)(2,1)S(1)}, u32[]{:S(2)}, u32[]{:S(2)}) collective-permute-start(bf16[160,256]{1,0:T(8,128)(2,1)S(1)} %get-tuple-element.45), channel_id=1, source_target_pairs={{0,16},{4,20},{8,24},{12,28},{16,0},{20,4},{24,8},{28,12},{1,17},{... | collective-permute-start | bytes 245768 | tf_op jit(solution)/shard_map/ppermute | solution.py:396
  40.0 9.5 %collective-permute-start.25 = (bf16[320,256]{1,0:T(8,128)(2,1)S(1)}, bf16[320,256]{1,0:T(8,128)(2,1)S(1)}, u32[]{:S(2)}, u32[]{:S(2)}) collective-permute-start(bf16[320,256]{1,0:T(8,128)(2,1)S(1)} %get-tuple-element.62), channel_id=1, source_target_pairs={{0,8},{4,12},{8,0},{12,4},{16,24},{20,28},{24,16},{28,20},{1,9},{5... | collective-permute-start | bytes 491528 | tf_op jit(solution)/shard_map/ppermute | solution.py:396
  42.9 5.2 %collective-permute-start.17 = (bf16[160,256]{1,0:T(8,128)(2,1)S(1)}, bf16[160,256]{1,0:T(8,128)(2,1)S(1)}, u32[]{:S(2)}, u32[]{:S(2)}) collective-permute-start(bf16[160,256]{1,0:T(8,128)(2,1)S(1)} %get-tuple-element.47.refs_2_), channel_id=1, source_target_pairs={{0,1},{1,0},{2,3},{3,2},{4,5},{5,4},{6,7},{7,6},{8,9},{9,8},{10,11... | collective-permute-start | bytes 245768 | tf_op jit(solution)/shard_map/ppermute | solution.py:399
  43.9 5.6 %collective-permute-start.23 = (bf16[80,384]{1,0:T(8,128)(2,1)S(1)}, bf16[80,384]{1,0:T(8,128)(2,1)S(1)}, u32[]{:S(2)}, u32[]{:S(2)}) collective-permute-start(bf16[80,384]{1,0:T(8,128)(2,1)S(1)} %get-tuple-element.59), channel_id=1, source_target_pairs={{0,2},{1,3},{2,0},{3,1},{4,6},{5,7},{6,4},{7,5},{8,10},{9,11},{10,... | collective-permute-start | bytes 184328 | tf_op jit(solution)/shard_map/ppermute | solution.py:399
  48.0 8.7 %collective-permute-start.18 = (bf16[160,256]{1,0:T(8,128)(2,1)S(1)}, bf16[160,256]{1,0:T(8,128)(2,1)S(1)}, u32[]{:S(2)}, u32[]{:S(2)}) collective-permute-start(bf16[160,256]{1,0:T(8,128)(2,1)S(1)} %get-tuple-element.49), channel_id=1, source_target_pairs={{0,2},{1,3},{2,0},{3,1},{4,6},{5,7},{6,4},{7,5},{8,10},{9,11},{10,... | collective-permute-start | bytes 245768 | tf_op jit(solution)/shard_map/ppermute | solution.py:399
  49.5 4.3 %collective-permute-start.26 = (bf16[80,384]{1,0:T(8,128)(2,1)S(1)}, bf16[80,384]{1,0:T(8,128)(2,1)S(1)}, u32[]{:S(2)}, u32[]{:S(2)}) collective-permute-start(bf16[80,384]{1,0:T(8,128)(2,1)S(1)} %shard_map.79.refs_2_), channel_id=1, source_target_pairs={{0,8},{4,12},{8,0},{12,4},{16,24},{20,28},{24,16},{28,20},{1,9},{5... | collective-permute-start | bytes 184328 | tf_op jit(solution)/shard_map/ppermute | solution.py:396
  50.1 4.2 %collective-permute-start.27 = (bf16[80,384]{1,0:T(8,128)(2,1)S(1)}, bf16[80,384]{1,0:T(8,128)(2,1)S(1)}, u32[]{:S(2)}, u32[]{:S(2)}) collective-permute-start(bf16[80,384]{1,0:T(8,128)(2,1)S(1)} %shard_map.79.refs_2_), channel_id=1, source_target_pairs={{0,16},{4,20},{8,24},{12,28},{16,0},{20,4},{24,8},{28,12},{1,17},{... | collective-permute-start | bytes 184328 | tf_op jit(solution)/shard_map/ppermute | solution.py:396
  51.6 5.1 %collective-permute-start.28 = (bf16[80,384]{1,0:T(8,128)(2,1)S(1)}, bf16[80,384]{1,0:T(8,128)(2,1)S(1)}, u32[]{:S(2)}, u32[]{:S(2)}) collective-permute-start(bf16[80,384]{1,0:T(8,128)(2,1)S(1)} %shard_map.79.refs_2_), channel_id=1, source_target_pairs={{0,24},{4,28},{8,16},{12,20},{16,8},{20,12},{24,0},{28,4},{1,25},{... | collective-permute-start | bytes 184328 | tf_op jit(solution)/shard_map/ppermute | solution.py:396
  57.6 3.5 %collective-permute-start.29 = (bf16[320,384]{1,0:T(8,128)(2,1)S(1)}, bf16[320,384]{1,0:T(8,128)(2,1)S(1)}, u32[]{:S(2)}, u32[]{:S(2)}) collective-permute-start(bf16[320,384]{1,0:T(8,128)(2,1)S(1)} %get-tuple-element.65.refs_0_), channel_id=1, source_target_pairs={{0,4},{4,0},{8,12},{12,8},{16,20},{20,16},{24,28},{28,24},{1,5},{5... | collective-permute-start | bytes 737288 | tf_op jit(solution)/shard_map/ppermute | solution.py:396
  57.6 5.1 %collective-permute-start.30 = (bf16[160,256]{1,0:T(8,128)(2,1)S(1)}, bf16[160,256]{1,0:T(8,128)(2,1)S(1)}, u32[]{:S(2)}, u32[]{:S(2)}) collective-permute-start(bf16[160,256]{1,0:T(8,128)(2,1)S(1)} %get-tuple-element.67.refs_0_), channel_id=1, source_target_pairs={{0,8},{4,12},{8,0},{12,4},{16,24},{20,28},{24,16},{28,20},{1,9},{5... | collective-permute-start | bytes 245768 | tf_op jit(solution)/shard_map/ppermute | solution.py:396
  59.1 6.3 %collective-permute-start.31 = (bf16[160,256]{1,0:T(8,128)(2,1)S(1)}, bf16[160,256]{1,0:T(8,128)(2,1)S(1)}, u32[]{:S(2)}, u32[]{:S(2)}) collective-permute-start(bf16[160,256]{1,0:T(8,128)(2,1)S(1)} %get-tuple-element.67.refs_0_), channel_id=1, source_target_pairs={{0,16},{4,20},{8,24},{12,28},{16,0},{20,4},{24,8},{28,12},{1,17},{... | collective-permute-start | bytes 245768 | tf_op jit(solution)/shard_map/ppermute | solution.py:396
  59.6 5.8 %collective-permute-start.32 = (bf16[160,256]{1,0:T(8,128)(2,1)S(1)}, bf16[160,256]{1,0:T(8,128)(2,1)S(1)}, u32[]{:S(2)}, u32[]{:S(2)}) collective-permute-start(bf16[160,256]{1,0:T(8,128)(2,1)S(1)} %get-tuple-element.67.refs_0_), channel_id=1, source_target_pairs={{0,24},{4,28},{8,16},{12,20},{16,8},{20,12},{24,0},{28,4},{1,25},{... | collective-permute-start | bytes 245768 | tf_op jit(solution)/shard_map/ppermute | solution.py:396
  65.4 1.7 %collective-permute-start.33 = (bf16[640,256]{1,0:T(8,128)(2,1)S(1)}, bf16[640,256]{1,0:T(8,128)(2,1)S(1)}, u32[]{:S(2)}, u32[]{:S(2)}) collective-permute-start(bf16[640,256]{1,0:T(8,128)(2,1)S(1)} %shard_map.82.refs_0_), channel_id=1, source_target_pairs={{0,4},{4,0},{8,12},{12,8},{16,20},{20,16},{24,28},{28,24},{1,5},{5... | collective-permute-start | bytes 983048 | tf_op jit(solution)/shard_map/ppermute | solution.py:396

commit v4 on v3

--- a/solution.py
+++ b/solution.py
@@ -347,15 +347,13 @@
     send_ref[...] = (keep_ref[chans:, :] + got_ref[chans:, :].astype(F32)).astype(BF16)
 
 
-def ends(plan, t_own, t_got, *refs):
-    chips, (f_own, f_got, g_ref, t_sum, s_all, f_out) = refs[:4], refs[4:]
+def ends(t_own, t_got, *refs):
+    chips, (t_sum, s_all) = refs[:4], refs[4:]
     summed(t_own, t_got, t_sum)
     stacked(*chips, s_all)
-    total = f_own[...] + f_got[...].astype(F32)
-    f_out[...] = (g_ref[...].astype(F32) + total.T).astype(BF16)
-
-
-def space_end(plan, here_ref, core_ref, out_ref, token_ref, held):
+
+
+def space_end(plan, here_ref, core_ref, f_own, f_got, g_ref, out_ref, f_out, token_ref, held):
     low, high, _ = plan.place()
     group, slab, rows = plan.group, plan.slab, plan.rows
     for core, ref in enumerate((here_ref, core_ref)):
@@ -368,6 +366,8 @@
         out_ref[tap] = jnp.concatenate(
             [held[index, :, tap * slab : (tap + 1) * slab] for index in range(group)], axis=1
         )
+    frame = f_own[...] + f_got[...].astype(F32)
+    f_out[...] = (g_ref[...].astype(F32) + frame.T).astype(BF16)
     token_ref[...] = jnp.zeros_like(token_ref)
 
 
@@ -521,21 +521,17 @@
     (s_sum,) = call(
         summed, [((rows, half), BF16)], s_own, trade(s_part, 2), after=[f_other]
     )
-    t_sum, s_all, f_out = call(
-        part(ends),
-        [(time, BF16), ((4 * rows, half), BF16), ((pixels, chans), BF16)],
-        t_own,
-        t_got,
-        *chips(s_sum),
+    t_sum, s_all = call(
+        ends, [(time, BF16), ((4 * rows, half), BF16)], t_own, t_got, *chips(s_sum)
+    )
+    s_out, f_out, token = call(
+        part(space_end),
+        [((9, rows, chans), F32), ((pixels, chans), BF16), ((8, LANES), F32)],
+        s_all,
+        swap(s_all, 1),
         f_own,
         f_other,
         clip_g,
-    )
-    s_out, token = call(
-        part(space_end),
-        [((9, rows, chans), F32), ((8, LANES), F32)],
-        s_all,
-        swap(s_all, 1),
         scratch=[pltpu.VMEM((group, rows, 2 * half), F32)],
     )
     (t_all,) = call(

time: 68.9 us -> 68.2 us (0.990)
  Pallas kernels: 9.96 us -> 9.25 us
    pallas_call x16, Pallas kernels: 8.49 us -> 7.78 us  [call(): pl.pallas_call(body, out_shape=tuple((jax.ShapeDtypeStruct(shape, dtype)...]
where the time goes in v4:
time: 68.2 us; the launch traced here: 68 us
  starting transfers between devices  34.5 us (51%)
  waiting for transfers between devices  23.4 us (34%)
  Pallas kernels  9.25 us (14%)
  between operations  0.83 us (1%)
    ppermute x25, waiting for transfers between devices, swap(): lax.ppermute(value, 'clip', [(i, i ^ distance) for i in range(plan.clips)])  21.2 us
    ppermute x25, starting transfers between devices, swap(): lax.ppermute(value, 'clip', [(i, i ^ distance) for i in range(plan.clips)])  19.7 us
    pallas_call x16, Pallas kernels, call(): pl.pallas_call(body, out_shape=tuple((jax.ShapeDtypeStruct(shape, dtype)...  7.78 us
    ppermute x3, starting transfers between devices, turn(): lax.ppermute(value, 'seq', [(i, (i + k) % seqs) for i in range(seqs)])  7.01 us
    ppermute x4, starting transfers between devices, trade(): return lax.ppermute(value, 'seq', [(i, i ^ distance) for i in range(seqs)])  5.12 us
    ppermute x2, starting transfers between devices, neighbours(): found.append(lax.ppermute(value, 'seq', list(other.items())))  2.72 us
    ppermute x4, waiting for transfers between devices, trade(): return lax.ppermute(value, 'seq', [(i, i ^ distance) for i in range(seqs)])  1.86 us
    pallas_call x1, Pallas kernels, per_device(): pl.pallas_call(part(prepare), out_shape=tuple((jax.ShapeDtypeStruct(shape...  1.47 us
  transfers between devices with their start and end apart: 34, of which 16 were waited for; matrix products, arithmetic and copies ran while one was open for 0% of the time, Pallas kernels for 9%

profile of v4, /device:TPU:0, one launch (start us, length us, event | category | flops | bytes accessed | tf_op | source)
XLA Modules:
  0.0 68.0 jit_solution(6922458790979964745)
XLA Ops:
  0.6 1.5 %shard_map.67 = (bf16[320,256]{1,0:T(8,128)(2,1)S(1)}, bf16[320,256]{1,0:T(8,128)(2,1)S(1)}, bf16[80,768]{1,0:T(8,128)(2,1)S(1)}, bf16[80,384]{1,0:T(8,128)(2,1)S(1)}) custom-call(bf16[256,320]{1,0:T(8,128)(2,1)} %bitcast.8, bf16[256,320]{1,0:T(8,128)(2,1)} %bitcast.5, bf16[9,80,320]{2,1,0:T(8,128)(2,1)} %bitcast.7), custom_call_target="tpu_custom_call" | custom-call | tf_op jit(solution)/shard_map/pallas_call | solution.py:426
  2.1 3.1 %collective-permute-start = (bf16[80,384]{1,0:T(8,128)(2,1)S(1)}, bf16[80,384]{1,0:T(8,128)(2,1)S(1)}, u32[]{:S(2)}, u32[]{:S(2)}) collective-permute-start(bf16[80,384]{1,0:T(8,128)(2,1)S(1)} %get-tuple-element.37), channel_id=1, source_target_pairs={{0,1},{1,2},{2,3},{3,0},{4,5},{5,6},{6,7},{7,4},{8,9},{9,10},{10,1... | collective-permute-start | bytes 184328 | tf_op jit(solution)/shard_map/ppermute | solution.py:402
  5.2 2.6 %collective-permute-start.1 = (bf16[80,384]{1,0:T(8,128)(2,1)S(1)}, bf16[80,384]{1,0:T(8,128)(2,1)S(1)}, u32[]{:S(2)}, u32[]{:S(2)}) collective-permute-start(bf16[80,384]{1,0:T(8,128)(2,1)S(1)} %get-tuple-element.37), channel_id=1, source_target_pairs={{0,2},{1,3},{2,0},{3,1},{4,6},{5,7},{6,4},{7,5},{8,10},{9,11},{10,... | collective-permute-start | bytes 184328 | tf_op jit(solution)/shard_map/ppermute | solution.py:402
  7.8 1.3 %collective-permute-start.2 = (bf16[80,384]{1,0:T(8,128)(2,1)S(1)}, bf16[80,384]{1,0:T(8,128)(2,1)S(1)}, u32[]{:S(2)}, u32[]{:S(2)}) collective-permute-start(bf16[80,384]{1,0:T(8,128)(2,1)S(1)} %get-tuple-element.37), channel_id=1, source_target_pairs={{0,3},{1,0},{2,1},{3,2},{4,7},{5,4},{6,5},{7,6},{8,11},{9,8},{10,9... | collective-permute-start | bytes 184328 | tf_op jit(solution)/shard_map/ppermute | solution.py:402
  9.1 0.7 collective-permute-start.9
  9.8 2.1 %collective-permute-start.8 = (bf16[320,256]{1,0:T(8,128)(2,1)S(1)}, bf16[320,256]{1,0:T(8,128)(2,1)S(1)}, u32[]{:S(2)}, u32[]{:S(2)}) collective-permute-start(bf16[320,256]{1,0:T(8,128)(2,1)S(1)} %get-tuple-element.38.refs_1_), channel_id=1, source_target_pairs={{0,1},{1,0},{2,3},{3,2},{4,5},{5,4},{6,7},{7,6},{8,9},{9,8},{10,11... | collective-permute-start | bytes 491528 | tf_op jit(solution)/shard_map/ppermute | solution.py:411
  11.9 1.6 %collective-permute-start.4 = (bf16[320,256]{1,0:T(8,128)(2,1)S(1)}, bf16[320,256]{1,0:T(8,128)(2,1)S(1)}, u32[]{:S(2)}, u32[]{:S(2)}) collective-permute-start(bf16[320,256]{1,0:T(8,128)(2,1)S(1)} %get-tuple-element.38.refs_1_), channel_id=1, source_target_pairs={{0,8},{4,12},{8,0},{12,4},{16,24},{20,28},{24,16},{28,20},{1,9},{5... | collective-permute-start | bytes 491528 | tf_op jit(solution)/shard_map/ppermute | solution.py:396
  13.5 0.4 collective-permute-start.6
  13.9 1.7 %collective-permute-start.3 = (bf16[240,384]{1,0:T(8,128)(2,1)S(1)}, bf16[240,384]{1,0:T(8,128)(2,1)S(1)}, u32[]{:S(2)}, u32[]{:S(2)}) collective-permute-start(bf16[240,384]{1,0:T(8,128)(2,1)S(1)} %pad_maximum_fusion), channel_id=1, source_target_pairs={{0,16},{4,20},{8,24},{12,28},{16,0},{20,4},{24,8},{28,12},{1,17},{... | collective-permute-start | bytes 552968 | tf_op jit(solution)/shard_map/ppermute | solution.py:396
  15.7 0.3 collective-permute-done.8
  16.0 0.4 shard_map.69
  16.4 1.5 %collective-permute-start.10 = (bf16[160,256]{1,0:T(8,128)(2,1)S(1)}, bf16[160,256]{1,0:T(8,128)(2,1)S(1)}, u32[]{:S(2)}, u32[]{:S(2)}) collective-permute-start(bf16[160,256]{1,0:T(8,128)(2,1)S(1)} %get-tuple-element.41), channel_id=1, source_target_pairs={{0,8},{4,12},{8,0},{12,4},{16,24},{20,28},{24,16},{28,20},{1,9},{5... | collective-permute-start | bytes 245768 | tf_op jit(solution)/shard_map/ppermute | solution.py:396
  17.9 0.9 %collective-permute-done.4.refs_5_.refs_3_ = bf16[320,256]{1,0:T(8,128)(2,1)S(1)} collective-permute-done((bf16[320,256]{1,0:T(8,128)(2,1)S(1)}, bf16[320,256]{1,0:T(8,128)(2,1)S(1)}, u32[]{:S(2)}, u32[]{:S(2)}) %collective-permute-start.4) | collective-permute-done | bytes 163872 | tf_op jit(solution)/shard_map/ppermute | solution.py:396
  18.8 0.7 %collective-permute-done.3.refs_4_ = bf16[240,384]{1,0:T(8,128)(2,1)S(1)} collective-permute-done((bf16[240,384]{1,0:T(8,128)(2,1)S(1)}, bf16[240,384]{1,0:T(8,128)(2,1)S(1)}, u32[]{:S(2)}, u32[]{:S(2)}) %collective-permute-start.3) | collective-permute-done | bytes 184352 | tf_op jit(solution)/shard_map/ppermute | solution.py:396
  19.8 2.2 %collective-permute-done.10.refs_5_.refs_3_ = bf16[160,256]{1,0:T(8,128)(2,1)S(1)} collective-permute-done((bf16[160,256]{1,0:T(8,128)(2,1)S(1)}, bf16[160,256]{1,0:T(8,128)(2,1)S(1)}, u32[]{:S(2)}, u32[]{:S(2)}) %collective-permute-start.10) | collective-permute-done | bytes 81952 | tf_op jit(solution)/shard_map/ppermute | solution.py:396
  22.0 1.5 %collective-permute-start.14 = (bf16[640,256]{1,0:T(8,128)(2,1)S(1)}, bf16[640,256]{1,0:T(8,128)(2,1)S(1)}, u32[]{:S(2)}, u32[]{:S(2)}) collective-permute-start(bf16[640,256]{1,0:T(8,128)(2,1)S(1)} %shard_map.71.refs_5_), channel_id=1, source_target_pairs={{0,8},{4,12},{8,0},{12,4},{16,24},{20,28},{24,16},{28,20},{1,9},{5... | collective-permute-start | bytes 983048 | tf_op jit(solution)/shard_map/ppermute | solution.py:396
  23.6 0.5 collective-permute-start.7
  24.1 0.5 collective-permute-start.20
  24.6 0.4 collective-permute-done.5.refs_2_
  25.2 1.3 %shard_map.70 = (bf16[320,1024]{1,0:T(8,128)(2,1)S(1)}, bf16[80,1024]{1,0:T(8,128)(2,1)S(1)}, f32[80,1024]{1,0:T(8,128)S(1)}) custom-call(bf16[768,320]{1,0:T(8,128)(2,1)S(1)} %get-tuple-element.39.refs_0_, bf16[320,256]{1,0:T(8,128)(2,1)S(1)} %get-tuple-element.40.refs_1_, bf16[320,256]{1,0:T(8,128)(2,1)S(1)} %collective-permute-done.5.refs_2_, ...), custom_call_target="tpu_custom_call" | custom-call | tf_op jit(solution)/shard_map/pallas_call | solution.py:126
  26.5 1.4 %shard_map.75 = (bf16[320,384]{1,0:T(8,128)(2,1)S(1)}, f32[320,384]{1,0:T(8,128)S(1)}, bf16[640,256]{1,0:T(8,128)(2,1)S(1)}, f32[640,256]{1,0:T(8,128)S(1)}) custom-call(bf16[320,768]{1,0:T(8,128)(2,1)S(1)} %get-tuple-element.43.refs_2_.refs_0_, bf16[320,1024]{1,0:T(8,128)(2,1)S(1)} %get-tuple-element.50.refs_1_, f32[80,1024]{1,0:T(8,128)S(1)} %get-tuple-element.51.refs_2_, ...), custom_call_target="tpu_custom_call" | custom-call | tf_op jit(solution)/shard_map/pallas_call | solution.py:126
  27.9 1.6 %collective-permute-start.21 = (bf16[320,384]{1,0:T(8,128)(2,1)S(1)}, bf16[320,384]{1,0:T(8,128)(2,1)S(1)}, u32[]{:S(2)}, u32[]{:S(2)}) collective-permute-start(bf16[320,384]{1,0:T(8,128)(2,1)S(1)} %get-tuple-element.55), channel_id=1, source_target_pairs={{0,16},{4,20},{8,24},{12,28},{16,0},{20,4},{24,8},{28,12},{1,17},{... | collective-permute-start | bytes 737288 | tf_op jit(solution)/shard_map/ppermute | solution.py:396
  29.7 0.3 collective-permute-start.15
  30.2 0.3 collective-permute-start.11
  30.5 5.6 %collective-permute-done.21.refs_1_ = bf16[320,384]{1,0:T(8,128)(2,1)S(1)} collective-permute-done((bf16[320,384]{1,0:T(8,128)(2,1)S(1)}, bf16[320,384]{1,0:T(8,128)(2,1)S(1)}, u32[]{:S(2)}, u32[]{:S(2)}) %collective-permute-start.21) | collective-permute-done | bytes 245792 | tf_op jit(solution)/shard_map/ppermute | solution.py:396
  36.2 0.4 collective-permute-start.22
  36.7 0.8 %collective-permute-done.12.refs_4_ = bf16[320,256]{1,0:T(8,128)(2,1)S(1)} collective-permute-done((bf16[320,256]{1,0:T(8,128)(2,1)S(1)}, bf16[320,256]{1,0:T(8,128)(2,1)S(1)}, u32[]{:S(2)}, u32[]{:S(2)}) %collective-permute-start.12) | collective-permute-done | bytes 163872 | tf_op jit(solution)/shard_map/ppermute | solution.py:396
  37.5 0.8 %shard_map.72 = (bf16[160,256]{1,0:T(8,128)(2,1)S(1)}, f32[160,256]{1,0:T(8,128)S(1)}) custom-call(bf16[80,1024]{1,0:T(8,128)(2,1)S(1)} %get-tuple-element.42.refs_0_, bf16[320,256]{1,0:T(8,128)(2,1)S(1)} %get-tuple-element.38.refs_1_, bf16[320,256]{1,0:T(8,128)(2,1)S(1)} %collective-permute-done.11.refs_2_, ...), custom_call_target="tpu_custom_call" | custom-call | tf_op jit(solution)/shard_map/pallas_call | solution.py:126
  38.3 1.6 %collective-permute-start.16 = (bf16[160,256]{1,0:T(8,128)(2,1)S(1)}, bf16[160,256]{1,0:T(8,128)(2,1)S(1)}, u32[]{:S(2)}, u32[]{:S(2)}) collective-permute-start(bf16[160,256]{1,0:T(8,128)(2,1)S(1)} %get-tuple-element.45), channel_id=1, source_target_pairs={{0,16},{4,20},{8,24},{12,28},{16,0},{20,4},{24,8},{28,12},{1,17},{... | collective-permute-start | bytes 245768 | tf_op jit(solution)/shard_map/ppermute | solution.py:396
  40.0 0.6 collective-permute-start.25
  40.6 2.3 %collective-permute-done.16.refs_1_ = bf16[160,256]{1,0:T(8,128)(2,1)S(1)} collective-permute-done((bf16[160,256]{1,0:T(8,128)(2,1)S(1)}, bf16[160,256]{1,0:T(8,128)(2,1)S(1)}, u32[]{:S(2)}, u32[]{:S(2)}) %collective-permute-start.16) | collective-permute-done | bytes 81952 | tf_op jit(solution)/shard_map/ppermute | solution.py:396
  42.9 1.0 %collective-permute-start.17 = (bf16[160,256]{1,0:T(8,128)(2,1)S(1)}, bf16[160,256]{1,0:T(8,128)(2,1)S(1)}, u32[]{:S(2)}, u32[]{:S(2)}) collective-permute-start(bf16[160,256]{1,0:T(8,128)(2,1)S(1)} %get-tuple-element.47.refs_2_), channel_id=1, source_target_pairs={{0,1},{1,0},{2,3},{3,2},{4,5},{5,4},{6,7},{7,6},{8,9},{9,8},{10,11... | collective-permute-start | bytes 245768 | tf_op jit(solution)/shard_map/ppermute | solution.py:399
  43.9 2.3 %collective-permute-start.23 = (bf16[80,384]{1,0:T(8,128)(2,1)S(1)}, bf16[80,384]{1,0:T(8,128)(2,1)S(1)}, u32[]{:S(2)}, u32[]{:S(2)}) collective-permute-start(bf16[80,384]{1,0:T(8,128)(2,1)S(1)} %get-tuple-element.59), channel_id=1, source_target_pairs={{0,2},{1,3},{2,0},{3,1},{4,6},{5,7},{6,4},{7,5},{8,10},{9,11},{10,... | collective-permute-start | bytes 184328 | tf_op jit(solution)/shard_map/ppermute | solution.py:399
  46.2 1.9 %collective-permute-done.17.refs_1_ = bf16[160,256]{1,0:T(8,128)(2,1)S(1)} collective-permute-done((bf16[160,256]{1,0:T(8,128)(2,1)S(1)}, bf16[160,256]{1,0:T(8,128)(2,1)S(1)}, u32[]{:S(2)}, u32[]{:S(2)}) %collective-permute-start.17) | collective-permute-done | bytes 81952 | tf_op jit(solution)/shard_map/ppermute | solution.py:399
  48.1 1.4 %collective-permute-start.18 = (bf16[160,256]{1,0:T(8,128)(2,1)S(1)}, bf16[160,256]{1,0:T(8,128)(2,1)S(1)}, u32[]{:S(2)}, u32[]{:S(2)}) collective-permute-start(bf16[160,256]{1,0:T(8,128)(2,1)S(1)} %get-tuple-element.49), channel_id=1, source_target_pairs={{0,2},{1,3},{2,0},{3,1},{4,6},{5,7},{6,4},{7,5},{8,10},{9,11},{10,... | collective-permute-start | bytes 245768 | tf_op jit(solution)/shard_map/ppermute | solution.py:399
  49.5 0.6 collective-permute-start.26
  50.1 1.5 %collective-permute-start.27 = (bf16[80,384]{1,0:T(8,128)(2,1)S(1)}, bf16[80,384]{1,0:T(8,128)(2,1)S(1)}, u32[]{:S(2)}, u32[]{:S(2)}) collective-permute-start(bf16[80,384]{1,0:T(8,128)(2,1)S(1)} %shard_map.79.refs_2_), channel_id=1, source_target_pairs={{0,16},{4,20},{8,24},{12,28},{16,0},{20,4},{24,8},{28,12},{1,17},{... | collective-permute-start | bytes 184328 | tf_op jit(solution)/shard_map/ppermute | solution.py:396
  51.6 1.4 %collective-permute-start.28 = (bf16[80,384]{1,0:T(8,128)(2,1)S(1)}, bf16[80,384]{1,0:T(8,128)(2,1)S(1)}, u32[]{:S(2)}, u32[]{:S(2)}) collective-permute-start(bf16[80,384]{1,0:T(8,128)(2,1)S(1)} %shard_map.79.refs_2_), channel_id=1, source_target_pairs={{0,24},{4,28},{8,16},{12,20},{16,8},{20,12},{24,0},{28,4},{1,25},{... | collective-permute-start | bytes 184328 | tf_op jit(solution)/shard_map/ppermute | solution.py:396
  53.0 0.7 %collective-permute-done.26.refs_3_ = bf16[80,384]{1,0:T(8,128)(2,1)S(1)} collective-permute-done((bf16[80,384]{1,0:T(8,128)(2,1)S(1)}, bf16[80,384]{1,0:T(8,128)(2,1)S(1)}, u32[]{:S(2)}, u32[]{:S(2)}) %collective-permute-start.26) | collective-permute-done | bytes 61472 | tf_op jit(solution)/shard_map/ppermute | solution.py:396
  53.8 0.5 collective-permute-done.27.refs_4_
  54.3 2.4 %collective-permute-done.28.refs_5_ = bf16[80,384]{1,0:T(8,128)(2,1)S(1)} collective-permute-done((bf16[80,384]{1,0:T(8,128)(2,1)S(1)}, bf16[80,384]{1,0:T(8,128)(2,1)S(1)}, u32[]{:S(2)}, u32[]{:S(2)}) %collective-permute-start.28) | collective-permute-done | bytes 61472 | tf_op jit(solution)/shard_map/ppermute | solution.py:396
  56.9 1.5 %collective-permute-start.30 = (bf16[160,256]{1,0:T(8,128)(2,1)S(1)}, bf16[160,256]{1,0:T(8,128)(2,1)S(1)}, u32[]{:S(2)}, u32[]{:S(2)}) collective-permute-start(bf16[160,256]{1,0:T(8,128)(2,1)S(1)} %get-tuple-element.67.refs_0_), channel_id=1, source_target_pairs={{0,8},{4,12},{8,0},{12,4},{16,24},{20,28},{24,16},{28,20},{1,9},{5... | collective-permute-start | bytes 245768 | tf_op jit(solution)/shard_map/ppermute | solution.py:396
  58.4 0.5 collective-permute-start.31
  58.9 1.5 %collective-permute-start.32 = (bf16[160,256]{1,0:T(8,128)(2,1)S(1)}, bf16[160,256]{1,0:T(8,128)(2,1)S(1)}, u32[]{:S(2)}, u32[]{:S(2)}) collective-permute-start(bf16[160,256]{1,0:T(8,128)(2,1)S(1)} %get-tuple-element.67.refs_0_), channel_id=1, source_target_pairs={{0,24},{4,28},{8,16},{12,20},{16,8},{20,12},{24,0},{28,4},{1,25},{... | collective-permute-start | bytes 245768 | tf_op jit(solution)/shard_map/ppermute | solution.py:396
  60.4 1.7 %shard_map.81 = (f32[9,80,320]{2,1,0:T(8,128)}, bf16[256,320]{1,0:T(8,128)(2,1)}, f32[8,128]{1,0:T(8,128)S(1)}) custom-call(bf16[320,384]{1,0:T(8,128)(2,1)S(1)} %get-tuple-element.63.refs_0_, bf16[320,384]{1,0:T(8,128)(2,1)S(1)} %collective-permute-done.29.refs_1_, f32[320,256]{1,0:T(8,128)S(1)} %get-tuple-element.64.refs_2_, ...), custom_call_target="tpu_custom_call" | custom-call | tf_op jit(solution)/shard_map/pallas_call | solution.py:126
  62.2 2.5 %collective-permute-done.31.refs_2_ = bf16[160,256]{1,0:T(8,128)(2,1)S(1)} collective-permute-done((bf16[160,256]{1,0:T(8,128)(2,1)S(1)}, bf16[160,256]{1,0:T(8,128)(2,1)S(1)}, u32[]{:S(2)}, u32[]{:S(2)}) %collective-permute-start.31) | collective-permute-done | bytes 81952 | tf_op jit(solution)/shard_map/ppermute | solution.py:396
  64.8 1.6 %collective-permute-done.33.refs_1_ = bf16[640,256]{1,0:T(8,128)(2,1)S(1)} collective-permute-done((bf16[640,256]{1,0:T(8,128)(2,1)S(1)}, bf16[640,256]{1,0:T(8,128)(2,1)S(1)}, u32[]{:S(2)}, u32[]{:S(2)}) %collective-permute-start.33) | collective-permute-done | bytes 327712 | tf_op jit(solution)/shard_map/ppermute | solution.py:396
  66.4 1.6 %shard_map.83 = f32[3,320,320]{2,1,0:T(8,128)} custom-call(bf16[640,256]{1,0:T(8,128)(2,1)S(1)} %shard_map.82.refs_0_, bf16[640,256]{1,0:T(8,128)(2,1)S(1)} %collective-permute-done.33.refs_1_), custom_call_target="tpu_custom_call" | custom-call | tf_op jit(solution)/shard_map/pallas_call | solution.py:126
  (44 shorter events, 1.5 us)
Async XLA Ops:
  0.6 15.3 %copy-start.1 = (bf16[3,320,320]{2,1,0:T(8,128)(2,1)S(1)}, bf16[3,320,320]{2,1,0:T(8,128)(2,1)}, u32[]{:S(2)}) copy-start(bf16[3,320,320]{2,1,0:T(8,128)(2,1)} %refs_3_.1) | copy-start | bytes 1843204
  2.1 9.7 %collective-permute-start = (bf16[80,384]{1,0:T(8,128)(2,1)S(1)}, bf16[80,384]{1,0:T(8,128)(2,1)S(1)}, u32[]{:S(2)}, u32[]{:S(2)}) collective-permute-start(bf16[80,384]{1,0:T(8,128)(2,1)S(1)} %get-tuple-element.37), channel_id=1, source_target_pairs={{0,1},{1,2},{2,3},{3,0},{4,5},{5,6},{6,7},{7,4},{8,9},{9,10},{10,1... | collective-permute-start | bytes 184328 | tf_op jit(solution)/shard_map/ppermute | solution.py:402
  5.2 8.3 %collective-permute-start.1 = (bf16[80,384]{1,0:T(8,128)(2,1)S(1)}, bf16[80,384]{1,0:T(8,128)(2,1)S(1)}, u32[]{:S(2)}, u32[]{:S(2)}) collective-permute-start(bf16[80,384]{1,0:T(8,128)(2,1)S(1)} %get-tuple-element.37), channel_id=1, source_target_pairs={{0,2},{1,3},{2,0},{3,1},{4,6},{5,7},{6,4},{7,5},{8,10},{9,11},{10,... | collective-permute-start | bytes 184328 | tf_op jit(solution)/shard_map/ppermute | solution.py:402
  7.8 6.1 %collective-permute-start.2 = (bf16[80,384]{1,0:T(8,128)(2,1)S(1)}, bf16[80,384]{1,0:T(8,128)(2,1)S(1)}, u32[]{:S(2)}, u32[]{:S(2)}) collective-permute-start(bf16[80,384]{1,0:T(8,128)(2,1)S(1)} %get-tuple-element.37), channel_id=1, source_target_pairs={{0,3},{1,0},{2,1},{3,2},{4,7},{5,4},{6,5},{7,6},{8,11},{9,8},{10,9... | collective-permute-start | bytes 184328 | tf_op jit(solution)/shard_map/ppermute | solution.py:402
  9.1 6.5 %collective-permute-start.9 = (bf16[320,256]{1,0:T(8,128)(2,1)S(1)}, bf16[320,256]{1,0:T(8,128)(2,1)S(1)}, u32[]{:S(2)}, u32[]{:S(2)}) collective-permute-start(bf16[320,256]{1,0:T(8,128)(2,1)S(1)} %get-tuple-element.38.refs_1_), channel_id=1, source_target_pairs={{0,0},{1,2},{2,1},{3,3},{4,4},{5,6},{6,5},{7,7},{8,8},{9,10},{10,9... | collective-permute-start | bytes 491528 | tf_op jit(solution)/shard_map/ppermute | solution.py:411
  9.8 6.1 %collective-permute-start.8 = (bf16[320,256]{1,0:T(8,128)(2,1)S(1)}, bf16[320,256]{1,0:T(8,128)(2,1)S(1)}, u32[]{:S(2)}, u32[]{:S(2)}) collective-permute-start(bf16[320,256]{1,0:T(8,128)(2,1)S(1)} %get-tuple-element.38.refs_1_), channel_id=1, source_target_pairs={{0,1},{1,0},{2,3},{3,2},{4,5},{5,4},{6,7},{7,6},{8,9},{9,8},{10,11... | collective-permute-start | bytes 491528 | tf_op jit(solution)/shard_map/ppermute | solution.py:411
  11.9 7.0 %collective-permute-start.4 = (bf16[320,256]{1,0:T(8,128)(2,1)S(1)}, bf16[320,256]{1,0:T(8,128)(2,1)S(1)}, u32[]{:S(2)}, u32[]{:S(2)}) collective-permute-start(bf16[320,256]{1,0:T(8,128)(2,1)S(1)} %get-tuple-element.38.refs_1_), channel_id=1, source_target_pairs={{0,8},{4,12},{8,0},{12,4},{16,24},{20,28},{24,16},{28,20},{1,9},{5... | collective-permute-start | bytes 491528 | tf_op jit(solution)/shard_map/ppermute | solution.py:396
  13.5 10.1 %collective-permute-start.6 = (bf16[320,256]{1,0:T(8,128)(2,1)S(1)}, bf16[320,256]{1,0:T(8,128)(2,1)S(1)}, u32[]{:S(2)}, u32[]{:S(2)}) collective-permute-start(bf16[320,256]{1,0:T(8,128)(2,1)S(1)} %get-tuple-element.40.refs_1_), channel_id=1, source_target_pairs={{0,8},{4,12},{8,0},{12,4},{16,24},{20,28},{24,16},{28,20},{1,9},{5... | collective-permute-start | bytes 491528 | tf_op jit(solution)/shard_map/ppermute | solution.py:396
  13.9 5.6 %collective-permute-start.3 = (bf16[240,384]{1,0:T(8,128)(2,1)S(1)}, bf16[240,384]{1,0:T(8,128)(2,1)S(1)}, u32[]{:S(2)}, u32[]{:S(2)}) collective-permute-start(bf16[240,384]{1,0:T(8,128)(2,1)S(1)} %pad_maximum_fusion), channel_id=1, source_target_pairs={{0,16},{4,20},{8,24},{12,28},{16,0},{20,4},{24,8},{28,12},{1,17},{... | collective-permute-start | bytes 552968 | tf_op jit(solution)/shard_map/ppermute | solution.py:396
  16.4 5.6 %collective-permute-start.10 = (bf16[160,256]{1,0:T(8,128)(2,1)S(1)}, bf16[160,256]{1,0:T(8,128)(2,1)S(1)}, u32[]{:S(2)}, u32[]{:S(2)}) collective-permute-start(bf16[160,256]{1,0:T(8,128)(2,1)S(1)} %get-tuple-element.41), channel_id=1, source_target_pairs={{0,8},{4,12},{8,0},{12,4},{16,24},{20,28},{24,16},{28,20},{1,9},{5... | collective-permute-start | bytes 245768 | tf_op jit(solution)/shard_map/ppermute | solution.py:396
  22.0 7.7 %collective-permute-start.14 = (bf16[640,256]{1,0:T(8,128)(2,1)S(1)}, bf16[640,256]{1,0:T(8,128)(2,1)S(1)}, u32[]{:S(2)}, u32[]{:S(2)}) collective-permute-start(bf16[640,256]{1,0:T(8,128)(2,1)S(1)} %shard_map.71.refs_5_), channel_id=1, source_target_pairs={{0,8},{4,12},{8,0},{12,4},{16,24},{20,28},{24,16},{28,20},{1,9},{5... | collective-permute-start | bytes 983048 | tf_op jit(solution)/shard_map/ppermute | solution.py:396
  23.6 1.4 %collective-permute-start.5 = (bf16[320,256]{1,0:T(8,128)(2,1)S(1)}, bf16[320,256]{1,0:T(8,128)(2,1)S(1)}, u32[]{:S(2)}, u32[]{:S(2)}) collective-permute-start(bf16[320,256]{1,0:T(8,128)(2,1)S(1)} %get-tuple-element.40.refs_1_), channel_id=1, source_target_pairs={{0,4},{4,0},{8,12},{12,8},{16,20},{20,16},{24,28},{28,24},{1,5},{5... | collective-permute-start | bytes 491528 | tf_op jit(solution)/shard_map/ppermute | solution.py:396
  23.6 1.6 %collective-permute-start.7 = (bf16[320,256]{1,0:T(8,128)(2,1)S(1)}, bf16[320,256]{1,0:T(8,128)(2,1)S(1)}, u32[]{:S(2)}, u32[]{:S(2)}) collective-permute-start(bf16[320,256]{1,0:T(8,128)(2,1)S(1)} %collective-permute-done.6.refs_3_), channel_id=1, source_target_pairs={{0,4},{4,0},{8,12},{12,8},{16,20},{20,16},{24,28},{28,24},{1,5},{5... | collective-permute-start | bytes 491528 | tf_op jit(solution)/shard_map/ppermute | solution.py:396
  24.1 2.4 %collective-permute-start.19 = (bf16[80,256]{1,0:T(8,128)(2,1)S(1)}, bf16[80,256]{1,0:T(8,128)(2,1)S(1)}, u32[]{:S(2)}, u32[]{:S(2)}) collective-permute-start(bf16[80,256]{1,0:T(8,128)(2,1)S(1)} %get-tuple-element.53), channel_id=1, source_target_pairs={{0,4},{4,0},{8,12},{12,8},{16,20},{20,16},{24,28},{28,24},{1,5},{5... | collective-permute-start | bytes 122888 | tf_op jit(solution)/shard_map/ppermute | solution.py:396
  24.1 2.4 %collective-permute-start.20 = (bf16[80,256]{1,0:T(8,128)(2,1)S(1)}, bf16[80,256]{1,0:T(8,128)(2,1)S(1)}, u32[]{:S(2)}, u32[]{:S(2)}) collective-permute-start(bf16[80,256]{1,0:T(8,128)(2,1)S(1)} %slice.4), channel_id=1, source_target_pairs={{0,4},{4,0},{8,12},{12,8},{16,20},{20,16},{24,28},{28,24},{1,5},{5... | collective-permute-start | bytes 122888 | tf_op jit(solution)/shard_map/ppermute | solution.py:396
  27.9 8.2 %collective-permute-start.21 = (bf16[320,384]{1,0:T(8,128)(2,1)S(1)}, bf16[320,384]{1,0:T(8,128)(2,1)S(1)}, u32[]{:S(2)}, u32[]{:S(2)}) collective-permute-start(bf16[320,384]{1,0:T(8,128)(2,1)S(1)} %get-tuple-element.55), channel_id=1, source_target_pairs={{0,16},{4,20},{8,24},{12,28},{16,0},{20,4},{24,8},{28,12},{1,17},{... | collective-permute-start | bytes 737288 | tf_op jit(solution)/shard_map/ppermute | solution.py:396
  29.5 8.0 %collective-permute-start.13 = (bf16[640,256]{1,0:T(8,128)(2,1)S(1)}, bf16[640,256]{1,0:T(8,128)(2,1)S(1)}, u32[]{:S(2)}, u32[]{:S(2)}) collective-permute-start(bf16[640,256]{1,0:T(8,128)(2,1)S(1)} %shard_map.71.refs_5_), channel_id=1, source_target_pairs={{0,4},{4,0},{8,12},{12,8},{16,20},{20,16},{24,28},{28,24},{1,5},{5... | collective-permute-start | bytes 983048 | tf_op jit(solution)/shard_map/ppermute | solution.py:396
  29.7 7.8 %collective-permute-start.15 = (bf16[640,256]{1,0:T(8,128)(2,1)S(1)}, bf16[640,256]{1,0:T(8,128)(2,1)S(1)}, u32[]{:S(2)}, u32[]{:S(2)}) collective-permute-start(bf16[640,256]{1,0:T(8,128)(2,1)S(1)} %collective-permute-done.14.refs_7_), channel_id=1, source_target_pairs={{0,4},{4,0},{8,12},{12,8},{16,20},{20,16},{24,28},{28,24},{1,5},{5... | collective-permute-start | bytes 983048 | tf_op jit(solution)/shard_map/ppermute | solution.py:396
  30.0 9.9 %collective-permute-start.24 = (bf16[640,256]{1,0:T(8,128)(2,1)S(1)}, bf16[640,256]{1,0:T(8,128)(2,1)S(1)}, u32[]{:S(2)}, u32[]{:S(2)}) collective-permute-start(bf16[640,256]{1,0:T(8,128)(2,1)S(1)} %get-tuple-element.61), channel_id=1, source_target_pairs={{0,4},{4,0},{8,12},{12,8},{16,20},{20,16},{24,28},{28,24},{1,5},{5... | collective-permute-start | bytes 983048 | tf_op jit(solution)/shard_map/ppermute | solution.py:396
  30.2 6.0 %collective-permute-start.11 = (bf16[320,256]{1,0:T(8,128)(2,1)S(1)}, bf16[320,256]{1,0:T(8,128)(2,1)S(1)}, u32[]{:S(2)}, u32[]{:S(2)}) collective-permute-start(bf16[320,256]{1,0:T(8,128)(2,1)S(1)} %get-tuple-element.38.refs_1_), channel_id=1, source_target_pairs={{0,4},{4,0},{8,12},{12,8},{16,20},{20,16},{24,28},{28,24},{1,5},{5... | collective-permute-start | bytes 491528 | tf_op jit(solution)/shard_map/ppermute | solution.py:396
  36.1 1.4 %collective-permute-start.12 = (bf16[320,256]{1,0:T(8,128)(2,1)S(1)}, bf16[320,256]{1,0:T(8,128)(2,1)S(1)}, u32[]{:S(2)}, u32[]{:S(2)}) collective-permute-start(bf16[320,256]{1,0:T(8,128)(2,1)S(1)} %collective-permute-done.4.refs_5_.refs_3_), channel_id=1, source_target_pairs={{0,4},{4,0},{8,12},{12,8},{16,20},{20,16},{24,28},{28,24},{1,5},{5... | collective-permute-start | bytes 491528 | tf_op jit(solution)/shard_map/ppermute | solution.py:396
  36.2 7.6 %collective-permute-start.22 = (bf16[160,384]{1,0:T(8,128)(2,1)S(1)}, bf16[160,384]{1,0:T(8,128)(2,1)S(1)}, u32[]{:S(2)}, u32[]{:S(2)}) collective-permute-start(bf16[160,384]{1,0:T(8,128)(2,1)S(1)} %get-tuple-element.57), channel_id=1, source_target_pairs={{0,1},{1,0},{2,3},{3,2},{4,5},{5,4},{6,7},{7,6},{8,9},{9,8},{10,11... | collective-permute-start | bytes 368648 | tf_op jit(solution)/shard_map/ppermute | solution.py:399
  38.3 22.2 %copy-start = (bf16[1,1,16,16,320]{4,3,2,1,0:T(8,128)(2,1)S(1)}, bf16[1,1,16,16,320]{4,3,2,1,0:T(8,128)(2,1)}, u32[]{:S(2)}) copy-start(bf16[1,1,16,16,320]{4,3,2,1,0:T(8,128)(2,1)} %param.5) | copy-start | bytes 491524
  38.3 4.6 %collective-permute-start.16 = (bf16[160,256]{1,0:T(8,128)(2,1)S(1)}, bf16[160,256]{1,0:T(8,128)(2,1)S(1)}, u32[]{:S(2)}, u32[]{:S(2)}) collective-permute-start(bf16[160,256]{1,0:T(8,128)(2,1)S(1)} %get-tuple-element.45), channel_id=1, source_target_pairs={{0,16},{4,20},{8,24},{12,28},{16,0},{20,4},{24,8},{28,12},{1,17},{... | collective-permute-start | bytes 245768 | tf_op jit(solution)/shard_map/ppermute | solution.py:396
  40.0 9.5 %collective-permute-start.25 = (bf16[320,256]{1,0:T(8,128)(2,1)S(1)}, bf16[320,256]{1,0:T(8,128)(2,1)S(1)}, u32[]{:S(2)}, u32[]{:S(2)}) collective-permute-start(bf16[320,256]{1,0:T(8,128)(2,1)S(1)} %get-tuple-element.62), channel_id=1, source_target_pairs={{0,8},{4,12},{8,0},{12,4},{16,24},{20,28},{24,16},{28,20},{1,9},{5... | collective-permute-start | bytes 491528 | tf_op jit(solution)/shard_map/ppermute | solution.py:396
  42.9 5.2 %collective-permute-start.17 = (bf16[160,256]{1,0:T(8,128)(2,1)S(1)}, bf16[160,256]{1,0:T(8,128)(2,1)S(1)}, u32[]{:S(2)}, u32[]{:S(2)}) collective-permute-start(bf16[160,256]{1,0:T(8,128)(2,1)S(1)} %get-tuple-element.47.refs_2_), channel_id=1, source_target_pairs={{0,1},{1,0},{2,3},{3,2},{4,5},{5,4},{6,7},{7,6},{8,9},{9,8},{10,11... | collective-permute-start | bytes 245768 | tf_op jit(solution)/shard_map/ppermute | solution.py:399
  43.9 5.6 %collective-permute-start.23 = (bf16[80,384]{1,0:T(8,128)(2,1)S(1)}, bf16[80,384]{1,0:T(8,128)(2,1)S(1)}, u32[]{:S(2)}, u32[]{:S(2)}) collective-permute-start(bf16[80,384]{1,0:T(8,128)(2,1)S(1)} %get-tuple-element.59), channel_id=1, source_target_pairs={{0,2},{1,3},{2,0},{3,1},{4,6},{5,7},{6,4},{7,5},{8,10},{9,11},{10,... | collective-permute-start | bytes 184328 | tf_op jit(solution)/shard_map/ppermute | solution.py:399
  48.1 8.7 %collective-permute-start.18 = (bf16[160,256]{1,0:T(8,128)(2,1)S(1)}, bf16[160,256]{1,0:T(8,128)(2,1)S(1)}, u32[]{:S(2)}, u32[]{:S(2)}) collective-permute-start(bf16[160,256]{1,0:T(8,128)(2,1)S(1)} %get-tuple-element.49), channel_id=1, source_target_pairs={{0,2},{1,3},{2,0},{3,1},{4,6},{5,7},{6,4},{7,5},{8,10},{9,11},{10,... | collective-permute-start | bytes 245768 | tf_op jit(solution)/shard_map/ppermute | solution.py:399
  49.5 4.3 %collective-permute-start.26 = (bf16[80,384]{1,0:T(8,128)(2,1)S(1)}, bf16[80,384]{1,0:T(8,128)(2,1)S(1)}, u32[]{:S(2)}, u32[]{:S(2)}) collective-permute-start(bf16[80,384]{1,0:T(8,128)(2,1)S(1)} %shard_map.79.refs_2_), channel_id=1, source_target_pairs={{0,8},{4,12},{8,0},{12,4},{16,24},{20,28},{24,16},{28,20},{1,9},{5... | collective-permute-start | bytes 184328 | tf_op jit(solution)/shard_map/ppermute | solution.py:396
  50.1 4.2 %collective-permute-start.27 = (bf16[80,384]{1,0:T(8,128)(2,1)S(1)}, bf16[80,384]{1,0:T(8,128)(2,1)S(1)}, u32[]{:S(2)}, u32[]{:S(2)}) collective-permute-start(bf16[80,384]{1,0:T(8,128)(2,1)S(1)} %shard_map.79.refs_2_), channel_id=1, source_target_pairs={{0,16},{4,20},{8,24},{12,28},{16,0},{20,4},{24,8},{28,12},{1,17},{... | collective-permute-start | bytes 184328 | tf_op jit(solution)/shard_map/ppermute | solution.py:396
  51.6 5.1 %collective-permute-start.28 = (bf16[80,384]{1,0:T(8,128)(2,1)S(1)}, bf16[80,384]{1,0:T(8,128)(2,1)S(1)}, u32[]{:S(2)}, u32[]{:S(2)}) collective-permute-start(bf16[80,384]{1,0:T(8,128)(2,1)S(1)} %shard_map.79.refs_2_), channel_id=1, source_target_pairs={{0,24},{4,28},{8,16},{12,20},{16,8},{20,12},{24,0},{28,4},{1,25},{... | collective-permute-start | bytes 184328 | tf_op jit(solution)/shard_map/ppermute | solution.py:396
  56.8 3.6 %collective-permute-start.29 = (bf16[320,384]{1,0:T(8,128)(2,1)S(1)}, bf16[320,384]{1,0:T(8,128)(2,1)S(1)}, u32[]{:S(2)}, u32[]{:S(2)}) collective-permute-start(bf16[320,384]{1,0:T(8,128)(2,1)S(1)} %get-tuple-element.63.refs_0_), channel_id=1, source_target_pairs={{0,4},{4,0},{8,12},{12,8},{16,20},{20,16},{24,28},{28,24},{1,5},{5... | collective-permute-start | bytes 737288 | tf_op jit(solution)/shard_map/ppermute | solution.py:396
  56.9 5.3 %collective-permute-start.30 = (bf16[160,256]{1,0:T(8,128)(2,1)S(1)}, bf16[160,256]{1,0:T(8,128)(2,1)S(1)}, u32[]{:S(2)}, u32[]{:S(2)}) collective-permute-start(bf16[160,256]{1,0:T(8,128)(2,1)S(1)} %get-tuple-element.67.refs_0_), channel_id=1, source_target_pairs={{0,8},{4,12},{8,0},{12,4},{16,24},{20,28},{24,16},{28,20},{1,9},{5... | collective-permute-start | bytes 245768 | tf_op jit(solution)/shard_map/ppermute | solution.py:396
  58.4 6.3 %collective-permute-start.31 = (bf16[160,256]{1,0:T(8,128)(2,1)S(1)}, bf16[160,256]{1,0:T(8,128)(2,1)S(1)}, u32[]{:S(2)}, u32[]{:S(2)}) collective-permute-start(bf16[160,256]{1,0:T(8,128)(2,1)S(1)} %get-tuple-element.67.refs_0_), channel_id=1, source_target_pairs={{0,16},{4,20},{8,24},{12,28},{16,0},{20,4},{24,8},{28,12},{1,17},{... | collective-permute-start | bytes 245768 | tf_op jit(solution)/shard_map/ppermute | solution.py:396
  58.9 5.8 %collective-permute-start.32 = (bf16[160,256]{1,0:T(8,128)(2,1)S(1)}, bf16[160,256]{1,0:T(8,128)(2,1)S(1)}, u32[]{:S(2)}, u32[]{:S(2)}) collective-permute-start(bf16[160,256]{1,0:T(8,128)(2,1)S(1)} %get-tuple-element.67.refs_0_), channel_id=1, source_target_pairs={{0,24},{4,28},{8,16},{12,20},{16,8},{20,12},{24,0},{28,4},{1,25},{... | collective-permute-start | bytes 245768 | tf_op jit(solution)/shard_map/ppermute | solution.py:396
  64.7 1.7 %collective-permute-start.33 = (bf16[640,256]{1,0:T(8,128)(2,1)S(1)}, bf16[640,256]{1,0:T(8,128)(2,1)S(1)}, u32[]{:S(2)}, u32[]{:S(2)}) collective-permute-start(bf16[640,256]{1,0:T(8,128)(2,1)S(1)} %shard_map.82.refs_0_), channel_id=1, source_target_pairs={{0,4},{4,0},{8,12},{12,8},{16,20},{20,16},{24,28},{28,24},{1,5},{5... | collective-permute-start | bytes 983048 | tf_op jit(solution)/shard_map/ppermute | solution.py:396

commit v5 on v4

--- a/solution.py
+++ b/solution.py
@@ -459,16 +459,20 @@
         w_other,
         after=[pair_g],
     )
-    (halo,) = call(
-        stacked, [((2 * chans, pixels), BF16)], before, after, after=[w_all, d_pair]
-    )
     f_all, acts, slope = call(
         part(forward),
         [((chans, lanes), BF16), ((slab, lanes), BF16), ((slab, lanes), F32)],
         w_turned,
         *gathered(frame_f, pair_f),
-        after=[d_pair],
         scratch=[pltpu.VMEM((plan.cols, lanes), F32)],
+    )
+    d_core, d_last = swap(d_core, 1), swap(d_pair[slab:], 1)
+    (halo,) = call(
+        stacked,
+        [((2 * chans, pixels), BF16)],
+        before,
+        after,
+        after=[w_all, d_pair, d_core, f_all],
     )
     s_send, s_keep, f_send, f_keep = call(
         part(spatial),
@@ -482,9 +486,9 @@
         f_all,
         slope,
         d_mine,
-        swap(d_core, 1),
+        d_core,
         d_pair,
-        swap(d_pair[slab:], 1),
+        d_last,
         scratch=[pltpu.VMEM((plan.cols, lanes), BF16), pltpu.VMEM((chans, 2 * half), F32)],
     )
     time = (plan.thalf, plan.tcols)
@@ -501,9 +505,6 @@
         part(frame_half), [(frame, BF16), (frame, F32)], f_keep, swap(f_send, 1)
     )
     f_other = swap(f_half, 2)
-    t_own, t_part = call(added, [(time, F32), (time, BF16)], t_keep, swap(t_send, group))
-    t_own, t_part2 = call(added, [(time, F32), (time, BF16)], t_own, trade(t_part, 1))
-    t_got = trade(t_part2, 2)
     s_own, s_part = call(
         part(space_halves),
         [((2 * rows, half), F32), ((2 * rows, half), BF16)],
@@ -516,8 +517,12 @@
         [((rows, half), F32), ((rows, half), BF16)],
         s_own,
         trade(s_part, 1),
-        after=[t_part],
-    )
+    )
+    t_own, t_part = call(
+        added, [(time, F32), (time, BF16)], t_keep, swap(t_send, group), after=[s_own]
+    )
+    t_own, t_part = call(added, [(time, F32), (time, BF16)], t_own, trade(t_part, 1))
+    t_got = trade(t_part, 2)
     (s_sum,) = call(
         summed, [((rows, half), BF16)], s_own, trade(s_part, 2), after=[f_other]
     )

time: 68.2 us -> 67.3 us (0.987)
    ppermute x25, waiting for transfers between devices: 21.2 us -> 18.8 us  [swap(): lax.ppermute(value, 'clip', [(i, i ^ distance) for i in range(plan.clips)])]
    ppermute x4, waiting for transfers between devices: 1.86 us -> 3.23 us  [trade(): return lax.ppermute(value, 'seq', [(i, i ^ distance) for i in range(seqs)])]
    ppermute x25, starting transfers between devices: 19.7 us -> 18.5 us  [swap(): lax.ppermute(value, 'clip', [(i, i ^ distance) for i in range(plan.clips)])]
  transfers between devices with their start and end apart: 34 -> 34, of which waited for: 16 -> 15; matrix products, arithmetic and copies ran while one was open for 0% -> 0% of each run, Pallas kernels for 9% -> 9%
where the time goes in v5:
time: 67.3 us; the launch traced here: 67.1 us
  starting transfers between devices  34.1 us (51%)
  waiting for transfers between devices  22.9 us (34%)
  Pallas kernels  9.23 us (14%)
  between operations  0.85 us (1%)
    ppermute x25, waiting for transfers between devices, swap(): lax.ppermute(value, 'clip', [(i, i ^ distance) for i in range(plan.clips)])  18.8 us
    ppermute x25, starting transfers between devices, swap(): lax.ppermute(value, 'clip', [(i, i ^ distance) for i in range(plan.clips)])  18.5 us
    pallas_call x16, Pallas kernels, call(): pl.pallas_call(body, out_shape=tuple((jax.ShapeDtypeStruct(shape, dtype)...  7.76 us
    ppermute x3, starting transfers between devices, turn(): lax.ppermute(value, 'seq', [(i, (i + k) % seqs) for i in range(seqs)])  7.01 us
    ppermute x4, starting transfers between devices, trade(): return lax.ppermute(value, 'seq', [(i, i ^ distance) for i in range(seqs)])  5.78 us
    ppermute x4, waiting for transfers between devices, trade(): return lax.ppermute(value, 'seq', [(i, i ^ distance) for i in range(seqs)])  3.23 us
    ppermute x2, starting transfers between devices, neighbours(): found.append(lax.ppermute(value, 'seq', list(other.items())))  2.86 us
    pallas_call x1, Pallas kernels, per_device(): pl.pallas_call(part(prepare), out_shape=tuple((jax.ShapeDtypeStruct(shape...  1.47 us
  transfers between devices with their start and end apart: 34, of which 15 were waited for; matrix products, arithmetic and copies ran while one was open for 0% of the time, Pallas kernels for 9%

profile of v5, /device:TPU:0, one launch (start us, length us, event | category | flops | bytes accessed | tf_op | source)
XLA Modules:
  0.0 67.1 jit_solution(14126469511108166126)
XLA Ops:
  0.6 1.5 %shard_map.67 = (bf16[320,256]{1,0:T(8,128)(2,1)S(1)}, bf16[320,256]{1,0:T(8,128)(2,1)S(1)}, bf16[80,768]{1,0:T(8,128)(2,1)S(1)}, bf16[80,384]{1,0:T(8,128)(2,1)S(1)}) custom-call(bf16[256,320]{1,0:T(8,128)(2,1)} %bitcast.8, bf16[256,320]{1,0:T(8,128)(2,1)} %bitcast.5, bf16[9,80,320]{2,1,0:T(8,128)(2,1)} %bitcast.7), custom_call_target="tpu_custom_call" | custom-call | tf_op jit(solution)/shard_map/pallas_call | solution.py:426
  2.1 3.1 %collective-permute-start = (bf16[80,384]{1,0:T(8,128)(2,1)S(1)}, bf16[80,384]{1,0:T(8,128)(2,1)S(1)}, u32[]{:S(2)}, u32[]{:S(2)}) collective-permute-start(bf16[80,384]{1,0:T(8,128)(2,1)S(1)} %get-tuple-element.37), channel_id=1, source_target_pairs={{0,1},{1,2},{2,3},{3,0},{4,5},{5,6},{6,7},{7,4},{8,9},{9,10},{10,1... | collective-permute-start | bytes 184328 | tf_op jit(solution)/shard_map/ppermute | solution.py:402
  5.2 2.6 %collective-permute-start.1 = (bf16[80,384]{1,0:T(8,128)(2,1)S(1)}, bf16[80,384]{1,0:T(8,128)(2,1)S(1)}, u32[]{:S(2)}, u32[]{:S(2)}) collective-permute-start(bf16[80,384]{1,0:T(8,128)(2,1)S(1)} %get-tuple-element.37), channel_id=1, source_target_pairs={{0,2},{1,3},{2,0},{3,1},{4,6},{5,7},{6,4},{7,5},{8,10},{9,11},{10,... | collective-permute-start | bytes 184328 | tf_op jit(solution)/shard_map/ppermute | solution.py:402
  7.8 1.3 %collective-permute-start.2 = (bf16[80,384]{1,0:T(8,128)(2,1)S(1)}, bf16[80,384]{1,0:T(8,128)(2,1)S(1)}, u32[]{:S(2)}, u32[]{:S(2)}) collective-permute-start(bf16[80,384]{1,0:T(8,128)(2,1)S(1)} %get-tuple-element.37), channel_id=1, source_target_pairs={{0,3},{1,0},{2,1},{3,2},{4,7},{5,4},{6,5},{7,6},{8,11},{9,8},{10,9... | collective-permute-start | bytes 184328 | tf_op jit(solution)/shard_map/ppermute | solution.py:402
  9.1 1.5 %collective-permute-start.6 = (bf16[320,256]{1,0:T(8,128)(2,1)S(1)}, bf16[320,256]{1,0:T(8,128)(2,1)S(1)}, u32[]{:S(2)}, u32[]{:S(2)}) collective-permute-start(bf16[320,256]{1,0:T(8,128)(2,1)S(1)} %get-tuple-element.40.refs_1_), channel_id=1, source_target_pairs={{0,8},{4,12},{8,0},{12,4},{16,24},{20,28},{24,16},{28,20},{1,9},{5... | collective-permute-start | bytes 491528 | tf_op jit(solution)/shard_map/ppermute | solution.py:396
  10.6 0.7 collective-permute-start.11
  11.3 2.2 %collective-permute-start.10 = (bf16[320,256]{1,0:T(8,128)(2,1)S(1)}, bf16[320,256]{1,0:T(8,128)(2,1)S(1)}, u32[]{:S(2)}, u32[]{:S(2)}) collective-permute-start(bf16[320,256]{1,0:T(8,128)(2,1)S(1)} %get-tuple-element.38.refs_1_), channel_id=1, source_target_pairs={{0,1},{1,0},{2,3},{3,2},{4,5},{5,4},{6,7},{7,6},{8,9},{9,8},{10,11... | collective-permute-start | bytes 491528 | tf_op jit(solution)/shard_map/ppermute | solution.py:411
  13.5 0.4 collective-permute-start.4
  13.9 0.5 collective-permute-done.6.refs_3_
  14.5 1.5 %collective-permute-start.3 = (bf16[240,384]{1,0:T(8,128)(2,1)S(1)}, bf16[240,384]{1,0:T(8,128)(2,1)S(1)}, u32[]{:S(2)}, u32[]{:S(2)}) collective-permute-start(bf16[240,384]{1,0:T(8,128)(2,1)S(1)} %pad_maximum_fusion), channel_id=1, source_target_pairs={{0,16},{4,20},{8,24},{12,28},{16,0},{20,4},{24,8},{28,12},{1,17},{... | collective-permute-start | bytes 552968 | tf_op jit(solution)/shard_map/ppermute | solution.py:396
  16.0 0.8 %collective-permute-done.10 = bf16[320,256]{1,0:T(8,128)(2,1)S(1)} collective-permute-done((bf16[320,256]{1,0:T(8,128)(2,1)S(1)}, bf16[320,256]{1,0:T(8,128)(2,1)S(1)}, u32[]{:S(2)}, u32[]{:S(2)}) %collective-permute-start.10) | collective-permute-done | bytes 163872 | tf_op jit(solution)/shard_map/ppermute | solution.py:411
  16.8 0.4 shard_map.70
  17.3 1.6 %collective-permute-start.12 = (bf16[160,256]{1,0:T(8,128)(2,1)S(1)}, bf16[160,256]{1,0:T(8,128)(2,1)S(1)}, u32[]{:S(2)}, u32[]{:S(2)}) collective-permute-start(bf16[160,256]{1,0:T(8,128)(2,1)S(1)} %get-tuple-element.43), channel_id=1, source_target_pairs={{0,8},{4,12},{8,0},{12,4},{16,24},{20,28},{24,16},{28,20},{1,9},{5... | collective-permute-start | bytes 245768 | tf_op jit(solution)/shard_map/ppermute | solution.py:396
  18.9 0.2 collective-permute-start.13
  19.1 2.0 %collective-permute-done.3.refs_4_ = bf16[240,384]{1,0:T(8,128)(2,1)S(1)} collective-permute-done((bf16[240,384]{1,0:T(8,128)(2,1)S(1)}, bf16[240,384]{1,0:T(8,128)(2,1)S(1)}, u32[]{:S(2)}, u32[]{:S(2)}) %collective-permute-start.3) | collective-permute-done | bytes 184352 | tf_op jit(solution)/shard_map/ppermute | solution.py:396
  21.1 0.3 shard_map.68
  21.3 1.3 %shard_map.69 = (bf16[320,1024]{1,0:T(8,128)(2,1)S(1)}, bf16[80,1024]{1,0:T(8,128)(2,1)S(1)}, f32[80,1024]{1,0:T(8,128)S(1)}) custom-call(bf16[768,320]{1,0:T(8,128)(2,1)S(1)} %get-tuple-element.39.refs_0_, bf16[320,256]{1,0:T(8,128)(2,1)S(1)} %get-tuple-element.40.refs_1_, bf16[320,256]{1,0:T(8,128)(2,1)S(1)} %collective-permute-done.5.refs_2_, ...), custom_call_target="tpu_custom_call" | custom-call | tf_op jit(solution)/shard_map/pallas_call | solution.py:126
  22.7 1.7 %collective-permute-start.15 = (bf16[640,256]{1,0:T(8,128)(2,1)S(1)}, bf16[640,256]{1,0:T(8,128)(2,1)S(1)}, u32[]{:S(2)}, u32[]{:S(2)}) collective-permute-start(bf16[640,256]{1,0:T(8,128)(2,1)S(1)} %shard_map.71.refs_5_), channel_id=1, source_target_pairs={{0,8},{4,12},{8,0},{12,4},{16,24},{20,28},{24,16},{28,20},{1,9},{5... | collective-permute-start | bytes 983048 | tf_op jit(solution)/shard_map/ppermute | solution.py:396
  24.4 1.2 %collective-permute-done.18.refs_6_ = bf16[80,256]{1,0:T(8,128)(2,1)S(1)} collective-permute-done((bf16[80,256]{1,0:T(8,128)(2,1)S(1)}, bf16[80,256]{1,0:T(8,128)(2,1)S(1)}, u32[]{:S(2)}, u32[]{:S(2)}) %collective-permute-start.18) | collective-permute-done | bytes 40992 | tf_op jit(solution)/shard_map/ppermute | solution.py:396
  25.6 1.4 %shard_map.73 = (bf16[320,384]{1,0:T(8,128)(2,1)S(1)}, f32[320,384]{1,0:T(8,128)S(1)}, bf16[640,256]{1,0:T(8,128)(2,1)S(1)}, f32[640,256]{1,0:T(8,128)S(1)}) custom-call(bf16[320,768]{1,0:T(8,128)(2,1)S(1)} %get-tuple-element.42.refs_2_.refs_0_, bf16[320,1024]{1,0:T(8,128)(2,1)S(1)} %get-tuple-element.45.refs_5_.refs_1_, ...), custom_call_target="tpu_custom_call" | custom-call | tf_op jit(solution)/shard_map/pallas_call | solution.py:126
  27.0 1.6 %collective-permute-start.19 = (bf16[320,384]{1,0:T(8,128)(2,1)S(1)}, bf16[320,384]{1,0:T(8,128)(2,1)S(1)}, u32[]{:S(2)}, u32[]{:S(2)}) collective-permute-start(bf16[320,384]{1,0:T(8,128)(2,1)S(1)} %get-tuple-element.51), channel_id=1, source_target_pairs={{0,16},{4,20},{8,24},{12,28},{16,0},{20,4},{24,8},{28,12},{1,17},{... | collective-permute-start | bytes 737288 | tf_op jit(solution)/shard_map/ppermute | solution.py:396
  28.6 3.0 %collective-permute-done.15.refs_7_ = bf16[640,256]{1,0:T(8,128)(2,1)S(1)} collective-permute-done((bf16[640,256]{1,0:T(8,128)(2,1)S(1)}, bf16[640,256]{1,0:T(8,128)(2,1)S(1)}, u32[]{:S(2)}, u32[]{:S(2)}) %collective-permute-start.15) | collective-permute-done | bytes 327712 | tf_op jit(solution)/shard_map/ppermute | solution.py:396
  31.6 0.5 collective-permute-start.24
  32.1 3.0 %collective-permute-done.19.refs_1_ = bf16[320,384]{1,0:T(8,128)(2,1)S(1)} collective-permute-done((bf16[320,384]{1,0:T(8,128)(2,1)S(1)}, bf16[320,384]{1,0:T(8,128)(2,1)S(1)}, u32[]{:S(2)}, u32[]{:S(2)}) %collective-permute-start.19) | collective-permute-done | bytes 245792 | tf_op jit(solution)/shard_map/ppermute | solution.py:396
  35.2 0.9 %collective-permute-start.20 = (bf16[160,384]{1,0:T(8,128)(2,1)S(1)}, bf16[160,384]{1,0:T(8,128)(2,1)S(1)}, u32[]{:S(2)}, u32[]{:S(2)}) collective-permute-start(bf16[160,384]{1,0:T(8,128)(2,1)S(1)} %get-tuple-element.53), channel_id=1, source_target_pairs={{0,1},{1,0},{2,3},{3,2},{4,5},{5,4},{6,7},{7,6},{8,9},{9,8},{10,11... | collective-permute-start | bytes 368648 | tf_op jit(solution)/shard_map/ppermute | solution.py:399
  36.1 0.4 collective-permute-done.9.refs_4_
  36.5 0.7 %shard_map.72 = (bf16[160,256]{1,0:T(8,128)(2,1)S(1)}, f32[160,256]{1,0:T(8,128)S(1)}) custom-call(bf16[80,1024]{1,0:T(8,128)(2,1)S(1)} %get-tuple-element.41.refs_0_, bf16[320,256]{1,0:T(8,128)(2,1)S(1)} %get-tuple-element.38.refs_1_, bf16[320,256]{1,0:T(8,128)(2,1)S(1)} %collective-permute-done.8.refs_2_, ...), custom_call_target="tpu_custom_call" | custom-call | tf_op jit(solution)/shard_map/pallas_call | solution.py:126
  37.3 1.6 %collective-permute-start.17 = (bf16[160,256]{1,0:T(8,128)(2,1)S(1)}, bf16[160,256]{1,0:T(8,128)(2,1)S(1)}, u32[]{:S(2)}, u32[]{:S(2)}) collective-permute-start(bf16[160,256]{1,0:T(8,128)(2,1)S(1)} %get-tuple-element.47), channel_id=1, source_target_pairs={{0,16},{4,20},{8,24},{12,28},{16,0},{20,4},{24,8},{28,12},{1,17},{... | collective-permute-start | bytes 245768 | tf_op jit(solution)/shard_map/ppermute | solution.py:396
  38.9 0.6 collective-permute-start.25
  39.5 1.4 %collective-permute-done.20.refs_1_ = bf16[160,384]{1,0:T(8,128)(2,1)S(1)} collective-permute-done((bf16[160,384]{1,0:T(8,128)(2,1)S(1)}, bf16[160,384]{1,0:T(8,128)(2,1)S(1)}, u32[]{:S(2)}, u32[]{:S(2)}) %collective-permute-start.20) | collective-permute-done | bytes 122912 | tf_op jit(solution)/shard_map/ppermute | solution.py:399
  41.0 0.8 %collective-permute-done.17.refs_1_ = bf16[160,256]{1,0:T(8,128)(2,1)S(1)} collective-permute-done((bf16[160,256]{1,0:T(8,128)(2,1)S(1)}, bf16[160,256]{1,0:T(8,128)(2,1)S(1)}, u32[]{:S(2)}, u32[]{:S(2)}) %collective-permute-start.17) | collective-permute-done | bytes 81952 | tf_op jit(solution)/shard_map/ppermute | solution.py:396
  41.8 1.0 %collective-permute-start.21 = (bf16[160,256]{1,0:T(8,128)(2,1)S(1)}, bf16[160,256]{1,0:T(8,128)(2,1)S(1)}, u32[]{:S(2)}, u32[]{:S(2)}) collective-permute-start(bf16[160,256]{1,0:T(8,128)(2,1)S(1)} %get-tuple-element.56), channel_id=1, source_target_pairs={{0,1},{1,0},{2,3},{3,2},{4,5},{5,4},{6,7},{7,6},{8,9},{9,8},{10,11... | collective-permute-start | bytes 245768 | tf_op jit(solution)/shard_map/ppermute | solution.py:399
  42.8 2.4 %collective-permute-start.23 = (bf16[80,384]{1,0:T(8,128)(2,1)S(1)}, bf16[80,384]{1,0:T(8,128)(2,1)S(1)}, u32[]{:S(2)}, u32[]{:S(2)}) collective-permute-start(bf16[80,384]{1,0:T(8,128)(2,1)S(1)} %get-tuple-element.59), channel_id=1, source_target_pairs={{0,2},{1,3},{2,0},{3,1},{4,6},{5,7},{6,4},{7,5},{8,10},{9,11},{10,... | collective-permute-start | bytes 184328 | tf_op jit(solution)/shard_map/ppermute | solution.py:399
  45.2 1.8 %collective-permute-done.21.refs_1_ = bf16[160,256]{1,0:T(8,128)(2,1)S(1)} collective-permute-done((bf16[160,256]{1,0:T(8,128)(2,1)S(1)}, bf16[160,256]{1,0:T(8,128)(2,1)S(1)}, u32[]{:S(2)}, u32[]{:S(2)}) %collective-permute-start.21) | collective-permute-done | bytes 81952 | tf_op jit(solution)/shard_map/ppermute | solution.py:399
  47.0 1.6 %collective-permute-start.22 = (bf16[160,256]{1,0:T(8,128)(2,1)S(1)}, bf16[160,256]{1,0:T(8,128)(2,1)S(1)}, u32[]{:S(2)}, u32[]{:S(2)}) collective-permute-start(bf16[160,256]{1,0:T(8,128)(2,1)S(1)} %get-tuple-element.58), channel_id=1, source_target_pairs={{0,2},{1,3},{2,0},{3,1},{4,6},{5,7},{6,4},{7,5},{8,10},{9,11},{10,... | collective-permute-start | bytes 245768 | tf_op jit(solution)/shard_map/ppermute | solution.py:399
  48.6 0.9 %collective-permute-start.26 = (bf16[80,384]{1,0:T(8,128)(2,1)S(1)}, bf16[80,384]{1,0:T(8,128)(2,1)S(1)}, u32[]{:S(2)}, u32[]{:S(2)}) collective-permute-start(bf16[80,384]{1,0:T(8,128)(2,1)S(1)} %shard_map.79.refs_2_), channel_id=1, source_target_pairs={{0,8},{4,12},{8,0},{12,4},{16,24},{20,28},{24,16},{28,20},{1,9},{5... | collective-permute-start | bytes 184328 | tf_op jit(solution)/shard_map/ppermute | solution.py:396
  49.5 1.5 %collective-permute-start.27 = (bf16[80,384]{1,0:T(8,128)(2,1)S(1)}, bf16[80,384]{1,0:T(8,128)(2,1)S(1)}, u32[]{:S(2)}, u32[]{:S(2)}) collective-permute-start(bf16[80,384]{1,0:T(8,128)(2,1)S(1)} %shard_map.79.refs_2_), channel_id=1, source_target_pairs={{0,16},{4,20},{8,24},{12,28},{16,0},{20,4},{24,8},{28,12},{1,17},{... | collective-permute-start | bytes 184328 | tf_op jit(solution)/shard_map/ppermute | solution.py:396
  51.0 1.1 %collective-permute-start.28 = (bf16[80,384]{1,0:T(8,128)(2,1)S(1)}, bf16[80,384]{1,0:T(8,128)(2,1)S(1)}, u32[]{:S(2)}, u32[]{:S(2)}) collective-permute-start(bf16[80,384]{1,0:T(8,128)(2,1)S(1)} %shard_map.79.refs_2_), channel_id=1, source_target_pairs={{0,24},{4,28},{8,16},{12,20},{16,8},{20,12},{24,0},{28,4},{1,25},{... | collective-permute-start | bytes 184328 | tf_op jit(solution)/shard_map/ppermute | solution.py:396
  52.1 0.7 %collective-permute-done.26.refs_3_ = bf16[80,384]{1,0:T(8,128)(2,1)S(1)} collective-permute-done((bf16[80,384]{1,0:T(8,128)(2,1)S(1)}, bf16[80,384]{1,0:T(8,128)(2,1)S(1)}, u32[]{:S(2)}, u32[]{:S(2)}) %collective-permute-start.26) | collective-permute-done | bytes 61472 | tf_op jit(solution)/shard_map/ppermute | solution.py:396
  52.9 0.8 %collective-permute-done.27.refs_4_ = bf16[80,384]{1,0:T(8,128)(2,1)S(1)} collective-permute-done((bf16[80,384]{1,0:T(8,128)(2,1)S(1)}, bf16[80,384]{1,0:T(8,128)(2,1)S(1)}, u32[]{:S(2)}, u32[]{:S(2)}) %collective-permute-start.27) | collective-permute-done | bytes 61472 | tf_op jit(solution)/shard_map/ppermute | solution.py:396
  53.7 2.4 %collective-permute-done.28.refs_5_ = bf16[80,384]{1,0:T(8,128)(2,1)S(1)} collective-permute-done((bf16[80,384]{1,0:T(8,128)(2,1)S(1)}, bf16[80,384]{1,0:T(8,128)(2,1)S(1)}, u32[]{:S(2)}, u32[]{:S(2)}) %collective-permute-start.28) | collective-permute-done | bytes 61472 | tf_op jit(solution)/shard_map/ppermute | solution.py:396
  56.3 1.3 %collective-permute-start.30 = (bf16[160,256]{1,0:T(8,128)(2,1)S(1)}, bf16[160,256]{1,0:T(8,128)(2,1)S(1)}, u32[]{:S(2)}, u32[]{:S(2)}) collective-permute-start(bf16[160,256]{1,0:T(8,128)(2,1)S(1)} %get-tuple-element.67.refs_0_), channel_id=1, source_target_pairs={{0,8},{4,12},{8,0},{12,4},{16,24},{20,28},{24,16},{28,20},{1,9},{5... | collective-permute-start | bytes 245768 | tf_op jit(solution)/shard_map/ppermute | solution.py:396
  57.5 0.5 collective-permute-start.31
  58.0 1.8 %collective-permute-start.32 = (bf16[160,256]{1,0:T(8,128)(2,1)S(1)}, bf16[160,256]{1,0:T(8,128)(2,1)S(1)}, u32[]{:S(2)}, u32[]{:S(2)}) collective-permute-start(bf16[160,256]{1,0:T(8,128)(2,1)S(1)} %get-tuple-element.67.refs_0_), channel_id=1, source_target_pairs={{0,24},{4,28},{8,16},{12,20},{16,8},{20,12},{24,0},{28,4},{1,25},{... | collective-permute-start | bytes 245768 | tf_op jit(solution)/shard_map/ppermute | solution.py:396
  59.8 1.7 %shard_map.81 = (f32[9,80,320]{2,1,0:T(8,128)}, bf16[256,320]{1,0:T(8,128)(2,1)}, f32[8,128]{1,0:T(8,128)S(1)}) custom-call(bf16[320,384]{1,0:T(8,128)(2,1)S(1)} %get-tuple-element.63.refs_0_, bf16[320,384]{1,0:T(8,128)(2,1)S(1)} %collective-permute-done.29.refs_1_, f32[320,256]{1,0:T(8,128)S(1)} %get-tuple-element.64.refs_2_, ...), custom_call_target="tpu_custom_call" | custom-call | tf_op jit(solution)/shard_map/pallas_call | solution.py:126
  61.6 2.2 %collective-permute-done.31.refs_2_ = bf16[160,256]{1,0:T(8,128)(2,1)S(1)} collective-permute-done((bf16[160,256]{1,0:T(8,128)(2,1)S(1)}, bf16[160,256]{1,0:T(8,128)(2,1)S(1)}, u32[]{:S(2)}, u32[]{:S(2)}) %collective-permute-start.31) | collective-permute-done | bytes 81952 | tf_op jit(solution)/shard_map/ppermute | solution.py:396
  63.9 1.6 %collective-permute-done.33.refs_1_ = bf16[640,256]{1,0:T(8,128)(2,1)S(1)} collective-permute-done((bf16[640,256]{1,0:T(8,128)(2,1)S(1)}, bf16[640,256]{1,0:T(8,128)(2,1)S(1)}, u32[]{:S(2)}, u32[]{:S(2)}) %collective-permute-start.33) | collective-permute-done | bytes 327712 | tf_op jit(solution)/shard_map/ppermute | solution.py:396
  65.5 1.6 %shard_map.83 = f32[3,320,320]{2,1,0:T(8,128)} custom-call(bf16[640,256]{1,0:T(8,128)(2,1)S(1)} %shard_map.82.refs_0_, bf16[640,256]{1,0:T(8,128)(2,1)S(1)} %collective-permute-done.33.refs_1_), custom_call_target="tpu_custom_call" | custom-call | tf_op jit(solution)/shard_map/pallas_call | solution.py:126
  (44 shorter events, 0.6 us)
Async XLA Ops:
  0.6 16.2 %copy-start.1 = (bf16[3,320,320]{2,1,0:T(8,128)(2,1)S(1)}, bf16[3,320,320]{2,1,0:T(8,128)(2,1)}, u32[]{:S(2)}) copy-start(bf16[3,320,320]{2,1,0:T(8,128)(2,1)} %refs_3_.1) | copy-start | bytes 1843204
  2.1 9.2 %collective-permute-start = (bf16[80,384]{1,0:T(8,128)(2,1)S(1)}, bf16[80,384]{1,0:T(8,128)(2,1)S(1)}, u32[]{:S(2)}, u32[]{:S(2)}) collective-permute-start(bf16[80,384]{1,0:T(8,128)(2,1)S(1)} %get-tuple-element.37), channel_id=1, source_target_pairs={{0,1},{1,2},{2,3},{3,0},{4,5},{5,6},{6,7},{7,4},{8,9},{9,10},{10,1... | collective-permute-start | bytes 184328 | tf_op jit(solution)/shard_map/ppermute | solution.py:402
  5.2 8.3 %collective-permute-start.1 = (bf16[80,384]{1,0:T(8,128)(2,1)S(1)}, bf16[80,384]{1,0:T(8,128)(2,1)S(1)}, u32[]{:S(2)}, u32[]{:S(2)}) collective-permute-start(bf16[80,384]{1,0:T(8,128)(2,1)S(1)} %get-tuple-element.37), channel_id=1, source_target_pairs={{0,2},{1,3},{2,0},{3,1},{4,6},{5,7},{6,4},{7,5},{8,10},{9,11},{10,... | collective-permute-start | bytes 184328 | tf_op jit(solution)/shard_map/ppermute | solution.py:402
  7.8 6.1 %collective-permute-start.2 = (bf16[80,384]{1,0:T(8,128)(2,1)S(1)}, bf16[80,384]{1,0:T(8,128)(2,1)S(1)}, u32[]{:S(2)}, u32[]{:S(2)}) collective-permute-start(bf16[80,384]{1,0:T(8,128)(2,1)S(1)} %get-tuple-element.37), channel_id=1, source_target_pairs={{0,3},{1,0},{2,1},{3,2},{4,7},{5,4},{6,5},{7,6},{8,11},{9,8},{10,9... | collective-permute-start | bytes 184328 | tf_op jit(solution)/shard_map/ppermute | solution.py:402
  9.1 5.3 %collective-permute-start.6 = (bf16[320,256]{1,0:T(8,128)(2,1)S(1)}, bf16[320,256]{1,0:T(8,128)(2,1)S(1)}, u32[]{:S(2)}, u32[]{:S(2)}) collective-permute-start(bf16[320,256]{1,0:T(8,128)(2,1)S(1)} %get-tuple-element.40.refs_1_), channel_id=1, source_target_pairs={{0,8},{4,12},{8,0},{12,4},{16,24},{20,28},{24,16},{28,20},{1,9},{5... | collective-permute-start | bytes 491528 | tf_op jit(solution)/shard_map/ppermute | solution.py:396
  10.6 5.4 %collective-permute-start.11 = (bf16[320,256]{1,0:T(8,128)(2,1)S(1)}, bf16[320,256]{1,0:T(8,128)(2,1)S(1)}, u32[]{:S(2)}, u32[]{:S(2)}) collective-permute-start(bf16[320,256]{1,0:T(8,128)(2,1)S(1)} %get-tuple-element.38.refs_1_), channel_id=1, source_target_pairs={{0,0},{1,2},{2,1},{3,3},{4,4},{5,6},{6,5},{7,7},{8,8},{9,10},{10,9... | collective-permute-start | bytes 491528 | tf_op jit(solution)/shard_map/ppermute | solution.py:411
  11.3 5.5 %collective-permute-start.10 = (bf16[320,256]{1,0:T(8,128)(2,1)S(1)}, bf16[320,256]{1,0:T(8,128)(2,1)S(1)}, u32[]{:S(2)}, u32[]{:S(2)}) collective-permute-start(bf16[320,256]{1,0:T(8,128)(2,1)S(1)} %get-tuple-element.38.refs_1_), channel_id=1, source_target_pairs={{0,1},{1,0},{2,3},{3,2},{4,5},{5,4},{6,7},{7,6},{8,9},{9,8},{10,11... | collective-permute-start | bytes 491528 | tf_op jit(solution)/shard_map/ppermute | solution.py:411
  13.5 5.3 %collective-permute-start.4 = (bf16[320,256]{1,0:T(8,128)(2,1)S(1)}, bf16[320,256]{1,0:T(8,128)(2,1)S(1)}, u32[]{:S(2)}, u32[]{:S(2)}) collective-permute-start(bf16[320,256]{1,0:T(8,128)(2,1)S(1)} %get-tuple-element.38.refs_1_), channel_id=1, source_target_pairs={{0,8},{4,12},{8,0},{12,4},{16,24},{20,28},{24,16},{28,20},{1,9},{5... | collective-permute-start | bytes 491528 | tf_op jit(solution)/shard_map/ppermute | solution.py:396
  13.9 7.4 %collective-permute-start.5 = (bf16[320,256]{1,0:T(8,128)(2,1)S(1)}, bf16[320,256]{1,0:T(8,128)(2,1)S(1)}, u32[]{:S(2)}, u32[]{:S(2)}) collective-permute-start(bf16[320,256]{1,0:T(8,128)(2,1)S(1)} %get-tuple-element.40.refs_1_), channel_id=1, source_target_pairs={{0,4},{4,0},{8,12},{12,8},{16,20},{20,16},{24,28},{28,24},{1,5},{5... | collective-permute-start | bytes 491528 | tf_op jit(solution)/shard_map/ppermute | solution.py:396
  14.5 6.6 %collective-permute-start.3 = (bf16[240,384]{1,0:T(8,128)(2,1)S(1)}, bf16[240,384]{1,0:T(8,128)(2,1)S(1)}, u32[]{:S(2)}, u32[]{:S(2)}) collective-permute-start(bf16[240,384]{1,0:T(8,128)(2,1)S(1)} %pad_maximum_fusion), channel_id=1, source_target_pairs={{0,16},{4,20},{8,24},{12,28},{16,0},{20,4},{24,8},{28,12},{1,17},{... | collective-permute-start | bytes 552968 | tf_op jit(solution)/shard_map/ppermute | solution.py:396
  16.0 5.4 %collective-permute-start.7 = (bf16[320,256]{1,0:T(8,128)(2,1)S(1)}, bf16[320,256]{1,0:T(8,128)(2,1)S(1)}, u32[]{:S(2)}, u32[]{:S(2)}) collective-permute-start(bf16[320,256]{1,0:T(8,128)(2,1)S(1)} %collective-permute-done.6.refs_3_), channel_id=1, source_target_pairs={{0,4},{4,0},{8,12},{12,8},{16,20},{20,16},{24,28},{28,24},{1,5},{5... | collective-permute-start | bytes 491528 | tf_op jit(solution)/shard_map/ppermute | solution.py:396
  17.3 5.4 %collective-permute-start.12 = (bf16[160,256]{1,0:T(8,128)(2,1)S(1)}, bf16[160,256]{1,0:T(8,128)(2,1)S(1)}, u32[]{:S(2)}, u32[]{:S(2)}) collective-permute-start(bf16[160,256]{1,0:T(8,128)(2,1)S(1)} %get-tuple-element.43), channel_id=1, source_target_pairs={{0,8},{4,12},{8,0},{12,4},{16,24},{20,28},{24,16},{28,20},{1,9},{5... | collective-permute-start | bytes 245768 | tf_op jit(solution)/shard_map/ppermute | solution.py:396
  18.9 3.8 %collective-permute-start.13 = (bf16[80,256]{1,0:T(8,128)(2,1)S(1)}, bf16[80,256]{1,0:T(8,128)(2,1)S(1)}, u32[]{:S(2)}, u32[]{:S(2)}) collective-permute-start(bf16[80,256]{1,0:T(8,128)(2,1)S(1)} %get-tuple-element.44), channel_id=1, source_target_pairs={{0,4},{4,0},{8,12},{12,8},{16,20},{20,16},{24,28},{28,24},{1,5},{5... | collective-permute-start | bytes 122888 | tf_op jit(solution)/shard_map/ppermute | solution.py:396
  22.7 8.9 %collective-permute-start.15 = (bf16[640,256]{1,0:T(8,128)(2,1)S(1)}, bf16[640,256]{1,0:T(8,128)(2,1)S(1)}, u32[]{:S(2)}, u32[]{:S(2)}) collective-permute-start(bf16[640,256]{1,0:T(8,128)(2,1)S(1)} %shard_map.71.refs_5_), channel_id=1, source_target_pairs={{0,8},{4,12},{8,0},{12,4},{16,24},{20,28},{24,16},{28,20},{1,9},{5... | collective-permute-start | bytes 983048 | tf_op jit(solution)/shard_map/ppermute | solution.py:396
  24.4 1.2 %collective-permute-start.18 = (bf16[80,256]{1,0:T(8,128)(2,1)S(1)}, bf16[80,256]{1,0:T(8,128)(2,1)S(1)}, u32[]{:S(2)}, u32[]{:S(2)}) collective-permute-start(bf16[80,256]{1,0:T(8,128)(2,1)S(1)} %slice.4), channel_id=1, source_target_pairs={{0,4},{4,0},{8,12},{12,8},{16,20},{20,16},{24,28},{28,24},{1,5},{5... | collective-permute-start | bytes 122888 | tf_op jit(solution)/shard_map/ppermute | solution.py:396
  27.0 8.1 %collective-permute-start.19 = (bf16[320,384]{1,0:T(8,128)(2,1)S(1)}, bf16[320,384]{1,0:T(8,128)(2,1)S(1)}, u32[]{:S(2)}, u32[]{:S(2)}) collective-permute-start(bf16[320,384]{1,0:T(8,128)(2,1)S(1)} %get-tuple-element.51), channel_id=1, source_target_pairs={{0,16},{4,20},{8,24},{12,28},{16,0},{20,4},{24,8},{28,12},{1,17},{... | collective-permute-start | bytes 737288 | tf_op jit(solution)/shard_map/ppermute | solution.py:396
  28.6 7.9 %collective-permute-start.14 = (bf16[640,256]{1,0:T(8,128)(2,1)S(1)}, bf16[640,256]{1,0:T(8,128)(2,1)S(1)}, u32[]{:S(2)}, u32[]{:S(2)}) collective-permute-start(bf16[640,256]{1,0:T(8,128)(2,1)S(1)} %shard_map.71.refs_5_), channel_id=1, source_target_pairs={{0,4},{4,0},{8,12},{12,8},{16,20},{20,16},{24,28},{28,24},{1,5},{5... | collective-permute-start | bytes 983048 | tf_op jit(solution)/shard_map/ppermute | solution.py:396
  31.6 4.9 %collective-permute-start.16 = (bf16[640,256]{1,0:T(8,128)(2,1)S(1)}, bf16[640,256]{1,0:T(8,128)(2,1)S(1)}, u32[]{:S(2)}, u32[]{:S(2)}) collective-permute-start(bf16[640,256]{1,0:T(8,128)(2,1)S(1)} %collective-permute-done.15.refs_7_), channel_id=1, source_target_pairs={{0,4},{4,0},{8,12},{12,8},{16,20},{20,16},{24,28},{28,24},{1,5},{5... | collective-permute-start | bytes 983048 | tf_op jit(solution)/shard_map/ppermute | solution.py:396
  31.6 7.3 %collective-permute-start.24 = (bf16[640,256]{1,0:T(8,128)(2,1)S(1)}, bf16[640,256]{1,0:T(8,128)(2,1)S(1)}, u32[]{:S(2)}, u32[]{:S(2)}) collective-permute-start(bf16[640,256]{1,0:T(8,128)(2,1)S(1)} %get-tuple-element.61), channel_id=1, source_target_pairs={{0,4},{4,0},{8,12},{12,8},{16,20},{20,16},{24,28},{28,24},{1,5},{5... | collective-permute-start | bytes 983048 | tf_op jit(solution)/shard_map/ppermute | solution.py:396
  32.1 3.1 %collective-permute-start.8 = (bf16[320,256]{1,0:T(8,128)(2,1)S(1)}, bf16[320,256]{1,0:T(8,128)(2,1)S(1)}, u32[]{:S(2)}, u32[]{:S(2)}) collective-permute-start(bf16[320,256]{1,0:T(8,128)(2,1)S(1)} %get-tuple-element.38.refs_1_), channel_id=1, source_target_pairs={{0,4},{4,0},{8,12},{12,8},{16,20},{20,16},{24,28},{28,24},{1,5},{5... | collective-permute-start | bytes 491528 | tf_op jit(solution)/shard_map/ppermute | solution.py:396
  35.1 1.4 %collective-permute-start.9 = (bf16[320,256]{1,0:T(8,128)(2,1)S(1)}, bf16[320,256]{1,0:T(8,128)(2,1)S(1)}, u32[]{:S(2)}, u32[]{:S(2)}) collective-permute-start(bf16[320,256]{1,0:T(8,128)(2,1)S(1)} %collective-permute-done.4.refs_5_.refs_3_), channel_id=1, source_target_pairs={{0,4},{4,0},{8,12},{12,8},{16,20},{20,16},{24,28},{28,24},{1,5},{5... | collective-permute-start | bytes 491528 | tf_op jit(solution)/shard_map/ppermute | solution.py:396
  35.2 5.8 %collective-permute-start.20 = (bf16[160,384]{1,0:T(8,128)(2,1)S(1)}, bf16[160,384]{1,0:T(8,128)(2,1)S(1)}, u32[]{:S(2)}, u32[]{:S(2)}) collective-permute-start(bf16[160,384]{1,0:T(8,128)(2,1)S(1)} %get-tuple-element.53), channel_id=1, source_target_pairs={{0,1},{1,0},{2,3},{3,2},{4,5},{5,4},{6,7},{7,6},{8,9},{9,8},{10,11... | collective-permute-start | bytes 368648 | tf_op jit(solution)/shard_map/ppermute | solution.py:399
  37.2 22.6 %copy-start = (bf16[1,1,16,16,320]{4,3,2,1,0:T(8,128)(2,1)S(1)}, bf16[1,1,16,16,320]{4,3,2,1,0:T(8,128)(2,1)}, u32[]{:S(2)}) copy-start(bf16[1,1,16,16,320]{4,3,2,1,0:T(8,128)(2,1)} %param.5) | copy-start | bytes 491524
  37.3 4.6 %collective-permute-start.17 = (bf16[160,256]{1,0:T(8,128)(2,1)S(1)}, bf16[160,256]{1,0:T(8,128)(2,1)S(1)}, u32[]{:S(2)}, u32[]{:S(2)}) collective-permute-start(bf16[160,256]{1,0:T(8,128)(2,1)S(1)} %get-tuple-element.47), channel_id=1, source_target_pairs={{0,16},{4,20},{8,24},{12,28},{16,0},{20,4},{24,8},{28,12},{1,17},{... | collective-permute-start | bytes 245768 | tf_op jit(solution)/shard_map/ppermute | solution.py:396
  38.9 9.6 %collective-permute-start.25 = (bf16[320,256]{1,0:T(8,128)(2,1)S(1)}, bf16[320,256]{1,0:T(8,128)(2,1)S(1)}, u32[]{:S(2)}, u32[]{:S(2)}) collective-permute-start(bf16[320,256]{1,0:T(8,128)(2,1)S(1)} %get-tuple-element.62), channel_id=1, source_target_pairs={{0,8},{4,12},{8,0},{12,4},{16,24},{20,28},{24,16},{28,20},{1,9},{5... | collective-permute-start | bytes 491528 | tf_op jit(solution)/shard_map/ppermute | solution.py:396
  41.8 5.1 %collective-permute-start.21 = (bf16[160,256]{1,0:T(8,128)(2,1)S(1)}, bf16[160,256]{1,0:T(8,128)(2,1)S(1)}, u32[]{:S(2)}, u32[]{:S(2)}) collective-permute-start(bf16[160,256]{1,0:T(8,128)(2,1)S(1)} %get-tuple-element.56), channel_id=1, source_target_pairs={{0,1},{1,0},{2,3},{3,2},{4,5},{5,4},{6,7},{7,6},{8,9},{9,8},{10,11... | collective-permute-start | bytes 245768 | tf_op jit(solution)/shard_map/ppermute | solution.py:399
  42.8 5.8 %collective-permute-start.23 = (bf16[80,384]{1,0:T(8,128)(2,1)S(1)}, bf16[80,384]{1,0:T(8,128)(2,1)S(1)}, u32[]{:S(2)}, u32[]{:S(2)}) collective-permute-start(bf16[80,384]{1,0:T(8,128)(2,1)S(1)} %get-tuple-element.59), channel_id=1, source_target_pairs={{0,2},{1,3},{2,0},{3,1},{4,6},{5,7},{6,4},{7,5},{8,10},{9,11},{10,... | collective-permute-start | bytes 184328 | tf_op jit(solution)/shard_map/ppermute | solution.py:399
  47.0 9.2 %collective-permute-start.22 = (bf16[160,256]{1,0:T(8,128)(2,1)S(1)}, bf16[160,256]{1,0:T(8,128)(2,1)S(1)}, u32[]{:S(2)}, u32[]{:S(2)}) collective-permute-start(bf16[160,256]{1,0:T(8,128)(2,1)S(1)} %get-tuple-element.58), channel_id=1, source_target_pairs={{0,2},{1,3},{2,0},{3,1},{4,6},{5,7},{6,4},{7,5},{8,10},{9,11},{10,... | collective-permute-start | bytes 245768 | tf_op jit(solution)/shard_map/ppermute | solution.py:399
  48.6 4.3 %collective-permute-start.26 = (bf16[80,384]{1,0:T(8,128)(2,1)S(1)}, bf16[80,384]{1,0:T(8,128)(2,1)S(1)}, u32[]{:S(2)}, u32[]{:S(2)}) collective-permute-start(bf16[80,384]{1,0:T(8,128)(2,1)S(1)} %shard_map.79.refs_2_), channel_id=1, source_target_pairs={{0,8},{4,12},{8,0},{12,4},{16,24},{20,28},{24,16},{28,20},{1,9},{5... | collective-permute-start | bytes 184328 | tf_op jit(solution)/shard_map/ppermute | solution.py:396
  49.5 4.2 %collective-permute-start.27 = (bf16[80,384]{1,0:T(8,128)(2,1)S(1)}, bf16[80,384]{1,0:T(8,128)(2,1)S(1)}, u32[]{:S(2)}, u32[]{:S(2)}) collective-permute-start(bf16[80,384]{1,0:T(8,128)(2,1)S(1)} %shard_map.79.refs_2_), channel_id=1, source_target_pairs={{0,16},{4,20},{8,24},{12,28},{16,0},{20,4},{24,8},{28,12},{1,17},{... | collective-permute-start | bytes 184328 | tf_op jit(solution)/shard_map/ppermute | solution.py:396
  51.0 5.1 %collective-permute-start.28 = (bf16[80,384]{1,0:T(8,128)(2,1)S(1)}, bf16[80,384]{1,0:T(8,128)(2,1)S(1)}, u32[]{:S(2)}, u32[]{:S(2)}) collective-permute-start(bf16[80,384]{1,0:T(8,128)(2,1)S(1)} %shard_map.79.refs_2_), channel_id=1, source_target_pairs={{0,24},{4,28},{8,16},{12,20},{16,8},{20,12},{24,0},{28,4},{1,25},{... | collective-permute-start | bytes 184328 | tf_op jit(solution)/shard_map/ppermute | solution.py:396
  56.2 3.6 %collective-permute-start.29 = (bf16[320,384]{1,0:T(8,128)(2,1)S(1)}, bf16[320,384]{1,0:T(8,128)(2,1)S(1)}, u32[]{:S(2)}, u32[]{:S(2)}) collective-permute-start(bf16[320,384]{1,0:T(8,128)(2,1)S(1)} %get-tuple-element.63.refs_0_), channel_id=1, source_target_pairs={{0,4},{4,0},{8,12},{12,8},{16,20},{20,16},{24,28},{28,24},{1,5},{5... | collective-permute-start | bytes 737288 | tf_op jit(solution)/shard_map/ppermute | solution.py:396
  56.3 5.3 %collective-permute-start.30 = (bf16[160,256]{1,0:T(8,128)(2,1)S(1)}, bf16[160,256]{1,0:T(8,128)(2,1)S(1)}, u32[]{:S(2)}, u32[]{:S(2)}) collective-permute-start(bf16[160,256]{1,0:T(8,128)(2,1)S(1)} %get-tuple-element.67.refs_0_), channel_id=1, source_target_pairs={{0,8},{4,12},{8,0},{12,4},{16,24},{20,28},{24,16},{28,20},{1,9},{5... | collective-permute-start | bytes 245768 | tf_op jit(solution)/shard_map/ppermute | solution.py:396
  57.5 6.3 %collective-permute-start.31 = (bf16[160,256]{1,0:T(8,128)(2,1)S(1)}, bf16[160,256]{1,0:T(8,128)(2,1)S(1)}, u32[]{:S(2)}, u32[]{:S(2)}) collective-permute-start(bf16[160,256]{1,0:T(8,128)(2,1)S(1)} %get-tuple-element.67.refs_0_), channel_id=1, source_target_pairs={{0,16},{4,20},{8,24},{12,28},{16,0},{20,4},{24,8},{28,12},{1,17},{... | collective-permute-start | bytes 245768 | tf_op jit(solution)/shard_map/ppermute | solution.py:396
  58.0 5.8 %collective-permute-start.32 = (bf16[160,256]{1,0:T(8,128)(2,1)S(1)}, bf16[160,256]{1,0:T(8,128)(2,1)S(1)}, u32[]{:S(2)}, u32[]{:S(2)}) collective-permute-start(bf16[160,256]{1,0:T(8,128)(2,1)S(1)} %get-tuple-element.67.refs_0_), channel_id=1, source_target_pairs={{0,24},{4,28},{8,16},{12,20},{16,8},{20,12},{24,0},{28,4},{1,25},{... | collective-permute-start | bytes 245768 | tf_op jit(solution)/shard_map/ppermute | solution.py:396
  63.8 1.7 %collective-permute-start.33 = (bf16[640,256]{1,0:T(8,128)(2,1)S(1)}, bf16[640,256]{1,0:T(8,128)(2,1)S(1)}, u32[]{:S(2)}, u32[]{:S(2)}) collective-permute-start(bf16[640,256]{1,0:T(8,128)(2,1)S(1)} %shard_map.82.refs_0_), channel_id=1, source_target_pairs={{0,4},{4,0},{8,12},{12,8},{16,20},{20,16},{24,28},{28,24},{1,5},{5... | collective-permute-start | bytes 983048 | tf_op jit(solution)/shard_map/ppermute | solution.py:396

commit v6 on v5

--- a/solution.py
+++ b/solution.py
@@ -145,6 +145,7 @@
         self.half = round_up(round_up(self.cols, 2 * LANES) // 2, LANES)
         self.tcols = round_up(3 * self.slab, LANES)
         self.thalf = chans // 2
+        self.chips = (0, self.group + 2, self.group, 2)
         self.factor = 1.0 / math.sqrt(clips * seqs * self.pixels)
 
     def fits(self):
@@ -357,11 +358,11 @@
     low, high, _ = plan.place()
     group, slab, rows = plan.group, plan.slab, plan.rows
     for core, ref in enumerate((here_ref, core_ref)):
-        for chip in range(4):
-            other = high if chip < 2 else 1 - high
+        for chip, distance in enumerate(plan.chips):
+            other = high if distance < group else 1 - high
             lane = pl.multiple_of(other * plan.half, LANES)
             piece = ref[chip * rows : (chip + 1) * rows, :].astype(F32) * plan.factor
-            held[low ^ (2 * (chip % 2) + core), :, pl.ds(lane, plan.half)] = piece
+            held[low ^ (distance % group + core), :, pl.ds(lane, plan.half)] = piece
     for tap in range(9):
         out_ref[tap] = jnp.concatenate(
             [held[index, :, tap * slab : (tap + 1) * slab] for index in range(group)], axis=1
@@ -378,8 +379,10 @@
     far = pl.ds(pl.multiple_of((1 - high) * size, 16), size)
     for core, ref in enumerate((here_ref, core_ref)):
         for pair in range(2):
-            held[near, :] = ref[pair * size : (pair + 1) * size, :].astype(F32)
-            held[far, :] = ref[(2 + pair) * size : (3 + pair) * size, :].astype(F32)
+            first = plan.chips.index(2 * pair) * size
+            second = plan.chips.index(plan.group + 2 * pair) * size
+            held[near, :] = ref[first : first + size, :].astype(F32)
+            held[far, :] = ref[second : second + size, :].astype(F32)
             turned = held[...].T * plan.factor
             for k in range(3):
                 here = pl.ds(pl.multiple_of((low ^ (2 * pair + core)) * slab, 16), slab)
@@ -417,7 +420,7 @@
         return own, swap(own, 1), pair, swap(pair, 1)
 
     def chips(value):
-        return value, swap(value, 2), swap(value, group), swap(value, group + 2)
+        return (value, *(swap(value, distance) for distance in plan.chips[1:]))
 
     clip_f, clip_g = frames.reshape(pixels, chans), cotangent.reshape(pixels, chans)
     taps = jnp.transpose(w_space, (1, 0, 2))

time: 67.3 us -> 66.4 us (0.987)
  waiting for transfers between devices: 22.9 us -> 22 us
    ppermute x25, waiting for transfers between devices: 18.8 us -> 17.9 us  [swap(): lax.ppermute(value, 'clip', [(i, i ^ distance) for i in range(plan.clips)])]
  transfers between devices with their start and end apart: 34 -> 34, of which waited for: 15 -> 17; matrix products, arithmetic and copies ran while one was open for 0% -> 0% of each run, Pallas kernels for 9% -> 9%
where the time goes in v6:
time: 66.4 us; the launch traced here: 66.2 us
  starting transfers between devices  34.1 us (51%)
  waiting for transfers between devices  22 us (33%)
  Pallas kernels  9.23 us (14%)
  between operations  0.85 us (1%)
    ppermute x25, starting transfers between devices, swap(): lax.ppermute(value, 'clip', [(i, i ^ distance) for i in range(plan.clips)])  18.5 us
    ppermute x25, waiting for transfers between devices, swap(): lax.ppermute(value, 'clip', [(i, i ^ distance) for i in range(plan.clips)])  17.9 us
    pallas_call x16, Pallas kernels, call(): pl.pallas_call(body, out_shape=tuple((jax.ShapeDtypeStruct(shape, dtype)...  7.76 us
    ppermute x3, starting transfers between devices, turn(): lax.ppermute(value, 'seq', [(i, (i + k) % seqs) for i in range(seqs)])  7.01 us
    ppermute x4, starting transfers between devices, trade(): return lax.ppermute(value, 'seq', [(i, i ^ distance) for i in range(seqs)])  5.78 us
    ppermute x4, waiting for transfers between devices, trade(): return lax.ppermute(value, 'seq', [(i, i ^ distance) for i in range(seqs)])  3.23 us
    ppermute x2, starting transfers between devices, neighbours(): found.append(lax.ppermute(value, 'seq', list(other.items())))  2.86 us
    pallas_call x1, Pallas kernels, per_device(): pl.pallas_call(part(prepare), out_shape=tuple((jax.ShapeDtypeStruct(shape...  1.47 us
  transfers between devices with their start and end apart: 34, of which 17 were waited for; matrix products, arithmetic and copies ran while one was open for 0% of the time, Pallas kernels for 9%

profile of v6, /device:TPU:0, one launch (start us, length us, event | category | flops | bytes accessed | tf_op | source)
XLA Modules:
  0.0 66.2 jit_solution(3748397863859785068)
XLA Ops:
  0.6 1.5 %shard_map.67 = (bf16[320,256]{1,0:T(8,128)(2,1)S(1)}, bf16[320,256]{1,0:T(8,128)(2,1)S(1)}, bf16[80,768]{1,0:T(8,128)(2,1)S(1)}, bf16[80,384]{1,0:T(8,128)(2,1)S(1)}) custom-call(bf16[256,320]{1,0:T(8,128)(2,1)} %bitcast.8, bf16[256,320]{1,0:T(8,128)(2,1)} %bitcast.5, bf16[9,80,320]{2,1,0:T(8,128)(2,1)} %bitcast.7), custom_call_target="tpu_custom_call" | custom-call | tf_op jit(solution)/shard_map/pallas_call | solution.py:429
  2.1 3.1 %collective-permute-start = (bf16[80,384]{1,0:T(8,128)(2,1)S(1)}, bf16[80,384]{1,0:T(8,128)(2,1)S(1)}, u32[]{:S(2)}, u32[]{:S(2)}) collective-permute-start(bf16[80,384]{1,0:T(8,128)(2,1)S(1)} %get-tuple-element.37), channel_id=1, source_target_pairs={{0,1},{1,2},{2,3},{3,0},{4,5},{5,6},{6,7},{7,4},{8,9},{9,10},{10,1... | collective-permute-start | bytes 184328 | tf_op jit(solution)/shard_map/ppermute | solution.py:405
  5.2 2.6 %collective-permute-start.1 = (bf16[80,384]{1,0:T(8,128)(2,1)S(1)}, bf16[80,384]{1,0:T(8,128)(2,1)S(1)}, u32[]{:S(2)}, u32[]{:S(2)}) collective-permute-start(bf16[80,384]{1,0:T(8,128)(2,1)S(1)} %get-tuple-element.37), channel_id=1, source_target_pairs={{0,2},{1,3},{2,0},{3,1},{4,6},{5,7},{6,4},{7,5},{8,10},{9,11},{10,... | collective-permute-start | bytes 184328 | tf_op jit(solution)/shard_map/ppermute | solution.py:405
  7.8 1.3 %collective-permute-start.2 = (bf16[80,384]{1,0:T(8,128)(2,1)S(1)}, bf16[80,384]{1,0:T(8,128)(2,1)S(1)}, u32[]{:S(2)}, u32[]{:S(2)}) collective-permute-start(bf16[80,384]{1,0:T(8,128)(2,1)S(1)} %get-tuple-element.37), channel_id=1, source_target_pairs={{0,3},{1,0},{2,1},{3,2},{4,7},{5,4},{6,5},{7,6},{8,11},{9,8},{10,9... | collective-permute-start | bytes 184328 | tf_op jit(solution)/shard_map/ppermute | solution.py:405
  9.1 1.5 %collective-permute-start.6 = (bf16[320,256]{1,0:T(8,128)(2,1)S(1)}, bf16[320,256]{1,0:T(8,128)(2,1)S(1)}, u32[]{:S(2)}, u32[]{:S(2)}) collective-permute-start(bf16[320,256]{1,0:T(8,128)(2,1)S(1)} %get-tuple-element.40.refs_1_), channel_id=1, source_target_pairs={{0,8},{4,12},{8,0},{12,4},{16,24},{20,28},{24,16},{28,20},{1,9},{5... | collective-permute-start | bytes 491528 | tf_op jit(solution)/shard_map/ppermute | solution.py:399
  10.6 0.7 collective-permute-start.11
  11.3 2.2 %collective-permute-start.10 = (bf16[320,256]{1,0:T(8,128)(2,1)S(1)}, bf16[320,256]{1,0:T(8,128)(2,1)S(1)}, u32[]{:S(2)}, u32[]{:S(2)}) collective-permute-start(bf16[320,256]{1,0:T(8,128)(2,1)S(1)} %get-tuple-element.38.refs_1_), channel_id=1, source_target_pairs={{0,1},{1,0},{2,3},{3,2},{4,5},{5,4},{6,7},{7,6},{8,9},{9,8},{10,11... | collective-permute-start | bytes 491528 | tf_op jit(solution)/shard_map/ppermute | solution.py:414
  13.5 0.4 collective-permute-start.4
  13.9 0.5 collective-permute-done.6.refs_3_
  14.5 1.5 %collective-permute-start.3 = (bf16[240,384]{1,0:T(8,128)(2,1)S(1)}, bf16[240,384]{1,0:T(8,128)(2,1)S(1)}, u32[]{:S(2)}, u32[]{:S(2)}) collective-permute-start(bf16[240,384]{1,0:T(8,128)(2,1)S(1)} %pad_maximum_fusion), channel_id=1, source_target_pairs={{0,16},{4,20},{8,24},{12,28},{16,0},{20,4},{24,8},{28,12},{1,17},{... | collective-permute-start | bytes 552968 | tf_op jit(solution)/shard_map/ppermute | solution.py:399
  16.0 0.8 %collective-permute-done.10 = bf16[320,256]{1,0:T(8,128)(2,1)S(1)} collective-permute-done((bf16[320,256]{1,0:T(8,128)(2,1)S(1)}, bf16[320,256]{1,0:T(8,128)(2,1)S(1)}, u32[]{:S(2)}, u32[]{:S(2)}) %collective-permute-start.10) | collective-permute-done | bytes 163872 | tf_op jit(solution)/shard_map/ppermute | solution.py:414
  16.8 0.4 shard_map.70
  17.3 1.6 %collective-permute-start.12 = (bf16[160,256]{1,0:T(8,128)(2,1)S(1)}, bf16[160,256]{1,0:T(8,128)(2,1)S(1)}, u32[]{:S(2)}, u32[]{:S(2)}) collective-permute-start(bf16[160,256]{1,0:T(8,128)(2,1)S(1)} %get-tuple-element.43), channel_id=1, source_target_pairs={{0,8},{4,12},{8,0},{12,4},{16,24},{20,28},{24,16},{28,20},{1,9},{5... | collective-permute-start | bytes 245768 | tf_op jit(solution)/shard_map/ppermute | solution.py:399
  19.1 2.0 %collective-permute-done.3.refs_4_ = bf16[240,384]{1,0:T(8,128)(2,1)S(1)} collective-permute-done((bf16[240,384]{1,0:T(8,128)(2,1)S(1)}, bf16[240,384]{1,0:T(8,128)(2,1)S(1)}, u32[]{:S(2)}, u32[]{:S(2)}) %collective-permute-start.3) | collective-permute-done | bytes 184352 | tf_op jit(solution)/shard_map/ppermute | solution.py:399
  21.1 0.3 shard_map.68
  21.3 1.3 %shard_map.69 = (bf16[320,1024]{1,0:T(8,128)(2,1)S(1)}, bf16[80,1024]{1,0:T(8,128)(2,1)S(1)}, f32[80,1024]{1,0:T(8,128)S(1)}) custom-call(bf16[768,320]{1,0:T(8,128)(2,1)S(1)} %get-tuple-element.39.refs_0_, bf16[320,256]{1,0:T(8,128)(2,1)S(1)} %get-tuple-element.40.refs_1_, bf16[320,256]{1,0:T(8,128)(2,1)S(1)} %collective-permute-done.5.refs_2_, ...), custom_call_target="tpu_custom_call" | custom-call | tf_op jit(solution)/shard_map/pallas_call | solution.py:126
  22.7 1.7 %collective-permute-start.15 = (bf16[640,256]{1,0:T(8,128)(2,1)S(1)}, bf16[640,256]{1,0:T(8,128)(2,1)S(1)}, u32[]{:S(2)}, u32[]{:S(2)}) collective-permute-start(bf16[640,256]{1,0:T(8,128)(2,1)S(1)} %shard_map.71.refs_5_), channel_id=1, source_target_pairs={{0,8},{4,12},{8,0},{12,4},{16,24},{20,28},{24,16},{28,20},{1,9},{5... | collective-permute-start | bytes 983048 | tf_op jit(solution)/shard_map/ppermute | solution.py:399
  24.4 1.2 %collective-permute-done.18.refs_6_ = bf16[80,256]{1,0:T(8,128)(2,1)S(1)} collective-permute-done((bf16[80,256]{1,0:T(8,128)(2,1)S(1)}, bf16[80,256]{1,0:T(8,128)(2,1)S(1)}, u32[]{:S(2)}, u32[]{:S(2)}) %collective-permute-start.18) | collective-permute-done | bytes 40992 | tf_op jit(solution)/shard_map/ppermute | solution.py:399
  25.6 1.4 %shard_map.73 = (bf16[320,384]{1,0:T(8,128)(2,1)S(1)}, f32[320,384]{1,0:T(8,128)S(1)}, bf16[640,256]{1,0:T(8,128)(2,1)S(1)}, f32[640,256]{1,0:T(8,128)S(1)}) custom-call(bf16[320,768]{1,0:T(8,128)(2,1)S(1)} %get-tuple-element.42.refs_2_.refs_0_, bf16[320,1024]{1,0:T(8,128)(2,1)S(1)} %get-tuple-element.45.refs_5_.refs_1_, ...), custom_call_target="tpu_custom_call" | custom-call | tf_op jit(solution)/shard_map/pallas_call | solution.py:126
  27.0 1.6 %collective-permute-start.19 = (bf16[320,384]{1,0:T(8,128)(2,1)S(1)}, bf16[320,384]{1,0:T(8,128)(2,1)S(1)}, u32[]{:S(2)}, u32[]{:S(2)}) collective-permute-start(bf16[320,384]{1,0:T(8,128)(2,1)S(1)} %get-tuple-element.51), channel_id=1, source_target_pairs={{0,16},{4,20},{8,24},{12,28},{16,0},{20,4},{24,8},{28,12},{1,17},{... | collective-permute-start | bytes 737288 | tf_op jit(solution)/shard_map/ppermute | solution.py:399
  28.6 3.0 %collective-permute-done.15.refs_7_ = bf16[640,256]{1,0:T(8,128)(2,1)S(1)} collective-permute-done((bf16[640,256]{1,0:T(8,128)(2,1)S(1)}, bf16[640,256]{1,0:T(8,128)(2,1)S(1)}, u32[]{:S(2)}, u32[]{:S(2)}) %collective-permute-start.15) | collective-permute-done | bytes 327712 | tf_op jit(solution)/shard_map/ppermute | solution.py:399
  31.6 0.5 collective-permute-start.24
  32.1 3.0 %collective-permute-done.19.refs_1_ = bf16[320,384]{1,0:T(8,128)(2,1)S(1)} collective-permute-done((bf16[320,384]{1,0:T(8,128)(2,1)S(1)}, bf16[320,384]{1,0:T(8,128)(2,1)S(1)}, u32[]{:S(2)}, u32[]{:S(2)}) %collective-permute-start.19) | collective-permute-done | bytes 245792 | tf_op jit(solution)/shard_map/ppermute | solution.py:399
  35.2 0.9 %collective-permute-start.20 = (bf16[160,384]{1,0:T(8,128)(2,1)S(1)}, bf16[160,384]{1,0:T(8,128)(2,1)S(1)}, u32[]{:S(2)}, u32[]{:S(2)}) collective-permute-start(bf16[160,384]{1,0:T(8,128)(2,1)S(1)} %get-tuple-element.53), channel_id=1, source_target_pairs={{0,1},{1,0},{2,3},{3,2},{4,5},{5,4},{6,7},{7,6},{8,9},{9,8},{10,11... | collective-permute-start | bytes 368648 | tf_op jit(solution)/shard_map/ppermute | solution.py:402
  36.1 0.4 collective-permute-done.9.refs_4_
  36.5 0.7 %shard_map.72 = (bf16[160,256]{1,0:T(8,128)(2,1)S(1)}, f32[160,256]{1,0:T(8,128)S(1)}) custom-call(bf16[80,1024]{1,0:T(8,128)(2,1)S(1)} %get-tuple-element.41.refs_0_, bf16[320,256]{1,0:T(8,128)(2,1)S(1)} %get-tuple-element.38.refs_1_, bf16[320,256]{1,0:T(8,128)(2,1)S(1)} %collective-permute-done.8.refs_2_, ...), custom_call_target="tpu_custom_call" | custom-call | tf_op jit(solution)/shard_map/pallas_call | solution.py:126
  37.3 1.6 %collective-permute-start.17 = (bf16[160,256]{1,0:T(8,128)(2,1)S(1)}, bf16[160,256]{1,0:T(8,128)(2,1)S(1)}, u32[]{:S(2)}, u32[]{:S(2)}) collective-permute-start(bf16[160,256]{1,0:T(8,128)(2,1)S(1)} %get-tuple-element.47), channel_id=1, source_target_pairs={{0,16},{4,20},{8,24},{12,28},{16,0},{20,4},{24,8},{28,12},{1,17},{... | collective-permute-start | bytes 245768 | tf_op jit(solution)/shard_map/ppermute | solution.py:399
  38.9 0.6 collective-permute-start.25
  39.5 1.4 %collective-permute-done.20.refs_1_ = bf16[160,384]{1,0:T(8,128)(2,1)S(1)} collective-permute-done((bf16[160,384]{1,0:T(8,128)(2,1)S(1)}, bf16[160,384]{1,0:T(8,128)(2,1)S(1)}, u32[]{:S(2)}, u32[]{:S(2)}) %collective-permute-start.20) | collective-permute-done | bytes 122912 | tf_op jit(solution)/shard_map/ppermute | solution.py:402
  41.0 0.8 %collective-permute-done.17.refs_1_ = bf16[160,256]{1,0:T(8,128)(2,1)S(1)} collective-permute-done((bf16[160,256]{1,0:T(8,128)(2,1)S(1)}, bf16[160,256]{1,0:T(8,128)(2,1)S(1)}, u32[]{:S(2)}, u32[]{:S(2)}) %collective-permute-start.17) | collective-permute-done | bytes 81952 | tf_op jit(solution)/shard_map/ppermute | solution.py:399
  41.8 1.0 %collective-permute-start.21 = (bf16[160,256]{1,0:T(8,128)(2,1)S(1)}, bf16[160,256]{1,0:T(8,128)(2,1)S(1)}, u32[]{:S(2)}, u32[]{:S(2)}) collective-permute-start(bf16[160,256]{1,0:T(8,128)(2,1)S(1)} %get-tuple-element.56), channel_id=1, source_target_pairs={{0,1},{1,0},{2,3},{3,2},{4,5},{5,4},{6,7},{7,6},{8,9},{9,8},{10,11... | collective-permute-start | bytes 245768 | tf_op jit(solution)/shard_map/ppermute | solution.py:402
  42.8 2.4 %collective-permute-start.23 = (bf16[80,384]{1,0:T(8,128)(2,1)S(1)}, bf16[80,384]{1,0:T(8,128)(2,1)S(1)}, u32[]{:S(2)}, u32[]{:S(2)}) collective-permute-start(bf16[80,384]{1,0:T(8,128)(2,1)S(1)} %get-tuple-element.59), channel_id=1, source_target_pairs={{0,2},{1,3},{2,0},{3,1},{4,6},{5,7},{6,4},{7,5},{8,10},{9,11},{10,... | collective-permute-start | bytes 184328 | tf_op jit(solution)/shard_map/ppermute | solution.py:402
  45.2 1.8 %collective-permute-done.21.refs_1_ = bf16[160,256]{1,0:T(8,128)(2,1)S(1)} collective-permute-done((bf16[160,256]{1,0:T(8,128)(2,1)S(1)}, bf16[160,256]{1,0:T(8,128)(2,1)S(1)}, u32[]{:S(2)}, u32[]{:S(2)}) %collective-permute-start.21) | collective-permute-done | bytes 81952 | tf_op jit(solution)/shard_map/ppermute | solution.py:402
  47.0 1.6 %collective-permute-start.22 = (bf16[160,256]{1,0:T(8,128)(2,1)S(1)}, bf16[160,256]{1,0:T(8,128)(2,1)S(1)}, u32[]{:S(2)}, u32[]{:S(2)}) collective-permute-start(bf16[160,256]{1,0:T(8,128)(2,1)S(1)} %get-tuple-element.58), channel_id=1, source_target_pairs={{0,2},{1,3},{2,0},{3,1},{4,6},{5,7},{6,4},{7,5},{8,10},{9,11},{10,... | collective-permute-start | bytes 245768 | tf_op jit(solution)/shard_map/ppermute | solution.py:402
  48.6 1.9 %collective-permute-start.26 = (bf16[80,384]{1,0:T(8,128)(2,1)S(1)}, bf16[80,384]{1,0:T(8,128)(2,1)S(1)}, u32[]{:S(2)}, u32[]{:S(2)}) collective-permute-start(bf16[80,384]{1,0:T(8,128)(2,1)S(1)} %shard_map.79.refs_2_), channel_id=1, source_target_pairs={{0,24},{4,28},{8,16},{12,20},{16,8},{20,12},{24,0},{28,4},{1,25},{... | collective-permute-start | bytes 184328 | tf_op jit(solution)/shard_map/ppermute | solution.py:399
  50.4 0.5 collective-permute-start.27
  50.9 1.2 %collective-permute-start.28 = (bf16[80,384]{1,0:T(8,128)(2,1)S(1)}, bf16[80,384]{1,0:T(8,128)(2,1)S(1)}, u32[]{:S(2)}, u32[]{:S(2)}) collective-permute-start(bf16[80,384]{1,0:T(8,128)(2,1)S(1)} %shard_map.79.refs_2_), channel_id=1, source_target_pairs={{0,8},{4,12},{8,0},{12,4},{16,24},{20,28},{24,16},{28,20},{1,9},{5... | collective-permute-start | bytes 184328 | tf_op jit(solution)/shard_map/ppermute | solution.py:399
  52.1 1.6 %collective-permute-done.26.refs_3_ = bf16[80,384]{1,0:T(8,128)(2,1)S(1)} collective-permute-done((bf16[80,384]{1,0:T(8,128)(2,1)S(1)}, bf16[80,384]{1,0:T(8,128)(2,1)S(1)}, u32[]{:S(2)}, u32[]{:S(2)}) %collective-permute-start.26) | collective-permute-done | bytes 61472 | tf_op jit(solution)/shard_map/ppermute | solution.py:399
  53.8 0.9 %collective-permute-done.27.refs_4_ = bf16[80,384]{1,0:T(8,128)(2,1)S(1)} collective-permute-done((bf16[80,384]{1,0:T(8,128)(2,1)S(1)}, bf16[80,384]{1,0:T(8,128)(2,1)S(1)}, u32[]{:S(2)}, u32[]{:S(2)}) %collective-permute-start.27) | collective-permute-done | bytes 61472 | tf_op jit(solution)/shard_map/ppermute | solution.py:399
  54.7 0.5 collective-permute-done.28.refs_5_
  55.3 2.2 %collective-permute-start.30 = (bf16[160,256]{1,0:T(8,128)(2,1)S(1)}, bf16[160,256]{1,0:T(8,128)(2,1)S(1)}, u32[]{:S(2)}, u32[]{:S(2)}) collective-permute-start(bf16[160,256]{1,0:T(8,128)(2,1)S(1)} %get-tuple-element.67.refs_0_), channel_id=1, source_target_pairs={{0,24},{4,28},{8,16},{12,20},{16,8},{20,12},{24,0},{28,4},{1,25},{... | collective-permute-start | bytes 245768 | tf_op jit(solution)/shard_map/ppermute | solution.py:399
  57.5 0.5 collective-permute-start.31
  58.0 0.8 %collective-permute-start.32 = (bf16[160,256]{1,0:T(8,128)(2,1)S(1)}, bf16[160,256]{1,0:T(8,128)(2,1)S(1)}, u32[]{:S(2)}, u32[]{:S(2)}) collective-permute-start(bf16[160,256]{1,0:T(8,128)(2,1)S(1)} %get-tuple-element.67.refs_0_), channel_id=1, source_target_pairs={{0,8},{4,12},{8,0},{12,4},{16,24},{20,28},{24,16},{28,20},{1,9},{5... | collective-permute-start | bytes 245768 | tf_op jit(solution)/shard_map/ppermute | solution.py:399
  58.8 1.7 %shard_map.81 = (f32[9,80,320]{2,1,0:T(8,128)}, bf16[256,320]{1,0:T(8,128)(2,1)}, f32[8,128]{1,0:T(8,128)S(1)}) custom-call(bf16[320,384]{1,0:T(8,128)(2,1)S(1)} %get-tuple-element.63.refs_0_, bf16[320,384]{1,0:T(8,128)(2,1)S(1)} %collective-permute-done.29.refs_1_, f32[320,256]{1,0:T(8,128)S(1)} %get-tuple-element.64.refs_2_, ...), custom_call_target="tpu_custom_call" | custom-call | tf_op jit(solution)/shard_map/pallas_call | solution.py:126
  60.6 0.5 collective-permute-done.30.refs_1_
  61.1 1.7 %collective-permute-done.31.refs_2_ = bf16[160,256]{1,0:T(8,128)(2,1)S(1)} collective-permute-done((bf16[160,256]{1,0:T(8,128)(2,1)S(1)}, bf16[160,256]{1,0:T(8,128)(2,1)S(1)}, u32[]{:S(2)}, u32[]{:S(2)}) %collective-permute-start.31) | collective-permute-done | bytes 81952 | tf_op jit(solution)/shard_map/ppermute | solution.py:399
  63.0 1.6 %collective-permute-done.33.refs_1_ = bf16[640,256]{1,0:T(8,128)(2,1)S(1)} collective-permute-done((bf16[640,256]{1,0:T(8,128)(2,1)S(1)}, bf16[640,256]{1,0:T(8,128)(2,1)S(1)}, u32[]{:S(2)}, u32[]{:S(2)}) %collective-permute-start.33) | collective-permute-done | bytes 327712 | tf_op jit(solution)/shard_map/ppermute | solution.py:399
  64.6 1.6 %shard_map.83 = f32[3,320,320]{2,1,0:T(8,128)} custom-call(bf16[640,256]{1,0:T(8,128)(2,1)S(1)} %shard_map.82.refs_0_, bf16[640,256]{1,0:T(8,128)(2,1)S(1)} %collective-permute-done.33.refs_1_), custom_call_target="tpu_custom_call" | custom-call | tf_op jit(solution)/shard_map/pallas_call | solution.py:126
  (44 shorter events, 0.9 us)
Async XLA Ops:
  0.6 16.2 %copy-start.1 = (bf16[3,320,320]{2,1,0:T(8,128)(2,1)S(1)}, bf16[3,320,320]{2,1,0:T(8,128)(2,1)}, u32[]{:S(2)}) copy-start(bf16[3,320,320]{2,1,0:T(8,128)(2,1)} %refs_3_.1) | copy-start | bytes 1843204
  2.1 9.2 %collective-permute-start = (bf16[80,384]{1,0:T(8,128)(2,1)S(1)}, bf16[80,384]{1,0:T(8,128)(2,1)S(1)}, u32[]{:S(2)}, u32[]{:S(2)}) collective-permute-start(bf16[80,384]{1,0:T(8,128)(2,1)S(1)} %get-tuple-element.37), channel_id=1, source_target_pairs={{0,1},{1,2},{2,3},{3,0},{4,5},{5,6},{6,7},{7,4},{8,9},{9,10},{10,1... | collective-permute-start | bytes 184328 | tf_op jit(solution)/shard_map/ppermute | solution.py:405
  5.2 8.3 %collective-permute-start.1 = (bf16[80,384]{1,0:T(8,128)(2,1)S(1)}, bf16[80,384]{1,0:T(8,128)(2,1)S(1)}, u32[]{:S(2)}, u32[]{:S(2)}) collective-permute-start(bf16[80,384]{1,0:T(8,128)(2,1)S(1)} %get-tuple-element.37), channel_id=1, source_target_pairs={{0,2},{1,3},{2,0},{3,1},{4,6},{5,7},{6,4},{7,5},{8,10},{9,11},{10,... | collective-permute-start | bytes 184328 | tf_op jit(solution)/shard_map/ppermute | solution.py:405
  7.8 6.1 %collective-permute-start.2 = (bf16[80,384]{1,0:T(8,128)(2,1)S(1)}, bf16[80,384]{1,0:T(8,128)(2,1)S(1)}, u32[]{:S(2)}, u32[]{:S(2)}) collective-permute-start(bf16[80,384]{1,0:T(8,128)(2,1)S(1)} %get-tuple-element.37), channel_id=1, source_target_pairs={{0,3},{1,0},{2,1},{3,2},{4,7},{5,4},{6,5},{7,6},{8,11},{9,8},{10,9... | collective-permute-start | bytes 184328 | tf_op jit(solution)/shard_map/ppermute | solution.py:405
  9.1 5.3 %collective-permute-start.6 = (bf16[320,256]{1,0:T(8,128)(2,1)S(1)}, bf16[320,256]{1,0:T(8,128)(2,1)S(1)}, u32[]{:S(2)}, u32[]{:S(2)}) collective-permute-start(bf16[320,256]{1,0:T(8,128)(2,1)S(1)} %get-tuple-element.40.refs_1_), channel_id=1, source_target_pairs={{0,8},{4,12},{8,0},{12,4},{16,24},{20,28},{24,16},{28,20},{1,9},{5... | collective-permute-start | bytes 491528 | tf_op jit(solution)/shard_map/ppermute | solution.py:399
  10.6 5.4 %collective-permute-start.11 = (bf16[320,256]{1,0:T(8,128)(2,1)S(1)}, bf16[320,256]{1,0:T(8,128)(2,1)S(1)}, u32[]{:S(2)}, u32[]{:S(2)}) collective-permute-start(bf16[320,256]{1,0:T(8,128)(2,1)S(1)} %get-tuple-element.38.refs_1_), channel_id=1, source_target_pairs={{0,0},{1,2},{2,1},{3,3},{4,4},{5,6},{6,5},{7,7},{8,8},{9,10},{10,9... | collective-permute-start | bytes 491528 | tf_op jit(solution)/shard_map/ppermute | solution.py:414
  11.3 5.5 %collective-permute-start.10 = (bf16[320,256]{1,0:T(8,128)(2,1)S(1)}, bf16[320,256]{1,0:T(8,128)(2,1)S(1)}, u32[]{:S(2)}, u32[]{:S(2)}) collective-permute-start(bf16[320,256]{1,0:T(8,128)(2,1)S(1)} %get-tuple-element.38.refs_1_), channel_id=1, source_target_pairs={{0,1},{1,0},{2,3},{3,2},{4,5},{5,4},{6,7},{7,6},{8,9},{9,8},{10,11... | collective-permute-start | bytes 491528 | tf_op jit(solution)/shard_map/ppermute | solution.py:414
  13.5 5.3 %collective-permute-start.4 = (bf16[320,256]{1,0:T(8,128)(2,1)S(1)}, bf16[320,256]{1,0:T(8,128)(2,1)S(1)}, u32[]{:S(2)}, u32[]{:S(2)}) collective-permute-start(bf16[320,256]{1,0:T(8,128)(2,1)S(1)} %get-tuple-element.38.refs_1_), channel_id=1, source_target_pairs={{0,8},{4,12},{8,0},{12,4},{16,24},{20,28},{24,16},{28,20},{1,9},{5... | collective-permute-start | bytes 491528 | tf_op jit(solution)/shard_map/ppermute | solution.py:399
  13.9 7.4 %collective-permute-start.5 = (bf16[320,256]{1,0:T(8,128)(2,1)S(1)}, bf16[320,256]{1,0:T(8,128)(2,1)S(1)}, u32[]{:S(2)}, u32[]{:S(2)}) collective-permute-start(bf16[320,256]{1,0:T(8,128)(2,1)S(1)} %get-tuple-element.40.refs_1_), channel_id=1, source_target_pairs={{0,4},{4,0},{8,12},{12,8},{16,20},{20,16},{24,28},{28,24},{1,5},{5... | collective-permute-start | bytes 491528 | tf_op jit(solution)/shard_map/ppermute | solution.py:399
  14.5 6.6 %collective-permute-start.3 = (bf16[240,384]{1,0:T(8,128)(2,1)S(1)}, bf16[240,384]{1,0:T(8,128)(2,1)S(1)}, u32[]{:S(2)}, u32[]{:S(2)}) collective-permute-start(bf16[240,384]{1,0:T(8,128)(2,1)S(1)} %pad_maximum_fusion), channel_id=1, source_target_pairs={{0,16},{4,20},{8,24},{12,28},{16,0},{20,4},{24,8},{28,12},{1,17},{... | collective-permute-start | bytes 552968 | tf_op jit(solution)/shard_map/ppermute | solution.py:399
  16.0 5.4 %collective-permute-start.7 = (bf16[320,256]{1,0:T(8,128)(2,1)S(1)}, bf16[320,256]{1,0:T(8,128)(2,1)S(1)}, u32[]{:S(2)}, u32[]{:S(2)}) collective-permute-start(bf16[320,256]{1,0:T(8,128)(2,1)S(1)} %collective-permute-done.6.refs_3_), channel_id=1, source_target_pairs={{0,4},{4,0},{8,12},{12,8},{16,20},{20,16},{24,28},{28,24},{1,5},{5... | collective-permute-start | bytes 491528 | tf_op jit(solution)/shard_map/ppermute | solution.py:399
  17.3 5.4 %collective-permute-start.12 = (bf16[160,256]{1,0:T(8,128)(2,1)S(1)}, bf16[160,256]{1,0:T(8,128)(2,1)S(1)}, u32[]{:S(2)}, u32[]{:S(2)}) collective-permute-start(bf16[160,256]{1,0:T(8,128)(2,1)S(1)} %get-tuple-element.43), channel_id=1, source_target_pairs={{0,8},{4,12},{8,0},{12,4},{16,24},{20,28},{24,16},{28,20},{1,9},{5... | collective-permute-start | bytes 245768 | tf_op jit(solution)/shard_map/ppermute | solution.py:399
  18.9 3.8 %collective-permute-start.13 = (bf16[80,256]{1,0:T(8,128)(2,1)S(1)}, bf16[80,256]{1,0:T(8,128)(2,1)S(1)}, u32[]{:S(2)}, u32[]{:S(2)}) collective-permute-start(bf16[80,256]{1,0:T(8,128)(2,1)S(1)} %get-tuple-element.44), channel_id=1, source_target_pairs={{0,4},{4,0},{8,12},{12,8},{16,20},{20,16},{24,28},{28,24},{1,5},{5... | collective-permute-start | bytes 122888 | tf_op jit(solution)/shard_map/ppermute | solution.py:399
  22.7 8.9 %collective-permute-start.15 = (bf16[640,256]{1,0:T(8,128)(2,1)S(1)}, bf16[640,256]{1,0:T(8,128)(2,1)S(1)}, u32[]{:S(2)}, u32[]{:S(2)}) collective-permute-start(bf16[640,256]{1,0:T(8,128)(2,1)S(1)} %shard_map.71.refs_5_), channel_id=1, source_target_pairs={{0,8},{4,12},{8,0},{12,4},{16,24},{20,28},{24,16},{28,20},{1,9},{5... | collective-permute-start | bytes 983048 | tf_op jit(solution)/shard_map/ppermute | solution.py:399
  24.4 1.2 %collective-permute-start.18 = (bf16[80,256]{1,0:T(8,128)(2,1)S(1)}, bf16[80,256]{1,0:T(8,128)(2,1)S(1)}, u32[]{:S(2)}, u32[]{:S(2)}) collective-permute-start(bf16[80,256]{1,0:T(8,128)(2,1)S(1)} %slice.4), channel_id=1, source_target_pairs={{0,4},{4,0},{8,12},{12,8},{16,20},{20,16},{24,28},{28,24},{1,5},{5... | collective-permute-start | bytes 122888 | tf_op jit(solution)/shard_map/ppermute | solution.py:399
  27.0 8.1 %collective-permute-start.19 = (bf16[320,384]{1,0:T(8,128)(2,1)S(1)}, bf16[320,384]{1,0:T(8,128)(2,1)S(1)}, u32[]{:S(2)}, u32[]{:S(2)}) collective-permute-start(bf16[320,384]{1,0:T(8,128)(2,1)S(1)} %get-tuple-element.51), channel_id=1, source_target_pairs={{0,16},{4,20},{8,24},{12,28},{16,0},{20,4},{24,8},{28,12},{1,17},{... | collective-permute-start | bytes 737288 | tf_op jit(solution)/shard_map/ppermute | solution.py:399
  28.6 7.9 %collective-permute-start.14 = (bf16[640,256]{1,0:T(8,128)(2,1)S(1)}, bf16[640,256]{1,0:T(8,128)(2,1)S(1)}, u32[]{:S(2)}, u32[]{:S(2)}) collective-permute-start(bf16[640,256]{1,0:T(8,128)(2,1)S(1)} %shard_map.71.refs_5_), channel_id=1, source_target_pairs={{0,4},{4,0},{8,12},{12,8},{16,20},{20,16},{24,28},{28,24},{1,5},{5... | collective-permute-start | bytes 983048 | tf_op jit(solution)/shard_map/ppermute | solution.py:399
  31.6 4.9 %collective-permute-start.16 = (bf16[640,256]{1,0:T(8,128)(2,1)S(1)}, bf16[640,256]{1,0:T(8,128)(2,1)S(1)}, u32[]{:S(2)}, u32[]{:S(2)}) collective-permute-start(bf16[640,256]{1,0:T(8,128)(2,1)S(1)} %collective-permute-done.15.refs_7_), channel_id=1, source_target_pairs={{0,4},{4,0},{8,12},{12,8},{16,20},{20,16},{24,28},{28,24},{1,5},{5... | collective-permute-start | bytes 983048 | tf_op jit(solution)/shard_map/ppermute | solution.py:399
  31.6 7.3 %collective-permute-start.24 = (bf16[640,256]{1,0:T(8,128)(2,1)S(1)}, bf16[640,256]{1,0:T(8,128)(2,1)S(1)}, u32[]{:S(2)}, u32[]{:S(2)}) collective-permute-start(bf16[640,256]{1,0:T(8,128)(2,1)S(1)} %get-tuple-element.61), channel_id=1, source_target_pairs={{0,4},{4,0},{8,12},{12,8},{16,20},{20,16},{24,28},{28,24},{1,5},{5... | collective-permute-start | bytes 983048 | tf_op jit(solution)/shard_map/ppermute | solution.py:399
  32.1 3.1 %collective-permute-start.8 = (bf16[320,256]{1,0:T(8,128)(2,1)S(1)}, bf16[320,256]{1,0:T(8,128)(2,1)S(1)}, u32[]{:S(2)}, u32[]{:S(2)}) collective-permute-start(bf16[320,256]{1,0:T(8,128)(2,1)S(1)} %get-tuple-element.38.refs_1_), channel_id=1, source_target_pairs={{0,4},{4,0},{8,12},{12,8},{16,20},{20,16},{24,28},{28,24},{1,5},{5... | collective-permute-start | bytes 491528 | tf_op jit(solution)/shard_map/ppermute | solution.py:399
  35.1 1.4 %collective-permute-start.9 = (bf16[320,256]{1,0:T(8,128)(2,1)S(1)}, bf16[320,256]{1,0:T(8,128)(2,1)S(1)}, u32[]{:S(2)}, u32[]{:S(2)}) collective-permute-start(bf16[320,256]{1,0:T(8,128)(2,1)S(1)} %collective-permute-done.4.refs_5_.refs_3_), channel_id=1, source_target_pairs={{0,4},{4,0},{8,12},{12,8},{16,20},{20,16},{24,28},{28,24},{1,5},{5... | collective-permute-start | bytes 491528 | tf_op jit(solution)/shard_map/ppermute | solution.py:399
  35.2 5.8 %collective-permute-start.20 = (bf16[160,384]{1,0:T(8,128)(2,1)S(1)}, bf16[160,384]{1,0:T(8,128)(2,1)S(1)}, u32[]{:S(2)}, u32[]{:S(2)}) collective-permute-start(bf16[160,384]{1,0:T(8,128)(2,1)S(1)} %get-tuple-element.53), channel_id=1, source_target_pairs={{0,1},{1,0},{2,3},{3,2},{4,5},{5,4},{6,7},{7,6},{8,9},{9,8},{10,11... | collective-permute-start | bytes 368648 | tf_op jit(solution)/shard_map/ppermute | solution.py:402
  37.2 21.6 %copy-start = (bf16[1,1,16,16,320]{4,3,2,1,0:T(8,128)(2,1)S(1)}, bf16[1,1,16,16,320]{4,3,2,1,0:T(8,128)(2,1)}, u32[]{:S(2)}) copy-start(bf16[1,1,16,16,320]{4,3,2,1,0:T(8,128)(2,1)} %param.5) | copy-start | bytes 491524
  37.3 4.6 %collective-permute-start.17 = (bf16[160,256]{1,0:T(8,128)(2,1)S(1)}, bf16[160,256]{1,0:T(8,128)(2,1)S(1)}, u32[]{:S(2)}, u32[]{:S(2)}) collective-permute-start(bf16[160,256]{1,0:T(8,128)(2,1)S(1)} %get-tuple-element.47), channel_id=1, source_target_pairs={{0,16},{4,20},{8,24},{12,28},{16,0},{20,4},{24,8},{28,12},{1,17},{... | collective-permute-start | bytes 245768 | tf_op jit(solution)/shard_map/ppermute | solution.py:399
  38.9 9.6 %collective-permute-start.25 = (bf16[320,256]{1,0:T(8,128)(2,1)S(1)}, bf16[320,256]{1,0:T(8,128)(2,1)S(1)}, u32[]{:S(2)}, u32[]{:S(2)}) collective-permute-start(bf16[320,256]{1,0:T(8,128)(2,1)S(1)} %get-tuple-element.62), channel_id=1, source_target_pairs={{0,8},{4,12},{8,0},{12,4},{16,24},{20,28},{24,16},{28,20},{1,9},{5... | collective-permute-start | bytes 491528 | tf_op jit(solution)/shard_map/ppermute | solution.py:399
  41.8 5.1 %collective-permute-start.21 = (bf16[160,256]{1,0:T(8,128)(2,1)S(1)}, bf16[160,256]{1,0:T(8,128)(2,1)S(1)}, u32[]{:S(2)}, u32[]{:S(2)}) collective-permute-start(bf16[160,256]{1,0:T(8,128)(2,1)S(1)} %get-tuple-element.56), channel_id=1, source_target_pairs={{0,1},{1,0},{2,3},{3,2},{4,5},{5,4},{6,7},{7,6},{8,9},{9,8},{10,11... | collective-permute-start | bytes 245768 | tf_op jit(solution)/shard_map/ppermute | solution.py:402
  42.8 5.8 %collective-permute-start.23 = (bf16[80,384]{1,0:T(8,128)(2,1)S(1)}, bf16[80,384]{1,0:T(8,128)(2,1)S(1)}, u32[]{:S(2)}, u32[]{:S(2)}) collective-permute-start(bf16[80,384]{1,0:T(8,128)(2,1)S(1)} %get-tuple-element.59), channel_id=1, source_target_pairs={{0,2},{1,3},{2,0},{3,1},{4,6},{5,7},{6,4},{7,5},{8,10},{9,11},{10,... | collective-permute-start | bytes 184328 | tf_op jit(solution)/shard_map/ppermute | solution.py:402
  47.0 8.2 %collective-permute-start.22 = (bf16[160,256]{1,0:T(8,128)(2,1)S(1)}, bf16[160,256]{1,0:T(8,128)(2,1)S(1)}, u32[]{:S(2)}, u32[]{:S(2)}) collective-permute-start(bf16[160,256]{1,0:T(8,128)(2,1)S(1)} %get-tuple-element.58), channel_id=1, source_target_pairs={{0,2},{1,3},{2,0},{3,1},{4,6},{5,7},{6,4},{7,5},{8,10},{9,11},{10,... | collective-permute-start | bytes 245768 | tf_op jit(solution)/shard_map/ppermute | solution.py:402
  48.6 5.2 %collective-permute-start.26 = (bf16[80,384]{1,0:T(8,128)(2,1)S(1)}, bf16[80,384]{1,0:T(8,128)(2,1)S(1)}, u32[]{:S(2)}, u32[]{:S(2)}) collective-permute-start(bf16[80,384]{1,0:T(8,128)(2,1)S(1)} %shard_map.79.refs_2_), channel_id=1, source_target_pairs={{0,24},{4,28},{8,16},{12,20},{16,8},{20,12},{24,0},{28,4},{1,25},{... | collective-permute-start | bytes 184328 | tf_op jit(solution)/shard_map/ppermute | solution.py:399
  50.4 4.2 %collective-permute-start.27 = (bf16[80,384]{1,0:T(8,128)(2,1)S(1)}, bf16[80,384]{1,0:T(8,128)(2,1)S(1)}, u32[]{:S(2)}, u32[]{:S(2)}) collective-permute-start(bf16[80,384]{1,0:T(8,128)(2,1)S(1)} %shard_map.79.refs_2_), channel_id=1, source_target_pairs={{0,16},{4,20},{8,24},{12,28},{16,0},{20,4},{24,8},{28,12},{1,17},{... | collective-permute-start | bytes 184328 | tf_op jit(solution)/shard_map/ppermute | solution.py:399
  50.9 4.2 %collective-permute-start.28 = (bf16[80,384]{1,0:T(8,128)(2,1)S(1)}, bf16[80,384]{1,0:T(8,128)(2,1)S(1)}, u32[]{:S(2)}, u32[]{:S(2)}) collective-permute-start(bf16[80,384]{1,0:T(8,128)(2,1)S(1)} %shard_map.79.refs_2_), channel_id=1, source_target_pairs={{0,8},{4,12},{8,0},{12,4},{16,24},{20,28},{24,16},{28,20},{1,9},{5... | collective-permute-start | bytes 184328 | tf_op jit(solution)/shard_map/ppermute | solution.py:399
  55.2 3.6 %collective-permute-start.29 = (bf16[320,384]{1,0:T(8,128)(2,1)S(1)}, bf16[320,384]{1,0:T(8,128)(2,1)S(1)}, u32[]{:S(2)}, u32[]{:S(2)}) collective-permute-start(bf16[320,384]{1,0:T(8,128)(2,1)S(1)} %get-tuple-element.63.refs_0_), channel_id=1, source_target_pairs={{0,4},{4,0},{8,12},{12,8},{16,20},{20,16},{24,28},{28,24},{1,5},{5... | collective-permute-start | bytes 737288 | tf_op jit(solution)/shard_map/ppermute | solution.py:399
  55.3 5.8 %collective-permute-start.30 = (bf16[160,256]{1,0:T(8,128)(2,1)S(1)}, bf16[160,256]{1,0:T(8,128)(2,1)S(1)}, u32[]{:S(2)}, u32[]{:S(2)}) collective-permute-start(bf16[160,256]{1,0:T(8,128)(2,1)S(1)} %get-tuple-element.67.refs_0_), channel_id=1, source_target_pairs={{0,24},{4,28},{8,16},{12,20},{16,8},{20,12},{24,0},{28,4},{1,25},{... | collective-permute-start | bytes 245768 | tf_op jit(solution)/shard_map/ppermute | solution.py:399
  57.5 5.3 %collective-permute-start.31 = (bf16[160,256]{1,0:T(8,128)(2,1)S(1)}, bf16[160,256]{1,0:T(8,128)(2,1)S(1)}, u32[]{:S(2)}, u32[]{:S(2)}) collective-permute-start(bf16[160,256]{1,0:T(8,128)(2,1)S(1)} %get-tuple-element.67.refs_0_), channel_id=1, source_target_pairs={{0,16},{4,20},{8,24},{12,28},{16,0},{20,4},{24,8},{28,12},{1,17},{... | collective-permute-start | bytes 245768 | tf_op jit(solution)/shard_map/ppermute | solution.py:399
  58.0 4.9 %collective-permute-start.32 = (bf16[160,256]{1,0:T(8,128)(2,1)S(1)}, bf16[160,256]{1,0:T(8,128)(2,1)S(1)}, u32[]{:S(2)}, u32[]{:S(2)}) collective-permute-start(bf16[160,256]{1,0:T(8,128)(2,1)S(1)} %get-tuple-element.67.refs_0_), channel_id=1, source_target_pairs={{0,8},{4,12},{8,0},{12,4},{16,24},{20,28},{24,16},{28,20},{1,9},{5... | collective-permute-start | bytes 245768 | tf_op jit(solution)/shard_map/ppermute | solution.py:399
  62.9 1.7 %collective-permute-start.33 = (bf16[640,256]{1,0:T(8,128)(2,1)S(1)}, bf16[640,256]{1,0:T(8,128)(2,1)S(1)}, u32[]{:S(2)}, u32[]{:S(2)}) collective-permute-start(bf16[640,256]{1,0:T(8,128)(2,1)S(1)} %shard_map.82.refs_0_), channel_id=1, source_target_pairs={{0,4},{4,0},{8,12},{12,8},{16,20},{20,16},{24,28},{28,24},{1,5},{5... | collective-permute-start | bytes 983048 | tf_op jit(solution)/shard_map/ppermute | solution.py:399

commit v7 on v6

--- a/solution.py
+++ b/solution.py
@@ -372,21 +372,28 @@
     token_ref[...] = jnp.zeros_like(token_ref)
 
 
-def time_end(plan, here_ref, core_ref, out_ref, held):
-    low, high, _ = plan.place()
-    slab, size = plan.slab, plan.thalf
+def time_turn(plan, ref, out_ref, held):
+    _, high, _ = plan.place()
+    size = plan.thalf
     near = pl.ds(pl.multiple_of(high * size, 16), size)
     far = pl.ds(pl.multiple_of((1 - high) * size, 16), size)
-    for core, ref in enumerate((here_ref, core_ref)):
+    for pair in range(2):
+        first = plan.chips.index(2 * pair) * size
+        second = plan.chips.index(plan.group + 2 * pair) * size
+        held[near, :] = ref[first : first + size, :].astype(F32)
+        held[far, :] = ref[second : second + size, :].astype(F32)
+        out_ref[pair] = held[...].T * plan.factor
+
+
+def time_end(plan, here_ref, core_ref, out_ref, held, turned):
+    low, _, _ = plan.place()
+    slab = plan.slab
+    time_turn(plan, core_ref, turned, held)
+    for core, ref in enumerate((here_ref, turned)):
         for pair in range(2):
-            first = plan.chips.index(2 * pair) * size
-            second = plan.chips.index(plan.group + 2 * pair) * size
-            held[near, :] = ref[first : first + size, :].astype(F32)
-            held[far, :] = ref[second : second + size, :].astype(F32)
-            turned = held[...].T * plan.factor
             for k in range(3):
                 here = pl.ds(pl.multiple_of((low ^ (2 * pair + core)) * slab, 16), slab)
-                out_ref[k, here, :] = turned[k * slab : (k + 1) * slab, :]
+                out_ref[k, here, :] = ref[pair, k * slab : (k + 1) * slab, :]
 
 
 def per_device(plan, frames, cotangent, w_space, w_time):
@@ -545,12 +552,15 @@
     (t_all,) = call(
         stacked, [((4 * plan.thalf, plan.tcols), BF16)], *chips(t_sum), after=[token]
     )
+    turned = (2, plan.tcols, chans)
+    held = pltpu.VMEM((chans, plan.tcols), F32)
+    (t_here,) = call(part(time_turn), [(turned, F32)], t_all, scratch=[held])
     (t_out,) = call(
         part(time_end),
         [((3, chans, chans), F32)],
-        t_all,
+        t_here,
         swap(t_all, 1),
-        scratch=[pltpu.VMEM((chans, plan.tcols), F32)],
+        scratch=[held, pltpu.VMEM(turned, F32)],
     )
     return f_out.reshape(frames.shape), jnp.transpose(s_out, (1, 0, 2)), t_out
 

time: 66.4 us -> 66.3 us (level)
    pallas_call x16 -> x17, Pallas kernels: 7.76 us -> 7.92 us  [call(): pl.pallas_call(body, out_shape=tuple((jax.ShapeDtypeStruct(shape, dtype)...]
  transfers between devices with their start and end apart: 34 -> 34, of which waited for: 17 -> 17; matrix products, arithmetic and copies ran while one was open for 0% -> 0% of each run, Pallas kernels for 9% -> 10%
where the time goes in v7:
time: 66.3 us; the launch traced here: 66.1 us
  starting transfers between devices  34.1 us (51%)
  waiting for transfers between devices  21.7 us (33%)
  Pallas kernels  9.39 us (14%)
  between operations  0.86 us (1%)
    ppermute x25, starting transfers between devices, swap(): lax.ppermute(value, 'clip', [(i, i ^ distance) for i in range(plan.clips)])  18.5 us
    ppermute x25, waiting for transfers between devices, swap(): lax.ppermute(value, 'clip', [(i, i ^ distance) for i in range(plan.clips)])  17.6 us
    pallas_call x17, Pallas kernels, call(): pl.pallas_call(body, out_shape=tuple((jax.ShapeDtypeStruct(shape, dtype)...  7.92 us
    ppermute x3, starting transfers between devices, turn(): lax.ppermute(value, 'seq', [(i, (i + k) % seqs) for i in range(seqs)])  7.01 us
    ppermute x4, starting transfers between devices, trade(): return lax.ppermute(value, 'seq', [(i, i ^ distance) for i in range(seqs)])  5.78 us
    ppermute x4, waiting for transfers between devices, trade(): return lax.ppermute(value, 'seq', [(i, i ^ distance) for i in range(seqs)])  3.23 us
    ppermute x2, starting transfers between devices, neighbours(): found.append(lax.ppermute(value, 'seq', list(other.items())))  2.86 us
    pallas_call x1, Pallas kernels, per_device(): pl.pallas_call(part(prepare), out_shape=tuple((jax.ShapeDtypeStruct(shape...  1.47 us
  transfers between devices with their start and end apart: 34, of which 17 were waited for; matrix products, arithmetic and copies ran while one was open for 0% of the time, Pallas kernels for 10%

profile of v7, /device:TPU:0, one launch (start us, length us, event | category | flops | bytes accessed | tf_op | source)
XLA Modules:
  0.0 66.1 jit_solution(12711150388184880724)
XLA Ops:
  0.6 1.5 %shard_map.67 = (bf16[320,256]{1,0:T(8,128)(2,1)S(1)}, bf16[320,256]{1,0:T(8,128)(2,1)S(1)}, bf16[80,768]{1,0:T(8,128)(2,1)S(1)}, bf16[80,384]{1,0:T(8,128)(2,1)S(1)}) custom-call(bf16[256,320]{1,0:T(8,128)(2,1)} %bitcast.8, bf16[256,320]{1,0:T(8,128)(2,1)} %bitcast.5, bf16[9,80,320]{2,1,0:T(8,128)(2,1)} %bitcast.7), custom_call_target="tpu_custom_call" | custom-call | tf_op jit(solution)/shard_map/pallas_call | solution.py:436
  2.1 3.1 %collective-permute-start = (bf16[80,384]{1,0:T(8,128)(2,1)S(1)}, bf16[80,384]{1,0:T(8,128)(2,1)S(1)}, u32[]{:S(2)}, u32[]{:S(2)}) collective-permute-start(bf16[80,384]{1,0:T(8,128)(2,1)S(1)} %get-tuple-element.37), channel_id=1, source_target_pairs={{0,1},{1,2},{2,3},{3,0},{4,5},{5,6},{6,7},{7,4},{8,9},{9,10},{10,1... | collective-permute-start | bytes 184328 | tf_op jit(solution)/shard_map/ppermute | solution.py:412
  5.2 2.6 %collective-permute-start.1 = (bf16[80,384]{1,0:T(8,128)(2,1)S(1)}, bf16[80,384]{1,0:T(8,128)(2,1)S(1)}, u32[]{:S(2)}, u32[]{:S(2)}) collective-permute-start(bf16[80,384]{1,0:T(8,128)(2,1)S(1)} %get-tuple-element.37), channel_id=1, source_target_pairs={{0,2},{1,3},{2,0},{3,1},{4,6},{5,7},{6,4},{7,5},{8,10},{9,11},{10,... | collective-permute-start | bytes 184328 | tf_op jit(solution)/shard_map/ppermute | solution.py:412
  7.8 1.3 %collective-permute-start.2 = (bf16[80,384]{1,0:T(8,128)(2,1)S(1)}, bf16[80,384]{1,0:T(8,128)(2,1)S(1)}, u32[]{:S(2)}, u32[]{:S(2)}) collective-permute-start(bf16[80,384]{1,0:T(8,128)(2,1)S(1)} %get-tuple-element.37), channel_id=1, source_target_pairs={{0,3},{1,0},{2,1},{3,2},{4,7},{5,4},{6,5},{7,6},{8,11},{9,8},{10,9... | collective-permute-start | bytes 184328 | tf_op jit(solution)/shard_map/ppermute | solution.py:412
  9.1 1.5 %collective-permute-start.6 = (bf16[320,256]{1,0:T(8,128)(2,1)S(1)}, bf16[320,256]{1,0:T(8,128)(2,1)S(1)}, u32[]{:S(2)}, u32[]{:S(2)}) collective-permute-start(bf16[320,256]{1,0:T(8,128)(2,1)S(1)} %get-tuple-element.40.refs_1_), channel_id=1, source_target_pairs={{0,8},{4,12},{8,0},{12,4},{16,24},{20,28},{24,16},{28,20},{1,9},{5... | collective-permute-start | bytes 491528 | tf_op jit(solution)/shard_map/ppermute | solution.py:406
  10.6 0.7 collective-permute-start.11
  11.3 2.2 %collective-permute-start.10 = (bf16[320,256]{1,0:T(8,128)(2,1)S(1)}, bf16[320,256]{1,0:T(8,128)(2,1)S(1)}, u32[]{:S(2)}, u32[]{:S(2)}) collective-permute-start(bf16[320,256]{1,0:T(8,128)(2,1)S(1)} %get-tuple-element.38.refs_1_), channel_id=1, source_target_pairs={{0,1},{1,0},{2,3},{3,2},{4,5},{5,4},{6,7},{7,6},{8,9},{9,8},{10,11... | collective-permute-start | bytes 491528 | tf_op jit(solution)/shard_map/ppermute | solution.py:421
  13.5 0.4 collective-permute-start.4
  13.9 0.5 collective-permute-done.6.refs_3_
  14.5 1.5 %collective-permute-start.3 = (bf16[240,384]{1,0:T(8,128)(2,1)S(1)}, bf16[240,384]{1,0:T(8,128)(2,1)S(1)}, u32[]{:S(2)}, u32[]{:S(2)}) collective-permute-start(bf16[240,384]{1,0:T(8,128)(2,1)S(1)} %pad_maximum_fusion), channel_id=1, source_target_pairs={{0,16},{4,20},{8,24},{12,28},{16,0},{20,4},{24,8},{28,12},{1,17},{... | collective-permute-start | bytes 552968 | tf_op jit(solution)/shard_map/ppermute | solution.py:406
  16.0 0.8 %collective-permute-done.10 = bf16[320,256]{1,0:T(8,128)(2,1)S(1)} collective-permute-done((bf16[320,256]{1,0:T(8,128)(2,1)S(1)}, bf16[320,256]{1,0:T(8,128)(2,1)S(1)}, u32[]{:S(2)}, u32[]{:S(2)}) %collective-permute-start.10) | collective-permute-done | bytes 163872 | tf_op jit(solution)/shard_map/ppermute | solution.py:421
  16.8 0.4 shard_map.70
  17.3 1.6 %collective-permute-start.12 = (bf16[160,256]{1,0:T(8,128)(2,1)S(1)}, bf16[160,256]{1,0:T(8,128)(2,1)S(1)}, u32[]{:S(2)}, u32[]{:S(2)}) collective-permute-start(bf16[160,256]{1,0:T(8,128)(2,1)S(1)} %get-tuple-element.43), channel_id=1, source_target_pairs={{0,8},{4,12},{8,0},{12,4},{16,24},{20,28},{24,16},{28,20},{1,9},{5... | collective-permute-start | bytes 245768 | tf_op jit(solution)/shard_map/ppermute | solution.py:406
  19.1 2.0 %collective-permute-done.3.refs_4_ = bf16[240,384]{1,0:T(8,128)(2,1)S(1)} collective-permute-done((bf16[240,384]{1,0:T(8,128)(2,1)S(1)}, bf16[240,384]{1,0:T(8,128)(2,1)S(1)}, u32[]{:S(2)}, u32[]{:S(2)}) %collective-permute-start.3) | collective-permute-done | bytes 184352 | tf_op jit(solution)/shard_map/ppermute | solution.py:406
  21.3 1.3 %shard_map.69 = (bf16[320,1024]{1,0:T(8,128)(2,1)S(1)}, bf16[80,1024]{1,0:T(8,128)(2,1)S(1)}, f32[80,1024]{1,0:T(8,128)S(1)}) custom-call(bf16[768,320]{1,0:T(8,128)(2,1)S(1)} %get-tuple-element.39.refs_0_, bf16[320,256]{1,0:T(8,128)(2,1)S(1)} %get-tuple-element.40.refs_1_, bf16[320,256]{1,0:T(8,128)(2,1)S(1)} %collective-permute-done.5.refs_2_, ...), custom_call_target="tpu_custom_call" | custom-call | tf_op jit(solution)/shard_map/pallas_call | solution.py:126
  22.7 1.7 %collective-permute-start.15 = (bf16[640,256]{1,0:T(8,128)(2,1)S(1)}, bf16[640,256]{1,0:T(8,128)(2,1)S(1)}, u32[]{:S(2)}, u32[]{:S(2)}) collective-permute-start(bf16[640,256]{1,0:T(8,128)(2,1)S(1)} %shard_map.71.refs_5_), channel_id=1, source_target_pairs={{0,8},{4,12},{8,0},{12,4},{16,24},{20,28},{24,16},{28,20},{1,9},{5... | collective-permute-start | bytes 983048 | tf_op jit(solution)/shard_map/ppermute | solution.py:406
  24.4 1.2 %collective-permute-done.18.refs_6_ = bf16[80,256]{1,0:T(8,128)(2,1)S(1)} collective-permute-done((bf16[80,256]{1,0:T(8,128)(2,1)S(1)}, bf16[80,256]{1,0:T(8,128)(2,1)S(1)}, u32[]{:S(2)}, u32[]{:S(2)}) %collective-permute-start.18) | collective-permute-done | bytes 40992 | tf_op jit(solution)/shard_map/ppermute | solution.py:406
  25.6 1.4 %shard_map.73 = (bf16[320,384]{1,0:T(8,128)(2,1)S(1)}, f32[320,384]{1,0:T(8,128)S(1)}, bf16[640,256]{1,0:T(8,128)(2,1)S(1)}, f32[640,256]{1,0:T(8,128)S(1)}) custom-call(bf16[320,768]{1,0:T(8,128)(2,1)S(1)} %get-tuple-element.42.refs_2_.refs_0_, bf16[320,1024]{1,0:T(8,128)(2,1)S(1)} %get-tuple-element.45.refs_5_.refs_1_, ...), custom_call_target="tpu_custom_call" | custom-call | tf_op jit(solution)/shard_map/pallas_call | solution.py:126
  27.0 1.6 %collective-permute-start.19 = (bf16[320,384]{1,0:T(8,128)(2,1)S(1)}, bf16[320,384]{1,0:T(8,128)(2,1)S(1)}, u32[]{:S(2)}, u32[]{:S(2)}) collective-permute-start(bf16[320,384]{1,0:T(8,128)(2,1)S(1)} %get-tuple-element.51), channel_id=1, source_target_pairs={{0,16},{4,20},{8,24},{12,28},{16,0},{20,4},{24,8},{28,12},{1,17},{... | collective-permute-start | bytes 737288 | tf_op jit(solution)/shard_map/ppermute | solution.py:406
  28.6 3.0 %collective-permute-done.15.refs_7_ = bf16[640,256]{1,0:T(8,128)(2,1)S(1)} collective-permute-done((bf16[640,256]{1,0:T(8,128)(2,1)S(1)}, bf16[640,256]{1,0:T(8,128)(2,1)S(1)}, u32[]{:S(2)}, u32[]{:S(2)}) %collective-permute-start.15) | collective-permute-done | bytes 327712 | tf_op jit(solution)/shard_map/ppermute | solution.py:406
  31.6 0.5 collective-permute-start.24
  32.1 3.0 %collective-permute-done.19.refs_1_ = bf16[320,384]{1,0:T(8,128)(2,1)S(1)} collective-permute-done((bf16[320,384]{1,0:T(8,128)(2,1)S(1)}, bf16[320,384]{1,0:T(8,128)(2,1)S(1)}, u32[]{:S(2)}, u32[]{:S(2)}) %collective-permute-start.19) | collective-permute-done | bytes 245792 | tf_op jit(solution)/shard_map/ppermute | solution.py:406
  35.2 0.9 %collective-permute-start.20 = (bf16[160,384]{1,0:T(8,128)(2,1)S(1)}, bf16[160,384]{1,0:T(8,128)(2,1)S(1)}, u32[]{:S(2)}, u32[]{:S(2)}) collective-permute-start(bf16[160,384]{1,0:T(8,128)(2,1)S(1)} %get-tuple-element.53), channel_id=1, source_target_pairs={{0,1},{1,0},{2,3},{3,2},{4,5},{5,4},{6,7},{7,6},{8,9},{9,8},{10,11... | collective-permute-start | bytes 368648 | tf_op jit(solution)/shard_map/ppermute | solution.py:409
  36.1 0.4 collective-permute-done.9.refs_4_
  36.5 0.7 %shard_map.72 = (bf16[160,256]{1,0:T(8,128)(2,1)S(1)}, f32[160,256]{1,0:T(8,128)S(1)}) custom-call(bf16[80,1024]{1,0:T(8,128)(2,1)S(1)} %get-tuple-element.41.refs_0_, bf16[320,256]{1,0:T(8,128)(2,1)S(1)} %get-tuple-element.38.refs_1_, bf16[320,256]{1,0:T(8,128)(2,1)S(1)} %collective-permute-done.8.refs_2_, ...), custom_call_target="tpu_custom_call" | custom-call | tf_op jit(solution)/shard_map/pallas_call | solution.py:126
  37.3 1.6 %collective-permute-start.17 = (bf16[160,256]{1,0:T(8,128)(2,1)S(1)}, bf16[160,256]{1,0:T(8,128)(2,1)S(1)}, u32[]{:S(2)}, u32[]{:S(2)}) collective-permute-start(bf16[160,256]{1,0:T(8,128)(2,1)S(1)} %get-tuple-element.47), channel_id=1, source_target_pairs={{0,16},{4,20},{8,24},{12,28},{16,0},{20,4},{24,8},{28,12},{1,17},{... | collective-permute-start | bytes 245768 | tf_op jit(solution)/shard_map/ppermute | solution.py:406
  38.9 0.6 collective-permute-start.25
  39.5 1.4 %collective-permute-done.20.refs_1_ = bf16[160,384]{1,0:T(8,128)(2,1)S(1)} collective-permute-done((bf16[160,384]{1,0:T(8,128)(2,1)S(1)}, bf16[160,384]{1,0:T(8,128)(2,1)S(1)}, u32[]{:S(2)}, u32[]{:S(2)}) %collective-permute-start.20) | collective-permute-done | bytes 122912 | tf_op jit(solution)/shard_map/ppermute | solution.py:409
  41.0 0.8 %collective-permute-done.17.refs_1_ = bf16[160,256]{1,0:T(8,128)(2,1)S(1)} collective-permute-done((bf16[160,256]{1,0:T(8,128)(2,1)S(1)}, bf16[160,256]{1,0:T(8,128)(2,1)S(1)}, u32[]{:S(2)}, u32[]{:S(2)}) %collective-permute-start.17) | collective-permute-done | bytes 81952 | tf_op jit(solution)/shard_map/ppermute | solution.py:406
  41.8 1.0 %collective-permute-start.21 = (bf16[160,256]{1,0:T(8,128)(2,1)S(1)}, bf16[160,256]{1,0:T(8,128)(2,1)S(1)}, u32[]{:S(2)}, u32[]{:S(2)}) collective-permute-start(bf16[160,256]{1,0:T(8,128)(2,1)S(1)} %get-tuple-element.56), channel_id=1, source_target_pairs={{0,1},{1,0},{2,3},{3,2},{4,5},{5,4},{6,7},{7,6},{8,9},{9,8},{10,11... | collective-permute-start | bytes 245768 | tf_op jit(solution)/shard_map/ppermute | solution.py:409
  42.8 2.4 %collective-permute-start.23 = (bf16[80,384]{1,0:T(8,128)(2,1)S(1)}, bf16[80,384]{1,0:T(8,128)(2,1)S(1)}, u32[]{:S(2)}, u32[]{:S(2)}) collective-permute-start(bf16[80,384]{1,0:T(8,128)(2,1)S(1)} %get-tuple-element.59), channel_id=1, source_target_pairs={{0,2},{1,3},{2,0},{3,1},{4,6},{5,7},{6,4},{7,5},{8,10},{9,11},{10,... | collective-permute-start | bytes 184328 | tf_op jit(solution)/shard_map/ppermute | solution.py:409
  45.2 1.8 %collective-permute-done.21.refs_1_ = bf16[160,256]{1,0:T(8,128)(2,1)S(1)} collective-permute-done((bf16[160,256]{1,0:T(8,128)(2,1)S(1)}, bf16[160,256]{1,0:T(8,128)(2,1)S(1)}, u32[]{:S(2)}, u32[]{:S(2)}) %collective-permute-start.21) | collective-permute-done | bytes 81952 | tf_op jit(solution)/shard_map/ppermute | solution.py:409
  47.0 1.6 %collective-permute-start.22 = (bf16[160,256]{1,0:T(8,128)(2,1)S(1)}, bf16[160,256]{1,0:T(8,128)(2,1)S(1)}, u32[]{:S(2)}, u32[]{:S(2)}) collective-permute-start(bf16[160,256]{1,0:T(8,128)(2,1)S(1)} %get-tuple-element.58), channel_id=1, source_target_pairs={{0,2},{1,3},{2,0},{3,1},{4,6},{5,7},{6,4},{7,5},{8,10},{9,11},{10,... | collective-permute-start | bytes 245768 | tf_op jit(solution)/shard_map/ppermute | solution.py:409
  48.6 1.9 %collective-permute-start.26 = (bf16[80,384]{1,0:T(8,128)(2,1)S(1)}, bf16[80,384]{1,0:T(8,128)(2,1)S(1)}, u32[]{:S(2)}, u32[]{:S(2)}) collective-permute-start(bf16[80,384]{1,0:T(8,128)(2,1)S(1)} %shard_map.79.refs_2_), channel_id=1, source_target_pairs={{0,24},{4,28},{8,16},{12,20},{16,8},{20,12},{24,0},{28,4},{1,25},{... | collective-permute-start | bytes 184328 | tf_op jit(solution)/shard_map/ppermute | solution.py:406
  50.4 0.5 collective-permute-start.27
  50.9 1.2 %collective-permute-start.28 = (bf16[80,384]{1,0:T(8,128)(2,1)S(1)}, bf16[80,384]{1,0:T(8,128)(2,1)S(1)}, u32[]{:S(2)}, u32[]{:S(2)}) collective-permute-start(bf16[80,384]{1,0:T(8,128)(2,1)S(1)} %shard_map.79.refs_2_), channel_id=1, source_target_pairs={{0,8},{4,12},{8,0},{12,4},{16,24},{20,28},{24,16},{28,20},{1,9},{5... | collective-permute-start | bytes 184328 | tf_op jit(solution)/shard_map/ppermute | solution.py:406
  52.1 1.6 %collective-permute-done.26.refs_3_ = bf16[80,384]{1,0:T(8,128)(2,1)S(1)} collective-permute-done((bf16[80,384]{1,0:T(8,128)(2,1)S(1)}, bf16[80,384]{1,0:T(8,128)(2,1)S(1)}, u32[]{:S(2)}, u32[]{:S(2)}) %collective-permute-start.26) | collective-permute-done | bytes 61472 | tf_op jit(solution)/shard_map/ppermute | solution.py:406
  53.8 0.9 %collective-permute-done.27.refs_4_ = bf16[80,384]{1,0:T(8,128)(2,1)S(1)} collective-permute-done((bf16[80,384]{1,0:T(8,128)(2,1)S(1)}, bf16[80,384]{1,0:T(8,128)(2,1)S(1)}, u32[]{:S(2)}, u32[]{:S(2)}) %collective-permute-start.27) | collective-permute-done | bytes 61472 | tf_op jit(solution)/shard_map/ppermute | solution.py:406
  54.7 0.5 collective-permute-done.28.refs_5_
  55.3 2.2 %collective-permute-start.30 = (bf16[160,256]{1,0:T(8,128)(2,1)S(1)}, bf16[160,256]{1,0:T(8,128)(2,1)S(1)}, u32[]{:S(2)}, u32[]{:S(2)}) collective-permute-start(bf16[160,256]{1,0:T(8,128)(2,1)S(1)} %get-tuple-element.67.refs_0_), channel_id=1, source_target_pairs={{0,24},{4,28},{8,16},{12,20},{16,8},{20,12},{24,0},{28,4},{1,25},{... | collective-permute-start | bytes 245768 | tf_op jit(solution)/shard_map/ppermute | solution.py:406
  57.5 0.5 collective-permute-start.31
  58.0 0.8 %collective-permute-start.32 = (bf16[160,256]{1,0:T(8,128)(2,1)S(1)}, bf16[160,256]{1,0:T(8,128)(2,1)S(1)}, u32[]{:S(2)}, u32[]{:S(2)}) collective-permute-start(bf16[160,256]{1,0:T(8,128)(2,1)S(1)} %get-tuple-element.67.refs_0_), channel_id=1, source_target_pairs={{0,8},{4,12},{8,0},{12,4},{16,24},{20,28},{24,16},{28,20},{1,9},{5... | collective-permute-start | bytes 245768 | tf_op jit(solution)/shard_map/ppermute | solution.py:406
  58.9 1.7 %shard_map.81 = (f32[9,80,320]{2,1,0:T(8,128)}, bf16[256,320]{1,0:T(8,128)(2,1)}, f32[8,128]{1,0:T(8,128)S(1)}) custom-call(bf16[320,384]{1,0:T(8,128)(2,1)S(1)} %get-tuple-element.63.refs_0_, bf16[320,384]{1,0:T(8,128)(2,1)S(1)} %collective-permute-done.29.refs_1_, f32[320,256]{1,0:T(8,128)S(1)} %get-tuple-element.64.refs_2_, ...), custom_call_target="tpu_custom_call" | custom-call | tf_op jit(solution)/shard_map/pallas_call | solution.py:126
  60.6 0.5 collective-permute-done.30.refs_1_
  61.1 1.7 %collective-permute-done.31.refs_2_ = bf16[160,256]{1,0:T(8,128)(2,1)S(1)} collective-permute-done((bf16[160,256]{1,0:T(8,128)(2,1)S(1)}, bf16[160,256]{1,0:T(8,128)(2,1)S(1)}, u32[]{:S(2)}, u32[]{:S(2)}) %collective-permute-start.31) | collective-permute-done | bytes 81952 | tf_op jit(solution)/shard_map/ppermute | solution.py:406
  63.0 0.3 shard_map.83.refs_0_
  63.3 1.3 %collective-permute-done.33.refs_1_ = bf16[640,256]{1,0:T(8,128)(2,1)S(1)} collective-permute-done((bf16[640,256]{1,0:T(8,128)(2,1)S(1)}, bf16[640,256]{1,0:T(8,128)(2,1)S(1)}, u32[]{:S(2)}, u32[]{:S(2)}) %collective-permute-start.33) | collective-permute-done | bytes 327712 | tf_op jit(solution)/shard_map/ppermute | solution.py:406
  64.6 1.5 %shard_map.84 = f32[3,320,320]{2,1,0:T(8,128)} custom-call(f32[2,256,320]{2,1,0:T(8,128)S(1)} %shard_map.83.refs_0_, bf16[640,256]{1,0:T(8,128)(2,1)S(1)} %collective-permute-done.33.refs_1_), custom_call_target="tpu_custom_call" | custom-call | tf_op jit(solution)/shard_map/pallas_call | solution.py:126
  (45 shorter events, 1.2 us)
Async XLA Ops:
  0.6 16.2 %copy-start.1 = (bf16[3,320,320]{2,1,0:T(8,128)(2,1)S(1)}, bf16[3,320,320]{2,1,0:T(8,128)(2,1)}, u32[]{:S(2)}) copy-start(bf16[3,320,320]{2,1,0:T(8,128)(2,1)} %refs_3_.1) | copy-start | bytes 1843204
  2.1 9.2 %collective-permute-start = (bf16[80,384]{1,0:T(8,128)(2,1)S(1)}, bf16[80,384]{1,0:T(8,128)(2,1)S(1)}, u32[]{:S(2)}, u32[]{:S(2)}) collective-permute-start(bf16[80,384]{1,0:T(8,128)(2,1)S(1)} %get-tuple-element.37), channel_id=1, source_target_pairs={{0,1},{1,2},{2,3},{3,0},{4,5},{5,6},{6,7},{7,4},{8,9},{9,10},{10,1... | collective-permute-start | bytes 184328 | tf_op jit(solution)/shard_map/ppermute | solution.py:412
  5.2 8.3 %collective-permute-start.1 = (bf16[80,384]{1,0:T(8,128)(2,1)S(1)}, bf16[80,384]{1,0:T(8,128)(2,1)S(1)}, u32[]{:S(2)}, u32[]{:S(2)}) collective-permute-start(bf16[80,384]{1,0:T(8,128)(2,1)S(1)} %get-tuple-element.37), channel_id=1, source_target_pairs={{0,2},{1,3},{2,0},{3,1},{4,6},{5,7},{6,4},{7,5},{8,10},{9,11},{10,... | collective-permute-start | bytes 184328 | tf_op jit(solution)/shard_map/ppermute | solution.py:412
  7.8 6.1 %collective-permute-start.2 = (bf16[80,384]{1,0:T(8,128)(2,1)S(1)}, bf16[80,384]{1,0:T(8,128)(2,1)S(1)}, u32[]{:S(2)}, u32[]{:S(2)}) collective-permute-start(bf16[80,384]{1,0:T(8,128)(2,1)S(1)} %get-tuple-element.37), channel_id=1, source_target_pairs={{0,3},{1,0},{2,1},{3,2},{4,7},{5,4},{6,5},{7,6},{8,11},{9,8},{10,9... | collective-permute-start | bytes 184328 | tf_op jit(solution)/shard_map/ppermute | solution.py:412
  9.1 5.3 %collective-permute-start.6 = (bf16[320,256]{1,0:T(8,128)(2,1)S(1)}, bf16[320,256]{1,0:T(8,128)(2,1)S(1)}, u32[]{:S(2)}, u32[]{:S(2)}) collective-permute-start(bf16[320,256]{1,0:T(8,128)(2,1)S(1)} %get-tuple-element.40.refs_1_), channel_id=1, source_target_pairs={{0,8},{4,12},{8,0},{12,4},{16,24},{20,28},{24,16},{28,20},{1,9},{5... | collective-permute-start | bytes 491528 | tf_op jit(solution)/shard_map/ppermute | solution.py:406
  10.6 5.4 %collective-permute-start.11 = (bf16[320,256]{1,0:T(8,128)(2,1)S(1)}, bf16[320,256]{1,0:T(8,128)(2,1)S(1)}, u32[]{:S(2)}, u32[]{:S(2)}) collective-permute-start(bf16[320,256]{1,0:T(8,128)(2,1)S(1)} %get-tuple-element.38.refs_1_), channel_id=1, source_target_pairs={{0,0},{1,2},{2,1},{3,3},{4,4},{5,6},{6,5},{7,7},{8,8},{9,10},{10,9... | collective-permute-start | bytes 491528 | tf_op jit(solution)/shard_map/ppermute | solution.py:421
  11.3 5.5 %collective-permute-start.10 = (bf16[320,256]{1,0:T(8,128)(2,1)S(1)}, bf16[320,256]{1,0:T(8,128)(2,1)S(1)}, u32[]{:S(2)}, u32[]{:S(2)}) collective-permute-start(bf16[320,256]{1,0:T(8,128)(2,1)S(1)} %get-tuple-element.38.refs_1_), channel_id=1, source_target_pairs={{0,1},{1,0},{2,3},{3,2},{4,5},{5,4},{6,7},{7,6},{8,9},{9,8},{10,11... | collective-permute-start | bytes 491528 | tf_op jit(solution)/shard_map/ppermute | solution.py:421
  13.5 5.3 %collective-permute-start.4 = (bf16[320,256]{1,0:T(8,128)(2,1)S(1)}, bf16[320,256]{1,0:T(8,128)(2,1)S(1)}, u32[]{:S(2)}, u32[]{:S(2)}) collective-permute-start(bf16[320,256]{1,0:T(8,128)(2,1)S(1)} %get-tuple-element.38.refs_1_), channel_id=1, source_target_pairs={{0,8},{4,12},{8,0},{12,4},{16,24},{20,28},{24,16},{28,20},{1,9},{5... | collective-permute-start | bytes 491528 | tf_op jit(solution)/shard_map/ppermute | solution.py:406
  13.9 7.4 %collective-permute-start.5 = (bf16[320,256]{1,0:T(8,128)(2,1)S(1)}, bf16[320,256]{1,0:T(8,128)(2,1)S(1)}, u32[]{:S(2)}, u32[]{:S(2)}) collective-permute-start(bf16[320,256]{1,0:T(8,128)(2,1)S(1)} %get-tuple-element.40.refs_1_), channel_id=1, source_target_pairs={{0,4},{4,0},{8,12},{12,8},{16,20},{20,16},{24,28},{28,24},{1,5},{5... | collective-permute-start | bytes 491528 | tf_op jit(solution)/shard_map/ppermute | solution.py:406
  14.5 6.6 %collective-permute-start.3 = (bf16[240,384]{1,0:T(8,128)(2,1)S(1)}, bf16[240,384]{1,0:T(8,128)(2,1)S(1)}, u32[]{:S(2)}, u32[]{:S(2)}) collective-permute-start(bf16[240,384]{1,0:T(8,128)(2,1)S(1)} %pad_maximum_fusion), channel_id=1, source_target_pairs={{0,16},{4,20},{8,24},{12,28},{16,0},{20,4},{24,8},{28,12},{1,17},{... | collective-permute-start | bytes 552968 | tf_op jit(solution)/shard_map/ppermute | solution.py:406
  16.0 5.4 %collective-permute-start.7 = (bf16[320,256]{1,0:T(8,128)(2,1)S(1)}, bf16[320,256]{1,0:T(8,128)(2,1)S(1)}, u32[]{:S(2)}, u32[]{:S(2)}) collective-permute-start(bf16[320,256]{1,0:T(8,128)(2,1)S(1)} %collective-permute-done.6.refs_3_), channel_id=1, source_target_pairs={{0,4},{4,0},{8,12},{12,8},{16,20},{20,16},{24,28},{28,24},{1,5},{5... | collective-permute-start | bytes 491528 | tf_op jit(solution)/shard_map/ppermute | solution.py:406
  17.3 5.4 %collective-permute-start.12 = (bf16[160,256]{1,0:T(8,128)(2,1)S(1)}, bf16[160,256]{1,0:T(8,128)(2,1)S(1)}, u32[]{:S(2)}, u32[]{:S(2)}) collective-permute-start(bf16[160,256]{1,0:T(8,128)(2,1)S(1)} %get-tuple-element.43), channel_id=1, source_target_pairs={{0,8},{4,12},{8,0},{12,4},{16,24},{20,28},{24,16},{28,20},{1,9},{5... | collective-permute-start | bytes 245768 | tf_op jit(solution)/shard_map/ppermute | solution.py:406
  18.9 3.8 %collective-permute-start.13 = (bf16[80,256]{1,0:T(8,128)(2,1)S(1)}, bf16[80,256]{1,0:T(8,128)(2,1)S(1)}, u32[]{:S(2)}, u32[]{:S(2)}) collective-permute-start(bf16[80,256]{1,0:T(8,128)(2,1)S(1)} %get-tuple-element.44), channel_id=1, source_target_pairs={{0,4},{4,0},{8,12},{12,8},{16,20},{20,16},{24,28},{28,24},{1,5},{5... | collective-permute-start | bytes 122888 | tf_op jit(solution)/shard_map/ppermute | solution.py:406
  22.7 8.9 %collective-permute-start.15 = (bf16[640,256]{1,0:T(8,128)(2,1)S(1)}, bf16[640,256]{1,0:T(8,128)(2,1)S(1)}, u32[]{:S(2)}, u32[]{:S(2)}) collective-permute-start(bf16[640,256]{1,0:T(8,128)(2,1)S(1)} %shard_map.71.refs_5_), channel_id=1, source_target_pairs={{0,8},{4,12},{8,0},{12,4},{16,24},{20,28},{24,16},{28,20},{1,9},{5... | collective-permute-start | bytes 983048 | tf_op jit(solution)/shard_map/ppermute | solution.py:406
  24.4 1.2 %collective-permute-start.18 = (bf16[80,256]{1,0:T(8,128)(2,1)S(1)}, bf16[80,256]{1,0:T(8,128)(2,1)S(1)}, u32[]{:S(2)}, u32[]{:S(2)}) collective-permute-start(bf16[80,256]{1,0:T(8,128)(2,1)S(1)} %slice.4), channel_id=1, source_target_pairs={{0,4},{4,0},{8,12},{12,8},{16,20},{20,16},{24,28},{28,24},{1,5},{5... | collective-permute-start | bytes 122888 | tf_op jit(solution)/shard_map/ppermute | solution.py:406
  27.0 8.1 %collective-permute-start.19 = (bf16[320,384]{1,0:T(8,128)(2,1)S(1)}, bf16[320,384]{1,0:T(8,128)(2,1)S(1)}, u32[]{:S(2)}, u32[]{:S(2)}) collective-permute-start(bf16[320,384]{1,0:T(8,128)(2,1)S(1)} %get-tuple-element.51), channel_id=1, source_target_pairs={{0,16},{4,20},{8,24},{12,28},{16,0},{20,4},{24,8},{28,12},{1,17},{... | collective-permute-start | bytes 737288 | tf_op jit(solution)/shard_map/ppermute | solution.py:406
  28.6 7.9 %collective-permute-start.14 = (bf16[640,256]{1,0:T(8,128)(2,1)S(1)}, bf16[640,256]{1,0:T(8,128)(2,1)S(1)}, u32[]{:S(2)}, u32[]{:S(2)}) collective-permute-start(bf16[640,256]{1,0:T(8,128)(2,1)S(1)} %shard_map.71.refs_5_), channel_id=1, source_target_pairs={{0,4},{4,0},{8,12},{12,8},{16,20},{20,16},{24,28},{28,24},{1,5},{5... | collective-permute-start | bytes 983048 | tf_op jit(solution)/shard_map/ppermute | solution.py:406
  31.6 4.9 %collective-permute-start.16 = (bf16[640,256]{1,0:T(8,128)(2,1)S(1)}, bf16[640,256]{1,0:T(8,128)(2,1)S(1)}, u32[]{:S(2)}, u32[]{:S(2)}) collective-permute-start(bf16[640,256]{1,0:T(8,128)(2,1)S(1)} %collective-permute-done.15.refs_7_), channel_id=1, source_target_pairs={{0,4},{4,0},{8,12},{12,8},{16,20},{20,16},{24,28},{28,24},{1,5},{5... | collective-permute-start | bytes 983048 | tf_op jit(solution)/shard_map/ppermute | solution.py:406
  31.6 7.3 %collective-permute-start.24 = (bf16[640,256]{1,0:T(8,128)(2,1)S(1)}, bf16[640,256]{1,0:T(8,128)(2,1)S(1)}, u32[]{:S(2)}, u32[]{:S(2)}) collective-permute-start(bf16[640,256]{1,0:T(8,128)(2,1)S(1)} %get-tuple-element.61), channel_id=1, source_target_pairs={{0,4},{4,0},{8,12},{12,8},{16,20},{20,16},{24,28},{28,24},{1,5},{5... | collective-permute-start | bytes 983048 | tf_op jit(solution)/shard_map/ppermute | solution.py:406
  32.1 3.1 %collective-permute-start.8 = (bf16[320,256]{1,0:T(8,128)(2,1)S(1)}, bf16[320,256]{1,0:T(8,128)(2,1)S(1)}, u32[]{:S(2)}, u32[]{:S(2)}) collective-permute-start(bf16[320,256]{1,0:T(8,128)(2,1)S(1)} %get-tuple-element.38.refs_1_), channel_id=1, source_target_pairs={{0,4},{4,0},{8,12},{12,8},{16,20},{20,16},{24,28},{28,24},{1,5},{5... | collective-permute-start | bytes 491528 | tf_op jit(solution)/shard_map/ppermute | solution.py:406
  35.1 1.4 %collective-permute-start.9 = (bf16[320,256]{1,0:T(8,128)(2,1)S(1)}, bf16[320,256]{1,0:T(8,128)(2,1)S(1)}, u32[]{:S(2)}, u32[]{:S(2)}) collective-permute-start(bf16[320,256]{1,0:T(8,128)(2,1)S(1)} %collective-permute-done.4.refs_5_.refs_3_), channel_id=1, source_target_pairs={{0,4},{4,0},{8,12},{12,8},{16,20},{20,16},{24,28},{28,24},{1,5},{5... | collective-permute-start | bytes 491528 | tf_op jit(solution)/shard_map/ppermute | solution.py:406
  35.2 5.8 %collective-permute-start.20 = (bf16[160,384]{1,0:T(8,128)(2,1)S(1)}, bf16[160,384]{1,0:T(8,128)(2,1)S(1)}, u32[]{:S(2)}, u32[]{:S(2)}) collective-permute-start(bf16[160,384]{1,0:T(8,128)(2,1)S(1)} %get-tuple-element.53), channel_id=1, source_target_pairs={{0,1},{1,0},{2,3},{3,2},{4,5},{5,4},{6,7},{7,6},{8,9},{9,8},{10,11... | collective-permute-start | bytes 368648 | tf_op jit(solution)/shard_map/ppermute | solution.py:409
  37.2 21.6 %copy-start = (bf16[1,1,16,16,320]{4,3,2,1,0:T(8,128)(2,1)S(1)}, bf16[1,1,16,16,320]{4,3,2,1,0:T(8,128)(2,1)}, u32[]{:S(2)}) copy-start(bf16[1,1,16,16,320]{4,3,2,1,0:T(8,128)(2,1)} %param.5) | copy-start | bytes 491524
  37.3 4.6 %collective-permute-start.17 = (bf16[160,256]{1,0:T(8,128)(2,1)S(1)}, bf16[160,256]{1,0:T(8,128)(2,1)S(1)}, u32[]{:S(2)}, u32[]{:S(2)}) collective-permute-start(bf16[160,256]{1,0:T(8,128)(2,1)S(1)} %get-tuple-element.47), channel_id=1, source_target_pairs={{0,16},{4,20},{8,24},{12,28},{16,0},{20,4},{24,8},{28,12},{1,17},{... | collective-permute-start | bytes 245768 | tf_op jit(solution)/shard_map/ppermute | solution.py:406
  38.9 9.6 %collective-permute-start.25 = (bf16[320,256]{1,0:T(8,128)(2,1)S(1)}, bf16[320,256]{1,0:T(8,128)(2,1)S(1)}, u32[]{:S(2)}, u32[]{:S(2)}) collective-permute-start(bf16[320,256]{1,0:T(8,128)(2,1)S(1)} %get-tuple-element.62), channel_id=1, source_target_pairs={{0,8},{4,12},{8,0},{12,4},{16,24},{20,28},{24,16},{28,20},{1,9},{5... | collective-permute-start | bytes 491528 | tf_op jit(solution)/shard_map/ppermute | solution.py:406
  41.8 5.1 %collective-permute-start.21 = (bf16[160,256]{1,0:T(8,128)(2,1)S(1)}, bf16[160,256]{1,0:T(8,128)(2,1)S(1)}, u32[]{:S(2)}, u32[]{:S(2)}) collective-permute-start(bf16[160,256]{1,0:T(8,128)(2,1)S(1)} %get-tuple-element.56), channel_id=1, source_target_pairs={{0,1},{1,0},{2,3},{3,2},{4,5},{5,4},{6,7},{7,6},{8,9},{9,8},{10,11... | collective-permute-start | bytes 245768 | tf_op jit(solution)/shard_map/ppermute | solution.py:409
  42.8 5.8 %collective-permute-start.23 = (bf16[80,384]{1,0:T(8,128)(2,1)S(1)}, bf16[80,384]{1,0:T(8,128)(2,1)S(1)}, u32[]{:S(2)}, u32[]{:S(2)}) collective-permute-start(bf16[80,384]{1,0:T(8,128)(2,1)S(1)} %get-tuple-element.59), channel_id=1, source_target_pairs={{0,2},{1,3},{2,0},{3,1},{4,6},{5,7},{6,4},{7,5},{8,10},{9,11},{10,... | collective-permute-start | bytes 184328 | tf_op jit(solution)/shard_map/ppermute | solution.py:409
  47.0 8.2 %collective-permute-start.22 = (bf16[160,256]{1,0:T(8,128)(2,1)S(1)}, bf16[160,256]{1,0:T(8,128)(2,1)S(1)}, u32[]{:S(2)}, u32[]{:S(2)}) collective-permute-start(bf16[160,256]{1,0:T(8,128)(2,1)S(1)} %get-tuple-element.58), channel_id=1, source_target_pairs={{0,2},{1,3},{2,0},{3,1},{4,6},{5,7},{6,4},{7,5},{8,10},{9,11},{10,... | collective-permute-start | bytes 245768 | tf_op jit(solution)/shard_map/ppermute | solution.py:409
  48.6 5.2 %collective-permute-start.26 = (bf16[80,384]{1,0:T(8,128)(2,1)S(1)}, bf16[80,384]{1,0:T(8,128)(2,1)S(1)}, u32[]{:S(2)}, u32[]{:S(2)}) collective-permute-start(bf16[80,384]{1,0:T(8,128)(2,1)S(1)} %shard_map.79.refs_2_), channel_id=1, source_target_pairs={{0,24},{4,28},{8,16},{12,20},{16,8},{20,12},{24,0},{28,4},{1,25},{... | collective-permute-start | bytes 184328 | tf_op jit(solution)/shard_map/ppermute | solution.py:406
  50.4 4.2 %collective-permute-start.27 = (bf16[80,384]{1,0:T(8,128)(2,1)S(1)}, bf16[80,384]{1,0:T(8,128)(2,1)S(1)}, u32[]{:S(2)}, u32[]{:S(2)}) collective-permute-start(bf16[80,384]{1,0:T(8,128)(2,1)S(1)} %shard_map.79.refs_2_), channel_id=1, source_target_pairs={{0,16},{4,20},{8,24},{12,28},{16,0},{20,4},{24,8},{28,12},{1,17},{... | collective-permute-start | bytes 184328 | tf_op jit(solution)/shard_map/ppermute | solution.py:406
  50.9 4.2 %collective-permute-start.28 = (bf16[80,384]{1,0:T(8,128)(2,1)S(1)}, bf16[80,384]{1,0:T(8,128)(2,1)S(1)}, u32[]{:S(2)}, u32[]{:S(2)}) collective-permute-start(bf16[80,384]{1,0:T(8,128)(2,1)S(1)} %shard_map.79.refs_2_), channel_id=1, source_target_pairs={{0,8},{4,12},{8,0},{12,4},{16,24},{20,28},{24,16},{28,20},{1,9},{5... | collective-permute-start | bytes 184328 | tf_op jit(solution)/shard_map/ppermute | solution.py:406
  55.2 3.6 %collective-permute-start.29 = (bf16[320,384]{1,0:T(8,128)(2,1)S(1)}, bf16[320,384]{1,0:T(8,128)(2,1)S(1)}, u32[]{:S(2)}, u32[]{:S(2)}) collective-permute-start(bf16[320,384]{1,0:T(8,128)(2,1)S(1)} %get-tuple-element.63.refs_0_), channel_id=1, source_target_pairs={{0,4},{4,0},{8,12},{12,8},{16,20},{20,16},{24,28},{28,24},{1,5},{5... | collective-permute-start | bytes 737288 | tf_op jit(solution)/shard_map/ppermute | solution.py:406
  55.3 5.8 %collective-permute-start.30 = (bf16[160,256]{1,0:T(8,128)(2,1)S(1)}, bf16[160,256]{1,0:T(8,128)(2,1)S(1)}, u32[]{:S(2)}, u32[]{:S(2)}) collective-permute-start(bf16[160,256]{1,0:T(8,128)(2,1)S(1)} %get-tuple-element.67.refs_0_), channel_id=1, source_target_pairs={{0,24},{4,28},{8,16},{12,20},{16,8},{20,12},{24,0},{28,4},{1,25},{... | collective-permute-start | bytes 245768 | tf_op jit(solution)/shard_map/ppermute | solution.py:406
  57.5 5.3 %collective-permute-start.31 = (bf16[160,256]{1,0:T(8,128)(2,1)S(1)}, bf16[160,256]{1,0:T(8,128)(2,1)S(1)}, u32[]{:S(2)}, u32[]{:S(2)}) collective-permute-start(bf16[160,256]{1,0:T(8,128)(2,1)S(1)} %get-tuple-element.67.refs_0_), channel_id=1, source_target_pairs={{0,16},{4,20},{8,24},{12,28},{16,0},{20,4},{24,8},{28,12},{1,17},{... | collective-permute-start | bytes 245768 | tf_op jit(solution)/shard_map/ppermute | solution.py:406
  58.0 4.9 %collective-permute-start.32 = (bf16[160,256]{1,0:T(8,128)(2,1)S(1)}, bf16[160,256]{1,0:T(8,128)(2,1)S(1)}, u32[]{:S(2)}, u32[]{:S(2)}) collective-permute-start(bf16[160,256]{1,0:T(8,128)(2,1)S(1)} %get-tuple-element.67.refs_0_), channel_id=1, source_target_pairs={{0,8},{4,12},{8,0},{12,4},{16,24},{20,28},{24,16},{28,20},{1,9},{5... | collective-permute-start | bytes 245768 | tf_op jit(solution)/shard_map/ppermute | solution.py:406
  62.9 1.7 %collective-permute-start.33 = (bf16[640,256]{1,0:T(8,128)(2,1)S(1)}, bf16[640,256]{1,0:T(8,128)(2,1)S(1)}, u32[]{:S(2)}, u32[]{:S(2)}) collective-permute-start(bf16[640,256]{1,0:T(8,128)(2,1)S(1)} %shard_map.82.refs_0_), channel_id=1, source_target_pairs={{0,4},{4,0},{8,12},{12,8},{16,20},{20,16},{24,28},{28,24},{1,5},{5... | collective-permute-start | bytes 983048 | tf_op jit(solution)/shard_map/ppermute | solution.py:406

commit v8 on v7

--- a/solution.py
+++ b/solution.py
@@ -372,28 +372,31 @@
     token_ref[...] = jnp.zeros_like(token_ref)
 
 
-def time_turn(plan, ref, out_ref, held):
+def turned_part(plan, pair, ref, held):
     _, high, _ = plan.place()
     size = plan.thalf
+    first = plan.chips.index(2 * pair) * size
+    second = plan.chips.index(plan.group + 2 * pair) * size
     near = pl.ds(pl.multiple_of(high * size, 16), size)
     far = pl.ds(pl.multiple_of((1 - high) * size, 16), size)
+    held[near, :] = ref[first : first + size, :].astype(F32)
+    held[far, :] = ref[second : second + size, :].astype(F32)
+    return held[...].T * plan.factor
+
+
+def time_turn(plan, ref, out_ref, held):
     for pair in range(2):
-        first = plan.chips.index(2 * pair) * size
-        second = plan.chips.index(plan.group + 2 * pair) * size
-        held[near, :] = ref[first : first + size, :].astype(F32)
-        held[far, :] = ref[second : second + size, :].astype(F32)
-        out_ref[pair] = held[...].T * plan.factor
-
-
-def time_end(plan, here_ref, core_ref, out_ref, held, turned):
+        out_ref[pair] = turned_part(plan, pair, ref, held)
+
+
+def time_end(plan, here_ref, core_ref, out_ref, held):
     low, _, _ = plan.place()
     slab = plan.slab
-    time_turn(plan, core_ref, turned, held)
-    for core, ref in enumerate((here_ref, turned)):
-        for pair in range(2):
+    for pair in range(2):
+        for core, turned in enumerate((here_ref[pair], turned_part(plan, pair, core_ref, held))):
             for k in range(3):
                 here = pl.ds(pl.multiple_of((low ^ (2 * pair + core)) * slab, 16), slab)
-                out_ref[k, here, :] = ref[pair, k * slab : (k + 1) * slab, :]
+                out_ref[k, here, :] = turned[k * slab : (k + 1) * slab, :]
 
 
 def per_device(plan, frames, cotangent, w_space, w_time):
@@ -560,7 +563,7 @@
         [((3, chans, chans), F32)],
         t_here,
         swap(t_all, 1),
-        scratch=[held, pltpu.VMEM(turned, F32)],
+        scratch=[held],
     )
     return f_out.reshape(frames.shape), jnp.transpose(s_out, (1, 0, 2)), t_out
 

time: 66.3 us -> 66.2 us (level)
  no operation moved by 1% of the time
where the time goes in v8:
time: 66.2 us; the launch traced here: 66.1 us
  starting transfers between devices  34.1 us (52%)
  waiting for transfers between devices  21.7 us (33%)
  Pallas kernels  9.37 us (14%)
  between operations  0.86 us (1%)
    ppermute x25, starting transfers between devices, swap(): lax.ppermute(value, 'clip', [(i, i ^ distance) for i in range(plan.clips)])  18.5 us
    ppermute x25, waiting for transfers between devices, swap(): lax.ppermute(value, 'clip', [(i, i ^ distance) for i in range(plan.clips)])  17.6 us
    pallas_call x17, Pallas kernels, call(): pl.pallas_call(body, out_shape=tuple((jax.ShapeDtypeStruct(shape, dtype)...  7.89 us
    ppermute x3, starting transfers between devices, turn(): lax.ppermute(value, 'seq', [(i, (i + k) % seqs) for i in range(seqs)])  7.01 us
    ppermute x4, starting transfers between devices, trade(): return lax.ppermute(value, 'seq', [(i, i ^ distance) for i in range(seqs)])  5.78 us
    ppermute x4, waiting for transfers between devices, trade(): return lax.ppermute(value, 'seq', [(i, i ^ distance) for i in range(seqs)])  3.23 us
    ppermute x2, starting transfers between devices, neighbours(): found.append(lax.ppermute(value, 'seq', list(other.items())))  2.86 us
    pallas_call x1, Pallas kernels, per_device(): pl.pallas_call(part(prepare), out_shape=tuple((jax.ShapeDtypeStruct(shape...  1.47 us
  transfers between devices with their start and end apart: 34, of which 17 were waited for; matrix products, arithmetic and copies ran while one was open for 0% of the time, Pallas kernels for 10%

profile of v8, /device:TPU:0, one launch (start us, length us, event | category | flops | bytes accessed | tf_op | source)
XLA Modules:
  0.0 66.1 jit_solution(385256385641677495)
XLA Ops:
  0.6 1.5 %shard_map.67 = (bf16[320,256]{1,0:T(8,128)(2,1)S(1)}, bf16[320,256]{1,0:T(8,128)(2,1)S(1)}, bf16[80,768]{1,0:T(8,128)(2,1)S(1)}, bf16[80,384]{1,0:T(8,128)(2,1)S(1)}) custom-call(bf16[256,320]{1,0:T(8,128)(2,1)} %bitcast.8, bf16[256,320]{1,0:T(8,128)(2,1)} %bitcast.5, bf16[9,80,320]{2,1,0:T(8,128)(2,1)} %bitcast.7), custom_call_target="tpu_custom_call" | custom-call | tf_op jit(solution)/shard_map/pallas_call | solution.py:439
  2.1 3.1 %collective-permute-start = (bf16[80,384]{1,0:T(8,128)(2,1)S(1)}, bf16[80,384]{1,0:T(8,128)(2,1)S(1)}, u32[]{:S(2)}, u32[]{:S(2)}) collective-permute-start(bf16[80,384]{1,0:T(8,128)(2,1)S(1)} %get-tuple-element.37), channel_id=1, source_target_pairs={{0,1},{1,2},{2,3},{3,0},{4,5},{5,6},{6,7},{7,4},{8,9},{9,10},{10,1... | collective-permute-start | bytes 184328 | tf_op jit(solution)/shard_map/ppermute | solution.py:415
  5.2 2.6 %collective-permute-start.1 = (bf16[80,384]{1,0:T(8,128)(2,1)S(1)}, bf16[80,384]{1,0:T(8,128)(2,1)S(1)}, u32[]{:S(2)}, u32[]{:S(2)}) collective-permute-start(bf16[80,384]{1,0:T(8,128)(2,1)S(1)} %get-tuple-element.37), channel_id=1, source_target_pairs={{0,2},{1,3},{2,0},{3,1},{4,6},{5,7},{6,4},{7,5},{8,10},{9,11},{10,... | collective-permute-start | bytes 184328 | tf_op jit(solution)/shard_map/ppermute | solution.py:415
  7.8 1.3 %collective-permute-start.2 = (bf16[80,384]{1,0:T(8,128)(2,1)S(1)}, bf16[80,384]{1,0:T(8,128)(2,1)S(1)}, u32[]{:S(2)}, u32[]{:S(2)}) collective-permute-start(bf16[80,384]{1,0:T(8,128)(2,1)S(1)} %get-tuple-element.37), channel_id=1, source_target_pairs={{0,3},{1,0},{2,1},{3,2},{4,7},{5,4},{6,5},{7,6},{8,11},{9,8},{10,9... | collective-permute-start | bytes 184328 | tf_op jit(solution)/shard_map/ppermute | solution.py:415
  9.1 1.5 %collective-permute-start.6 = (bf16[320,256]{1,0:T(8,128)(2,1)S(1)}, bf16[320,256]{1,0:T(8,128)(2,1)S(1)}, u32[]{:S(2)}, u32[]{:S(2)}) collective-permute-start(bf16[320,256]{1,0:T(8,128)(2,1)S(1)} %get-tuple-element.40.refs_1_), channel_id=1, source_target_pairs={{0,8},{4,12},{8,0},{12,4},{16,24},{20,28},{24,16},{28,20},{1,9},{5... | collective-permute-start | bytes 491528 | tf_op jit(solution)/shard_map/ppermute | solution.py:409
  10.6 0.7 collective-permute-start.11
  11.3 2.2 %collective-permute-start.10 = (bf16[320,256]{1,0:T(8,128)(2,1)S(1)}, bf16[320,256]{1,0:T(8,128)(2,1)S(1)}, u32[]{:S(2)}, u32[]{:S(2)}) collective-permute-start(bf16[320,256]{1,0:T(8,128)(2,1)S(1)} %get-tuple-element.38.refs_1_), channel_id=1, source_target_pairs={{0,1},{1,0},{2,3},{3,2},{4,5},{5,4},{6,7},{7,6},{8,9},{9,8},{10,11... | collective-permute-start | bytes 491528 | tf_op jit(solution)/shard_map/ppermute | solution.py:424
  13.5 0.4 collective-permute-start.4
  13.9 0.5 collective-permute-done.6.refs_3_
  14.5 1.5 %collective-permute-start.3 = (bf16[240,384]{1,0:T(8,128)(2,1)S(1)}, bf16[240,384]{1,0:T(8,128)(2,1)S(1)}, u32[]{:S(2)}, u32[]{:S(2)}) collective-permute-start(bf16[240,384]{1,0:T(8,128)(2,1)S(1)} %pad_maximum_fusion), channel_id=1, source_target_pairs={{0,16},{4,20},{8,24},{12,28},{16,0},{20,4},{24,8},{28,12},{1,17},{... | collective-permute-start | bytes 552968 | tf_op jit(solution)/shard_map/ppermute | solution.py:409
  16.0 0.8 %collective-permute-done.10 = bf16[320,256]{1,0:T(8,128)(2,1)S(1)} collective-permute-done((bf16[320,256]{1,0:T(8,128)(2,1)S(1)}, bf16[320,256]{1,0:T(8,128)(2,1)S(1)}, u32[]{:S(2)}, u32[]{:S(2)}) %collective-permute-start.10) | collective-permute-done | bytes 163872 | tf_op jit(solution)/shard_map/ppermute | solution.py:424
  16.8 0.4 shard_map.70
  17.3 1.6 %collective-permute-start.12 = (bf16[160,256]{1,0:T(8,128)(2,1)S(1)}, bf16[160,256]{1,0:T(8,128)(2,1)S(1)}, u32[]{:S(2)}, u32[]{:S(2)}) collective-permute-start(bf16[160,256]{1,0:T(8,128)(2,1)S(1)} %get-tuple-element.43), channel_id=1, source_target_pairs={{0,8},{4,12},{8,0},{12,4},{16,24},{20,28},{24,16},{28,20},{1,9},{5... | collective-permute-start | bytes 245768 | tf_op jit(solution)/shard_map/ppermute | solution.py:409
  19.1 2.0 %collective-permute-done.3.refs_4_ = bf16[240,384]{1,0:T(8,128)(2,1)S(1)} collective-permute-done((bf16[240,384]{1,0:T(8,128)(2,1)S(1)}, bf16[240,384]{1,0:T(8,128)(2,1)S(1)}, u32[]{:S(2)}, u32[]{:S(2)}) %collective-permute-start.3) | collective-permute-done | bytes 184352 | tf_op jit(solution)/shard_map/ppermute | solution.py:409
  21.3 1.3 %shard_map.69 = (bf16[320,1024]{1,0:T(8,128)(2,1)S(1)}, bf16[80,1024]{1,0:T(8,128)(2,1)S(1)}, f32[80,1024]{1,0:T(8,128)S(1)}) custom-call(bf16[768,320]{1,0:T(8,128)(2,1)S(1)} %get-tuple-element.39.refs_0_, bf16[320,256]{1,0:T(8,128)(2,1)S(1)} %get-tuple-element.40.refs_1_, bf16[320,256]{1,0:T(8,128)(2,1)S(1)} %collective-permute-done.5.refs_2_, ...), custom_call_target="tpu_custom_call" | custom-call | tf_op jit(solution)/shard_map/pallas_call | solution.py:126
  22.7 1.7 %collective-permute-start.15 = (bf16[640,256]{1,0:T(8,128)(2,1)S(1)}, bf16[640,256]{1,0:T(8,128)(2,1)S(1)}, u32[]{:S(2)}, u32[]{:S(2)}) collective-permute-start(bf16[640,256]{1,0:T(8,128)(2,1)S(1)} %shard_map.71.refs_5_), channel_id=1, source_target_pairs={{0,8},{4,12},{8,0},{12,4},{16,24},{20,28},{24,16},{28,20},{1,9},{5... | collective-permute-start | bytes 983048 | tf_op jit(solution)/shard_map/ppermute | solution.py:409
  24.4 1.2 %collective-permute-done.18.refs_6_ = bf16[80,256]{1,0:T(8,128)(2,1)S(1)} collective-permute-done((bf16[80,256]{1,0:T(8,128)(2,1)S(1)}, bf16[80,256]{1,0:T(8,128)(2,1)S(1)}, u32[]{:S(2)}, u32[]{:S(2)}) %collective-permute-start.18) | collective-permute-done | bytes 40992 | tf_op jit(solution)/shard_map/ppermute | solution.py:409
  25.6 1.4 %shard_map.73 = (bf16[320,384]{1,0:T(8,128)(2,1)S(1)}, f32[320,384]{1,0:T(8,128)S(1)}, bf16[640,256]{1,0:T(8,128)(2,1)S(1)}, f32[640,256]{1,0:T(8,128)S(1)}) custom-call(bf16[320,768]{1,0:T(8,128)(2,1)S(1)} %get-tuple-element.42.refs_2_.refs_0_, bf16[320,1024]{1,0:T(8,128)(2,1)S(1)} %get-tuple-element.45.refs_5_.refs_1_, ...), custom_call_target="tpu_custom_call" | custom-call | tf_op jit(solution)/shard_map/pallas_call | solution.py:126
  27.0 1.6 %collective-permute-start.19 = (bf16[320,384]{1,0:T(8,128)(2,1)S(1)}, bf16[320,384]{1,0:T(8,128)(2,1)S(1)}, u32[]{:S(2)}, u32[]{:S(2)}) collective-permute-start(bf16[320,384]{1,0:T(8,128)(2,1)S(1)} %get-tuple-element.51), channel_id=1, source_target_pairs={{0,16},{4,20},{8,24},{12,28},{16,0},{20,4},{24,8},{28,12},{1,17},{... | collective-permute-start | bytes 737288 | tf_op jit(solution)/shard_map/ppermute | solution.py:409
  28.6 3.0 %collective-permute-done.15.refs_7_ = bf16[640,256]{1,0:T(8,128)(2,1)S(1)} collective-permute-done((bf16[640,256]{1,0:T(8,128)(2,1)S(1)}, bf16[640,256]{1,0:T(8,128)(2,1)S(1)}, u32[]{:S(2)}, u32[]{:S(2)}) %collective-permute-start.15) | collective-permute-done | bytes 327712 | tf_op jit(solution)/shard_map/ppermute | solution.py:409
  31.6 0.5 collective-permute-start.24
  32.1 3.0 %collective-permute-done.19.refs_1_ = bf16[320,384]{1,0:T(8,128)(2,1)S(1)} collective-permute-done((bf16[320,384]{1,0:T(8,128)(2,1)S(1)}, bf16[320,384]{1,0:T(8,128)(2,1)S(1)}, u32[]{:S(2)}, u32[]{:S(2)}) %collective-permute-start.19) | collective-permute-done | bytes 245792 | tf_op jit(solution)/shard_map/ppermute | solution.py:409
  35.2 0.9 %collective-permute-start.20 = (bf16[160,384]{1,0:T(8,128)(2,1)S(1)}, bf16[160,384]{1,0:T(8,128)(2,1)S(1)}, u32[]{:S(2)}, u32[]{:S(2)}) collective-permute-start(bf16[160,384]{1,0:T(8,128)(2,1)S(1)} %get-tuple-element.53), channel_id=1, source_target_pairs={{0,1},{1,0},{2,3},{3,2},{4,5},{5,4},{6,7},{7,6},{8,9},{9,8},{10,11... | collective-permute-start | bytes 368648 | tf_op jit(solution)/shard_map/ppermute | solution.py:412
  36.1 0.4 collective-permute-done.9.refs_4_
  36.5 0.7 %shard_map.72 = (bf16[160,256]{1,0:T(8,128)(2,1)S(1)}, f32[160,256]{1,0:T(8,128)S(1)}) custom-call(bf16[80,1024]{1,0:T(8,128)(2,1)S(1)} %get-tuple-element.41.refs_0_, bf16[320,256]{1,0:T(8,128)(2,1)S(1)} %get-tuple-element.38.refs_1_, bf16[320,256]{1,0:T(8,128)(2,1)S(1)} %collective-permute-done.8.refs_2_, ...), custom_call_target="tpu_custom_call" | custom-call | tf_op jit(solution)/shard_map/pallas_call | solution.py:126
  37.3 1.6 %collective-permute-start.17 = (bf16[160,256]{1,0:T(8,128)(2,1)S(1)}, bf16[160,256]{1,0:T(8,128)(2,1)S(1)}, u32[]{:S(2)}, u32[]{:S(2)}) collective-permute-start(bf16[160,256]{1,0:T(8,128)(2,1)S(1)} %get-tuple-element.47), channel_id=1, source_target_pairs={{0,16},{4,20},{8,24},{12,28},{16,0},{20,4},{24,8},{28,12},{1,17},{... | collective-permute-start | bytes 245768 | tf_op jit(solution)/shard_map/ppermute | solution.py:409
  38.9 0.6 collective-permute-start.25
  39.5 1.4 %collective-permute-done.20.refs_1_ = bf16[160,384]{1,0:T(8,128)(2,1)S(1)} collective-permute-done((bf16[160,384]{1,0:T(8,128)(2,1)S(1)}, bf16[160,384]{1,0:T(8,128)(2,1)S(1)}, u32[]{:S(2)}, u32[]{:S(2)}) %collective-permute-start.20) | collective-permute-done | bytes 122912 | tf_op jit(solution)/shard_map/ppermute | solution.py:412
  41.0 0.8 %collective-permute-done.17.refs_1_ = bf16[160,256]{1,0:T(8,128)(2,1)S(1)} collective-permute-done((bf16[160,256]{1,0:T(8,128)(2,1)S(1)}, bf16[160,256]{1,0:T(8,128)(2,1)S(1)}, u32[]{:S(2)}, u32[]{:S(2)}) %collective-permute-start.17) | collective-permute-done | bytes 81952 | tf_op jit(solution)/shard_map/ppermute | solution.py:409
  41.8 1.0 %collective-permute-start.21 = (bf16[160,256]{1,0:T(8,128)(2,1)S(1)}, bf16[160,256]{1,0:T(8,128)(2,1)S(1)}, u32[]{:S(2)}, u32[]{:S(2)}) collective-permute-start(bf16[160,256]{1,0:T(8,128)(2,1)S(1)} %get-tuple-element.56), channel_id=1, source_target_pairs={{0,1},{1,0},{2,3},{3,2},{4,5},{5,4},{6,7},{7,6},{8,9},{9,8},{10,11... | collective-permute-start | bytes 245768 | tf_op jit(solution)/shard_map/ppermute | solution.py:412
  42.8 2.4 %collective-permute-start.23 = (bf16[80,384]{1,0:T(8,128)(2,1)S(1)}, bf16[80,384]{1,0:T(8,128)(2,1)S(1)}, u32[]{:S(2)}, u32[]{:S(2)}) collective-permute-start(bf16[80,384]{1,0:T(8,128)(2,1)S(1)} %get-tuple-element.59), channel_id=1, source_target_pairs={{0,2},{1,3},{2,0},{3,1},{4,6},{5,7},{6,4},{7,5},{8,10},{9,11},{10,... | collective-permute-start | bytes 184328 | tf_op jit(solution)/shard_map/ppermute | solution.py:412
  45.2 1.8 %collective-permute-done.21.refs_1_ = bf16[160,256]{1,0:T(8,128)(2,1)S(1)} collective-permute-done((bf16[160,256]{1,0:T(8,128)(2,1)S(1)}, bf16[160,256]{1,0:T(8,128)(2,1)S(1)}, u32[]{:S(2)}, u32[]{:S(2)}) %collective-permute-start.21) | collective-permute-done | bytes 81952 | tf_op jit(solution)/shard_map/ppermute | solution.py:412
  47.0 1.6 %collective-permute-start.22 = (bf16[160,256]{1,0:T(8,128)(2,1)S(1)}, bf16[160,256]{1,0:T(8,128)(2,1)S(1)}, u32[]{:S(2)}, u32[]{:S(2)}) collective-permute-start(bf16[160,256]{1,0:T(8,128)(2,1)S(1)} %get-tuple-element.58), channel_id=1, source_target_pairs={{0,2},{1,3},{2,0},{3,1},{4,6},{5,7},{6,4},{7,5},{8,10},{9,11},{10,... | collective-permute-start | bytes 245768 | tf_op jit(solution)/shard_map/ppermute | solution.py:412
  48.6 1.9 %collective-permute-start.26 = (bf16[80,384]{1,0:T(8,128)(2,1)S(1)}, bf16[80,384]{1,0:T(8,128)(2,1)S(1)}, u32[]{:S(2)}, u32[]{:S(2)}) collective-permute-start(bf16[80,384]{1,0:T(8,128)(2,1)S(1)} %shard_map.79.refs_2_), channel_id=1, source_target_pairs={{0,24},{4,28},{8,16},{12,20},{16,8},{20,12},{24,0},{28,4},{1,25},{... | collective-permute-start | bytes 184328 | tf_op jit(solution)/shard_map/ppermute | solution.py:409
  50.4 0.5 collective-permute-start.27
  50.9 1.2 %collective-permute-start.28 = (bf16[80,384]{1,0:T(8,128)(2,1)S(1)}, bf16[80,384]{1,0:T(8,128)(2,1)S(1)}, u32[]{:S(2)}, u32[]{:S(2)}) collective-permute-start(bf16[80,384]{1,0:T(8,128)(2,1)S(1)} %shard_map.79.refs_2_), channel_id=1, source_target_pairs={{0,8},{4,12},{8,0},{12,4},{16,24},{20,28},{24,16},{28,20},{1,9},{5... | collective-permute-start | bytes 184328 | tf_op jit(solution)/shard_map/ppermute | solution.py:409
  52.1 1.6 %collective-permute-done.26.refs_3_ = bf16[80,384]{1,0:T(8,128)(2,1)S(1)} collective-permute-done((bf16[80,384]{1,0:T(8,128)(2,1)S(1)}, bf16[80,384]{1,0:T(8,128)(2,1)S(1)}, u32[]{:S(2)}, u32[]{:S(2)}) %collective-permute-start.26) | collective-permute-done | bytes 61472 | tf_op jit(solution)/shard_map/ppermute | solution.py:409
  53.8 0.9 %collective-permute-done.27.refs_4_ = bf16[80,384]{1,0:T(8,128)(2,1)S(1)} collective-permute-done((bf16[80,384]{1,0:T(8,128)(2,1)S(1)}, bf16[80,384]{1,0:T(8,128)(2,1)S(1)}, u32[]{:S(2)}, u32[]{:S(2)}) %collective-permute-start.27) | collective-permute-done | bytes 61472 | tf_op jit(solution)/shard_map/ppermute | solution.py:409
  54.7 0.5 collective-permute-done.28.refs_5_
  55.3 2.2 %collective-permute-start.30 = (bf16[160,256]{1,0:T(8,128)(2,1)S(1)}, bf16[160,256]{1,0:T(8,128)(2,1)S(1)}, u32[]{:S(2)}, u32[]{:S(2)}) collective-permute-start(bf16[160,256]{1,0:T(8,128)(2,1)S(1)} %get-tuple-element.67.refs_0_), channel_id=1, source_target_pairs={{0,24},{4,28},{8,16},{12,20},{16,8},{20,12},{24,0},{28,4},{1,25},{... | collective-permute-start | bytes 245768 | tf_op jit(solution)/shard_map/ppermute | solution.py:409
  57.5 0.5 collective-permute-start.31
  58.0 0.8 %collective-permute-start.32 = (bf16[160,256]{1,0:T(8,128)(2,1)S(1)}, bf16[160,256]{1,0:T(8,128)(2,1)S(1)}, u32[]{:S(2)}, u32[]{:S(2)}) collective-permute-start(bf16[160,256]{1,0:T(8,128)(2,1)S(1)} %get-tuple-element.67.refs_0_), channel_id=1, source_target_pairs={{0,8},{4,12},{8,0},{12,4},{16,24},{20,28},{24,16},{28,20},{1,9},{5... | collective-permute-start | bytes 245768 | tf_op jit(solution)/shard_map/ppermute | solution.py:409
  58.9 1.7 %shard_map.81 = (f32[9,80,320]{2,1,0:T(8,128)}, bf16[256,320]{1,0:T(8,128)(2,1)}, f32[8,128]{1,0:T(8,128)S(1)}) custom-call(bf16[320,384]{1,0:T(8,128)(2,1)S(1)} %get-tuple-element.63.refs_0_, bf16[320,384]{1,0:T(8,128)(2,1)S(1)} %collective-permute-done.29.refs_1_, f32[320,256]{1,0:T(8,128)S(1)} %get-tuple-element.64.refs_2_, ...), custom_call_target="tpu_custom_call" | custom-call | tf_op jit(solution)/shard_map/pallas_call | solution.py:126
  60.6 0.5 collective-permute-done.30.refs_1_
  61.1 1.7 %collective-permute-done.31.refs_2_ = bf16[160,256]{1,0:T(8,128)(2,1)S(1)} collective-permute-done((bf16[160,256]{1,0:T(8,128)(2,1)S(1)}, bf16[160,256]{1,0:T(8,128)(2,1)S(1)}, u32[]{:S(2)}, u32[]{:S(2)}) %collective-permute-start.31) | collective-permute-done | bytes 81952 | tf_op jit(solution)/shard_map/ppermute | solution.py:409
  63.0 0.3 shard_map.83.refs_0_
  63.3 1.3 %collective-permute-done.33.refs_1_ = bf16[640,256]{1,0:T(8,128)(2,1)S(1)} collective-permute-done((bf16[640,256]{1,0:T(8,128)(2,1)S(1)}, bf16[640,256]{1,0:T(8,128)(2,1)S(1)}, u32[]{:S(2)}, u32[]{:S(2)}) %collective-permute-start.33) | collective-permute-done | bytes 327712 | tf_op jit(solution)/shard_map/ppermute | solution.py:409
  64.6 1.4 %shard_map.84 = f32[3,320,320]{2,1,0:T(8,128)} custom-call(f32[2,256,320]{2,1,0:T(8,128)S(1)} %shard_map.83.refs_0_, bf16[640,256]{1,0:T(8,128)(2,1)S(1)} %collective-permute-done.33.refs_1_), custom_call_target="tpu_custom_call" | custom-call | tf_op jit(solution)/shard_map/pallas_call | solution.py:126
  (45 shorter events, 1.2 us)
Async XLA Ops:
  0.6 16.2 %copy-start.1 = (bf16[3,320,320]{2,1,0:T(8,128)(2,1)S(1)}, bf16[3,320,320]{2,1,0:T(8,128)(2,1)}, u32[]{:S(2)}) copy-start(bf16[3,320,320]{2,1,0:T(8,128)(2,1)} %refs_3_.1) | copy-start | bytes 1843204
  2.1 9.2 %collective-permute-start = (bf16[80,384]{1,0:T(8,128)(2,1)S(1)}, bf16[80,384]{1,0:T(8,128)(2,1)S(1)}, u32[]{:S(2)}, u32[]{:S(2)}) collective-permute-start(bf16[80,384]{1,0:T(8,128)(2,1)S(1)} %get-tuple-element.37), channel_id=1, source_target_pairs={{0,1},{1,2},{2,3},{3,0},{4,5},{5,6},{6,7},{7,4},{8,9},{9,10},{10,1... | collective-permute-start | bytes 184328 | tf_op jit(solution)/shard_map/ppermute | solution.py:415
  5.2 8.3 %collective-permute-start.1 = (bf16[80,384]{1,0:T(8,128)(2,1)S(1)}, bf16[80,384]{1,0:T(8,128)(2,1)S(1)}, u32[]{:S(2)}, u32[]{:S(2)}) collective-permute-start(bf16[80,384]{1,0:T(8,128)(2,1)S(1)} %get-tuple-element.37), channel_id=1, source_target_pairs={{0,2},{1,3},{2,0},{3,1},{4,6},{5,7},{6,4},{7,5},{8,10},{9,11},{10,... | collective-permute-start | bytes 184328 | tf_op jit(solution)/shard_map/ppermute | solution.py:415
  7.8 6.1 %collective-permute-start.2 = (bf16[80,384]{1,0:T(8,128)(2,1)S(1)}, bf16[80,384]{1,0:T(8,128)(2,1)S(1)}, u32[]{:S(2)}, u32[]{:S(2)}) collective-permute-start(bf16[80,384]{1,0:T(8,128)(2,1)S(1)} %get-tuple-element.37), channel_id=1, source_target_pairs={{0,3},{1,0},{2,1},{3,2},{4,7},{5,4},{6,5},{7,6},{8,11},{9,8},{10,9... | collective-permute-start | bytes 184328 | tf_op jit(solution)/shard_map/ppermute | solution.py:415
  9.1 5.3 %collective-permute-start.6 = (bf16[320,256]{1,0:T(8,128)(2,1)S(1)}, bf16[320,256]{1,0:T(8,128)(2,1)S(1)}, u32[]{:S(2)}, u32[]{:S(2)}) collective-permute-start(bf16[320,256]{1,0:T(8,128)(2,1)S(1)} %get-tuple-element.40.refs_1_), channel_id=1, source_target_pairs={{0,8},{4,12},{8,0},{12,4},{16,24},{20,28},{24,16},{28,20},{1,9},{5... | collective-permute-start | bytes 491528 | tf_op jit(solution)/shard_map/ppermute | solution.py:409
  10.6 5.4 %collective-permute-start.11 = (bf16[320,256]{1,0:T(8,128)(2,1)S(1)}, bf16[320,256]{1,0:T(8,128)(2,1)S(1)}, u32[]{:S(2)}, u32[]{:S(2)}) collective-permute-start(bf16[320,256]{1,0:T(8,128)(2,1)S(1)} %get-tuple-element.38.refs_1_), channel_id=1, source_target_pairs={{0,0},{1,2},{2,1},{3,3},{4,4},{5,6},{6,5},{7,7},{8,8},{9,10},{10,9... | collective-permute-start | bytes 491528 | tf_op jit(solution)/shard_map/ppermute | solution.py:424
  11.3 5.5 %collective-permute-start.10 = (bf16[320,256]{1,0:T(8,128)(2,1)S(1)}, bf16[320,256]{1,0:T(8,128)(2,1)S(1)}, u32[]{:S(2)}, u32[]{:S(2)}) collective-permute-start(bf16[320,256]{1,0:T(8,128)(2,1)S(1)} %get-tuple-element.38.refs_1_), channel_id=1, source_target_pairs={{0,1},{1,0},{2,3},{3,2},{4,5},{5,4},{6,7},{7,6},{8,9},{9,8},{10,11... | collective-permute-start | bytes 491528 | tf_op jit(solution)/shard_map/ppermute | solution.py:424
  13.5 5.3 %collective-permute-start.4 = (bf16[320,256]{1,0:T(8,128)(2,1)S(1)}, bf16[320,256]{1,0:T(8,128)(2,1)S(1)}, u32[]{:S(2)}, u32[]{:S(2)}) collective-permute-start(bf16[320,256]{1,0:T(8,128)(2,1)S(1)} %get-tuple-element.38.refs_1_), channel_id=1, source_target_pairs={{0,8},{4,12},{8,0},{12,4},{16,24},{20,28},{24,16},{28,20},{1,9},{5... | collective-permute-start | bytes 491528 | tf_op jit(solution)/shard_map/ppermute | solution.py:409
  13.9 7.4 %collective-permute-start.5 = (bf16[320,256]{1,0:T(8,128)(2,1)S(1)}, bf16[320,256]{1,0:T(8,128)(2,1)S(1)}, u32[]{:S(2)}, u32[]{:S(2)}) collective-permute-start(bf16[320,256]{1,0:T(8,128)(2,1)S(1)} %get-tuple-element.40.refs_1_), channel_id=1, source_target_pairs={{0,4},{4,0},{8,12},{12,8},{16,20},{20,16},{24,28},{28,24},{1,5},{5... | collective-permute-start | bytes 491528 | tf_op jit(solution)/shard_map/ppermute | solution.py:409
  14.5 6.6 %collective-permute-start.3 = (bf16[240,384]{1,0:T(8,128)(2,1)S(1)}, bf16[240,384]{1,0:T(8,128)(2,1)S(1)}, u32[]{:S(2)}, u32[]{:S(2)}) collective-permute-start(bf16[240,384]{1,0:T(8,128)(2,1)S(1)} %pad_maximum_fusion), channel_id=1, source_target_pairs={{0,16},{4,20},{8,24},{12,28},{16,0},{20,4},{24,8},{28,12},{1,17},{... | collective-permute-start | bytes 552968 | tf_op jit(solution)/shard_map/ppermute | solution.py:409
  16.0 5.4 %collective-permute-start.7 = (bf16[320,256]{1,0:T(8,128)(2,1)S(1)}, bf16[320,256]{1,0:T(8,128)(2,1)S(1)}, u32[]{:S(2)}, u32[]{:S(2)}) collective-permute-start(bf16[320,256]{1,0:T(8,128)(2,1)S(1)} %collective-permute-done.6.refs_3_), channel_id=1, source_target_pairs={{0,4},{4,0},{8,12},{12,8},{16,20},{20,16},{24,28},{28,24},{1,5},{5... | collective-permute-start | bytes 491528 | tf_op jit(solution)/shard_map/ppermute | solution.py:409
  17.3 5.4 %collective-permute-start.12 = (bf16[160,256]{1,0:T(8,128)(2,1)S(1)}, bf16[160,256]{1,0:T(8,128)(2,1)S(1)}, u32[]{:S(2)}, u32[]{:S(2)}) collective-permute-start(bf16[160,256]{1,0:T(8,128)(2,1)S(1)} %get-tuple-element.43), channel_id=1, source_target_pairs={{0,8},{4,12},{8,0},{12,4},{16,24},{20,28},{24,16},{28,20},{1,9},{5... | collective-permute-start | bytes 245768 | tf_op jit(solution)/shard_map/ppermute | solution.py:409
  18.9 3.8 %collective-permute-start.13 = (bf16[80,256]{1,0:T(8,128)(2,1)S(1)}, bf16[80,256]{1,0:T(8,128)(2,1)S(1)}, u32[]{:S(2)}, u32[]{:S(2)}) collective-permute-start(bf16[80,256]{1,0:T(8,128)(2,1)S(1)} %get-tuple-element.44), channel_id=1, source_target_pairs={{0,4},{4,0},{8,12},{12,8},{16,20},{20,16},{24,28},{28,24},{1,5},{5... | collective-permute-start | bytes 122888 | tf_op jit(solution)/shard_map/ppermute | solution.py:409
  22.7 8.9 %collective-permute-start.15 = (bf16[640,256]{1,0:T(8,128)(2,1)S(1)}, bf16[640,256]{1,0:T(8,128)(2,1)S(1)}, u32[]{:S(2)}, u32[]{:S(2)}) collective-permute-start(bf16[640,256]{1,0:T(8,128)(2,1)S(1)} %shard_map.71.refs_5_), channel_id=1, source_target_pairs={{0,8},{4,12},{8,0},{12,4},{16,24},{20,28},{24,16},{28,20},{1,9},{5... | collective-permute-start | bytes 983048 | tf_op jit(solution)/shard_map/ppermute | solution.py:409
  24.4 1.2 %collective-permute-start.18 = (bf16[80,256]{1,0:T(8,128)(2,1)S(1)}, bf16[80,256]{1,0:T(8,128)(2,1)S(1)}, u32[]{:S(2)}, u32[]{:S(2)}) collective-permute-start(bf16[80,256]{1,0:T(8,128)(2,1)S(1)} %slice.4), channel_id=1, source_target_pairs={{0,4},{4,0},{8,12},{12,8},{16,20},{20,16},{24,28},{28,24},{1,5},{5... | collective-permute-start | bytes 122888 | tf_op jit(solution)/shard_map/ppermute | solution.py:409
  27.0 8.1 %collective-permute-start.19 = (bf16[320,384]{1,0:T(8,128)(2,1)S(1)}, bf16[320,384]{1,0:T(8,128)(2,1)S(1)}, u32[]{:S(2)}, u32[]{:S(2)}) collective-permute-start(bf16[320,384]{1,0:T(8,128)(2,1)S(1)} %get-tuple-element.51), channel_id=1, source_target_pairs={{0,16},{4,20},{8,24},{12,28},{16,0},{20,4},{24,8},{28,12},{1,17},{... | collective-permute-start | bytes 737288 | tf_op jit(solution)/shard_map/ppermute | solution.py:409
  28.6 7.9 %collective-permute-start.14 = (bf16[640,256]{1,0:T(8,128)(2,1)S(1)}, bf16[640,256]{1,0:T(8,128)(2,1)S(1)}, u32[]{:S(2)}, u32[]{:S(2)}) collective-permute-start(bf16[640,256]{1,0:T(8,128)(2,1)S(1)} %shard_map.71.refs_5_), channel_id=1, source_target_pairs={{0,4},{4,0},{8,12},{12,8},{16,20},{20,16},{24,28},{28,24},{1,5},{5... | collective-permute-start | bytes 983048 | tf_op jit(solution)/shard_map/ppermute | solution.py:409
  31.6 4.9 %collective-permute-start.16 = (bf16[640,256]{1,0:T(8,128)(2,1)S(1)}, bf16[640,256]{1,0:T(8,128)(2,1)S(1)}, u32[]{:S(2)}, u32[]{:S(2)}) collective-permute-start(bf16[640,256]{1,0:T(8,128)(2,1)S(1)} %collective-permute-done.15.refs_7_), channel_id=1, source_target_pairs={{0,4},{4,0},{8,12},{12,8},{16,20},{20,16},{24,28},{28,24},{1,5},{5... | collective-permute-start | bytes 983048 | tf_op jit(solution)/shard_map/ppermute | solution.py:409
  31.6 7.3 %collective-permute-start.24 = (bf16[640,256]{1,0:T(8,128)(2,1)S(1)}, bf16[640,256]{1,0:T(8,128)(2,1)S(1)}, u32[]{:S(2)}, u32[]{:S(2)}) collective-permute-start(bf16[640,256]{1,0:T(8,128)(2,1)S(1)} %get-tuple-element.61), channel_id=1, source_target_pairs={{0,4},{4,0},{8,12},{12,8},{16,20},{20,16},{24,28},{28,24},{1,5},{5... | collective-permute-start | bytes 983048 | tf_op jit(solution)/shard_map/ppermute | solution.py:409
  32.1 3.1 %collective-permute-start.8 = (bf16[320,256]{1,0:T(8,128)(2,1)S(1)}, bf16[320,256]{1,0:T(8,128)(2,1)S(1)}, u32[]{:S(2)}, u32[]{:S(2)}) collective-permute-start(bf16[320,256]{1,0:T(8,128)(2,1)S(1)} %get-tuple-element.38.refs_1_), channel_id=1, source_target_pairs={{0,4},{4,0},{8,12},{12,8},{16,20},{20,16},{24,28},{28,24},{1,5},{5... | collective-permute-start | bytes 491528 | tf_op jit(solution)/shard_map/ppermute | solution.py:409
  35.1 1.4 %collective-permute-start.9 = (bf16[320,256]{1,0:T(8,128)(2,1)S(1)}, bf16[320,256]{1,0:T(8,128)(2,1)S(1)}, u32[]{:S(2)}, u32[]{:S(2)}) collective-permute-start(bf16[320,256]{1,0:T(8,128)(2,1)S(1)} %collective-permute-done.4.refs_5_.refs_3_), channel_id=1, source_target_pairs={{0,4},{4,0},{8,12},{12,8},{16,20},{20,16},{24,28},{28,24},{1,5},{5... | collective-permute-start | bytes 491528 | tf_op jit(solution)/shard_map/ppermute | solution.py:409
  35.2 5.8 %collective-permute-start.20 = (bf16[160,384]{1,0:T(8,128)(2,1)S(1)}, bf16[160,384]{1,0:T(8,128)(2,1)S(1)}, u32[]{:S(2)}, u32[]{:S(2)}) collective-permute-start(bf16[160,384]{1,0:T(8,128)(2,1)S(1)} %get-tuple-element.53), channel_id=1, source_target_pairs={{0,1},{1,0},{2,3},{3,2},{4,5},{5,4},{6,7},{7,6},{8,9},{9,8},{10,11... | collective-permute-start | bytes 368648 | tf_op jit(solution)/shard_map/ppermute | solution.py:412
  37.2 21.6 %copy-start = (bf16[1,1,16,16,320]{4,3,2,1,0:T(8,128)(2,1)S(1)}, bf16[1,1,16,16,320]{4,3,2,1,0:T(8,128)(2,1)}, u32[]{:S(2)}) copy-start(bf16[1,1,16,16,320]{4,3,2,1,0:T(8,128)(2,1)} %param.5) | copy-start | bytes 491524
  37.3 4.6 %collective-permute-start.17 = (bf16[160,256]{1,0:T(8,128)(2,1)S(1)}, bf16[160,256]{1,0:T(8,128)(2,1)S(1)}, u32[]{:S(2)}, u32[]{:S(2)}) collective-permute-start(bf16[160,256]{1,0:T(8,128)(2,1)S(1)} %get-tuple-element.47), channel_id=1, source_target_pairs={{0,16},{4,20},{8,24},{12,28},{16,0},{20,4},{24,8},{28,12},{1,17},{... | collective-permute-start | bytes 245768 | tf_op jit(solution)/shard_map/ppermute | solution.py:409
  38.9 9.6 %collective-permute-start.25 = (bf16[320,256]{1,0:T(8,128)(2,1)S(1)}, bf16[320,256]{1,0:T(8,128)(2,1)S(1)}, u32[]{:S(2)}, u32[]{:S(2)}) collective-permute-start(bf16[320,256]{1,0:T(8,128)(2,1)S(1)} %get-tuple-element.62), channel_id=1, source_target_pairs={{0,8},{4,12},{8,0},{12,4},{16,24},{20,28},{24,16},{28,20},{1,9},{5... | collective-permute-start | bytes 491528 | tf_op jit(solution)/shard_map/ppermute | solution.py:409
  41.8 5.1 %collective-permute-start.21 = (bf16[160,256]{1,0:T(8,128)(2,1)S(1)}, bf16[160,256]{1,0:T(8,128)(2,1)S(1)}, u32[]{:S(2)}, u32[]{:S(2)}) collective-permute-start(bf16[160,256]{1,0:T(8,128)(2,1)S(1)} %get-tuple-element.56), channel_id=1, source_target_pairs={{0,1},{1,0},{2,3},{3,2},{4,5},{5,4},{6,7},{7,6},{8,9},{9,8},{10,11... | collective-permute-start | bytes 245768 | tf_op jit(solution)/shard_map/ppermute | solution.py:412
  42.8 5.8 %collective-permute-start.23 = (bf16[80,384]{1,0:T(8,128)(2,1)S(1)}, bf16[80,384]{1,0:T(8,128)(2,1)S(1)}, u32[]{:S(2)}, u32[]{:S(2)}) collective-permute-start(bf16[80,384]{1,0:T(8,128)(2,1)S(1)} %get-tuple-element.59), channel_id=1, source_target_pairs={{0,2},{1,3},{2,0},{3,1},{4,6},{5,7},{6,4},{7,5},{8,10},{9,11},{10,... | collective-permute-start | bytes 184328 | tf_op jit(solution)/shard_map/ppermute | solution.py:412
  47.0 8.2 %collective-permute-start.22 = (bf16[160,256]{1,0:T(8,128)(2,1)S(1)}, bf16[160,256]{1,0:T(8,128)(2,1)S(1)}, u32[]{:S(2)}, u32[]{:S(2)}) collective-permute-start(bf16[160,256]{1,0:T(8,128)(2,1)S(1)} %get-tuple-element.58), channel_id=1, source_target_pairs={{0,2},{1,3},{2,0},{3,1},{4,6},{5,7},{6,4},{7,5},{8,10},{9,11},{10,... | collective-permute-start | bytes 245768 | tf_op jit(solution)/shard_map/ppermute | solution.py:412
  48.6 5.2 %collective-permute-start.26 = (bf16[80,384]{1,0:T(8,128)(2,1)S(1)}, bf16[80,384]{1,0:T(8,128)(2,1)S(1)}, u32[]{:S(2)}, u32[]{:S(2)}) collective-permute-start(bf16[80,384]{1,0:T(8,128)(2,1)S(1)} %shard_map.79.refs_2_), channel_id=1, source_target_pairs={{0,24},{4,28},{8,16},{12,20},{16,8},{20,12},{24,0},{28,4},{1,25},{... | collective-permute-start | bytes 184328 | tf_op jit(solution)/shard_map/ppermute | solution.py:409
  50.4 4.2 %collective-permute-start.27 = (bf16[80,384]{1,0:T(8,128)(2,1)S(1)}, bf16[80,384]{1,0:T(8,128)(2,1)S(1)}, u32[]{:S(2)}, u32[]{:S(2)}) collective-permute-start(bf16[80,384]{1,0:T(8,128)(2,1)S(1)} %shard_map.79.refs_2_), channel_id=1, source_target_pairs={{0,16},{4,20},{8,24},{12,28},{16,0},{20,4},{24,8},{28,12},{1,17},{... | collective-permute-start | bytes 184328 | tf_op jit(solution)/shard_map/ppermute | solution.py:409
  50.9 4.2 %collective-permute-start.28 = (bf16[80,384]{1,0:T(8,128)(2,1)S(1)}, bf16[80,384]{1,0:T(8,128)(2,1)S(1)}, u32[]{:S(2)}, u32[]{:S(2)}) collective-permute-start(bf16[80,384]{1,0:T(8,128)(2,1)S(1)} %shard_map.79.refs_2_), channel_id=1, source_target_pairs={{0,8},{4,12},{8,0},{12,4},{16,24},{20,28},{24,16},{28,20},{1,9},{5... | collective-permute-start | bytes 184328 | tf_op jit(solution)/shard_map/ppermute | solution.py:409
  55.2 3.6 %collective-permute-start.29 = (bf16[320,384]{1,0:T(8,128)(2,1)S(1)}, bf16[320,384]{1,0:T(8,128)(2,1)S(1)}, u32[]{:S(2)}, u32[]{:S(2)}) collective-permute-start(bf16[320,384]{1,0:T(8,128)(2,1)S(1)} %get-tuple-element.63.refs_0_), channel_id=1, source_target_pairs={{0,4},{4,0},{8,12},{12,8},{16,20},{20,16},{24,28},{28,24},{1,5},{5... | collective-permute-start | bytes 737288 | tf_op jit(solution)/shard_map/ppermute | solution.py:409
  55.3 5.8 %collective-permute-start.30 = (bf16[160,256]{1,0:T(8,128)(2,1)S(1)}, bf16[160,256]{1,0:T(8,128)(2,1)S(1)}, u32[]{:S(2)}, u32[]{:S(2)}) collective-permute-start(bf16[160,256]{1,0:T(8,128)(2,1)S(1)} %get-tuple-element.67.refs_0_), channel_id=1, source_target_pairs={{0,24},{4,28},{8,16},{12,20},{16,8},{20,12},{24,0},{28,4},{1,25},{... | collective-permute-start | bytes 245768 | tf_op jit(solution)/shard_map/ppermute | solution.py:409
  57.5 5.3 %collective-permute-start.31 = (bf16[160,256]{1,0:T(8,128)(2,1)S(1)}, bf16[160,256]{1,0:T(8,128)(2,1)S(1)}, u32[]{:S(2)}, u32[]{:S(2)}) collective-permute-start(bf16[160,256]{1,0:T(8,128)(2,1)S(1)} %get-tuple-element.67.refs_0_), channel_id=1, source_target_pairs={{0,16},{4,20},{8,24},{12,28},{16,0},{20,4},{24,8},{28,12},{1,17},{... | collective-permute-start | bytes 245768 | tf_op jit(solution)/shard_map/ppermute | solution.py:409
  58.0 4.9 %collective-permute-start.32 = (bf16[160,256]{1,0:T(8,128)(2,1)S(1)}, bf16[160,256]{1,0:T(8,128)(2,1)S(1)}, u32[]{:S(2)}, u32[]{:S(2)}) collective-permute-start(bf16[160,256]{1,0:T(8,128)(2,1)S(1)} %get-tuple-element.67.refs_0_), channel_id=1, source_target_pairs={{0,8},{4,12},{8,0},{12,4},{16,24},{20,28},{24,16},{28,20},{1,9},{5... | collective-permute-start | bytes 245768 | tf_op jit(solution)/shard_map/ppermute | solution.py:409
  62.9 1.7 %collective-permute-start.33 = (bf16[640,256]{1,0:T(8,128)(2,1)S(1)}, bf16[640,256]{1,0:T(8,128)(2,1)S(1)}, u32[]{:S(2)}, u32[]{:S(2)}) collective-permute-start(bf16[640,256]{1,0:T(8,128)(2,1)S(1)} %shard_map.82.refs_0_), channel_id=1, source_target_pairs={{0,4},{4,0},{8,12},{12,8},{16,20},{20,16},{24,28},{28,24},{1,5},{5... | collective-permute-start | bytes 983048 | tf_op jit(solution)/shard_map/ppermute | solution.py:409
